TPU v7x, 32 devices: a whole 2x2x4 slice. The times are simulated.
32 devices in a mesh: dp: 16 (over z, y, core), section: 2 (over x).
Axes of the slice: x: 2, y: 2, z: 4, core: 2. Of those that a mesh axis runs over, the one named last changes fastest.
Arguments:
- layer_inputs: bfloat16 [2, 2048, 4096], P('section', 'dp'), may hold values from -6 to 6
- top_grad: bfloat16 [2048, 4096], P('dp'), may hold values from -2.5 to 2.5
- value_grads: bfloat16 [2, 2048, 128], P('section', 'dp'), may hold values from -6 to 6
- weights: bfloat16 [2, 4096, 128], P('section'), may hold values from -0.09375 to 0.09375
- norm_gains: float32 [2, 4096], P('section'), may hold values from 0.5 to 1.5
- counts: int32 [128], P('dp'), may hold values from 1 to 16, as said below
Outputs:
- input_grads: bfloat16 [2, 2048, 4096], P('section', 'dp')
- weight_grads: float32 [2, 528384], P('section', 'dp')
Inputs may be any that keep to these rules, and one draw needn't show every extreme that they name: Entry m of a device's block of counts belongs to its m-th micro-batch; slots at or past the count are padding. Some micro-batch holds 16 live slots and some holds 1.
All inputs are finite; a program needn't handle non-finite values.
Results may differ from a plain program's by a relative error of at most 0.0034.
Values may be sent and summed in bfloat16 or wider, within the bound.
No kernel may reach another device: no remote copies, remote signals or barrier semaphores. Data moves between devices by JAX's collectives and lax.ppermute only.
A program may use at most 64 MiB of HBM per device.

v0:
```python
import math

import jax
import jax.numpy as jnp
from jax import lax
from jax.sharding import PartitionSpec as P

eps_norm = 1e-05


def from_behind(array, axis, by):
    peers = lax.axis_size(axis)
    pairs = [(i, i + by) for i in range(peers) if 0 <= i + by < peers]
    return lax.ppermute(array, axis, pairs)


def run_chain(top_blocks, branch_blocks):
    groups = top_blocks.shape[0]
    section_here = lax.axis_index("section")
    last_section = lax.axis_size("section") - 1
    delay = last_section - section_here

    def advance(counter, carry):
        sent, result = carry
        received = from_behind(sent, "section", -1)
        micro_here = counter - delay
        picked = jnp.clip(micro_here, 0, groups - 1)
        top_piece = lax.dynamic_index_in_dim(top_blocks, picked, 0, keepdims=False)
        branch_piece = lax.dynamic_index_in_dim(branch_blocks, picked, 0, keepdims=False)
        incoming = jnp.where(section_here == last_section, top_piece, received)
        updated = (incoming.astype(jnp.float32) + branch_piece).astype(jnp.bfloat16)
        usable = (micro_here >= 0) & (micro_here < groups)
        current = lax.dynamic_index_in_dim(result, picked, 0, keepdims=False)
        result = lax.dynamic_update_index_in_dim(
            result, jnp.where(usable, updated, current), picked, 0
        )
        return (updated, result)

    start = (jnp.zeros(top_blocks.shape[1:], jnp.bfloat16), jnp.zeros_like(top_blocks))
    final_pair = lax.fori_loop(0, groups + last_section, advance, start)
    return final_pair[1]


def weight_owned(unit, back, normed, masked, factor):
    weight_term = lax.dot_general(
        normed, masked, (((0,), (0,)), ((), ())), preferred_element_type=jnp.float32
    )
    gain_term = jnp.sum(unit * back, axis=0)
    packed_terms = jnp.concatenate([gain_term, weight_term.reshape(-1)]) * factor
    return lax.psum_scatter(packed_terms, "dp", scatter_dimension=0, tiled=True)


def shards(layer_inputs, top_grad, value_grads, weights, norm_gains, counts):
    row_count = layer_inputs.shape[1]
    width = layer_inputs.shape[2]
    micro_count = counts.shape[0]
    slots = row_count // micro_count
    slot_index = jnp.arange(slots, dtype=jnp.int32)
    live = (slot_index[None, :] < counts[:, None]).reshape(row_count)
    factor = 1.0 / math.sqrt(row_count * lax.axis_size("dp"))
    inputs_wide = layer_inputs[0].astype(jnp.float32)
    scale = lax.rsqrt(jnp.mean(inputs_wide * inputs_wide, axis=1, keepdims=True) + eps_norm)
    unit = inputs_wide * scale
    gain_row = norm_gains[0]
    normed = (unit * gain_row).astype(jnp.bfloat16)
    masked = jnp.where(live[:, None], value_grads[0], jnp.zeros((), value_grads.dtype))
    back = lax.dot_general(
        masked, weights[0], (((1,), (1,)), ((), ())), preferred_element_type=jnp.float32
    )
    branch = scale * (
        gain_row * back - unit * jnp.mean(unit * gain_row * back, axis=1, keepdims=True)
    )
    group_size = 2
    top_blocks = top_grad.reshape(micro_count // group_size, group_size * slots, width)
    branch_blocks = branch.reshape(micro_count // group_size, group_size * slots, width)
    owned = weight_owned(unit, back, normed, masked, factor)
    chained = run_chain(top_blocks, branch_blocks)
    return (chained.reshape(1, row_count, width), owned[None, :])


def solution(mesh):
    placed = (
        P("section", "dp", None),
        P("dp", None),
        P("section", "dp", None),
        P("section", None, None),
        P("section", None),
        P("dp"),
    )
    return jax.shard_map(
        shards,
        mesh=mesh,
        in_specs=placed,
        out_specs=(P("section", "dp", None), P("section", "dp")),
        check_vma=False,
    )
```

profile of v0, /device:TPU:0, one launch (start us, length us, event | category | flops | bytes accessed | tf_op | source)
XLA Modules:
  0.0 174.2 jit_solution(8330674958703791808)
XLA Ops:
  7.2 0.0 copy-start
  7.2 0.0 copy-start.1
  7.2 0.0 copy-start.3
  7.2 0.0 copy-start.4
  7.2 0.0 all-reduce.3.cloned.1.call-start
  7.3 1.7 fusion.11
  8.9 0.7 iota_compare_fusion
  9.7 0.1 lt.48
  9.7 1.8 %convolution_bitcast_fusion = f32[524288]{0:T(1024)S(1)} fusion(bf16[1,128,4096]{2,1,0:T(8,128)(2,1)} %param.8, f32[4096]{0:T(1024)} %bitcast.69, f32[128]{0:T(128)S(1)} %add_rsqrt_fusion, bf16[1,128,128]{2,1,0:T(8,128)(2,1)} %param.10, pred[128]{0:T(512)(128)(4,1)S(1)} %lt.48), kind=kOutput, calls=%fused_computation.7 | convolution fusion | flops 136331264 | bytes 3195520 | tf_op jit(solution)/shard_map/dot_general | solution.py:45
  11.6 0.0 copy-done
  11.6 0.0 copy-done.1
  11.6 0.0 copy-done.3
  11.6 0.0 copy-done.4
  11.6 2.0 %fusion.10 = (f32[4096]{0:T(1024)S(1)}, f32[128]{0:T(128)S(1)}, f32[128,4096]{1,0:T(8,128)}) fusion(bf16[1,128,4096]{2,1,0:T(8,128)(2,1)S(1)} %copy-done.1, f32[128]{0:T(128)S(1)} %add_rsqrt_fusion, f32[4096]{0:T(1024)S(1)} %bitcast.70, bf16[1,4096,128]{2,1,0:T(8,128)(2,1)S(1)} %copy-done, bf16[1,128,128]{2,1,0:T(8,128)(2,1)S(1)} %copy-done.4, ...), kind=kOutput, calls=%fused_computation.20 | convolution fusion | flops 137899904 | bytes 4260992 | tf_op jit(solution)/shard_map/dot_general | solution.py:67
  13.6 1.5 maximum_multiply_fusion
  15.1 0.0 copy-start.5
  15.1 0.0 all-reduce.3.cloned.1.call-update
  15.1 0.6 copy-done.5
  15.7 0.6 dynamic-slice
  16.9 3.4 %fusion.9 = f32[128,4096]{1,0:T(8,128)} fusion(bf16[1,128,4096]{2,1,0:T(8,128)(2,1)S(1)} %copy-done.1, f32[128,4096]{1,0:T(8,128)} %get-tuple-element.215, f32[128]{0:T(128)S(1)} %broadcast_multiply_fusion, f32[4096]{0:T(1024)S(1)} %bitcast.71, f32[128]{0:T(128)S(1)} %add_rsqrt_fusion), kind=kLoop, calls=%fused_computation.19 | loop fusion | flops 3145728 | bytes 5260288 | tf_op jit(solution)/shard_map/mul | solution.py:70
  20.3 95.5 %all-reduce.3.cloned.1.call-done = f32[528384]{0:T(1024)} async-done(((f32[528384]{0:T(1024)}), f32[528384]{0:T(1024)}) %all-reduce.3.cloned.1.call-update) | async-done | bytes 2113552
  115.8 1.0 dynamic-slice.1
  116.8 0.7 broadcast_in_dim.39
  117.6 0.1 broadcast_in_dim.36
  117.7 48.7 %while.18 = (s32[]{:T(128)}, bf16[32,4096]{1,0:T(8,128)(2,1)S(1)}, bf16[4,32,4096]{2,1,0:T(8,128)(2,1)S(1)}, pred[]{:T(512)}, s32[]{:T(128)}, /*index=5*/bf16[4,...) while((s32[]{:T(128)}, bf16[32,4096]{1,0:T(8,128)(2,1)S(1)}, ...), condition=%wide.region_3.4_spmd.clone, body=%wide.region_2.3_spmd.clone.sunk | while | flops 786441 | bytes 3932386 | solution.py:40
  117.7 1.3 collective-permute-start
  119.1 7.8 %collective-permute-done = bf16[32,4096]{1,0:T(8,128)(2,1)S(1)} collective-permute-done((bf16[32,4096]{1,0:T(8,128)(2,1)S(1)}, bf16[32,4096]{1,0:T(8,128)(2,1)S(1)}, u32[]{:S(2)}, u32[]{:S(2)}) %collective-permute-start) | collective-permute-done | bytes 262176 | tf_op jit(solution)/shard_map/while/body/eval_jaxpr/ppermute | solution.py:14
  126.9 1.2 bitcast_dynamic-update-slice_fusion.2
  128.2 1.3 collective-permute-start
  129.5 6.9 %collective-permute-done = bf16[32,4096]{1,0:T(8,128)(2,1)S(1)} collective-permute-done((bf16[32,4096]{1,0:T(8,128)(2,1)S(1)}, bf16[32,4096]{1,0:T(8,128)(2,1)S(1)}, u32[]{:S(2)}, u32[]{:S(2)}) %collective-permute-start) | collective-permute-done | bytes 262176 | tf_op jit(solution)/shard_map/while/body/eval_jaxpr/ppermute | solution.py:14
  136.5 1.2 bitcast_dynamic-update-slice_fusion.2
  137.8 1.3 collective-permute-start
  139.1 6.9 %collective-permute-done = bf16[32,4096]{1,0:T(8,128)(2,1)S(1)} collective-permute-done((bf16[32,4096]{1,0:T(8,128)(2,1)S(1)}, bf16[32,4096]{1,0:T(8,128)(2,1)S(1)}, u32[]{:S(2)}, u32[]{:S(2)}) %collective-permute-start) | collective-permute-done | bytes 262176 | tf_op jit(solution)/shard_map/while/body/eval_jaxpr/ppermute | solution.py:14
  146.0 1.2 bitcast_dynamic-update-slice_fusion.2
  147.3 1.3 collective-permute-start
  148.6 6.9 %collective-permute-done = bf16[32,4096]{1,0:T(8,128)(2,1)S(1)} collective-permute-done((bf16[32,4096]{1,0:T(8,128)(2,1)S(1)}, bf16[32,4096]{1,0:T(8,128)(2,1)S(1)}, u32[]{:S(2)}, u32[]{:S(2)}) %collective-permute-start) | collective-permute-done | bytes 262176 | tf_op jit(solution)/shard_map/while/body/eval_jaxpr/ppermute | solution.py:14
  155.6 1.2 bitcast_dynamic-update-slice_fusion.2
  156.8 1.3 collective-permute-start
  158.2 6.9 %collective-permute-done = bf16[32,4096]{1,0:T(8,128)(2,1)S(1)} collective-permute-done((bf16[32,4096]{1,0:T(8,128)(2,1)S(1)}, bf16[32,4096]{1,0:T(8,128)(2,1)S(1)}, u32[]{:S(2)}, u32[]{:S(2)}) %collective-permute-start) | collective-permute-done | bytes 262176 | tf_op jit(solution)/shard_map/while/body/eval_jaxpr/ppermute | solution.py:14
  165.1 1.2 bitcast_dynamic-update-slice_fusion.2
  166.4 0.0 copy-start.2
  166.4 1.0 copy-done.2
  (13 shorter events, 0.3 us)
Async XLA Ops:
  7.2 4.4 %copy-start = (bf16[1,4096,128]{2,1,0:T(8,128)(2,1)S(1)}, bf16[1,4096,128]{2,1,0:T(8,128)(2,1)}, u32[]{:S(2)}) copy-start(bf16[1,4096,128]{2,1,0:T(8,128)(2,1)} %param.11) | copy-start | bytes 3145732
  7.2 4.4 %copy-start.1 = (bf16[1,128,4096]{2,1,0:T(8,128)(2,1)S(1)}, bf16[1,128,4096]{2,1,0:T(8,128)(2,1)}, u32[]{:S(2)}) copy-start(bf16[1,128,4096]{2,1,0:T(8,128)(2,1)} %param.8) | copy-start | bytes 3145732
  7.2 4.4 %copy-start.3 = (f32[1,4096]{1,0:T(1,128)S(1)}, f32[1,4096]{1,0:T(1,128)}, u32[]{:S(2)}) copy-start(f32[1,4096]{1,0:T(1,128)} %param.12) | copy-start | bytes 49156
  7.2 4.4 %copy-start.4 = (bf16[1,128,128]{2,1,0:T(8,128)(2,1)S(1)}, bf16[1,128,128]{2,1,0:T(8,128)(2,1)}, u32[]{:S(2)}) copy-start(bf16[1,128,128]{2,1,0:T(8,128)(2,1)} %param.10) | copy-start | bytes 98308
  7.2 108.6 %all-reduce.3.cloned.1.call-start = ((), (), s32[]{:S(2)}) async-start(), calls=%async_computation | async-start | bytes 4227072
  15.1 0.7 copy-start.5
  117.7 9.2 %collective-permute-start = (bf16[32,4096]{1,0:T(8,128)(2,1)S(1)}, bf16[32,4096]{1,0:T(8,128)(2,1)S(1)}, u32[]{:S(2)}, u32[]{:S(2)}) collective-permute-start(bf16[32,4096]{1,0:T(8,128)(2,1)S(1)} %broadcast_select_fusion.5), channel_id=1, source_target_pairs={{1,0},{3,2},{5,4},{7,6},{9,8},{11,10},{13,12},{15,14},{17,16},{19,... | collective-permute-start | bytes 786440 | tf_op jit(solution)/shard_map/while/body/eval_jaxpr/ppermute | solution.py:14
  128.2 8.3 %collective-permute-start = (bf16[32,4096]{1,0:T(8,128)(2,1)S(1)}, bf16[32,4096]{1,0:T(8,128)(2,1)S(1)}, u32[]{:S(2)}, u32[]{:S(2)}) collective-permute-start(bf16[32,4096]{1,0:T(8,128)(2,1)S(1)} %broadcast_select_fusion.5), channel_id=1, source_target_pairs={{1,0},{3,2},{5,4},{7,6},{9,8},{11,10},{13,12},{15,14},{17,16},{19,... | collective-permute-start | bytes 786440 | tf_op jit(solution)/shard_map/while/body/eval_jaxpr/ppermute | solution.py:14
  137.8 8.3 %collective-permute-start = (bf16[32,4096]{1,0:T(8,128)(2,1)S(1)}, bf16[32,4096]{1,0:T(8,128)(2,1)S(1)}, u32[]{:S(2)}, u32[]{:S(2)}) collective-permute-start(bf16[32,4096]{1,0:T(8,128)(2,1)S(1)} %broadcast_select_fusion.5), channel_id=1, source_target_pairs={{1,0},{3,2},{5,4},{7,6},{9,8},{11,10},{13,12},{15,14},{17,16},{19,... | collective-permute-start | bytes 786440 | tf_op jit(solution)/shard_map/while/body/eval_jaxpr/ppermute | solution.py:14
  147.3 8.3 %collective-permute-start = (bf16[32,4096]{1,0:T(8,128)(2,1)S(1)}, bf16[32,4096]{1,0:T(8,128)(2,1)S(1)}, u32[]{:S(2)}, u32[]{:S(2)}) collective-permute-start(bf16[32,4096]{1,0:T(8,128)(2,1)S(1)} %broadcast_select_fusion.5), channel_id=1, source_target_pairs={{1,0},{3,2},{5,4},{7,6},{9,8},{11,10},{13,12},{15,14},{17,16},{19,... | collective-permute-start | bytes 786440 | tf_op jit(solution)/shard_map/while/body/eval_jaxpr/ppermute | solution.py:14
  156.8 8.3 %collective-permute-start = (bf16[32,4096]{1,0:T(8,128)(2,1)S(1)}, bf16[32,4096]{1,0:T(8,128)(2,1)S(1)}, u32[]{:S(2)}, u32[]{:S(2)}) collective-permute-start(bf16[32,4096]{1,0:T(8,128)(2,1)S(1)} %broadcast_select_fusion.5), channel_id=1, source_target_pairs={{1,0},{3,2},{5,4},{7,6},{9,8},{11,10},{13,12},{15,14},{17,16},{19,... | collective-permute-start | bytes 786440 | tf_op jit(solution)/shard_map/while/body/eval_jaxpr/ppermute | solution.py:14
  166.4 1.0 copy-start.2
Sparse Core Ops, SparseCore 0:
  15.2 100.5 all-reduce.2
where the time goes:
time: 175 us; the launch traced here: 174 us
  waiting for transfers between devices  131 us (75%)
  between operations  14.8 us (8%)
  other arithmetic  13.6 us (8%)
  starting transfers between devices  6.5 us (4%)
  local copies, waits for them, and re-layouts  4.24 us (2%)
  matrix products  3.77 us (2%)
    unnamed x2, waiting for transfers between devices  95.5 us
    ppermute x5, waiting for transfers between devices, from_behind(): return lax.ppermute(array, axis, pairs)  35.5 us
    ppermute x5, starting transfers between devices, from_behind(): return lax.ppermute(array, axis, pairs)  6.46 us
    dynamic_update_slice x5, other arithmetic, advance(): lax.dynamic_update_index_in_dim(result, jnp.where(usable, updated, curren...  6.16 us
  transfers between devices with their start and end apart: 6, of which 6 were waited for; matrix products, arithmetic and copies ran while one was open for 2% of the time, Pallas kernels for 0%

commit v1 on v0

v1 whole, which is shorter than its diff:
```python
import functools
import math

import jax
import jax.numpy as jnp
from jax import lax
from jax.experimental import pallas as pl
from jax.experimental.pallas import tpu as pltpu
from jax.sharding import PartitionSpec as P

eps_norm = 1e-05
lanes = 128
tile_width = 512
pair = 2
f32 = jnp.float32
bf16 = jnp.bfloat16
contract_last = (((1,), (1,)), ((), ()))
contract_rows = (((0,), (0,)), ((), ()))


def branch_kernel(first, slots, counts, x, top, v, w, gain, sent, branch, normed, masked, gain_out, back):
    rows, width = sent.shape
    slot = lax.broadcasted_iota(jnp.int32, (slots, v.shape[2]), 0)
    pieces = []
    for k in range(rows // slots):
        piece = v[0, k * slots : (k + 1) * slots, :]
        pieces.append(jnp.where(slot < counts[first + k], piece, jnp.zeros_like(piece)))
    values = jnp.concatenate(pieces, axis=0)
    masked[...] = values
    squares = jnp.zeros((rows, lanes), f32)
    products = jnp.zeros((rows, lanes), f32)
    tiles = [pl.ds(at, tile_width) for at in range(0, width, tile_width)]
    for cut in tiles:
        wide = x[0, :, cut].astype(f32)
        here = lax.dot_general(values, w[0, cut, :], contract_last, preferred_element_type=f32)
        back[:, cut] = here
        square = wide * wide
        product = wide * here * gain[:, cut]
        for at in range(0, tile_width, lanes):
            squares += square[:, at : at + lanes]
            products += product[:, at : at + lanes]
    scale = lax.rsqrt(jnp.sum(squares, axis=1, keepdims=True) / width + eps_norm)
    pull = scale * jnp.sum(products, axis=1, keepdims=True) / width
    for cut in tiles:
        unit = x[0, :, cut].astype(f32) * scale
        here = back[:, cut]
        scaled = gain[:, cut]
        gain_out[:, cut] = jnp.sum(unit * here, axis=0, keepdims=True)
        normed[:, cut] = (unit * scaled).astype(bf16)
        own = scale * (scaled * here - unit * pull)
        branch[:, cut] = own
        sent[:, cut] = (top[:, cut].astype(f32) + own).astype(bf16)


def branch_chunk(chunk, rows, slots, counts, x, top, v, w, gain):
    width = x.shape[2]
    depth = v.shape[2]
    first = chunk * rows // slots
    return pl.pallas_call(
        functools.partial(branch_kernel, first, slots),
        grid=(1,),
        in_specs=[
            pl.BlockSpec(memory_space=pltpu.SMEM),
            pl.BlockSpec((1, rows, width), lambda i: (0, chunk, 0)),
            pl.BlockSpec((rows, width), lambda i: (chunk, 0)),
            pl.BlockSpec((1, rows, depth), lambda i: (0, chunk, 0)),
            pl.BlockSpec(w.shape, lambda i: (0, 0, 0)),
            pl.BlockSpec(gain.shape, lambda i: (0, 0)),
        ],
        out_specs=[
            pl.BlockSpec((rows, width), lambda i: (0, 0)),
            pl.BlockSpec((rows, width), lambda i: (0, 0)),
            pl.BlockSpec((rows, width), lambda i: (0, 0)),
            pl.BlockSpec((rows, depth), lambda i: (0, 0)),
            pl.BlockSpec((1, width), lambda i: (0, 0)),
        ],
        out_shape=[
            jax.ShapeDtypeStruct((rows, width), bf16),
            jax.ShapeDtypeStruct((rows, width), f32),
            jax.ShapeDtypeStruct((rows, width), bf16),
            jax.ShapeDtypeStruct((rows, depth), bf16),
            jax.ShapeDtypeStruct((1, width), f32),
        ],
        scratch_shapes=[pltpu.VMEM((rows, width), f32)],
        compiler_params=pltpu.CompilerParams(vmem_limit_bytes=32 << 20),
        cost_estimate=pl.CostEstimate(flops=2 * rows * width * depth, bytes_accessed=4 << 20, transcendentals=0),
    )(counts, x, top, v, w, gain)


def finish_kernel(start, is_last, top, received, branch, *rest):
    out = rest[-1]
    rows, width = branch.shape
    last = is_last[0] == 1
    for at in range(0, width, tile_width):
        cut = pl.ds(at, tile_width)
        incoming = jnp.where(last, top[:, cut].astype(f32), received[:, cut].astype(f32))
        out[0, :, cut] = (incoming + branch[:, cut]).astype(bf16)


def finish_chunk(chunk, is_last, top, received, branch, previous):
    rows, width = branch.shape
    in_specs = [
        pl.BlockSpec(memory_space=pltpu.SMEM),
        pl.BlockSpec((rows, width), lambda i: (chunk, 0)),
        pl.BlockSpec((rows, width), lambda i: (0, 0)),
        pl.BlockSpec((rows, width), lambda i: (0, 0)),
    ]
    operands = [is_last, top, received, branch]
    aliases = {}
    if previous is not None:
        in_specs.append(pl.BlockSpec(memory_space=pl.ANY))
        operands.append(previous)
        aliases = {4: 0}
    return pl.pallas_call(
        functools.partial(finish_kernel, chunk),
        grid=(1,),
        in_specs=in_specs,
        out_specs=pl.BlockSpec((1, rows, width), lambda i: (0, chunk, 0)),
        out_shape=jax.ShapeDtypeStruct((1,) + top.shape, bf16),
        input_output_aliases=aliases,
        compiler_params=pltpu.CompilerParams(vmem_limit_bytes=32 << 20),
        cost_estimate=pl.CostEstimate(flops=rows * width, bytes_accessed=8 * rows * width, transcendentals=0),
    )(*operands)


def terms_kernel(chunks, owned_rows, core, *refs):
    normed = refs[:chunks]
    masked = refs[chunks : 2 * chunks]
    gains = refs[2 * chunks : 3 * chunks]
    keep, give, total = refs[3 * chunks :]
    width = normed[0].shape[1]
    values = jnp.concatenate([m[...] for m in masked], axis=0)
    gain_rows = width // lanes
    gain_sum = sum(g[...] for g in gains)
    for k in range(gain_rows):
        total[k : k + 1, :] = gain_sum[:, k * lanes : (k + 1) * lanes]
    for at in range(0, width, tile_width):
        cut = pl.ds(at, tile_width)
        tall = jnp.concatenate([n[:, cut] for n in normed], axis=0)
        total[gain_rows + at : gain_rows + at + tile_width, :] = lax.dot_general(
            tall, values, contract_rows, preferred_element_type=f32
        )
    even_core = core[0] == 0
    padded = keep.shape[1]
    for j in range(keep.shape[0]):
        even = total[2 * j * owned_rows : 2 * j * owned_rows + owned_rows, :]
        odd = total[(2 * j + 1) * owned_rows : (2 * j + 2) * owned_rows, :]
        keep[j, :owned_rows, :] = jnp.where(even_core, even, odd)
        give[j, :owned_rows, :] = jnp.where(even_core, odd, even)
        if padded > owned_rows:
            blank = jnp.zeros((padded - owned_rows, lanes), f32)
            keep[j, owned_rows:, :] = blank
            give[j, owned_rows:, :] = blank


def pair_terms(core, normed, masked, gains, owned_rows, owners):
    chunks = len(normed)
    depth = masked[0].shape[1]
    width = normed[0].shape[1]
    padded = -(-owned_rows // 16) * 16
    half = jax.ShapeDtypeStruct((owners // pair, padded, lanes), f32)
    everywhere = pl.BlockSpec(memory_space=pltpu.VMEM)
    return pl.pallas_call(
        functools.partial(terms_kernel, chunks, owned_rows),
        in_specs=[pl.BlockSpec(memory_space=pltpu.SMEM)] + [everywhere] * (3 * chunks),
        out_specs=[everywhere, everywhere],
        out_shape=[half, half],
        scratch_shapes=[pltpu.VMEM((owners * owned_rows, lanes), f32)],
        compiler_params=pltpu.CompilerParams(vmem_limit_bytes=32 << 20),
        cost_estimate=pl.CostEstimate(
            flops=2 * depth * width * depth, bytes_accessed=6 << 20, transcendentals=0
        ),
    )(core, *normed, *masked, *gains)


def weight_owned(normed, masked, gains, factor):
    owners = lax.axis_size("dp")
    width = normed[0].shape[1]
    depth = masked[0].shape[1]
    elements = width + width * depth
    owned = elements // owners
    if depth != lanes or owned % lanes or owners % pair:
        weight_term = lax.dot_general(
            jnp.concatenate(normed, axis=0),
            jnp.concatenate(masked, axis=0),
            contract_rows,
            preferred_element_type=f32,
        )
        flat = jnp.concatenate([sum(gains).reshape(-1), weight_term.reshape(-1)]) * factor
        return lax.psum_scatter(flat, "dp", scatter_dimension=0, tiled=True)
    core = (lax.axis_index("dp") % pair).astype(jnp.int32).reshape(1)
    keep, give = pair_terms(core, normed, masked, gains, owned // lanes, owners)
    taken = lax.ppermute(give, "dp", [(i, i ^ 1) for i in range(owners)])
    chip = (keep + taken).astype(bf16)
    groups = [[i for i in range(owners) if i % pair == c] for c in range(pair)]
    landed = lax.all_to_all(chip, "dp", 0, 0, axis_index_groups=groups, tiled=True)
    total = jnp.sum(landed.astype(f32), axis=0) * factor
    return total[: owned // lanes].reshape(owned)


def shards(layer_inputs, top_grad, value_grads, weights, norm_gains, counts):
    row_count = layer_inputs.shape[1]
    micro_count = counts.shape[0]
    slots = row_count // micro_count
    factor = 1.0 / math.sqrt(row_count * lax.axis_size("dp"))
    sections = lax.axis_size("section")
    section_here = lax.axis_index("section")
    is_last = (section_here == sections - 1).astype(jnp.int32).reshape(1)
    chunks = 4 if micro_count % 4 == 0 else 1
    rows = row_count // chunks
    sent, branch, normed, masked, gains = zip(
        *[
            branch_chunk(c, rows, slots, counts, layer_inputs, top_grad, value_grads, weights, norm_gains)
            for c in range(chunks)
        ]
    )
    received = list(sent)
    for hop in range(sections - 1):
        target = sections - 2 - hop
        for c in range(chunks):
            outgoing = sent[c] if hop == 0 else (received[c].astype(f32) + branch[c]).astype(bf16)
            landed = lax.ppermute(outgoing, "section", [(target + 1, target)])
            received[c] = landed if hop == 0 else jnp.where(section_here == target, landed, received[c])
    owned = weight_owned(normed, masked, gains, factor)
    result = None
    for c in range(chunks):
        result = finish_chunk(c, is_last, top_grad, received[c], branch[c], result)
    return (result, owned[None, :])


def solution(mesh):
    placed = (
        P("section", "dp", None),
        P("dp", None),
        P("section", "dp", None),
        P("section", None, None),
        P("section", None),
        P("dp"),
    )
    return jax.shard_map(
        shards,
        mesh=mesh,
        in_specs=placed,
        out_specs=(P("section", "dp", None), P("section", "dp")),
        check_vma=False,
    )
```

time: 175 us -> 56.3 us (0.32)
  waiting for transfers between devices: 131 us -> 19 us
  between operations: 14.8 us -> 0.73 us
  Pallas kernels: 0 us -> 13.5 us
  other arithmetic: 13.6 us -> 2.08 us
  starting transfers between devices: 6.5 us -> 13 us
  matrix products: 3.77 us -> 0 us
  local copies, waits for them, and re-layouts: 4.24 us -> 7.29 us
    unnamed x2 -> x0, waiting for transfers between devices: 95.5 us -> none
    ppermute x5, waiting for transfers between devices: 35.5 us -> 19 us  [the longest x4 16.6 us: shards(): landed = lax.ppermute(outgoing, 'section', [(target + 1, target)])]
    pallas_call x0 -> x9, Pallas kernels: none -> 13.5 us  [the longest x4 6.91 us: branch_chunk(): pl.pallas_call(functools.partial(branch_kernel, first, slots), grid=(1,),...]
    all_to_all x0 -> x1, starting transfers between devices: none -> 7.34 us  [weight_owned(): lax.all_to_all(chip, 'dp', 0, 0, axis_index_groups=groups, tiled=True)]
    dynamic_update_slice x5 -> x0, other arithmetic: 6.16 us -> none  [advance(): lax.dynamic_update_index_in_dim(result, jnp.where(usable, updated, curren...]
    mul x2 -> x0, other arithmetic: 4.89 us -> none  [the longest x1 3.39 us: shards(): scale * (gain_row * back - unit * jnp.mean(unit * gain_row * back, axis=1...]
    unnamed x14 -> x17, local copies, waits for them, and re-layouts: 3.18 us -> 7.29 us
    dot_general x2 -> x0, matrix products: 3.77 us -> none  [the longest x1 1.96 us: shards(): lax.dot_general(masked, weights[0], (((1,), (1,)), ((), ())), preferred_e...]
  transfers between devices with their start and end apart: 6 -> 6, of which waited for: 6 -> 5; matrix products, arithmetic and copies ran while one was open for 2% -> 0% of each run, Pallas kernels for 0% -> 11%
where the time goes in v1:
time: 56.3 us; the launch traced here: 55.6 us
  waiting for transfers between devices  19 us (34%)
  Pallas kernels  13.5 us (24%)
  starting transfers between devices  13 us (23%)
  local copies, waits for them, and re-layouts  7.29 us (13%)
  other arithmetic  2.08 us (4%)
  between operations  0.73 us (1%)
    ppermute x4, waiting for transfers between devices, shards(): landed = lax.ppermute(outgoing, 'section', [(target + 1, target)])  16.6 us
    all_to_all x1, starting transfers between devices, weight_owned(): lax.all_to_all(chip, 'dp', 0, 0, axis_index_groups=groups, tiled=True)  7.34 us
    unnamed x17, local copies, waits for them, and re-layouts  7.29 us
    pallas_call x4, Pallas kernels, branch_chunk(): pl.pallas_call(functools.partial(branch_kernel, first, slots), grid=(1,),...  6.91 us
    pallas_call x4, Pallas kernels, finish_chunk(): pl.pallas_call(functools.partial(finish_kernel, chunk), grid=(1,), in_spe...  5.98 us
    ppermute x4, starting transfers between devices, shards(): landed = lax.ppermute(outgoing, 'section', [(target + 1, target)])  5.16 us
    ppermute x1, waiting for transfers between devices, weight_owned(): taken = lax.ppermute(give, 'dp', [(i, i ^ 1) for i in range(owners)])  2.38 us
    reduce_sum x1, other arithmetic, weight_owned(): total = jnp.sum(landed.astype(f32), axis=0) * factor  1.14 us
  transfers between devices with their start and end apart: 6, of which 5 were waited for; matrix products, arithmetic and copies ran while one was open for 0% of the time, Pallas kernels for 11%

profile of v1, /device:TPU:0, one launch (start us, length us, event | category | flops | bytes accessed | tf_op | source)
XLA Modules:
  0.0 55.6 jit_solution(2568111663418143358)
XLA Ops:
  0.6 0.0 copy-start
  0.7 1.2 %copy-done = bf16[128,4096]{1,0:T(8,128)(2,1)S(1)} copy-done((bf16[128,4096]{1,0:T(8,128)(2,1)S(1)}, bf16[128,4096]{1,0:T(8,128)(2,1)}, u32[]{:S(2)}) %copy-start) | copy-done | bytes 1048600
  1.9 0.0 copy-start.2
  1.9 1.2 %copy-done.2 = bf16[1,128,4096]{2,1,0:T(8,128)(2,1)S(1)} copy-done((bf16[1,128,4096]{2,1,0:T(8,128)(2,1)S(1)}, bf16[1,128,4096]{2,1,0:T(8,128)(2,1)}, u32[]{:S(2)}) %copy-start.2) | copy-done | bytes 1048600
  3.1 0.0 copy-start.3
  3.1 1.2 %copy-done.3 = bf16[1,4096,128]{2,1,0:T(8,128)(2,1)S(1)} copy-done((bf16[1,4096,128]{2,1,0:T(8,128)(2,1)S(1)}, bf16[1,4096,128]{2,1,0:T(8,128)(2,1)}, u32[]{:S(2)}) %copy-start.3) | copy-done | bytes 1048600
  4.3 0.0 copy-start.4
  4.3 0.8 %copy-done.4 = bf16[1,128,128]{2,1,0:T(8,128)(2,1)S(1)} copy-done((bf16[1,128,128]{2,1,0:T(8,128)(2,1)S(1)}, bf16[1,128,128]{2,1,0:T(8,128)(2,1)}, u32[]{:S(2)}) %copy-start.4) | copy-done | bytes 32792
  5.1 0.0 copy-start.5
  5.1 0.7 %copy-done.5 = f32[1,4096]{1,0:T(1,128)S(1)} copy-done((f32[1,4096]{1,0:T(1,128)S(1)}, f32[1,4096]{1,0:T(1,128)}, u32[]{:S(2)}) %copy-start.5) | copy-done | bytes 16408
  5.8 0.0 copy-start.6
  5.8 0.7 %copy-done.6 = s32[8]{0:T(128)S(1)} copy-done((s32[8]{0:T(128)S(1)}, s32[8]{0:T(128)}, u32[]{:S(2)}) %copy-start.6) | copy-done | bytes 56
  6.5 1.9 %shard_map.78 = (bf16[32,4096]{1,0:T(8,128)(2,1)}, f32[32,4096]{1,0:T(8,128)S(1)}, bf16[32,4096]{1,0:T(8,128)(2,1)S(1)}, bf16[32,128]{1,0:T(8,128)(2,1)S(1)}, f32[1,4096]{1,0:T(1,128)S(1)}) custom-call(s32[8]{0:T(128)S(1)} %copy-done.6, bf16[1,128,4096]{2,1,0:T(8,128)(2,1)S(1)} %copy-done.2, bf16[128,4096]{1,0:T(8,128)(2,1)S(1)} %copy-done, ...), custom_call_target="tpu_custom_call" | custom-call | flops 33554432 | bytes 4194304 | tf_op jit(solution)/shard_map/pallas_call | solution.py:59
  8.4 1.2 %shard_map.77 = (bf16[32,4096]{1,0:T(8,128)(2,1)S(1)}, f32[32,4096]{1,0:T(8,128)S(1)}, bf16[32,4096]{1,0:T(8,128)(2,1)S(1)}, bf16[32,128]{1,0:T(8,128)(2,1)S(1)}, f32[1,4096]{1,0:T(1,128)S(1)}) custom-call(s32[8]{0:T(128)S(1)} %copy-done.6, bf16[1,128,4096]{2,1,0:T(8,128)(2,1)S(1)} %copy-done.2, bf16[128,4096]{1,0:T(8,128)(2,1)S(1)} %copy-done, ...), custom_call_target="tpu_custom_call" | custom-call | flops 33554432 | bytes 4194304 | tf_op jit(solution)/shard_map/pallas_call | solution.py:59
  9.5 0.0 copy-start.7
  9.6 0.7 %copy-done.7 = bf16[32,4096]{1,0:T(8,128)(2,1)} copy-done((bf16[32,4096]{1,0:T(8,128)(2,1)}, bf16[32,4096]{1,0:T(8,128)(2,1)S(1)}, u32[]{:S(2)}) %copy-start.7) | copy-done | bytes 262168
  10.3 1.9 %shard_map.80 = (bf16[32,4096]{1,0:T(8,128)(2,1)}, f32[32,4096]{1,0:T(8,128)S(1)}, bf16[32,4096]{1,0:T(8,128)(2,1)S(1)}, bf16[32,128]{1,0:T(8,128)(2,1)S(1)}, f32[1,4096]{1,0:T(1,128)S(1)}) custom-call(s32[8]{0:T(128)S(1)} %copy-done.6, bf16[1,128,4096]{2,1,0:T(8,128)(2,1)S(1)} %copy-done.2, bf16[128,4096]{1,0:T(8,128)(2,1)S(1)} %copy-done, ...), custom_call_target="tpu_custom_call" | custom-call | flops 33554432 | bytes 4194304 | tf_op jit(solution)/shard_map/pallas_call | solution.py:59
  12.2 1.9 %shard_map.79 = (bf16[32,4096]{1,0:T(8,128)(2,1)}, f32[32,4096]{1,0:T(8,128)S(1)}, bf16[32,4096]{1,0:T(8,128)(2,1)S(1)}, bf16[32,128]{1,0:T(8,128)(2,1)S(1)}, f32[1,4096]{1,0:T(1,128)S(1)}) custom-call(s32[8]{0:T(128)S(1)} %copy-done.6, bf16[1,128,4096]{2,1,0:T(8,128)(2,1)S(1)} %copy-done.2, bf16[128,4096]{1,0:T(8,128)(2,1)S(1)} %copy-done, ...), custom_call_target="tpu_custom_call" | custom-call | flops 33554432 | bytes 4194304 | tf_op jit(solution)/shard_map/pallas_call | solution.py:59
  14.1 0.6 %shard_map.85 = (f32[8,272,128]{2,1,0:T(8,128)S(1)}, f32[8,272,128]{2,1,0:T(8,128)S(1)}) custom-call(s32[1]{0:T(128)} %bitcast.1.core, bf16[32,4096]{1,0:T(8,128)(2,1)S(1)} %get-tuple-element.32.refs_0_, bf16[32,4096]{1,0:T(8,128)(2,1)S(1)} %get-tuple-element.33.refs_1_, bf16[32,4096]{1,0:T(8,128)(2,1)S(1)} %get-tuple-element.34.refs_2_, ...), custom_call_target="tpu_custom_call" | custom-call | flops 134217728 | bytes 6291456 | tf_op jit(solution)/shard_map/pallas_call | solution.py:163
  14.7 0.5 collective-permute-start.4
  15.2 2.4 %collective-permute-done.4 = f32[8,272,128]{2,1,0:T(8,128)S(1)} collective-permute-done((f32[8,272,128]{2,1,0:T(8,128)S(1)}, f32[8,272,128]{2,1,0:T(8,128)S(1)}, u32[]{:S(2)}, u32[]{:S(2)}) %collective-permute-start.4) | collective-permute-done | bytes 1114144 | tf_op jit(solution)/shard_map/ppermute | solution.py:193
  17.6 0.9 %add_convert_fusion = bf16[8,272,128]{2,1,0:T(8,128)(2,1)} fusion(f32[8,272,128]{2,1,0:T(8,128)S(1)} %get-tuple-element.44, f32[8,272,128]{2,1,0:T(8,128)S(1)} %collective-permute-done.4), kind=kLoop, calls=%fused_computation.1 | loop fusion | flops 557056 | bytes 2785280 | tf_op jit(solution)/shard_map/convert_element_type | solution.py:194
  18.5 0.0 copy-start.1
  18.5 7.3 %all-to-all-start = ((bf16[8,272,128]{2,1,0:T(8,128)(2,1)}), bf16[8,272,128]{2,1,0:T(8,128)(2,1)}, u32[]{:S(2)}, u32[]{:S(2)}) async-start(bf16[8,272,128]{2,1,0:T(8,128)(2,1)} %add_convert_fusion), calls=%async_computation | async-start | bytes 1114112 | tf_op jit(solution)/shard_map/all_to_all | solution.py:196
  25.8 1.3 %collective-permute-start.3 = (bf16[32,4096]{1,0:T(8,128)(2,1)}, bf16[32,4096]{1,0:T(8,128)(2,1)}, u32[]{:S(2)}, u32[]{:S(2)}) collective-permute-start(bf16[32,4096]{1,0:T(8,128)(2,1)} %get-tuple-element.30), channel_id=1, source_target_pairs={{1,0},{3,2},{5,4},{7,6},{9,8},{11,10},{13,12},{15,14},{17,16},{19,... | collective-permute-start | bytes 786440 | tf_op jit(solution)/shard_map/ppermute | solution.py:222
  27.1 1.3 %collective-permute-start.2 = (bf16[32,4096]{1,0:T(8,128)(2,1)}, bf16[32,4096]{1,0:T(8,128)(2,1)}, u32[]{:S(2)}, u32[]{:S(2)}) collective-permute-start(bf16[32,4096]{1,0:T(8,128)(2,1)} %get-tuple-element.28), channel_id=1, source_target_pairs={{1,0},{3,2},{5,4},{7,6},{9,8},{11,10},{13,12},{15,14},{17,16},{19,... | collective-permute-start | bytes 786440 | tf_op jit(solution)/shard_map/ppermute | solution.py:222
  28.4 1.3 %collective-permute-start.1 = (bf16[32,4096]{1,0:T(8,128)(2,1)}, bf16[32,4096]{1,0:T(8,128)(2,1)}, u32[]{:S(2)}, u32[]{:S(2)}) collective-permute-start(bf16[32,4096]{1,0:T(8,128)(2,1)} %get-tuple-element.26), channel_id=1, source_target_pairs={{1,0},{3,2},{5,4},{7,6},{9,8},{11,10},{13,12},{15,14},{17,16},{19,... | collective-permute-start | bytes 786440 | tf_op jit(solution)/shard_map/ppermute | solution.py:222
  29.7 1.3 %collective-permute-start = (bf16[32,4096]{1,0:T(8,128)(2,1)}, bf16[32,4096]{1,0:T(8,128)(2,1)S(1)}, u32[]{:S(2)}, u32[]{:S(2)}) collective-permute-start(bf16[32,4096]{1,0:T(8,128)(2,1)} %copy-done.7), channel_id=1, source_target_pairs={{1,0},{3,2},{5,4},{7,6},{9,8},{11,10},{13,12},{15,14},{17,16},{19,... | collective-permute-start | bytes 786440 | tf_op jit(solution)/shard_map/ppermute | solution.py:222
  31.0 6.2 %collective-permute-done.3.received = bf16[32,4096]{1,0:T(8,128)(2,1)} collective-permute-done((bf16[32,4096]{1,0:T(8,128)(2,1)}, bf16[32,4096]{1,0:T(8,128)(2,1)}, u32[]{:S(2)}, u32[]{:S(2)}) %collective-permute-start.3) | collective-permute-done | bytes 262176 | tf_op jit(solution)/shard_map/ppermute | solution.py:222
  37.2 0.0 copy-done.1
  37.2 1.7 %shard_map.81.rest_0_ = bf16[1,128,4096]{2,1,0:T(8,128)(2,1)} custom-call(s32[1]{0:T(128)} %bitcast.is_last, bf16[128,4096]{1,0:T(8,128)(2,1)S(1)} %copy-done.1, bf16[32,4096]{1,0:T(8,128)(2,1)} %collective-permute-done.3.received, f32[32,4096]{1,0:T(8,128)S(1)} %get-tuple-element.31.branch), custom_call_target="tpu_custom_call" | custom-call | flops 131072 | bytes 1048576 | tf_op jit(solution)/shard_map/pallas_call | solution.py:114
  39.0 3.9 %collective-permute-done.2.received = bf16[32,4096]{1,0:T(8,128)(2,1)} collective-permute-done((bf16[32,4096]{1,0:T(8,128)(2,1)}, bf16[32,4096]{1,0:T(8,128)(2,1)}, u32[]{:S(2)}, u32[]{:S(2)}) %collective-permute-start.2) | collective-permute-done | bytes 262176 | tf_op jit(solution)/shard_map/ppermute | solution.py:222
  42.9 1.7 %shard_map.82.rest_0_ = bf16[1,128,4096]{2,1,0:T(8,128)(2,1)} custom-call(s32[1]{0:T(128)} %bitcast.is_last, bf16[128,4096]{1,0:T(8,128)(2,1)S(1)} %copy-done.1, bf16[32,4096]{1,0:T(8,128)(2,1)} %collective-permute-done.2.received, f32[32,4096]{1,0:T(8,128)S(1)} %get-tuple-element.29.branch, ...), custom_call_target="tpu_custom_call", output_to_operand_aliasing={{}: (4, {})} | custom-call | flops 131072 | bytes 1048576 | tf_op jit(solution)/shard_map/pallas_call | solution.py:114
  44.6 3.9 %collective-permute-done.1.received = bf16[32,4096]{1,0:T(8,128)(2,1)} collective-permute-done((bf16[32,4096]{1,0:T(8,128)(2,1)}, bf16[32,4096]{1,0:T(8,128)(2,1)}, u32[]{:S(2)}, u32[]{:S(2)}) %collective-permute-start.1) | collective-permute-done | bytes 262176 | tf_op jit(solution)/shard_map/ppermute | solution.py:222
  48.5 1.7 %shard_map.83.rest_0_ = bf16[1,128,4096]{2,1,0:T(8,128)(2,1)} custom-call(s32[1]{0:T(128)} %bitcast.is_last, bf16[128,4096]{1,0:T(8,128)(2,1)S(1)} %copy-done.1, bf16[32,4096]{1,0:T(8,128)(2,1)} %collective-permute-done.1.received, f32[32,4096]{1,0:T(8,128)S(1)} %get-tuple-element.27.branch, ...), custom_call_target="tpu_custom_call", output_to_operand_aliasing={{}: (4, {})} | custom-call | flops 131072 | bytes 1048576 | tf_op jit(solution)/shard_map/pallas_call | solution.py:114
  50.2 2.7 %collective-permute-done.received = bf16[32,4096]{1,0:T(8,128)(2,1)S(1)} collective-permute-done((bf16[32,4096]{1,0:T(8,128)(2,1)}, bf16[32,4096]{1,0:T(8,128)(2,1)S(1)}, u32[]{:S(2)}, u32[]{:S(2)}) %collective-permute-start) | collective-permute-done | bytes 262176 | tf_op jit(solution)/shard_map/ppermute | solution.py:222
  52.9 0.8 %shard_map.84 = bf16[1,128,4096]{2,1,0:T(8,128)(2,1)} custom-call(s32[1]{0:T(128)} %bitcast.is_last, bf16[128,4096]{1,0:T(8,128)(2,1)S(1)} %copy-done.1, bf16[32,4096]{1,0:T(8,128)(2,1)S(1)} %collective-permute-done.received, f32[32,4096]{1,0:T(8,128)S(1)} %get-tuple-element.25.branch, ...), custom_call_target="tpu_custom_call", output_to_operand_aliasing={{}: (4, {})} | custom-call | flops 131072 | bytes 1048576 | tf_op jit(solution)/shard_map/pallas_call | solution.py:114
  53.6 0.0 all-to-all-done
  53.6 1.1 %convert_reduce_fusion = f32[272,128]{1,0:T(8,128)S(1)} fusion(bf16[8,272,128]{2,1,0:T(8,128)(2,1)} %all-to-all-done), kind=kLoop, calls=%fused_computation | loop fusion | flops 522240 | bytes 696320 | tf_op jit(solution)/shard_map/reduce_sum | solution.py:197
  54.8 0.8 %copy.13 = f32[1,1,258,128]{3,1,2,0:T(1,128)} copy(f32[1,1,258,128]{3,2,1,0:T(8,128)S(1)} %fusion) | data formatting | bytes 264192
  (1 shorter events, 0.0 us)
Async XLA Ops:
  0.6 1.2 %copy-start = (bf16[128,4096]{1,0:T(8,128)(2,1)S(1)}, bf16[128,4096]{1,0:T(8,128)(2,1)}, u32[]{:S(2)}) copy-start(bf16[128,4096]{1,0:T(8,128)(2,1)} %top.15) | copy-start | bytes 3145732
  1.9 1.2 %copy-start.2 = (bf16[1,128,4096]{2,1,0:T(8,128)(2,1)S(1)}, bf16[1,128,4096]{2,1,0:T(8,128)(2,1)}, u32[]{:S(2)}) copy-start(bf16[1,128,4096]{2,1,0:T(8,128)(2,1)} %x.7) | copy-start | bytes 3145732
  3.1 1.2 %copy-start.3 = (bf16[1,4096,128]{2,1,0:T(8,128)(2,1)S(1)}, bf16[1,4096,128]{2,1,0:T(8,128)(2,1)}, u32[]{:S(2)}) copy-start(bf16[1,4096,128]{2,1,0:T(8,128)(2,1)} %w.7) | copy-start | bytes 3145732
  4.3 0.8 %copy-start.4 = (bf16[1,128,128]{2,1,0:T(8,128)(2,1)S(1)}, bf16[1,128,128]{2,1,0:T(8,128)(2,1)}, u32[]{:S(2)}) copy-start(bf16[1,128,128]{2,1,0:T(8,128)(2,1)} %v.7) | copy-start | bytes 98308
  5.1 0.7 %copy-start.5 = (f32[1,4096]{1,0:T(1,128)S(1)}, f32[1,4096]{1,0:T(1,128)}, u32[]{:S(2)}) copy-start(f32[1,4096]{1,0:T(1,128)} %gain.7) | copy-start | bytes 49156
  5.8 0.7 %copy-start.6 = (s32[8]{0:T(128)S(1)}, s32[8]{0:T(128)}, u32[]{:S(2)}) copy-start(s32[8]{0:T(128)} %counts.7) | copy-start | bytes 100
  9.5 0.7 %copy-start.7 = (bf16[32,4096]{1,0:T(8,128)(2,1)}, bf16[32,4096]{1,0:T(8,128)(2,1)S(1)}, u32[]{:S(2)}) copy-start(bf16[32,4096]{1,0:T(8,128)(2,1)S(1)} %get-tuple-element.24) | copy-start | bytes 786436
  14.7 2.9 %collective-permute-start.4 = (f32[8,272,128]{2,1,0:T(8,128)S(1)}, f32[8,272,128]{2,1,0:T(8,128)S(1)}, u32[]{:S(2)}, u32[]{:S(2)}) collective-permute-start(f32[8,272,128]{2,1,0:T(8,128)S(1)} %get-tuple-element.45), channel_id=1, source_target_pairs={{0,2},{2,0},{4,6},{6,4},{8,10},{10,8},{12,14},{14,12},{16,18},{18,... | collective-permute-start | bytes 3342344 | tf_op jit(solution)/shard_map/ppermute | solution.py:193
  18.5 18.7 %copy-start.1 = (bf16[128,4096]{1,0:T(8,128)(2,1)S(1)}, bf16[128,4096]{1,0:T(8,128)(2,1)}, u32[]{:S(2)}) copy-start(bf16[128,4096]{1,0:T(8,128)(2,1)} %top.15) | copy-start | bytes 3145732
  18.5 35.1 %all-to-all-start = ((bf16[8,272,128]{2,1,0:T(8,128)(2,1)}), bf16[8,272,128]{2,1,0:T(8,128)(2,1)}, u32[]{:S(2)}, u32[]{:S(2)}) async-start(bf16[8,272,128]{2,1,0:T(8,128)(2,1)} %add_convert_fusion), calls=%async_computation | async-start | bytes 1114112 | tf_op jit(solution)/shard_map/all_to_all | solution.py:196
  25.8 11.4 %collective-permute-start.3 = (bf16[32,4096]{1,0:T(8,128)(2,1)}, bf16[32,4096]{1,0:T(8,128)(2,1)}, u32[]{:S(2)}, u32[]{:S(2)}) collective-permute-start(bf16[32,4096]{1,0:T(8,128)(2,1)} %get-tuple-element.30), channel_id=1, source_target_pairs={{1,0},{3,2},{5,4},{7,6},{9,8},{11,10},{13,12},{15,14},{17,16},{19,... | collective-permute-start | bytes 786440 | tf_op jit(solution)/shard_map/ppermute | solution.py:222
  27.1 15.7 %collective-permute-start.2 = (bf16[32,4096]{1,0:T(8,128)(2,1)}, bf16[32,4096]{1,0:T(8,128)(2,1)}, u32[]{:S(2)}, u32[]{:S(2)}) collective-permute-start(bf16[32,4096]{1,0:T(8,128)(2,1)} %get-tuple-element.28), channel_id=1, source_target_pairs={{1,0},{3,2},{5,4},{7,6},{9,8},{11,10},{13,12},{15,14},{17,16},{19,... | collective-permute-start | bytes 786440 | tf_op jit(solution)/shard_map/ppermute | solution.py:222
  28.4 20.0 %collective-permute-start.1 = (bf16[32,4096]{1,0:T(8,128)(2,1)}, bf16[32,4096]{1,0:T(8,128)(2,1)}, u32[]{:S(2)}, u32[]{:S(2)}) collective-permute-start(bf16[32,4096]{1,0:T(8,128)(2,1)} %get-tuple-element.26), channel_id=1, source_target_pairs={{1,0},{3,2},{5,4},{7,6},{9,8},{11,10},{13,12},{15,14},{17,16},{19,... | collective-permute-start | bytes 786440 | tf_op jit(solution)/shard_map/ppermute | solution.py:222
  29.7 23.1 %collective-permute-start = (bf16[32,4096]{1,0:T(8,128)(2,1)}, bf16[32,4096]{1,0:T(8,128)(2,1)S(1)}, u32[]{:S(2)}, u32[]{:S(2)}) collective-permute-start(bf16[32,4096]{1,0:T(8,128)(2,1)} %copy-done.7), channel_id=1, source_target_pairs={{1,0},{3,2},{5,4},{7,6},{9,8},{11,10},{13,12},{15,14},{17,16},{19,... | collective-permute-start | bytes 786440 | tf_op jit(solution)/shard_map/ppermute | solution.py:222

commit v2 on v0

v2 whole, which is shorter than its diff:
```python
import functools
import math

import jax
import jax.numpy as jnp
from jax import lax
from jax.experimental import pallas as pl
from jax.experimental.pallas import tpu as pltpu
from jax.sharding import PartitionSpec as P

eps_norm = 1e-05
lanes = 128
sublanes = 8
pack_rows = 16
tile_width = 512
pair = 2
f32 = jnp.float32
bf16 = jnp.bfloat16
contract_last = (((1,), (1,)), ((), ()))
contract_rows = (((0,), (0,)), ((), ()))
small_cost = pl.CostEstimate(flops=1 << 20, bytes_accessed=1 << 16, transcendentals=0)
roomy = pltpu.CompilerParams(vmem_limit_bytes=32 << 20)
near = pl.BlockSpec(memory_space=pltpu.VMEM)
scalar = pl.BlockSpec(memory_space=pltpu.SMEM)


def far(array):
    return pltpu.with_memory_space_constraint(array, pltpu.HBM)


def cuts(width, step):
    return [pl.ds(at, step) for at in range(0, width, step)]


def one_hot(counts, micro_count, slots, low, size):
    slot = lax.broadcasted_iota(jnp.int32, (slots, size), 0)
    column = lax.broadcasted_iota(jnp.int32, (slots, size), 1) + low
    start = jnp.int32(0)
    pieces = []
    for m in range(micro_count):
        hit = (slot < counts[m]) & (slot + start == column)
        pieces.append(jnp.where(hit, 1.0, 0.0))
        start = start + counts[m]
    return jnp.concatenate(pieces, axis=0).astype(bf16)


def branch_kernel(
    counts_far, x_far, top_far, v_far, w_far, gain_far,
    sent, packed, branch, normed, masked, gain_out,
    counts, x, top, v, w, gain, back, gain_part, ready,
):
    rows, width = sent.shape
    micro_count = counts.shape[0]
    slots = rows // micro_count
    fetches = [
        pltpu.make_async_copy(v_far.at[0], v, ready.at[0]),
        pltpu.make_async_copy(counts_far, counts, ready.at[1]),
        pltpu.make_async_copy(w_far.at[0], w, ready.at[2]),
        pltpu.make_async_copy(x_far.at[0], x, ready.at[3]),
        pltpu.make_async_copy(gain_far, gain, ready.at[4]),
        pltpu.make_async_copy(top_far, top, ready.at[5]),
    ]
    for fetch in fetches:
        fetch.start()
    fetches[0].wait()
    fetches[1].wait()
    slot = lax.broadcasted_iota(jnp.int32, (slots, v.shape[1]), 0)
    for m in range(micro_count):
        piece = v[m * slots : (m + 1) * slots, :]
        masked[m * slots : (m + 1) * slots, :] = jnp.where(slot < counts[m], piece, jnp.zeros_like(piece))
    gather = one_hot(counts, micro_count, slots, 0, packed.shape[0])
    values = masked[...]
    fetches[2].wait()
    for cut in cuts(width, tile_width):
        back[:, cut] = lax.dot_general(values, w[cut, :], contract_last, preferred_element_type=f32)
    fetches[3].wait()
    fetches[4].wait()
    fetches[5].wait()
    for at in range(0, rows, 32):
        part = slice(at, at + 32)
        squares = jnp.zeros((32, lanes), f32)
        products = jnp.zeros((32, lanes), f32)
        for cut in cuts(width, lanes):
            wide = x[part, cut].astype(f32)
            squares += wide * wide
            products += wide * back[part, cut] * gain[:, cut]
        scale = lax.rsqrt(jnp.sum(squares, axis=1, keepdims=True) / width + eps_norm)
        pull = scale * jnp.sum(products, axis=1, keepdims=True) / width
        for cut in cuts(width, 2 * lanes):
            unit = x[part, cut].astype(f32) * scale
            here = back[part, cut]
            scaled = gain[:, cut]
            product = (unit * here).reshape(32 // sublanes, sublanes, 2 * lanes).sum(axis=0)
            if at:
                product += gain_part[:, cut]
            gain_part[:, cut] = product
            normed[part, cut] = (unit * scaled).astype(bf16)
            own = scale * (scaled * here - unit * pull)
            branch[part, cut] = own
            sent[part, cut] = (top[part, cut].astype(f32) + own).astype(bf16)
    for cut in cuts(width, tile_width):
        packed[:, cut] = lax.dot_general(
            gather, sent[:, cut], contract_rows, preferred_element_type=f32
        ).astype(bf16)
    for cut in cuts(width, tile_width):
        gain_out[:, cut] = jnp.sum(gain_part[:, cut], axis=0, keepdims=True)


def branch_rows(room, counts, x, top, v, w, gain):
    rows, width = top.shape
    depth = v.shape[2]
    return pl.pallas_call(
        branch_kernel,
        in_specs=[pl.BlockSpec(memory_space=pltpu.HBM)] * 6,
        out_specs=[near] * 6,
        out_shape=[
            jax.ShapeDtypeStruct((rows, width), bf16),
            jax.ShapeDtypeStruct((room, width), bf16),
            jax.ShapeDtypeStruct((rows, width), f32),
            jax.ShapeDtypeStruct((rows, width), bf16),
            jax.ShapeDtypeStruct((rows, depth), bf16),
            jax.ShapeDtypeStruct((1, width), f32),
        ],
        scratch_shapes=[
            pltpu.SMEM(counts.shape, jnp.int32),
            pltpu.VMEM((rows, width), bf16),
            pltpu.VMEM((rows, width), bf16),
            pltpu.VMEM((rows, depth), bf16),
            pltpu.VMEM((width, depth), bf16),
            pltpu.VMEM((1, width), f32),
            pltpu.VMEM((rows, width), f32),
            pltpu.VMEM((sublanes, width), f32),
            pltpu.SemaphoreType.DMA((6,)),
        ],
        compiler_params=roomy,
        cost_estimate=small_cost,
    )(*[far(a) for a in (counts, x, top, v, w, gain)])


def pack_kernel(low, counts, sent, packed):
    micro_count = counts.shape[0]
    gather = one_hot(counts, micro_count, sent.shape[0] // micro_count, low, packed.shape[0])
    for cut in cuts(sent.shape[1], tile_width):
        packed[:, cut] = lax.dot_general(
            gather, sent[:, cut], contract_rows, preferred_element_type=f32
        ).astype(bf16)


def pack(low, room, counts, sent):
    return pl.pallas_call(
        functools.partial(pack_kernel, low),
        in_specs=[scalar, near],
        out_specs=near,
        out_shape=jax.ShapeDtypeStruct((room, sent.shape[1]), bf16),
        compiler_params=roomy,
        cost_estimate=small_cost,
    )(counts, sent)


def receive_kernel(low, counts, is_target, received, branch, sent, out_far, out, done):
    rows, width = sent.shape
    micro_count = counts.shape[0]
    slots = rows // micro_count
    scatter = one_hot(counts, micro_count, slots, low, received.shape[0])
    covered = jnp.sum(scatter.astype(f32), axis=1, keepdims=True) * is_target[0].astype(f32) > 0.5
    step = 1024 if width % 1024 == 0 else width
    writes = []
    for k, wide_cut in enumerate(cuts(width, step)):
        for at in range(k * step, (k + 1) * step, tile_width if step % tile_width == 0 else step):
            cut = pl.ds(at, tile_width if step % tile_width == 0 else step)
            incoming = jnp.dot(scatter, received[:, cut], preferred_element_type=f32)
            updated = (incoming + branch[:, cut]).astype(bf16)
            out[:, cut] = jnp.where(covered, updated, sent[:, cut])
        write = pltpu.make_async_copy(out.at[:, wide_cut], out_far.at[:, wide_cut], done.at[k])
        write.start()
        writes.append(write)
    for write in writes:
        write.wait()


def receive(low, counts, is_target, received, branch, sent):
    rows, width = sent.shape
    pieces = width // 1024 if width % 1024 == 0 else 1
    return pl.pallas_call(
        functools.partial(receive_kernel, low),
        in_specs=[scalar, scalar, near, near, near],
        out_specs=pl.BlockSpec(memory_space=pltpu.HBM),
        out_shape=pltpu.HBM((rows, width), bf16),
        scratch_shapes=[pltpu.VMEM((rows, width), bf16), pltpu.SemaphoreType.DMA((pieces,))],
        compiler_params=roomy,
        cost_estimate=small_cost,
    )(counts, is_target, received, branch, sent)


def terms_kernel(owned_rows, core, normed, masked, gain, keep, give, total):
    width = normed.shape[1]
    values = masked[...]
    gain_rows = width // lanes
    for k in range(gain_rows):
        total[k : k + 1, :] = gain[:, k * lanes : (k + 1) * lanes]
    for at in range(0, width, tile_width):
        total[gain_rows + at : gain_rows + at + tile_width, :] = lax.dot_general(
            normed[:, at : at + tile_width], values, contract_rows, preferred_element_type=f32
        )
    even_core = core[0] == 0
    padded = keep.shape[1]
    for j in range(keep.shape[0]):
        even = total[2 * j * owned_rows : (2 * j + 1) * owned_rows, :]
        odd = total[(2 * j + 1) * owned_rows : (2 * j + 2) * owned_rows, :]
        keep[j, :owned_rows, :] = jnp.where(even_core, even, odd)
        give[j, :owned_rows, :] = jnp.where(even_core, odd, even)
        if padded > owned_rows:
            blank = jnp.zeros((padded - owned_rows, lanes), f32)
            keep[j, owned_rows:, :] = blank
            give[j, owned_rows:, :] = blank


def pair_terms(core, normed, masked, gain, owned_rows, owners):
    padded = -(-owned_rows // pack_rows) * pack_rows
    half = jax.ShapeDtypeStruct((owners // pair, padded, lanes), f32)
    return pl.pallas_call(
        functools.partial(terms_kernel, owned_rows),
        in_specs=[scalar, near, near, near],
        out_specs=[near, near],
        out_shape=[half, half],
        scratch_shapes=[pltpu.VMEM((owners * owned_rows, lanes), f32)],
        compiler_params=roomy,
        cost_estimate=small_cost,
    )(core, normed, masked, gain)


def merge_kernel(side, keep, taken, hold, give):
    mine = side[0]
    for k in range(hold.shape[0]):
        here = 2 * k + mine
        there = 2 * k + 1 - mine
        hold[k] = keep[here] + taken[here]
        give[k] = (keep[there] + taken[there]).astype(bf16)


def merge_terms(side, keep, taken):
    half = (keep.shape[0] // 2,) + keep.shape[1:]
    return pl.pallas_call(
        merge_kernel,
        in_specs=[scalar, near, near],
        out_specs=[near, near],
        out_shape=[jax.ShapeDtypeStruct(half, f32), jax.ShapeDtypeStruct(half, bf16)],
        compiler_params=roomy,
        cost_estimate=small_cost,
    )(side, keep, taken)


def split_kernel(place, hold, taken, own, *parts):
    count = hold.shape[0]
    own[...] = hold[place[0]] + taken[place[0]].astype(f32)
    for k in range(1, count):
        at = lax.rem(place[0] + k, count)
        parts[k - 1][...] = (hold[at] + taken[at].astype(f32)).astype(bf16)


def split_terms(place, hold, taken):
    count = hold.shape[0]
    return pl.pallas_call(
        split_kernel,
        in_specs=[scalar, near, near],
        out_specs=[near] * count,
        out_shape=[jax.ShapeDtypeStruct(hold.shape[1:], f32)]
        + [jax.ShapeDtypeStruct(hold.shape[1:], bf16)] * (count - 1),
        compiler_params=roomy,
        cost_estimate=small_cost,
    )(place, hold, taken)


def total_kernel(owned_rows, factor, own, *rest):
    out = rest[-1]
    total = own[...]
    for part in rest[:-1]:
        total += part[...].astype(f32)
    total = total * factor
    for k in range(owned_rows):
        out[:, k * lanes : (k + 1) * lanes] = total[k : k + 1, :]


def total_terms(owned_rows, factor, own, landed):
    return pl.pallas_call(
        functools.partial(total_kernel, owned_rows, factor),
        in_specs=[near] * (1 + len(landed)),
        out_specs=near,
        out_shape=jax.ShapeDtypeStruct((1, owned_rows * lanes), f32),
        compiler_params=roomy,
        cost_estimate=small_cost,
    )(own, *landed)


def plane_sum(owners, owned_rows, factor, spot, keep, taken):
    quad = 2 * pair
    hold, give = merge_terms((spot // pair % 2).reshape(1), keep, taken)
    across = lax.ppermute(give, "dp", [(i, i ^ pair) for i in range(owners)])
    own, *parts = split_terms((spot // quad).reshape(1), hold, across)
    landed = []
    for k, part in enumerate(parts):
        landed.append(lax.ppermute(part, "dp", [(i, (i + quad * (k + 1)) % owners) for i in range(owners)]))
    return total_terms(owned_rows, factor, own, landed)


def weight_owned(normed, masked, gain, factor):
    owners = lax.axis_size("dp")
    width = normed.shape[1]
    depth = masked.shape[1]
    owned = (width + width * depth) // owners
    if depth != lanes or owned % lanes or owners % (2 * pair):
        weight_term = lax.dot_general(normed, masked, contract_rows, preferred_element_type=f32)
        flat = jnp.concatenate([gain.reshape(-1), weight_term.reshape(-1)]) * factor
        return lax.psum_scatter(flat, "dp", scatter_dimension=0, tiled=True)[None, :]
    spot = lax.axis_index("dp").astype(jnp.int32)
    keep, give = pair_terms((spot % pair).reshape(1), normed, masked, gain, owned // lanes, owners)
    taken = lax.ppermute(give, "dp", [(i, i ^ 1) for i in range(owners)])
    return plane_sum(owners, owned // lanes, factor, spot, keep, taken)


def shards(layer_inputs, top_grad, value_grads, weights, norm_gains, counts):
    rows = layer_inputs.shape[1]
    factor = 1.0 / math.sqrt(rows * lax.axis_size("dp"))
    sections = lax.axis_size("section")
    section_here = lax.axis_index("section")
    room = -(-rows * 3 // 4 // pack_rows) * pack_rows
    spare = rows - room
    sent, packed, branch, normed, masked, gain = branch_rows(
        room, counts, layer_inputs, top_grad, value_grads, weights, norm_gains
    )
    result = sent
    overflow = jnp.sum(counts) > room
    for hop in range(sections - 1):
        target = sections - 2 - hop
        is_target = (section_here == target).astype(jnp.int32).reshape(1)
        if hop:
            packed = pack(0, room, counts, result)
        hops = [(target + 1, target)]
        before = result
        landed = lax.ppermute(packed, "section", hops)
        result = receive(0, counts, is_target, landed, branch, before)

        def rest(result):
            landed = lax.ppermute(pack(room, spare, counts, before), "section", hops)
            return receive(room, counts, is_target, landed, branch, result)

        result = lax.cond(overflow, rest, lambda result: result, result)
    owned = weight_owned(normed, masked, gain, factor)
    return (result[None], owned)


def solution(mesh):
    placed = (
        P("section", "dp", None),
        P("dp", None),
        P("section", "dp", None),
        P("section", None, None),
        P("section", None),
        P("dp"),
    )
    return jax.shard_map(
        shards,
        mesh=mesh,
        in_specs=placed,
        out_specs=(P("section", "dp", None), P("section", "dp")),
        check_vma=False,
    )
```

time: 175 us -> 34.6 us (0.20)
  waiting for transfers between devices: 131 us -> 8.83 us
  between operations: 14.8 us -> 1.42 us
  other arithmetic: 13.6 us -> 0.63 us
  Pallas kernels: 0 us -> 11.2 us
  starting transfers between devices: 6.5 us -> 10.4 us
  matrix products: 3.77 us -> 0 us
  local copies, waits for them, and re-layouts: 4.24 us -> 1.87 us
    unnamed x2 -> x0, waiting for transfers between devices: 95.5 us -> none
    ppermute x5 -> x6, waiting for transfers between devices: 35.5 us -> 8.83 us  [the longest x1 6.95 us: plane_sum(): across = lax.ppermute(give, 'dp', [(i, i ^ pair) for i in range(owners)])]
    pallas_call x0 -> x6, Pallas kernels: none -> 11.2 us  [the longest x1 5.45 us: branch_rows(): pl.pallas_call(branch_kernel, in_specs=[pl.BlockSpec(memory_space=pltpu.H...]
    dynamic_update_slice x5 -> x0, other arithmetic: 6.16 us -> none  [advance(): lax.dynamic_update_index_in_dim(result, jnp.where(usable, updated, curren...]
    mul x2 -> x0, other arithmetic: 4.89 us -> none  [the longest x1 3.39 us: shards(): scale * (gain_row * back - unit * jnp.mean(unit * gain_row * back, axis=1...]
    ppermute x5 -> x6, starting transfers between devices: 6.46 us -> 10.4 us  [the longest x3 5.8 us: plane_sum(): lax.ppermute(part, 'dp', [(i, (i + quad * (k + 1)) % owners) for i in ran...]
    dot_general x2 -> x0, matrix products: 3.77 us -> none  [the longest x1 1.96 us: shards(): lax.dot_general(masked, weights[0], (((1,), (1,)), ((), ())), preferred_e...]
  transfers between devices with their start and end apart: 6 -> 6, of which waited for: 6 -> 3; matrix products, arithmetic and copies ran while one was open for 2% -> 2% of each run, Pallas kernels for 0% -> 10%
where the time goes in v2:
time: 34.6 us; the launch traced here: 34.4 us
  Pallas kernels  11.2 us (32%)
  starting transfers between devices  10.4 us (30%)
  waiting for transfers between devices  8.83 us (26%)
  local copies, waits for them, and re-layouts  1.87 us (5%)
  between operations  1.42 us (4%)
  other arithmetic  0.63 us (2%)
    ppermute x1, waiting for transfers between devices, plane_sum(): across = lax.ppermute(give, 'dp', [(i, i ^ pair) for i in range(owners)])  6.95 us
    ppermute x3, starting transfers between devices, plane_sum(): lax.ppermute(part, 'dp', [(i, (i + quad * (k + 1)) % owners) for i in ran...  5.8 us
    pallas_call x1, Pallas kernels, branch_rows(): pl.pallas_call(branch_kernel, in_specs=[pl.BlockSpec(memory_space=pltpu.H...  5.45 us
    pallas_call x1, Pallas kernels, receive(): pl.pallas_call(functools.partial(receive_kernel, low), in_specs=[scalar,...  3.23 us
    ppermute x1, starting transfers between devices, plane_sum(): across = lax.ppermute(give, 'dp', [(i, i ^ pair) for i in range(owners)])  2.89 us
    unnamed x10, local copies, waits for them, and re-layouts  1.87 us
    pallas_call x1, Pallas kernels, pair_terms(): pl.pallas_call(functools.partial(terms_kernel, owned_rows), in_specs=[sca...  1.59 us
    ppermute x1, starting transfers between devices, shards(): landed = lax.ppermute(packed, 'section', hops)  1.28 us
  transfers between devices with their start and end apart: 6, of which 3 were waited for; matrix products, arithmetic and copies ran while one was open for 2% of the time, Pallas kernels for 10%

profile of v2, /device:TPU:0, one launch (start us, length us, event | category | flops | bytes accessed | tf_op | source)
XLA Modules:
  0.0 34.4 jit_solution(13391344098238237630)
XLA Ops:
  0.6 5.5 %shard_map.77 = (bf16[128,4096]{1,0:T(8,128)(2,1)}, bf16[96,4096]{1,0:T(8,128)(2,1)}, f32[128,4096]{1,0:T(8,128)}, bf16[128,4096]{1,0:T(8,128)(2,1)S(1)}, bf16[1...) custom-call(s32[8]{0:T(128)} %counts.1, bf16[1,128,4096]{2,1,0:T(8,128)(2,1)} %x_far.1, bf16[128,4096]{1,0:T(8,128)(2,1)} %top_far.1, ...), custom_call_target="tpu_custom_call" | custom-call | flops 1048576 | bytes 65536 | tf_op jit(solution)/shard_map/pallas_call | solution.py:112
  6.1 1.6 %shard_map.79 = (f32[8,272,128]{2,1,0:T(8,128)S(1)}, f32[8,272,128]{2,1,0:T(8,128)}) custom-call(s32[1]{0:T(128)} %bitcast.4.core, bf16[128,4096]{1,0:T(8,128)(2,1)S(1)} %get-tuple-element.44.normed, bf16[128,128]{1,0:T(8,128)(2,1)S(1)} %get-tuple-element.45.masked, f32[1,4096]{1,0:T(1,128)S(1)} %get-tuple-element.46.gain), custom_call_target="tpu_custom_call" | custom-call | flops 1048576 | bytes 65536 | tf_op jit(solution)/shard_map/pallas_call | solution.py:221
  7.7 0.4 %collective-permute-start.2 = (f32[8,272,128]{2,1,0:T(8,128)}, f32[8,272,128]{2,1,0:T(8,128)S(1)}, u32[]{:S(2)}, u32[]{:S(2)}) collective-permute-start(f32[8,272,128]{2,1,0:T(8,128)} %get-tuple-element.48), channel_id=1, source_target_pairs={{0,2},{2,0},{4,6},{6,4},{8,10},{10,8},{12,14},{14,12},{16,18},{18,... | collective-permute-start | bytes 3342344 | tf_op jit(solution)/shard_map/ppermute | solution.py:317
  8.1 1.3 %collective-permute-start.1 = (bf16[96,4096]{1,0:T(8,128)(2,1)}, bf16[96,4096]{1,0:T(8,128)(2,1)S(1)}, u32[]{:S(2)}, u32[]{:S(2)}) collective-permute-start(bf16[96,4096]{1,0:T(8,128)(2,1)} %get-tuple-element.41), channel_id=1, source_target_pairs={{1,0},{3,2},{5,4},{7,6},{9,8},{11,10},{13,12},{15,14},{17,16},{19,... | collective-permute-start | bytes 2359304 | tf_op jit(solution)/shard_map/ppermute | solution.py:340
  9.5 1.3 %collective-permute-done.2.taken = f32[8,272,128]{2,1,0:T(8,128)S(1)} collective-permute-done((f32[8,272,128]{2,1,0:T(8,128)}, f32[8,272,128]{2,1,0:T(8,128)S(1)}, u32[]{:S(2)}, u32[]{:S(2)}) %collective-permute-start.2) | collective-permute-done | bytes 1114144 | tf_op jit(solution)/shard_map/ppermute | solution.py:317
  10.7 0.0 copy-start.5
  10.7 0.1 shard_map.80
  10.9 0.0 copy-start
  10.9 0.8 %copy-done = f32[4,272,128]{2,1,0:T(8,128)} copy-done((f32[4,272,128]{2,1,0:T(8,128)}, f32[4,272,128]{2,1,0:T(8,128)S(1)}, u32[]{:S(2)}) %copy-start) | copy-done | bytes 557080
  11.7 2.9 %collective-permute-start.3 = (bf16[4,272,128]{2,1,0:T(8,128)(2,1)S(1)}, bf16[4,272,128]{2,1,0:T(8,128)(2,1)S(1)}, u32[]{:S(2)}, u32[]{:S(2)}) collective-permute-start(bf16[4,272,128]{2,1,0:T(8,128)(2,1)S(1)} %get-tuple-element.50), channel_id=1, source_target_pairs={{0,4},{2,6},{4,0},{6,2},{8,12},{10,14},{12,8},{14,10},{16,20},{18,... | collective-permute-start | bytes 835592 | tf_op jit(solution)/shard_map/ppermute | solution.py:298
  14.6 7.0 %collective-permute-done.3.taken = bf16[4,272,128]{2,1,0:T(8,128)(2,1)S(1)} collective-permute-done((bf16[4,272,128]{2,1,0:T(8,128)(2,1)S(1)}, bf16[4,272,128]{2,1,0:T(8,128)(2,1)S(1)}, u32[]{:S(2)}, u32[]{:S(2)}) %collective-permute-start.3) | collective-permute-done | bytes 278560 | tf_op jit(solution)/shard_map/ppermute | solution.py:298
  21.5 0.0 copy-start.1
  21.5 1.1 %copy-done.1 = f32[4,272,128]{2,1,0:T(8,128)S(1)} copy-done((f32[4,272,128]{2,1,0:T(8,128)S(1)}, f32[4,272,128]{2,1,0:T(8,128)}, u32[]{:S(2)}) %copy-start.1) | copy-done | bytes 557080
  22.6 0.1 shard_map.81
  22.6 1.9 %collective-permute-start.4 = (bf16[272,128]{1,0:T(8,128)(2,1)S(1)}, bf16[272,128]{1,0:T(8,128)(2,1)S(1)}, u32[]{:S(2)}, u32[]{:S(2)}) collective-permute-start(bf16[272,128]{1,0:T(8,128)(2,1)S(1)} %get-tuple-element.52), channel_id=1, source_target_pairs={{0,8},{2,10},{4,12},{6,14},{8,16},{10,18},{12,20},{14,22},{16,24},... | collective-permute-start | bytes 208904 | tf_op jit(solution)/shard_map/ppermute | solution.py:302
  24.5 2.6 %collective-permute-start.5 = (bf16[272,128]{1,0:T(8,128)(2,1)S(1)}, bf16[272,128]{1,0:T(8,128)(2,1)S(1)}, u32[]{:S(2)}, u32[]{:S(2)}) collective-permute-start(bf16[272,128]{1,0:T(8,128)(2,1)S(1)} %get-tuple-element.53), channel_id=1, source_target_pairs={{0,16},{2,18},{4,20},{6,22},{8,24},{10,26},{12,28},{14,30},{16,0},... | collective-permute-start | bytes 208904 | tf_op jit(solution)/shard_map/ppermute | solution.py:302
  27.1 1.3 %collective-permute-start.6 = (bf16[272,128]{1,0:T(8,128)(2,1)S(1)}, bf16[272,128]{1,0:T(8,128)(2,1)S(1)}, u32[]{:S(2)}, u32[]{:S(2)}) collective-permute-start(bf16[272,128]{1,0:T(8,128)(2,1)S(1)} %get-tuple-element.54), channel_id=1, source_target_pairs={{0,24},{2,26},{4,28},{6,30},{8,0},{10,2},{12,4},{14,6},{16,8},{18,... | collective-permute-start | bytes 208904 | tf_op jit(solution)/shard_map/ppermute | solution.py:302
  28.4 0.0 copy-done.5
  28.4 0.6 %reduce_sum.9 = s32[]{:T(128)} reduce(s32[8]{0:T(128)S(1)} %copy-done.5, s32[]{:T(128)} %constant.41.clone.1), dimensions={0}, to_apply=%region_0.0 | reduce | flops 7 | bytes 40 | tf_op jit(solution)/shard_map/reduce_sum | solution.py:332
  29.7 0.6 %collective-permute-done.1.received = bf16[96,4096]{1,0:T(8,128)(2,1)S(1)} collective-permute-done((bf16[96,4096]{1,0:T(8,128)(2,1)}, bf16[96,4096]{1,0:T(8,128)(2,1)S(1)}, u32[]{:S(2)}, u32[]{:S(2)}) %collective-permute-start.1) | collective-permute-done | bytes 786464 | tf_op jit(solution)/shard_map/ppermute | solution.py:340
  30.3 0.0 copy-start.2
  30.3 0.0 copy-start.4
  30.3 3.2 %shard_map.78 = bf16[128,4096]{1,0:T(8,128)(2,1)} custom-call(s32[8]{0:T(128)S(1)} %copy-done.5, s32[1]{0:T(128)} %bitcast.is_target, bf16[96,4096]{1,0:T(8,128)(2,1)S(1)} %collective-permute-done.1.received, f32[128,4096]{1,0:T(8,128)} %get-tuple-element.42.branch, bf16[128,4096]{1,0:T(8,128)(2,1)} %get-tuple-element.43.sent), custom_call_target="tpu_custom_call" | custom-call | flops 1048576 | bytes 65536 | tf_op jit(solution)/shard_map/pallas_call | solution.py:184
  33.6 0.0 copy-done.2
  33.6 0.0 copy-done.4
  33.6 0.0 collective-permute-done.4.rest_0_
  33.6 0.0 collective-permute-done.5.rest_1_
  33.6 0.0 collective-permute-done.6.rest_2_
  33.6 0.8 %shard_map.82 = f32[1,33024]{1,0:T(1,128)} custom-call(f32[272,128]{1,0:T(8,128)S(1)} %get-tuple-element.51.own, bf16[272,128]{1,0:T(8,128)(2,1)S(1)} %collective-permute-done.4.rest_0_, bf16[272,128]{1,0:T(8,128)(2,1)S(1)} %collective-permute-done.5.rest_1_, bf16[272,128]{1,0:T(8,128)(2,1)S(1)} %collective-permute-done.6.rest_2_), custom_call_target="tpu_custom_call" | custom-call | flops 1048576 | bytes 65536 | tf_op jit(solution)/shard_map/pallas_call | solution.py:285
  (1 shorter events, 0.0 us)
Async XLA Ops:
  7.7 3.0 %collective-permute-start.2 = (f32[8,272,128]{2,1,0:T(8,128)}, f32[8,272,128]{2,1,0:T(8,128)S(1)}, u32[]{:S(2)}, u32[]{:S(2)}) collective-permute-start(f32[8,272,128]{2,1,0:T(8,128)} %get-tuple-element.48), channel_id=1, source_target_pairs={{0,2},{2,0},{4,6},{6,4},{8,10},{10,8},{12,14},{14,12},{16,18},{18,... | collective-permute-start | bytes 3342344 | tf_op jit(solution)/shard_map/ppermute | solution.py:317
  8.1 22.2 %collective-permute-start.1 = (bf16[96,4096]{1,0:T(8,128)(2,1)}, bf16[96,4096]{1,0:T(8,128)(2,1)S(1)}, u32[]{:S(2)}, u32[]{:S(2)}) collective-permute-start(bf16[96,4096]{1,0:T(8,128)(2,1)} %get-tuple-element.41), channel_id=1, source_target_pairs={{1,0},{3,2},{5,4},{7,6},{9,8},{11,10},{13,12},{15,14},{17,16},{19,... | collective-permute-start | bytes 2359304 | tf_op jit(solution)/shard_map/ppermute | solution.py:340
  10.7 17.7 %copy-start.5 = (s32[8]{0:T(128)S(1)}, s32[8]{0:T(128)}, u32[]{:S(2)}) copy-start(s32[8]{0:T(128)} %counts.1) | copy-start | bytes 100
  10.9 0.8 %copy-start = (f32[4,272,128]{2,1,0:T(8,128)}, f32[4,272,128]{2,1,0:T(8,128)S(1)}, u32[]{:S(2)}) copy-start(f32[4,272,128]{2,1,0:T(8,128)S(1)} %get-tuple-element.49.hold) | copy-start | bytes 1671172
  11.7 9.8 %collective-permute-start.3 = (bf16[4,272,128]{2,1,0:T(8,128)(2,1)S(1)}, bf16[4,272,128]{2,1,0:T(8,128)(2,1)S(1)}, u32[]{:S(2)}, u32[]{:S(2)}) collective-permute-start(bf16[4,272,128]{2,1,0:T(8,128)(2,1)S(1)} %get-tuple-element.50), channel_id=1, source_target_pairs={{0,4},{2,6},{4,0},{6,2},{8,12},{10,14},{12,8},{14,10},{16,20},{18,... | collective-permute-start | bytes 835592 | tf_op jit(solution)/shard_map/ppermute | solution.py:298
  21.5 1.1 %copy-start.1 = (f32[4,272,128]{2,1,0:T(8,128)S(1)}, f32[4,272,128]{2,1,0:T(8,128)}, u32[]{:S(2)}) copy-start(f32[4,272,128]{2,1,0:T(8,128)} %copy-done) | copy-start | bytes 1671172
  22.6 11.0 %collective-permute-start.4 = (bf16[272,128]{1,0:T(8,128)(2,1)S(1)}, bf16[272,128]{1,0:T(8,128)(2,1)S(1)}, u32[]{:S(2)}, u32[]{:S(2)}) collective-permute-start(bf16[272,128]{1,0:T(8,128)(2,1)S(1)} %get-tuple-element.52), channel_id=1, source_target_pairs={{0,8},{2,10},{4,12},{6,14},{8,16},{10,18},{12,20},{14,22},{16,24},... | collective-permute-start | bytes 208904 | tf_op jit(solution)/shard_map/ppermute | solution.py:302
  24.5 9.1 %collective-permute-start.5 = (bf16[272,128]{1,0:T(8,128)(2,1)S(1)}, bf16[272,128]{1,0:T(8,128)(2,1)S(1)}, u32[]{:S(2)}, u32[]{:S(2)}) collective-permute-start(bf16[272,128]{1,0:T(8,128)(2,1)S(1)} %get-tuple-element.53), channel_id=1, source_target_pairs={{0,16},{2,18},{4,20},{6,22},{8,24},{10,26},{12,28},{14,30},{16,0},... | collective-permute-start | bytes 208904 | tf_op jit(solution)/shard_map/ppermute | solution.py:302
  27.1 6.5 %collective-permute-start.6 = (bf16[272,128]{1,0:T(8,128)(2,1)S(1)}, bf16[272,128]{1,0:T(8,128)(2,1)S(1)}, u32[]{:S(2)}, u32[]{:S(2)}) collective-permute-start(bf16[272,128]{1,0:T(8,128)(2,1)S(1)} %get-tuple-element.54), channel_id=1, source_target_pairs={{0,24},{2,26},{4,28},{6,30},{8,0},{10,2},{12,4},{14,6},{16,8},{18,... | collective-permute-start | bytes 208904 | tf_op jit(solution)/shard_map/ppermute | solution.py:302
  30.3 3.2 %copy-start.2 = (f32[128,4096]{1,0:T(8,128)S(1)}, f32[128,4096]{1,0:T(8,128)}, u32[]{:S(2)}) copy-start(f32[128,4096]{1,0:T(8,128)} %get-tuple-element.42.branch) | copy-start | bytes 6291460
  30.3 3.3 %copy-start.4 = (bf16[128,4096]{1,0:T(8,128)(2,1)S(1)}, bf16[128,4096]{1,0:T(8,128)(2,1)}, u32[]{:S(2)}) copy-start(bf16[128,4096]{1,0:T(8,128)(2,1)} %get-tuple-element.43.sent) | copy-start | bytes 3145732

commit v3 on v2

--- a/solution.py
+++ b/solution.py
@@ -45,8 +45,8 @@
 
 
 def branch_kernel(
-    counts_far, x_far, top_far, v_far, w_far, gain_far,
-    sent, packed, branch, normed, masked, gain_out,
+    low, counts_far, x_far, top_far, v_far, w_far, gain_far,
+    sent, packed, branch, scatter, more, normed, masked, gain_out,
     counts, x, top, v, w, gain, back, gain_part, ready,
 ):
     rows, width = sent.shape
@@ -68,7 +68,12 @@
     for m in range(micro_count):
         piece = v[m * slots : (m + 1) * slots, :]
         masked[m * slots : (m + 1) * slots, :] = jnp.where(slot < counts[m], piece, jnp.zeros_like(piece))
-    gather = one_hot(counts, micro_count, slots, 0, packed.shape[0])
+    live = jnp.int32(0)
+    for m in range(micro_count):
+        live += counts[m]
+    more[0] = (live > low + packed.shape[0]).astype(jnp.int32)
+    gather = one_hot(counts, micro_count, slots, low, packed.shape[0])
+    scatter[...] = gather
     values = masked[...]
     fetches[2].wait()
     for cut in cuts(width, tile_width):
@@ -106,17 +111,19 @@
         gain_out[:, cut] = jnp.sum(gain_part[:, cut], axis=0, keepdims=True)
 
 
-def branch_rows(room, counts, x, top, v, w, gain):
+def branch_rows(low, room, counts, x, top, v, w, gain):
     rows, width = top.shape
     depth = v.shape[2]
     return pl.pallas_call(
-        branch_kernel,
+        functools.partial(branch_kernel, low),
         in_specs=[pl.BlockSpec(memory_space=pltpu.HBM)] * 6,
-        out_specs=[near] * 6,
+        out_specs=[near] * 4 + [scalar] + [near] * 3,
         out_shape=[
             jax.ShapeDtypeStruct((rows, width), bf16),
             jax.ShapeDtypeStruct((room, width), bf16),
             jax.ShapeDtypeStruct((rows, width), f32),
+            jax.ShapeDtypeStruct((rows, room), bf16),
+            jax.ShapeDtypeStruct((1,), jnp.int32),
             jax.ShapeDtypeStruct((rows, width), bf16),
             jax.ShapeDtypeStruct((rows, depth), bf16),
             jax.ShapeDtypeStruct((1, width), f32),
@@ -137,62 +144,61 @@
     )(*[far(a) for a in (counts, x, top, v, w, gain)])
 
 
-def pack_kernel(low, counts, sent, packed):
-    micro_count = counts.shape[0]
-    gather = one_hot(counts, micro_count, sent.shape[0] // micro_count, low, packed.shape[0])
+def pack_kernel(gather, sent, packed):
     for cut in cuts(sent.shape[1], tile_width):
         packed[:, cut] = lax.dot_general(
-            gather, sent[:, cut], contract_rows, preferred_element_type=f32
+            gather[...], sent[:, cut], contract_rows, preferred_element_type=f32
         ).astype(bf16)
 
 
-def pack(low, room, counts, sent):
-    return pl.pallas_call(
-        functools.partial(pack_kernel, low),
-        in_specs=[scalar, near],
+def pack(gather, sent):
+    return pl.pallas_call(
+        pack_kernel,
+        in_specs=[near, near],
         out_specs=near,
-        out_shape=jax.ShapeDtypeStruct((room, sent.shape[1]), bf16),
-        compiler_params=roomy,
-        cost_estimate=small_cost,
-    )(counts, sent)
-
-
-def receive_kernel(low, counts, is_target, received, branch, sent, out_far, out, done):
+        out_shape=jax.ShapeDtypeStruct((gather.shape[1], sent.shape[1]), bf16),
+        compiler_params=roomy,
+        cost_estimate=small_cost,
+    )(gather, sent)
+
+
+def receive_kernel(target, step, scatter, received, branch, sent, more, *rest):
+    out_far, more_out, out, done = rest[-4:]
     rows, width = sent.shape
-    micro_count = counts.shape[0]
-    slots = rows // micro_count
-    scatter = one_hot(counts, micro_count, slots, low, received.shape[0])
-    covered = jnp.sum(scatter.astype(f32), axis=1, keepdims=True) * is_target[0].astype(f32) > 0.5
-    step = 1024 if width % 1024 == 0 else width
+    place = scatter[...]
+    here = (lax.axis_index("section") == target).astype(f32)
+    covered = jnp.sum(place.astype(f32), axis=1, keepdims=True) * here > 0.5
     writes = []
     for k, wide_cut in enumerate(cuts(width, step)):
-        for at in range(k * step, (k + 1) * step, tile_width if step % tile_width == 0 else step):
-            cut = pl.ds(at, tile_width if step % tile_width == 0 else step)
-            incoming = jnp.dot(scatter, received[:, cut], preferred_element_type=f32)
+        for at in range(k * step, (k + 1) * step, tile_width):
+            cut = pl.ds(at, tile_width)
+            incoming = jnp.dot(place, received[:, cut], preferred_element_type=f32)
             updated = (incoming + branch[:, cut]).astype(bf16)
             out[:, cut] = jnp.where(covered, updated, sent[:, cut])
-        write = pltpu.make_async_copy(out.at[:, wide_cut], out_far.at[:, wide_cut], done.at[k])
+        write = pltpu.make_async_copy(out.at[:, wide_cut], out_far.at[0, :, wide_cut], done.at[k])
         write.start()
         writes.append(write)
     for write in writes:
         write.wait()
 
 
-def receive(low, counts, is_target, received, branch, sent):
+def receive(target, scatter, received, branch, sent, more, after):
     rows, width = sent.shape
-    pieces = width // 1024 if width % 1024 == 0 else 1
-    return pl.pallas_call(
-        functools.partial(receive_kernel, low),
-        in_specs=[scalar, scalar, near, near, near],
-        out_specs=pl.BlockSpec(memory_space=pltpu.HBM),
-        out_shape=pltpu.HBM((rows, width), bf16),
-        scratch_shapes=[pltpu.VMEM((rows, width), bf16), pltpu.SemaphoreType.DMA((pieces,))],
-        compiler_params=roomy,
-        cost_estimate=small_cost,
-    )(counts, is_target, received, branch, sent)
-
-
-def terms_kernel(owned_rows, core, normed, masked, gain, keep, give, total):
+    step = 2 * tile_width if width % (2 * tile_width) == 0 else tile_width
+    away = pl.BlockSpec(memory_space=pltpu.HBM)
+    return pl.pallas_call(
+        functools.partial(receive_kernel, target, step),
+        in_specs=[near, near, near, near] + [away] * (1 + len(after)),
+        out_specs=[away, away],
+        out_shape=[pltpu.HBM((1, rows, width), bf16), pltpu.HBM(more.shape, more.dtype)],
+        input_output_aliases={4: 1},
+        scratch_shapes=[pltpu.VMEM((rows, width), bf16), pltpu.SemaphoreType.DMA((width // step,))],
+        compiler_params=roomy,
+        cost_estimate=small_cost,
+    )(scatter, received, branch, sent, more, *[far(a) for a in after])
+
+
+def terms_kernel(owned_rows, normed, masked, gain, keep, give, total):
     width = normed.shape[1]
     values = masked[...]
     gain_rows = width // lanes
@@ -202,7 +208,7 @@
         total[gain_rows + at : gain_rows + at + tile_width, :] = lax.dot_general(
             normed[:, at : at + tile_width], values, contract_rows, preferred_element_type=f32
         )
-    even_core = core[0] == 0
+    even_core = lax.axis_index("dp") % pair == 0
     padded = keep.shape[1]
     for j in range(keep.shape[0]):
         even = total[2 * j * owned_rows : (2 * j + 1) * owned_rows, :]
@@ -215,22 +221,22 @@
             give[j, owned_rows:, :] = blank
 
 
-def pair_terms(core, normed, masked, gain, owned_rows, owners):
+def pair_terms(normed, masked, gain, owned_rows, owners):
     padded = -(-owned_rows // pack_rows) * pack_rows
     half = jax.ShapeDtypeStruct((owners // pair, padded, lanes), f32)
     return pl.pallas_call(
         functools.partial(terms_kernel, owned_rows),
-        in_specs=[scalar, near, near, near],
+        in_specs=[near, near, near],
         out_specs=[near, near],
         out_shape=[half, half],
         scratch_shapes=[pltpu.VMEM((owners * owned_rows, lanes), f32)],
         compiler_params=roomy,
         cost_estimate=small_cost,
-    )(core, normed, masked, gain)
-
-
-def merge_kernel(side, keep, taken, hold, give):
-    mine = side[0]
+    )(normed, masked, gain)
+
+
+def merge_kernel(keep, taken, hold, give):
+    mine = lax.axis_index("dp") // pair % 2
     for k in range(hold.shape[0]):
         here = 2 * k + mine
         there = 2 * k + 1 - mine
@@ -238,37 +244,38 @@
         give[k] = (keep[there] + taken[there]).astype(bf16)
 
 
-def merge_terms(side, keep, taken):
+def merge_terms(keep, taken):
     half = (keep.shape[0] // 2,) + keep.shape[1:]
     return pl.pallas_call(
         merge_kernel,
-        in_specs=[scalar, near, near],
+        in_specs=[near, near],
         out_specs=[near, near],
         out_shape=[jax.ShapeDtypeStruct(half, f32), jax.ShapeDtypeStruct(half, bf16)],
         compiler_params=roomy,
         cost_estimate=small_cost,
-    )(side, keep, taken)
-
-
-def split_kernel(place, hold, taken, own, *parts):
+    )(keep, taken)
+
+
+def split_kernel(hold, taken, own, *parts):
     count = hold.shape[0]
-    own[...] = hold[place[0]] + taken[place[0]].astype(f32)
+    place = lax.axis_index("dp") // (2 * pair)
+    own[...] = hold[place] + taken[place].astype(f32)
     for k in range(1, count):
-        at = lax.rem(place[0] + k, count)
+        at = lax.rem(place + k, count)
         parts[k - 1][...] = (hold[at] + taken[at].astype(f32)).astype(bf16)
 
 
-def split_terms(place, hold, taken):
+def split_terms(hold, taken):
     count = hold.shape[0]
     return pl.pallas_call(
         split_kernel,
-        in_specs=[scalar, near, near],
+        in_specs=[near, near],
         out_specs=[near] * count,
         out_shape=[jax.ShapeDtypeStruct(hold.shape[1:], f32)]
         + [jax.ShapeDtypeStruct(hold.shape[1:], bf16)] * (count - 1),
         compiler_params=roomy,
         cost_estimate=small_cost,
-    )(place, hold, taken)
+    )(hold, taken)
 
 
 def total_kernel(owned_rows, factor, own, *rest):
@@ -292,11 +299,11 @@
     )(own, *landed)
 
 
-def plane_sum(owners, owned_rows, factor, spot, keep, taken):
+def plane_sum(owners, owned_rows, factor, keep, taken):
     quad = 2 * pair
-    hold, give = merge_terms((spot // pair % 2).reshape(1), keep, taken)
+    hold, give = merge_terms(keep, taken)
     across = lax.ppermute(give, "dp", [(i, i ^ pair) for i in range(owners)])
-    own, *parts = split_terms((spot // quad).reshape(1), hold, across)
+    own, *parts = split_terms(hold, across)
     landed = []
     for k, part in enumerate(parts):
         landed.append(lax.ppermute(part, "dp", [(i, (i + quad * (k + 1)) % owners) for i in range(owners)]))
@@ -312,40 +319,38 @@
         weight_term = lax.dot_general(normed, masked, contract_rows, preferred_element_type=f32)
         flat = jnp.concatenate([gain.reshape(-1), weight_term.reshape(-1)]) * factor
         return lax.psum_scatter(flat, "dp", scatter_dimension=0, tiled=True)[None, :]
-    spot = lax.axis_index("dp").astype(jnp.int32)
-    keep, give = pair_terms((spot % pair).reshape(1), normed, masked, gain, owned // lanes, owners)
+    keep, give = pair_terms(normed, masked, gain, owned // lanes, owners)
     taken = lax.ppermute(give, "dp", [(i, i ^ 1) for i in range(owners)])
-    return plane_sum(owners, owned // lanes, factor, spot, keep, taken)
+    return plane_sum(owners, owned // lanes, factor, keep, taken)
 
 
 def shards(layer_inputs, top_grad, value_grads, weights, norm_gains, counts):
     rows = layer_inputs.shape[1]
     factor = 1.0 / math.sqrt(rows * lax.axis_size("dp"))
     sections = lax.axis_size("section")
-    section_here = lax.axis_index("section")
     room = -(-rows * 3 // 4 // pack_rows) * pack_rows
     spare = rows - room
-    sent, packed, branch, normed, masked, gain = branch_rows(
-        room, counts, layer_inputs, top_grad, value_grads, weights, norm_gains
-    )
-    result = sent
-    overflow = jnp.sum(counts) > room
+    inputs = (counts, layer_inputs, top_grad, value_grads, weights, norm_gains)
+    result, packed, branch, scatter, more, normed, masked, gain = branch_rows(0, room, *inputs)
+    owned = weight_owned(normed, masked, gain, factor)
     for hop in range(sections - 1):
         target = sections - 2 - hop
-        is_target = (section_here == target).astype(jnp.int32).reshape(1)
-        if hop:
-            packed = pack(0, room, counts, result)
         hops = [(target + 1, target)]
         before = result
+        if hop:
+            packed = pack(scatter, before)
         landed = lax.ppermute(packed, "section", hops)
-        result = receive(0, counts, is_target, landed, branch, before)
-
-        def rest(result):
-            landed = lax.ppermute(pack(room, spare, counts, before), "section", hops)
-            return receive(room, counts, is_target, landed, branch, result)
-
-        result = lax.cond(overflow, rest, lambda result: result, result)
-    owned = weight_owned(normed, masked, gain, factor)
+        updated, more = receive(target, scatter, landed, branch, before, more, (owned,))
+
+        def rest(updated):
+            sent, packed, branch, scatter, more, *_ = branch_rows(room, spare, *inputs)
+            if hop:
+                packed = pack(scatter, before)
+            landed = lax.ppermute(packed, "section", hops)
+            return receive(target, scatter, landed, branch, updated[0], more, ())[0]
+
+        updated = lax.cond(more.reshape(()) > 0, rest, lambda updated: updated, updated)
+        result = updated[0]
     return (result[None], owned)
 
 

time: 34.6 us -> 31.1 us (0.90)
  Pallas kernels: 11.2 us -> 7.54 us
  waiting for transfers between devices: 8.83 us -> 11.5 us
  local copies, waits for them, and re-layouts: 1.87 us -> 0 us
  other arithmetic: 0.63 us -> 0 us
    pallas_call x5, Pallas kernels: 10.4 us -> 6.79 us  [the longest x1 3.67 us: branch_rows(): pl.pallas_call(functools.partial(branch_kernel, low), in_specs=[pl.BlockS...]
    ppermute x3, waiting for transfers between devices: 0.01 us -> 3.49 us  [plane_sum(): lax.ppermute(part, 'dp', [(i, (i + quad * (k + 1)) % owners) for i in ran...]
    unnamed x10 -> x0, local copies, waits for them, and re-layouts: 1.87 us -> none
    reduce_sum x1 -> x0, other arithmetic: 0.63 us -> none  [shards(): overflow = jnp.sum(counts) > room]
    ppermute x1, waiting for transfers between devices: 0.59 us -> 0.01 us  [shards(): landed = lax.ppermute(packed, 'section', hops)]
  transfers between devices with their start and end apart: 6 -> 6, of which waited for: 3 -> 4; matrix products, arithmetic and copies ran while one was open for 2% -> 0% of each run, Pallas kernels for 10% -> 3%
where the time goes in v3:
time: 31.1 us; the launch traced here: 30.9 us
  waiting for transfers between devices  11.5 us (37%)
  starting transfers between devices  10.5 us (34%)
  Pallas kernels  7.54 us (24%)
  between operations  1.31 us (4%)
    ppermute x1, waiting for transfers between devices, plane_sum(): across = lax.ppermute(give, 'dp', [(i, i ^ pair) for i in range(owners)])  6.96 us
    ppermute x3, starting transfers between devices, plane_sum(): lax.ppermute(part, 'dp', [(i, (i + quad * (k + 1)) % owners) for i in ran...  5.79 us
    pallas_call x1, Pallas kernels, branch_rows(): pl.pallas_call(functools.partial(branch_kernel, low), in_specs=[pl.BlockS...  3.67 us
    ppermute x3, waiting for transfers between devices, plane_sum(): lax.ppermute(part, 'dp', [(i, (i + quad * (k + 1)) % owners) for i in ran...  3.49 us
    ppermute x1, starting transfers between devices, plane_sum(): across = lax.ppermute(give, 'dp', [(i, i ^ pair) for i in range(owners)])  2.95 us
    pallas_call x1, Pallas kernels, receive(): pl.pallas_call(functools.partial(receive_kernel, target, step), in_specs=...  2.36 us
    ppermute x1, starting transfers between devices, shards(): landed = lax.ppermute(packed, 'section', hops)  1.28 us
    ppermute x1, waiting for transfers between devices, weight_owned(): taken = lax.ppermute(give, 'dp', [(i, i ^ 1) for i in range(owners)])  1.09 us
  transfers between devices with their start and end apart: 6, of which 4 were waited for; matrix products, arithmetic and copies ran while one was open for 0% of the time, Pallas kernels for 3%

profile of v3, /device:TPU:0, one launch (start us, length us, event | category | flops | bytes accessed | tf_op | source)
XLA Modules:
  0.0 30.9 jit_solution(8767657872833804883)
XLA Ops:
  0.6 3.7 %shard_map.77 = (bf16[128,4096]{1,0:T(8,128)(2,1)S(1)}, bf16[96,4096]{1,0:T(8,128)(2,1)S(1)}, f32[128,4096]{1,0:T(8,128)S(1)}, bf16[128,96]{1,0:T(8,128)(2,1)S(1...) custom-call(s32[8]{0:T(128)} %counts_far.1, ...), custom_call_target="tpu_custom_call" | custom-call | flops 1048576 | bytes 65536 | tf_op jit(solution)/shard_map/pallas_call | solution.py:117
  4.3 0.6 %shard_map.78 = (f32[8,272,128]{2,1,0:T(8,128)S(1)}, f32[8,272,128]{2,1,0:T(8,128)S(1)}) custom-call(bf16[128,4096]{1,0:T(8,128)(2,1)S(1)} %get-tuple-element.55.normed, bf16[128,128]{1,0:T(8,128)(2,1)S(1)} %get-tuple-element.56.masked, f32[1,4096]{1,0:T(1,128)S(1)} %get-tuple-element.57.gain), custom_call_target="tpu_custom_call" | custom-call | flops 1048576 | bytes 65536 | tf_op jit(solution)/shard_map/pallas_call | solution.py:227
  4.9 0.5 %collective-permute-start.2 = (f32[8,272,128]{2,1,0:T(8,128)S(1)}, f32[8,272,128]{2,1,0:T(8,128)S(1)}, u32[]{:S(2)}, u32[]{:S(2)}) collective-permute-start(f32[8,272,128]{2,1,0:T(8,128)S(1)} %get-tuple-element.59), channel_id=1, source_target_pairs={{0,2},{2,0},{4,6},{6,4},{8,10},{10,8},{12,14},{14,12},{16,18},{18,... | collective-permute-start | bytes 3342344 | tf_op jit(solution)/shard_map/ppermute | solution.py:323
  5.4 1.3 %collective-permute-start.1 = (bf16[96,4096]{1,0:T(8,128)(2,1)S(1)}, bf16[96,4096]{1,0:T(8,128)(2,1)S(1)}, u32[]{:S(2)}, u32[]{:S(2)}) collective-permute-start(bf16[96,4096]{1,0:T(8,128)(2,1)S(1)} %get-tuple-element.51), channel_id=1, source_target_pairs={{1,0},{3,2},{5,4},{7,6},{9,8},{11,10},{13,12},{15,14},{17,16},{19,... | collective-permute-start | bytes 2359304 | tf_op jit(solution)/shard_map/ppermute | solution.py:342
  6.7 1.1 %collective-permute-done.2.taken = f32[8,272,128]{2,1,0:T(8,128)S(1)} collective-permute-done((f32[8,272,128]{2,1,0:T(8,128)S(1)}, f32[8,272,128]{2,1,0:T(8,128)S(1)}, u32[]{:S(2)}, u32[]{:S(2)}) %collective-permute-start.2) | collective-permute-done | bytes 1114144 | tf_op jit(solution)/shard_map/ppermute | solution.py:323
  7.8 0.1 shard_map.79
  7.9 3.0 %collective-permute-start.3 = (bf16[4,272,128]{2,1,0:T(8,128)(2,1)S(1)}, bf16[4,272,128]{2,1,0:T(8,128)(2,1)S(1)}, u32[]{:S(2)}, u32[]{:S(2)}) collective-permute-start(bf16[4,272,128]{2,1,0:T(8,128)(2,1)S(1)} %get-tuple-element.61), channel_id=1, source_target_pairs={{0,4},{2,6},{4,0},{6,2},{8,12},{10,14},{12,8},{14,10},{16,20},{18,... | collective-permute-start | bytes 835592 | tf_op jit(solution)/shard_map/ppermute | solution.py:305
  10.9 7.0 %collective-permute-done.3.taken = bf16[4,272,128]{2,1,0:T(8,128)(2,1)S(1)} collective-permute-done((bf16[4,272,128]{2,1,0:T(8,128)(2,1)S(1)}, bf16[4,272,128]{2,1,0:T(8,128)(2,1)S(1)}, u32[]{:S(2)}, u32[]{:S(2)}) %collective-permute-start.3) | collective-permute-done | bytes 278560 | tf_op jit(solution)/shard_map/ppermute | solution.py:305
  17.8 0.1 shard_map.80
  17.9 1.9 %collective-permute-start.4 = (bf16[272,128]{1,0:T(8,128)(2,1)S(1)}, bf16[272,128]{1,0:T(8,128)(2,1)S(1)}, u32[]{:S(2)}, u32[]{:S(2)}) collective-permute-start(bf16[272,128]{1,0:T(8,128)(2,1)S(1)} %get-tuple-element.63), channel_id=1, source_target_pairs={{0,8},{2,10},{4,12},{6,14},{8,16},{10,18},{12,20},{14,22},{16,24},... | collective-permute-start | bytes 208904 | tf_op jit(solution)/shard_map/ppermute | solution.py:309
  19.7 2.6 %collective-permute-start.5 = (bf16[272,128]{1,0:T(8,128)(2,1)S(1)}, bf16[272,128]{1,0:T(8,128)(2,1)S(1)}, u32[]{:S(2)}, u32[]{:S(2)}) collective-permute-start(bf16[272,128]{1,0:T(8,128)(2,1)S(1)} %get-tuple-element.64), channel_id=1, source_target_pairs={{0,16},{2,18},{4,20},{6,22},{8,24},{10,26},{12,28},{14,30},{16,0},... | collective-permute-start | bytes 208904 | tf_op jit(solution)/shard_map/ppermute | solution.py:309
  22.3 1.3 %collective-permute-start.6 = (bf16[272,128]{1,0:T(8,128)(2,1)S(1)}, bf16[272,128]{1,0:T(8,128)(2,1)S(1)}, u32[]{:S(2)}, u32[]{:S(2)}) collective-permute-start(bf16[272,128]{1,0:T(8,128)(2,1)S(1)} %get-tuple-element.65), channel_id=1, source_target_pairs={{0,24},{2,26},{4,28},{6,30},{8,0},{10,2},{12,4},{14,6},{16,8},{18,... | collective-permute-start | bytes 208904 | tf_op jit(solution)/shard_map/ppermute | solution.py:309
  23.7 1.3 %collective-permute-done.4.rest_0_ = bf16[272,128]{1,0:T(8,128)(2,1)S(1)} collective-permute-done((bf16[272,128]{1,0:T(8,128)(2,1)S(1)}, bf16[272,128]{1,0:T(8,128)(2,1)S(1)}, u32[]{:S(2)}, u32[]{:S(2)}) %collective-permute-start.4) | collective-permute-done | bytes 69664 | tf_op jit(solution)/shard_map/ppermute | solution.py:309
  25.0 2.2 %collective-permute-done.5.rest_1_ = bf16[272,128]{1,0:T(8,128)(2,1)S(1)} collective-permute-done((bf16[272,128]{1,0:T(8,128)(2,1)S(1)}, bf16[272,128]{1,0:T(8,128)(2,1)S(1)}, u32[]{:S(2)}, u32[]{:S(2)}) %collective-permute-start.5) | collective-permute-done | bytes 69664 | tf_op jit(solution)/shard_map/ppermute | solution.py:309
  27.2 0.0 collective-permute-done.6.rest_2_
  27.2 0.8 %shard_map.81.rest_0_ = f32[1,33024]{1,0:T(1,128)} custom-call(f32[272,128]{1,0:T(8,128)S(1)} %get-tuple-element.62.own, bf16[272,128]{1,0:T(8,128)(2,1)S(1)} %collective-permute-done.4.rest_0_, bf16[272,128]{1,0:T(8,128)(2,1)S(1)} %collective-permute-done.5.rest_1_, bf16[272,128]{1,0:T(8,128)(2,1)S(1)} %collective-permute-done.6.rest_2_), custom_call_target="tpu_custom_call" | custom-call | flops 1048576 | bytes 65536 | tf_op jit(solution)/shard_map/pallas_call | solution.py:292
  27.9 0.0 collective-permute-done.1.received
  27.9 2.4 %shard_map.82 = (bf16[1,128,4096]{2,1,0:T(8,128)(2,1)}, s32[1]{0:T(128)}) custom-call(bf16[128,96]{1,0:T(8,128)(2,1)S(1)} %get-tuple-element.50.scatter, bf16[96,4096]{1,0:T(8,128)(2,1)S(1)} %collective-permute-done.1.received, f32[128,4096]{1,0:T(8,128)S(1)} %get-tuple-element.52.branch, ...), custom_call_target="tpu_custom_call", output_to_operand_aliasing={{1}: (4, {})} | custom-call | flops 1048576 | bytes 65536 | tf_op jit(solution)/shard_map/pallas_call | solution.py:189
  (1 shorter events, 0.0 us)
Async XLA Ops:
  4.9 2.9 %collective-permute-start.2 = (f32[8,272,128]{2,1,0:T(8,128)S(1)}, f32[8,272,128]{2,1,0:T(8,128)S(1)}, u32[]{:S(2)}, u32[]{:S(2)}) collective-permute-start(f32[8,272,128]{2,1,0:T(8,128)S(1)} %get-tuple-element.59), channel_id=1, source_target_pairs={{0,2},{2,0},{4,6},{6,4},{8,10},{10,8},{12,14},{14,12},{16,18},{18,... | collective-permute-start | bytes 3342344 | tf_op jit(solution)/shard_map/ppermute | solution.py:323
  5.4 22.5 %collective-permute-start.1 = (bf16[96,4096]{1,0:T(8,128)(2,1)S(1)}, bf16[96,4096]{1,0:T(8,128)(2,1)S(1)}, u32[]{:S(2)}, u32[]{:S(2)}) collective-permute-start(bf16[96,4096]{1,0:T(8,128)(2,1)S(1)} %get-tuple-element.51), channel_id=1, source_target_pairs={{1,0},{3,2},{5,4},{7,6},{9,8},{11,10},{13,12},{15,14},{17,16},{19,... | collective-permute-start | bytes 2359304 | tf_op jit(solution)/shard_map/ppermute | solution.py:342
  7.9 9.9 %collective-permute-start.3 = (bf16[4,272,128]{2,1,0:T(8,128)(2,1)S(1)}, bf16[4,272,128]{2,1,0:T(8,128)(2,1)S(1)}, u32[]{:S(2)}, u32[]{:S(2)}) collective-permute-start(bf16[4,272,128]{2,1,0:T(8,128)(2,1)S(1)} %get-tuple-element.61), channel_id=1, source_target_pairs={{0,4},{2,6},{4,0},{6,2},{8,12},{10,14},{12,8},{14,10},{16,20},{18,... | collective-permute-start | bytes 835592 | tf_op jit(solution)/shard_map/ppermute | solution.py:305
  17.9 7.1 %collective-permute-start.4 = (bf16[272,128]{1,0:T(8,128)(2,1)S(1)}, bf16[272,128]{1,0:T(8,128)(2,1)S(1)}, u32[]{:S(2)}, u32[]{:S(2)}) collective-permute-start(bf16[272,128]{1,0:T(8,128)(2,1)S(1)} %get-tuple-element.63), channel_id=1, source_target_pairs={{0,8},{2,10},{4,12},{6,14},{8,16},{10,18},{12,20},{14,22},{16,24},... | collective-permute-start | bytes 208904 | tf_op jit(solution)/shard_map/ppermute | solution.py:309
  19.7 7.4 %collective-permute-start.5 = (bf16[272,128]{1,0:T(8,128)(2,1)S(1)}, bf16[272,128]{1,0:T(8,128)(2,1)S(1)}, u32[]{:S(2)}, u32[]{:S(2)}) collective-permute-start(bf16[272,128]{1,0:T(8,128)(2,1)S(1)} %get-tuple-element.64), channel_id=1, source_target_pairs={{0,16},{2,18},{4,20},{6,22},{8,24},{10,26},{12,28},{14,30},{16,0},... | collective-permute-start | bytes 208904 | tf_op jit(solution)/shard_map/ppermute | solution.py:309
  22.3 4.8 %collective-permute-start.6 = (bf16[272,128]{1,0:T(8,128)(2,1)S(1)}, bf16[272,128]{1,0:T(8,128)(2,1)S(1)}, u32[]{:S(2)}, u32[]{:S(2)}) collective-permute-start(bf16[272,128]{1,0:T(8,128)(2,1)S(1)} %get-tuple-element.65), channel_id=1, source_target_pairs={{0,24},{2,26},{4,28},{6,30},{8,0},{10,2},{12,4},{14,6},{16,8},{18,... | collective-permute-start | bytes 208904 | tf_op jit(solution)/shard_map/ppermute | solution.py:309

commit v4 on v3

--- a/solution.py
+++ b/solution.py
@@ -46,10 +46,10 @@
 
 def branch_kernel(
     low, counts_far, x_far, top_far, v_far, w_far, gain_far,
-    sent, packed, branch, scatter, more, normed, masked, gain_out,
-    counts, x, top, v, w, gain, back, gain_part, ready,
+    packed, addend, scatter, more, normed, masked, gain_out,
+    counts, x, top, v, w, gain, back, gain_part, sent, ready,
 ):
-    rows, width = sent.shape
+    rows, width = addend.shape
     micro_count = counts.shape[0]
     slots = rows // micro_count
     fetches = [
@@ -73,7 +73,8 @@
         live += counts[m]
     more[0] = (live > low + packed.shape[0]).astype(jnp.int32)
     gather = one_hot(counts, micro_count, slots, low, packed.shape[0])
-    scatter[...] = gather
+    receives = lax.axis_index("section") < lax.axis_size("section") - 1
+    scatter[...] = jnp.where(receives, gather.astype(f32), 0.0).astype(bf16)
     values = masked[...]
     fetches[2].wait()
     for cut in cuts(width, tile_width):
@@ -91,6 +92,13 @@
             products += wide * back[part, cut] * gain[:, cut]
         scale = lax.rsqrt(jnp.sum(squares, axis=1, keepdims=True) / width + eps_norm)
         pull = scale * jnp.sum(products, axis=1, keepdims=True) / width
+        waits = jnp.concatenate(
+            [
+                lax.broadcasted_iota(jnp.int32, (slots, 1), 0) < jnp.where(receives, counts[m], 0)
+                for m in range(at // slots, (at + 32) // slots)
+            ],
+            axis=0,
+        )
         for cut in cuts(width, 2 * lanes):
             unit = x[part, cut].astype(f32) * scale
             here = back[part, cut]
@@ -101,8 +109,9 @@
             gain_part[:, cut] = product
             normed[part, cut] = (unit * scaled).astype(bf16)
             own = scale * (scaled * here - unit * pull)
-            branch[part, cut] = own
-            sent[part, cut] = (top[part, cut].astype(f32) + own).astype(bf16)
+            whole = (top[part, cut].astype(f32) + own).astype(bf16)
+            sent[part, cut] = whole
+            addend[part, cut] = jnp.where(waits, own, whole.astype(f32))
     for cut in cuts(width, tile_width):
         packed[:, cut] = lax.dot_general(
             gather, sent[:, cut], contract_rows, preferred_element_type=f32
@@ -117,13 +126,12 @@
     return pl.pallas_call(
         functools.partial(branch_kernel, low),
         in_specs=[pl.BlockSpec(memory_space=pltpu.HBM)] * 6,
-        out_specs=[near] * 4 + [scalar] + [near] * 3,
+        out_specs=[near] * 3 + [scalar] + [near] * 3,
         out_shape=[
-            jax.ShapeDtypeStruct((rows, width), bf16),
             jax.ShapeDtypeStruct((room, width), bf16),
             jax.ShapeDtypeStruct((rows, width), f32),
             jax.ShapeDtypeStruct((rows, room), bf16),
-            jax.ShapeDtypeStruct((1,), jnp.int32),
+            pltpu.SMEM((1,), jnp.int32),
             jax.ShapeDtypeStruct((rows, width), bf16),
             jax.ShapeDtypeStruct((rows, depth), bf16),
             jax.ShapeDtypeStruct((1, width), f32),
@@ -137,6 +145,7 @@
             pltpu.VMEM((1, width), f32),
             pltpu.VMEM((rows, width), f32),
             pltpu.VMEM((sublanes, width), f32),
+            pltpu.VMEM((rows, width), bf16),
             pltpu.SemaphoreType.DMA((6,)),
         ],
         compiler_params=roomy,
@@ -162,40 +171,40 @@
     )(gather, sent)
 
 
-def receive_kernel(target, step, scatter, received, branch, sent, more, *rest):
+def receive_kernel(target, first, scatter, received, addend, more, *rest):
     out_far, more_out, out, done = rest[-4:]
-    rows, width = sent.shape
+    more_out[0] = more[0]
+    rows, width = addend.shape
     place = scatter[...]
-    here = (lax.axis_index("section") == target).astype(f32)
-    covered = jnp.sum(place.astype(f32), axis=1, keepdims=True) * here > 0.5
+    if not first:
+        here = (lax.axis_index("section") == target).astype(f32)
+        covered = jnp.sum(place.astype(f32), axis=1, keepdims=True) * here > 0.5
     writes = []
-    for k, wide_cut in enumerate(cuts(width, step)):
-        for at in range(k * step, (k + 1) * step, tile_width):
-            cut = pl.ds(at, tile_width)
-            incoming = jnp.dot(place, received[:, cut], preferred_element_type=f32)
-            updated = (incoming + branch[:, cut]).astype(bf16)
-            out[:, cut] = jnp.where(covered, updated, sent[:, cut])
-        write = pltpu.make_async_copy(out.at[:, wide_cut], out_far.at[0, :, wide_cut], done.at[k])
+    for k, cut in enumerate(cuts(width, tile_width)):
+        total = jnp.dot(place, received[:, cut], preferred_element_type=f32) + addend[:, cut]
+        if not first:
+            total = jnp.where(covered, total, rest[0][:, cut].astype(f32))
+        out[:, cut] = total.astype(bf16)
+        write = pltpu.make_async_copy(out.at[:, cut], out_far.at[0, :, cut], done.at[k])
         write.start()
         writes.append(write)
     for write in writes:
         write.wait()
 
 
-def receive(target, scatter, received, branch, sent, more, after):
-    rows, width = sent.shape
-    step = 2 * tile_width if width % (2 * tile_width) == 0 else tile_width
+def receive(target, scatter, received, addend, more, after, previous=None):
+    rows, width = addend.shape
     away = pl.BlockSpec(memory_space=pltpu.HBM)
-    return pl.pallas_call(
-        functools.partial(receive_kernel, target, step),
-        in_specs=[near, near, near, near] + [away] * (1 + len(after)),
-        out_specs=[away, away],
-        out_shape=[pltpu.HBM((1, rows, width), bf16), pltpu.HBM(more.shape, more.dtype)],
-        input_output_aliases={4: 1},
-        scratch_shapes=[pltpu.VMEM((rows, width), bf16), pltpu.SemaphoreType.DMA((width // step,))],
-        compiler_params=roomy,
-        cost_estimate=small_cost,
-    )(scatter, received, branch, sent, more, *[far(a) for a in after])
+    others = [far(a) for a in after] if previous is None else [previous]
+    return pl.pallas_call(
+        functools.partial(receive_kernel, target, previous is None),
+        in_specs=[near, near, near, scalar] + [away if previous is None else near] * len(others),
+        out_specs=[away, scalar],
+        out_shape=[pltpu.HBM((1, rows, width), bf16), pltpu.SMEM(more.shape, more.dtype)],
+        scratch_shapes=[pltpu.VMEM((rows, width), bf16), pltpu.SemaphoreType.DMA((width // tile_width,))],
+        compiler_params=roomy,
+        cost_estimate=small_cost,
+    )(scatter, received, addend, more, *others)
 
 
 def terms_kernel(owned_rows, normed, masked, gain, keep, give, total):
@@ -235,22 +244,39 @@
     )(normed, masked, gain)
 
 
-def merge_kernel(keep, taken, hold, give):
-    mine = lax.axis_index("dp") // pair % 2
-    for k in range(hold.shape[0]):
+def merge_kernel(keep, taken, hold, give, hold_low, *give_low):
+    cut = hold.shape[1]
+    chip = lax.axis_index("dp") // pair
+    mine, place = chip % 2, chip // 2
+    count = hold.shape[0]
+    for k in range(count):
         here = 2 * k + mine
         there = 2 * k + 1 - mine
-        hold[k] = keep[here] + taken[here]
-        give[k] = (keep[there] + taken[there]).astype(bf16)
-
-
-def merge_terms(keep, taken):
-    half = (keep.shape[0] // 2,) + keep.shape[1:]
+        hold[k] = keep[here, :cut, :] + taken[here, :cut, :]
+        give[k] = (keep[there, :cut, :] + taken[there, :cut, :]).astype(bf16)
+    for side in range(2):
+        at = 2 * place + side
+        hold_low[side] = keep[at, cut:, :] + taken[at, cut:, :]
+        for k in range(1, count):
+            at = 2 * lax.rem(place + k, count) + side
+            give_low[k - 1][side] = (keep[at, cut:, :] + taken[at, cut:, :]).astype(bf16)
+
+
+def merge_terms(cut, keep, taken):
+    blocks, padded, _ = keep.shape
+    count = blocks // 2
+    high = (count, cut, lanes)
+    low = (2, padded - cut, lanes)
     return pl.pallas_call(
         merge_kernel,
         in_specs=[near, near],
-        out_specs=[near, near],
-        out_shape=[jax.ShapeDtypeStruct(half, f32), jax.ShapeDtypeStruct(half, bf16)],
+        out_specs=[near] * (2 + count),
+        out_shape=[
+            jax.ShapeDtypeStruct(high, f32),
+            jax.ShapeDtypeStruct(high, bf16),
+            jax.ShapeDtypeStruct(low, f32),
+        ]
+        + [jax.ShapeDtypeStruct(low, bf16)] * (count - 1),
         compiler_params=roomy,
         cost_estimate=small_cost,
     )(keep, taken)
@@ -278,36 +304,66 @@
     )(hold, taken)
 
 
-def total_kernel(owned_rows, factor, own, *rest):
+def cross_kernel(hold, *refs):
+    *landed, own, give = refs
+    mine = lax.axis_index("dp") // pair % 2
+    total = hold[mine]
+    passed = hold[1 - mine]
+    for part in landed:
+        total += part[mine].astype(f32)
+        passed += part[1 - mine].astype(f32)
+    own[...] = total
+    give[...] = passed.astype(bf16)
+
+
+def cross_terms(hold, landed):
+    return pl.pallas_call(
+        cross_kernel,
+        in_specs=[near] * (1 + len(landed)),
+        out_specs=[near, near],
+        out_shape=[jax.ShapeDtypeStruct(hold.shape[1:], f32), jax.ShapeDtypeStruct(hold.shape[1:], bf16)],
+        compiler_params=roomy,
+        cost_estimate=small_cost,
+    )(hold, *landed)
+
+
+def total_kernel(owned_rows, factor, own_low, landed_low, own, *rest):
     out = rest[-1]
     total = own[...]
     for part in rest[:-1]:
         total += part[...].astype(f32)
+    low = (own_low[...] + landed_low[...].astype(f32)) * factor
     total = total * factor
+    cut = total.shape[0]
     for k in range(owned_rows):
-        out[:, k * lanes : (k + 1) * lanes] = total[k : k + 1, :]
-
-
-def total_terms(owned_rows, factor, own, landed):
+        row = total[k : k + 1, :] if k < cut else low[k - cut : k - cut + 1, :]
+        out[:, k * lanes : (k + 1) * lanes] = row
+
+
+def total_terms(owned_rows, factor, own_low, landed_low, own, landed):
     return pl.pallas_call(
         functools.partial(total_kernel, owned_rows, factor),
-        in_specs=[near] * (1 + len(landed)),
+        in_specs=[near] * (3 + len(landed)),
         out_specs=near,
         out_shape=jax.ShapeDtypeStruct((1, owned_rows * lanes), f32),
         compiler_params=roomy,
         cost_estimate=small_cost,
-    )(own, *landed)
+    )(own_low, landed_low, own, *landed)
 
 
 def plane_sum(owners, owned_rows, factor, keep, taken):
     quad = 2 * pair
-    hold, give = merge_terms(keep, taken)
-    across = lax.ppermute(give, "dp", [(i, i ^ pair) for i in range(owners)])
+    shifts = range(quad, owners, quad)
+    near_by = [(i, i ^ pair) for i in range(owners)]
+    farther = [[(i, (i + shift) % owners) for i in range(owners)] for shift in shifts]
+    cut = -(-keep.shape[1] * 2 // 3 // pack_rows) * pack_rows
+    hold, give, hold_low, *give_low = merge_terms(cut, keep, taken)
+    across = lax.ppermute(give, "dp", near_by)
+    landed_low = [lax.ppermute(part, "dp", hops) for part, hops in zip(give_low, farther)]
     own, *parts = split_terms(hold, across)
-    landed = []
-    for k, part in enumerate(parts):
-        landed.append(lax.ppermute(part, "dp", [(i, (i + quad * (k + 1)) % owners) for i in range(owners)]))
-    return total_terms(owned_rows, factor, own, landed)
+    landed = [lax.ppermute(part, "dp", hops) for part, hops in zip(parts, farther)]
+    own_low, cross_low = cross_terms(hold_low, landed_low)
+    return total_terms(owned_rows, factor, own_low, lax.ppermute(cross_low, "dp", near_by), own, landed)
 
 
 def weight_owned(normed, masked, gain, factor):
@@ -331,8 +387,9 @@
     room = -(-rows * 3 // 4 // pack_rows) * pack_rows
     spare = rows - room
     inputs = (counts, layer_inputs, top_grad, value_grads, weights, norm_gains)
-    result, packed, branch, scatter, more, normed, masked, gain = branch_rows(0, room, *inputs)
+    packed, addend, scatter, more, normed, masked, gain = branch_rows(0, room, *inputs)
     owned = weight_owned(normed, masked, gain, factor)
+    result = None
     for hop in range(sections - 1):
         target = sections - 2 - hop
         hops = [(target + 1, target)]
@@ -340,14 +397,14 @@
         if hop:
             packed = pack(scatter, before)
         landed = lax.ppermute(packed, "section", hops)
-        updated, more = receive(target, scatter, landed, branch, before, more, (owned,))
+        updated, more = receive(target, scatter, landed, addend, more, (owned,), before)
 
         def rest(updated):
-            sent, packed, branch, scatter, more, *_ = branch_rows(room, spare, *inputs)
+            packed, addend, scatter, more, *_ = branch_rows(room, spare, *inputs)
             if hop:
                 packed = pack(scatter, before)
             landed = lax.ppermute(packed, "section", hops)
-            return receive(target, scatter, landed, branch, updated[0], more, ())[0]
+            return receive(target, scatter, landed, addend, more, (), updated[0])[0]
 
         updated = lax.cond(more.reshape(()) > 0, rest, lambda updated: updated, updated)
         result = updated[0]

time: 31.1 us -> 28.9 us (0.929)
  waiting for transfers between devices: 11.5 us -> 4.21 us
  starting transfers between devices: 10.5 us -> 17.3 us
  Pallas kernels: 7.54 us -> 6.52 us
  between operations: 1.31 us -> 0.69 us
    ppermute x4 -> x8, waiting for transfers between devices: 10.4 us -> 2.28 us  [the longest x1 2.27 us: plane_sum(): lax.ppermute(cross_low, 'dp', near_by)]
    ppermute x4 -> x8, starting transfers between devices: 8.74 us -> 15.5 us  [the longest x6 11 us: plane_sum(): lax.ppermute(part, 'dp', hops)]
    pallas_call x2 -> x3, Pallas kernels: 2.47 us -> 1.34 us  [the longest x1 1.2 us: receive(): pl.pallas_call(functools.partial(receive_kernel, target, previous is None...]
    ppermute x1, waiting for transfers between devices: 0.01 us -> 0.84 us  [shards(): landed = lax.ppermute(packed, 'section', hops)]
  transfers between devices with their start and end apart: 6 -> 10, of which waited for: 4 -> 3; matrix products, arithmetic and copies ran while one was open for 0% -> 0% of each run, Pallas kernels for 3% -> 3%
where the time goes in v4:
time: 28.9 us; the launch traced here: 28.7 us
  starting transfers between devices  17.3 us (60%)
  Pallas kernels  6.52 us (23%)
  waiting for transfers between devices  4.21 us (15%)
  between operations  0.69 us (2%)
    ppermute x6, starting transfers between devices, plane_sum(): lax.ppermute(part, 'dp', hops)  11 us
    pallas_call x1, Pallas kernels, branch_rows(): pl.pallas_call(functools.partial(branch_kernel, low), in_specs=[pl.BlockS...  3.8 us
    ppermute x1, starting transfers between devices, plane_sum(): across = lax.ppermute(give, 'dp', near_by)  2.95 us
    ppermute x1, waiting for transfers between devices, plane_sum(): lax.ppermute(cross_low, 'dp', near_by)  2.27 us
    ppermute x1, starting transfers between devices, plane_sum(): lax.ppermute(cross_low, 'dp', near_by)  1.58 us
    ppermute x1, starting transfers between devices, shards(): landed = lax.ppermute(packed, 'section', hops)  1.28 us
    pallas_call x1, Pallas kernels, receive(): pl.pallas_call(functools.partial(receive_kernel, target, previous is None...  1.2 us
    ppermute x1, waiting for transfers between devices, weight_owned(): taken = lax.ppermute(give, 'dp', [(i, i ^ 1) for i in range(owners)])  1.09 us
  transfers between devices with their start and end apart: 10, of which 3 were waited for; matrix products, arithmetic and copies ran while one was open for 0% of the time, Pallas kernels for 3%

profile of v4, /device:TPU:0, one launch (start us, length us, event | category | flops | bytes accessed | tf_op | source)
XLA Modules:
  0.0 28.7 jit_solution(2753051125626687062)
XLA Ops:
  0.6 3.8 %shard_map.77 = (bf16[96,4096]{1,0:T(8,128)(2,1)S(1)}, f32[128,4096]{1,0:T(8,128)S(1)}, bf16[128,96]{1,0:T(8,128)(2,1)S(1)}, s32[1]{0:T(128)S(4)}, bf16[128,4096...) custom-call(s32[8]{0:T(128)} %counts_far.1, bf16[1,128,4096]{2,1,0:T(8,128)(2,1)} %x_far.1, ...), custom_call_target="tpu_custom_call" | custom-call | flops 1048576 | bytes 65536 | tf_op jit(solution)/shard_map/pallas_call | solution.py:126
  4.4 0.6 %shard_map.78 = (f32[8,272,128]{2,1,0:T(8,128)S(1)}, f32[8,272,128]{2,1,0:T(8,128)S(1)}) custom-call(bf16[128,4096]{1,0:T(8,128)(2,1)S(1)} %get-tuple-element.59.normed, bf16[128,128]{1,0:T(8,128)(2,1)S(1)} %get-tuple-element.60.masked, f32[1,4096]{1,0:T(1,128)S(1)} %get-tuple-element.61.gain), custom_call_target="tpu_custom_call" | custom-call | flops 1048576 | bytes 65536 | tf_op jit(solution)/shard_map/pallas_call | solution.py:236
  5.0 0.5 %collective-permute-start.2 = (f32[8,272,128]{2,1,0:T(8,128)S(1)}, f32[8,272,128]{2,1,0:T(8,128)S(1)}, u32[]{:S(2)}, u32[]{:S(2)}) collective-permute-start(f32[8,272,128]{2,1,0:T(8,128)S(1)} %get-tuple-element.63), channel_id=1, source_target_pairs={{0,2},{2,0},{4,6},{6,4},{8,10},{10,8},{12,14},{14,12},{16,18},{18,... | collective-permute-start | bytes 3342344 | tf_op jit(solution)/shard_map/ppermute | solution.py:379
  5.6 1.3 %collective-permute-start.1 = (bf16[96,4096]{1,0:T(8,128)(2,1)S(1)}, bf16[96,4096]{1,0:T(8,128)(2,1)S(1)}, u32[]{:S(2)}, u32[]{:S(2)}) collective-permute-start(bf16[96,4096]{1,0:T(8,128)(2,1)S(1)} %get-tuple-element.56), channel_id=1, source_target_pairs={{1,0},{3,2},{5,4},{7,6},{9,8},{11,10},{13,12},{15,14},{17,16},{19,... | collective-permute-start | bytes 2359304 | tf_op jit(solution)/shard_map/ppermute | solution.py:399
  6.8 1.1 %collective-permute-done.2.taken = f32[8,272,128]{2,1,0:T(8,128)S(1)} collective-permute-done((f32[8,272,128]{2,1,0:T(8,128)S(1)}, f32[8,272,128]{2,1,0:T(8,128)S(1)}, u32[]{:S(2)}, u32[]{:S(2)}) %collective-permute-start.2) | collective-permute-done | bytes 1114144 | tf_op jit(solution)/shard_map/ppermute | solution.py:379
  7.9 0.1 shard_map.79
  8.1 3.0 %collective-permute-start.7 = (bf16[4,192,128]{2,1,0:T(8,128)(2,1)S(1)}, bf16[4,192,128]{2,1,0:T(8,128)(2,1)S(1)}, u32[]{:S(2)}, u32[]{:S(2)}) collective-permute-start(bf16[4,192,128]{2,1,0:T(8,128)(2,1)S(1)} %get-tuple-element.71), channel_id=1, source_target_pairs={{0,4},{2,6},{4,0},{6,2},{8,12},{10,14},{12,8},{14,10},{16,20},{18,... | collective-permute-start | bytes 589832 | tf_op jit(solution)/shard_map/ppermute | solution.py:361
  11.0 1.6 %collective-permute-start.3 = (bf16[2,80,128]{2,1,0:T(8,128)(2,1)S(1)}, bf16[2,80,128]{2,1,0:T(8,128)(2,1)S(1)}, u32[]{:S(2)}, u32[]{:S(2)}) collective-permute-start(bf16[2,80,128]{2,1,0:T(8,128)(2,1)S(1)} %get-tuple-element.65), channel_id=1, source_target_pairs={{0,8},{2,10},{4,12},{6,14},{8,16},{10,18},{12,20},{14,22},{16,24},... | collective-permute-start | bytes 122888 | tf_op jit(solution)/shard_map/ppermute | solution.py:362
  12.6 2.6 %collective-permute-start.4 = (bf16[2,80,128]{2,1,0:T(8,128)(2,1)S(1)}, bf16[2,80,128]{2,1,0:T(8,128)(2,1)S(1)}, u32[]{:S(2)}, u32[]{:S(2)}) collective-permute-start(bf16[2,80,128]{2,1,0:T(8,128)(2,1)S(1)} %get-tuple-element.66), channel_id=1, source_target_pairs={{0,16},{2,18},{4,20},{6,22},{8,24},{10,26},{12,28},{14,30},{16,0},... | collective-permute-start | bytes 122888 | tf_op jit(solution)/shard_map/ppermute | solution.py:362
  15.2 1.3 %collective-permute-start.5 = (bf16[2,80,128]{2,1,0:T(8,128)(2,1)S(1)}, bf16[2,80,128]{2,1,0:T(8,128)(2,1)S(1)}, u32[]{:S(2)}, u32[]{:S(2)}) collective-permute-start(bf16[2,80,128]{2,1,0:T(8,128)(2,1)S(1)} %get-tuple-element.67), channel_id=1, source_target_pairs={{0,24},{2,26},{4,28},{6,30},{8,0},{10,2},{12,4},{14,6},{16,8},{18,... | collective-permute-start | bytes 122888 | tf_op jit(solution)/shard_map/ppermute | solution.py:362
  16.5 0.0 collective-permute-done.7.taken
  16.6 1.5 %collective-permute-start.8 = (bf16[192,128]{1,0:T(8,128)(2,1)S(1)}, bf16[192,128]{1,0:T(8,128)(2,1)S(1)}, u32[]{:S(2)}, u32[]{:S(2)}) collective-permute-start(bf16[192,128]{1,0:T(8,128)(2,1)S(1)} %get-tuple-element.73), channel_id=1, source_target_pairs={{0,8},{2,10},{4,12},{6,14},{8,16},{10,18},{12,20},{14,22},{16,24},... | collective-permute-start | bytes 147464 | tf_op jit(solution)/shard_map/ppermute | solution.py:364
  18.1 0.0 collective-permute-done.3.refs_0_
  18.1 2.6 %collective-permute-start.9 = (bf16[192,128]{1,0:T(8,128)(2,1)S(1)}, bf16[192,128]{1,0:T(8,128)(2,1)S(1)}, u32[]{:S(2)}, u32[]{:S(2)}) collective-permute-start(bf16[192,128]{1,0:T(8,128)(2,1)S(1)} %get-tuple-element.74), channel_id=1, source_target_pairs={{0,16},{2,18},{4,20},{6,22},{8,24},{10,26},{12,28},{14,30},{16,0},... | collective-permute-start | bytes 147464 | tf_op jit(solution)/shard_map/ppermute | solution.py:364
  20.7 0.0 collective-permute-done.4.refs_1_
  20.7 1.3 %collective-permute-start.10 = (bf16[192,128]{1,0:T(8,128)(2,1)S(1)}, bf16[192,128]{1,0:T(8,128)(2,1)S(1)}, u32[]{:S(2)}, u32[]{:S(2)}) collective-permute-start(bf16[192,128]{1,0:T(8,128)(2,1)S(1)} %get-tuple-element.75), channel_id=1, source_target_pairs={{0,24},{2,26},{4,28},{6,30},{8,0},{10,2},{12,4},{14,6},{16,8},{18,... | collective-permute-start | bytes 147464 | tf_op jit(solution)/shard_map/ppermute | solution.py:364
  22.0 0.0 collective-permute-done.5.refs_2_
  22.1 1.6 %collective-permute-start.6 = (bf16[80,128]{1,0:T(8,128)(2,1)S(1)}, bf16[80,128]{1,0:T(8,128)(2,1)S(1)}, u32[]{:S(2)}, u32[]{:S(2)}) collective-permute-start(bf16[80,128]{1,0:T(8,128)(2,1)S(1)} %get-tuple-element.69), channel_id=1, source_target_pairs={{0,4},{2,6},{4,0},{6,2},{8,12},{10,14},{12,8},{14,10},{16,20},{18,... | collective-permute-start | bytes 61448 | tf_op jit(solution)/shard_map/ppermute | solution.py:366
  23.7 2.3 %collective-permute-done.6.landed_low = bf16[80,128]{1,0:T(8,128)(2,1)S(1)} collective-permute-done((bf16[80,128]{1,0:T(8,128)(2,1)S(1)}, bf16[80,128]{1,0:T(8,128)(2,1)S(1)}, u32[]{:S(2)}, u32[]{:S(2)}) %collective-permute-start.6) | collective-permute-done | bytes 20512 | tf_op jit(solution)/shard_map/ppermute | solution.py:366
  25.9 0.0 collective-permute-done.8.rest_0_
  25.9 0.0 collective-permute-done.9.rest_1_
  25.9 0.0 collective-permute-done.10.rest_2_
  25.9 0.7 %shard_map.82.rest_0_ = f32[1,33024]{1,0:T(1,128)} custom-call(f32[80,128]{1,0:T(8,128)S(1)} %get-tuple-element.68.own_low, bf16[80,128]{1,0:T(8,128)(2,1)S(1)} %collective-permute-done.6.landed_low, f32[192,128]{1,0:T(8,128)S(1)} %get-tuple-element.72.own, bf16[192,128]{1,0:T(8,128)(2,1)S(1)} %collective-permute-done.8.rest_0_, ...), custom_call_target="tpu_custom_call" | custom-call | flops 1048576 | bytes 65536 | tf_op jit(solution)/shard_map/pallas_call | solution.py:344
  26.7 0.8 %collective-permute-done.1.received = bf16[96,4096]{1,0:T(8,128)(2,1)S(1)} collective-permute-done((bf16[96,4096]{1,0:T(8,128)(2,1)S(1)}, bf16[96,4096]{1,0:T(8,128)(2,1)S(1)}, u32[]{:S(2)}, u32[]{:S(2)}) %collective-permute-start.1) | collective-permute-done | bytes 786464 | tf_op jit(solution)/shard_map/ppermute | solution.py:399
  27.5 1.2 %shard_map.83 = (bf16[1,128,4096]{2,1,0:T(8,128)(2,1)}, s32[1]{0:T(128)S(4)}) custom-call(bf16[128,96]{1,0:T(8,128)(2,1)S(1)} %get-tuple-element.55.scatter, bf16[96,4096]{1,0:T(8,128)(2,1)S(1)} %collective-permute-done.1.received, f32[128,4096]{1,0:T(8,128)S(1)} %get-tuple-element.57.addend, s32[1]{0:T(128)S(4)} %get-tuple-element.58.more, ...), custom_call_target="tpu_custom_call" | custom-call | flops 1048576 | bytes 65536 | tf_op jit(solution)/shard_map/pallas_call | solution.py:199
  (3 shorter events, 0.1 us)
Async XLA Ops:
  5.0 2.9 %collective-permute-start.2 = (f32[8,272,128]{2,1,0:T(8,128)S(1)}, f32[8,272,128]{2,1,0:T(8,128)S(1)}, u32[]{:S(2)}, u32[]{:S(2)}) collective-permute-start(f32[8,272,128]{2,1,0:T(8,128)S(1)} %get-tuple-element.63), channel_id=1, source_target_pairs={{0,2},{2,0},{4,6},{6,4},{8,10},{10,8},{12,14},{14,12},{16,18},{18,... | collective-permute-start | bytes 3342344 | tf_op jit(solution)/shard_map/ppermute | solution.py:379
  5.6 22.0 %collective-permute-start.1 = (bf16[96,4096]{1,0:T(8,128)(2,1)S(1)}, bf16[96,4096]{1,0:T(8,128)(2,1)S(1)}, u32[]{:S(2)}, u32[]{:S(2)}) collective-permute-start(bf16[96,4096]{1,0:T(8,128)(2,1)S(1)} %get-tuple-element.56), channel_id=1, source_target_pairs={{1,0},{3,2},{5,4},{7,6},{9,8},{11,10},{13,12},{15,14},{17,16},{19,... | collective-permute-start | bytes 2359304 | tf_op jit(solution)/shard_map/ppermute | solution.py:399
  8.1 8.5 %collective-permute-start.7 = (bf16[4,192,128]{2,1,0:T(8,128)(2,1)S(1)}, bf16[4,192,128]{2,1,0:T(8,128)(2,1)S(1)}, u32[]{:S(2)}, u32[]{:S(2)}) collective-permute-start(bf16[4,192,128]{2,1,0:T(8,128)(2,1)S(1)} %get-tuple-element.71), channel_id=1, source_target_pairs={{0,4},{2,6},{4,0},{6,2},{8,12},{10,14},{12,8},{14,10},{16,20},{18,... | collective-permute-start | bytes 589832 | tf_op jit(solution)/shard_map/ppermute | solution.py:361
  11.0 7.1 %collective-permute-start.3 = (bf16[2,80,128]{2,1,0:T(8,128)(2,1)S(1)}, bf16[2,80,128]{2,1,0:T(8,128)(2,1)S(1)}, u32[]{:S(2)}, u32[]{:S(2)}) collective-permute-start(bf16[2,80,128]{2,1,0:T(8,128)(2,1)S(1)} %get-tuple-element.65), channel_id=1, source_target_pairs={{0,8},{2,10},{4,12},{6,14},{8,16},{10,18},{12,20},{14,22},{16,24},... | collective-permute-start | bytes 122888 | tf_op jit(solution)/shard_map/ppermute | solution.py:362
  12.6 8.1 %collective-permute-start.4 = (bf16[2,80,128]{2,1,0:T(8,128)(2,1)S(1)}, bf16[2,80,128]{2,1,0:T(8,128)(2,1)S(1)}, u32[]{:S(2)}, u32[]{:S(2)}) collective-permute-start(bf16[2,80,128]{2,1,0:T(8,128)(2,1)S(1)} %get-tuple-element.66), channel_id=1, source_target_pairs={{0,16},{2,18},{4,20},{6,22},{8,24},{10,26},{12,28},{14,30},{16,0},... | collective-permute-start | bytes 122888 | tf_op jit(solution)/shard_map/ppermute | solution.py:362
  15.2 6.9 %collective-permute-start.5 = (bf16[2,80,128]{2,1,0:T(8,128)(2,1)S(1)}, bf16[2,80,128]{2,1,0:T(8,128)(2,1)S(1)}, u32[]{:S(2)}, u32[]{:S(2)}) collective-permute-start(bf16[2,80,128]{2,1,0:T(8,128)(2,1)S(1)} %get-tuple-element.67), channel_id=1, source_target_pairs={{0,24},{2,26},{4,28},{6,30},{8,0},{10,2},{12,4},{14,6},{16,8},{18,... | collective-permute-start | bytes 122888 | tf_op jit(solution)/shard_map/ppermute | solution.py:362
  16.6 9.4 %collective-permute-start.8 = (bf16[192,128]{1,0:T(8,128)(2,1)S(1)}, bf16[192,128]{1,0:T(8,128)(2,1)S(1)}, u32[]{:S(2)}, u32[]{:S(2)}) collective-permute-start(bf16[192,128]{1,0:T(8,128)(2,1)S(1)} %get-tuple-element.73), channel_id=1, source_target_pairs={{0,8},{2,10},{4,12},{6,14},{8,16},{10,18},{12,20},{14,22},{16,24},... | collective-permute-start | bytes 147464 | tf_op jit(solution)/shard_map/ppermute | solution.py:364
  18.1 7.8 %collective-permute-start.9 = (bf16[192,128]{1,0:T(8,128)(2,1)S(1)}, bf16[192,128]{1,0:T(8,128)(2,1)S(1)}, u32[]{:S(2)}, u32[]{:S(2)}) collective-permute-start(bf16[192,128]{1,0:T(8,128)(2,1)S(1)} %get-tuple-element.74), channel_id=1, source_target_pairs={{0,16},{2,18},{4,20},{6,22},{8,24},{10,26},{12,28},{14,30},{16,0},... | collective-permute-start | bytes 147464 | tf_op jit(solution)/shard_map/ppermute | solution.py:364
  20.7 5.2 %collective-permute-start.10 = (bf16[192,128]{1,0:T(8,128)(2,1)S(1)}, bf16[192,128]{1,0:T(8,128)(2,1)S(1)}, u32[]{:S(2)}, u32[]{:S(2)}) collective-permute-start(bf16[192,128]{1,0:T(8,128)(2,1)S(1)} %get-tuple-element.75), channel_id=1, source_target_pairs={{0,24},{2,26},{4,28},{6,30},{8,0},{10,2},{12,4},{14,6},{16,8},{18,... | collective-permute-start | bytes 147464 | tf_op jit(solution)/shard_map/ppermute | solution.py:364
  22.1 3.8 %collective-permute-start.6 = (bf16[80,128]{1,0:T(8,128)(2,1)S(1)}, bf16[80,128]{1,0:T(8,128)(2,1)S(1)}, u32[]{:S(2)}, u32[]{:S(2)}) collective-permute-start(bf16[80,128]{1,0:T(8,128)(2,1)S(1)} %get-tuple-element.69), channel_id=1, source_target_pairs={{0,4},{2,6},{4,0},{6,2},{8,12},{10,14},{12,8},{14,10},{16,20},{18,... | collective-permute-start | bytes 61448 | tf_op jit(solution)/shard_map/ppermute | solution.py:366

commit v5 on v4

--- a/solution.py
+++ b/solution.py
@@ -44,11 +44,25 @@
     return jnp.concatenate(pieces, axis=0).astype(bf16)
 
 
-def branch_kernel(
-    low, counts_far, x_far, top_far, v_far, w_far, gain_far,
-    packed, addend, scatter, more, normed, masked, gain_out,
-    counts, x, top, v, w, gain, back, gain_part, sent, ready,
+def branch_kernel(low, sending, counts_far, x_far, top_far, v_far, w_far, gain_far, *refs):
+    work = functools.partial(branch_work, low, sending, counts_far, x_far, top_far, v_far, w_far, gain_far)
+    if sending is None:
+        work(*refs)
+        return
+    later = lax.axis_index("section") == 0
+    pl.when(jnp.logical_not(later) if sending else later)(lambda: work(*refs[0 if sending else 6 :]))
+
+
+def branch_work(
+    low, sending, counts_far, x_far, top_far, v_far, w_far, gain_far,
+    addend, scatter, more, normed, masked, gain_out, *refs
 ):
+    if sending is False:
+        packed = None
+    else:
+        packed, *refs = refs
+    counts, x, top, v, w, gain, back, gain_part, sent, ready = refs
+    room = scatter.shape[1]
     rows, width = addend.shape
     micro_count = counts.shape[0]
     slots = rows // micro_count
@@ -71,8 +85,8 @@
     live = jnp.int32(0)
     for m in range(micro_count):
         live += counts[m]
-    more[0] = (live > low + packed.shape[0]).astype(jnp.int32)
-    gather = one_hot(counts, micro_count, slots, low, packed.shape[0])
+    more[0] = (live > low + room).astype(jnp.int32)
+    gather = one_hot(counts, micro_count, slots, low, room)
     receives = lax.axis_index("section") < lax.axis_size("section") - 1
     scatter[...] = jnp.where(receives, gather.astype(f32), 0.0).astype(bf16)
     values = masked[...]
@@ -112,30 +126,38 @@
             whole = (top[part, cut].astype(f32) + own).astype(bf16)
             sent[part, cut] = whole
             addend[part, cut] = jnp.where(waits, own, whole.astype(f32))
-    for cut in cuts(width, tile_width):
-        packed[:, cut] = lax.dot_general(
-            gather, sent[:, cut], contract_rows, preferred_element_type=f32
-        ).astype(bf16)
+    if packed is not None:
+        for cut in cuts(width, tile_width):
+            packed[:, cut] = lax.dot_general(
+                gather, sent[:, cut], contract_rows, preferred_element_type=f32
+            ).astype(bf16)
     for cut in cuts(width, tile_width):
         gain_out[:, cut] = jnp.sum(gain_part[:, cut], axis=0, keepdims=True)
 
 
-def branch_rows(low, room, counts, x, top, v, w, gain):
+def branch_rows(low, room, sending, inputs, made=()):
+    counts, x, top, v, w, gain = inputs
     rows, width = top.shape
     depth = v.shape[2]
-    return pl.pallas_call(
-        functools.partial(branch_kernel, low),
-        in_specs=[pl.BlockSpec(memory_space=pltpu.HBM)] * 6,
-        out_specs=[near] * 3 + [scalar] + [near] * 3,
-        out_shape=[
-            jax.ShapeDtypeStruct((room, width), bf16),
-            jax.ShapeDtypeStruct((rows, width), f32),
-            jax.ShapeDtypeStruct((rows, room), bf16),
-            pltpu.SMEM((1,), jnp.int32),
-            jax.ShapeDtypeStruct((rows, width), bf16),
-            jax.ShapeDtypeStruct((rows, depth), bf16),
-            jax.ShapeDtypeStruct((1, width), f32),
-        ],
+    outs = [
+        jax.ShapeDtypeStruct((rows, width), f32),
+        jax.ShapeDtypeStruct((rows, room), bf16),
+        pltpu.SMEM((1,), jnp.int32),
+        jax.ShapeDtypeStruct((rows, width), bf16),
+        jax.ShapeDtypeStruct((rows, depth), bf16),
+        jax.ShapeDtypeStruct((1, width), f32),
+    ]
+    specs = [near, near, scalar, near, near, near]
+    aliases = {}
+    if made:
+        aliases = {6 + k: k for k in range(len(made))}
+    extra = [] if made else [jax.ShapeDtypeStruct((room, width), bf16)]
+    return pl.pallas_call(
+        functools.partial(branch_kernel, low, sending),
+        in_specs=[pl.BlockSpec(memory_space=pltpu.HBM)] * 6 + (specs if made else []),
+        out_specs=specs + [near] * len(extra),
+        out_shape=outs + extra,
+        input_output_aliases=aliases,
         scratch_shapes=[
             pltpu.SMEM(counts.shape, jnp.int32),
             pltpu.VMEM((rows, width), bf16),
@@ -150,7 +172,7 @@
         ],
         compiler_params=roomy,
         cost_estimate=small_cost,
-    )(*[far(a) for a in (counts, x, top, v, w, gain)])
+    )(*[far(a) for a in inputs], *made)
 
 
 def pack_kernel(gather, sent, packed):
@@ -207,7 +229,7 @@
     )(scatter, received, addend, more, *others)
 
 
-def terms_kernel(owned_rows, normed, masked, gain, keep, give, total):
+def terms_kernel(owned_rows, normed, masked, gain, keep, give, keep_low, give_low, total):
     width = normed.shape[1]
     values = masked[...]
     gain_rows = width // lanes
@@ -218,65 +240,79 @@
             normed[:, at : at + tile_width], values, contract_rows, preferred_element_type=f32
         )
     even_core = lax.axis_index("dp") % pair == 0
-    padded = keep.shape[1]
-    for j in range(keep.shape[0]):
-        even = total[2 * j * owned_rows : (2 * j + 1) * owned_rows, :]
-        odd = total[(2 * j + 1) * owned_rows : (2 * j + 2) * owned_rows, :]
-        keep[j, :owned_rows, :] = jnp.where(even_core, even, odd)
-        give[j, :owned_rows, :] = jnp.where(even_core, odd, even)
-        if padded > owned_rows:
-            blank = jnp.zeros((padded - owned_rows, lanes), f32)
-            keep[j, owned_rows:, :] = blank
-            give[j, owned_rows:, :] = blank
-
-
-def pair_terms(normed, masked, gain, owned_rows, owners):
+    blocks, cut, _ = keep.shape
+    blank = jnp.zeros((cut + keep_low.shape[1] - owned_rows, lanes), f32)
+    for j in range(blocks):
+        for low, high, mine, other in ((0, cut, keep, give), (cut, owned_rows, keep_low, give_low)):
+            even = total[2 * j * owned_rows + low : 2 * j * owned_rows + high, :]
+            odd = total[(2 * j + 1) * owned_rows + low : (2 * j + 1) * owned_rows + high, :]
+            if low and blank.shape[0]:
+                even = jnp.concatenate([even, blank], axis=0)
+                odd = jnp.concatenate([odd, blank], axis=0)
+            mine[j] = jnp.where(even_core, even, odd)
+            other[j] = jnp.where(even_core, odd, even).astype(bf16)
+
+
+def pair_terms(normed, masked, gain, cut, owned_rows, owners):
     padded = -(-owned_rows // pack_rows) * pack_rows
-    half = jax.ShapeDtypeStruct((owners // pair, padded, lanes), f32)
+    high = (owners // pair, cut, lanes)
+    low = (owners // pair, padded - cut, lanes)
     return pl.pallas_call(
         functools.partial(terms_kernel, owned_rows),
         in_specs=[near, near, near],
-        out_specs=[near, near],
-        out_shape=[half, half],
-        scratch_shapes=[pltpu.VMEM((owners * owned_rows, lanes), f32)],
-        compiler_params=roomy,
-        cost_estimate=small_cost,
-    )(normed, masked, gain)
-
-
-def merge_kernel(keep, taken, hold, give, hold_low, *give_low):
-    cut = hold.shape[1]
-    chip = lax.axis_index("dp") // pair
-    mine, place = chip % 2, chip // 2
-    count = hold.shape[0]
-    for k in range(count):
-        here = 2 * k + mine
-        there = 2 * k + 1 - mine
-        hold[k] = keep[here, :cut, :] + taken[here, :cut, :]
-        give[k] = (keep[there, :cut, :] + taken[there, :cut, :]).astype(bf16)
-    for side in range(2):
-        at = 2 * place + side
-        hold_low[side] = keep[at, cut:, :] + taken[at, cut:, :]
-        for k in range(1, count):
-            at = 2 * lax.rem(place + k, count) + side
-            give_low[k - 1][side] = (keep[at, cut:, :] + taken[at, cut:, :]).astype(bf16)
-
-
-def merge_terms(cut, keep, taken):
-    blocks, padded, _ = keep.shape
-    count = blocks // 2
-    high = (count, cut, lanes)
-    low = (2, padded - cut, lanes)
-    return pl.pallas_call(
-        merge_kernel,
-        in_specs=[near, near],
-        out_specs=[near] * (2 + count),
+        out_specs=[near] * 4,
         out_shape=[
             jax.ShapeDtypeStruct(high, f32),
             jax.ShapeDtypeStruct(high, bf16),
             jax.ShapeDtypeStruct(low, f32),
-        ]
-        + [jax.ShapeDtypeStruct(low, bf16)] * (count - 1),
+            jax.ShapeDtypeStruct(low, bf16),
+        ],
+        scratch_shapes=[pltpu.VMEM((owners * owned_rows, lanes), f32)],
+        compiler_params=roomy,
+        cost_estimate=small_cost,
+    )(normed, masked, gain)
+
+
+def merge_kernel(keep, taken, hold, give):
+    mine = lax.axis_index("dp") // pair % 2
+    for k in range(hold.shape[0]):
+        here = 2 * k + mine
+        there = 2 * k + 1 - mine
+        hold[k] = keep[here] + taken[here].astype(f32)
+        give[k] = (keep[there] + taken[there].astype(f32)).astype(bf16)
+
+
+def merge_terms(keep, taken):
+    half = (keep.shape[0] // 2,) + keep.shape[1:]
+    return pl.pallas_call(
+        merge_kernel,
+        in_specs=[near, near],
+        out_specs=[near, near],
+        out_shape=[jax.ShapeDtypeStruct(half, f32), jax.ShapeDtypeStruct(half, bf16)],
+        compiler_params=roomy,
+        cost_estimate=small_cost,
+    )(keep, taken)
+
+
+def spread_kernel(keep, taken, hold, *give):
+    place = lax.axis_index("dp") // (2 * pair)
+    count = keep.shape[0] // 2
+    for side in range(2):
+        at = 2 * place + side
+        hold[side] = keep[at] + taken[at].astype(f32)
+        for k in range(1, count):
+            at = 2 * lax.rem(place + k, count) + side
+            give[k - 1][side] = (keep[at] + taken[at].astype(f32)).astype(bf16)
+
+
+def spread_terms(keep, taken):
+    count = keep.shape[0] // 2
+    two = (2,) + keep.shape[1:]
+    return pl.pallas_call(
+        spread_kernel,
+        in_specs=[near, near],
+        out_specs=[near] * count,
+        out_shape=[jax.ShapeDtypeStruct(two, f32)] + [jax.ShapeDtypeStruct(two, bf16)] * (count - 1),
         compiler_params=roomy,
         cost_estimate=small_cost,
     )(keep, taken)
@@ -351,33 +387,32 @@
     )(own_low, landed_low, own, *landed)
 
 
-def plane_sum(owners, owned_rows, factor, keep, taken):
-    quad = 2 * pair
-    shifts = range(quad, owners, quad)
-    near_by = [(i, i ^ pair) for i in range(owners)]
-    farther = [[(i, (i + shift) % owners) for i in range(owners)] for shift in shifts]
-    cut = -(-keep.shape[1] * 2 // 3 // pack_rows) * pack_rows
-    hold, give, hold_low, *give_low = merge_terms(cut, keep, taken)
-    across = lax.ppermute(give, "dp", near_by)
-    landed_low = [lax.ppermute(part, "dp", hops) for part, hops in zip(give_low, farther)]
-    own, *parts = split_terms(hold, across)
-    landed = [lax.ppermute(part, "dp", hops) for part, hops in zip(parts, farther)]
-    own_low, cross_low = cross_terms(hold_low, landed_low)
-    return total_terms(owned_rows, factor, own_low, lax.ppermute(cross_low, "dp", near_by), own, landed)
-
-
 def weight_owned(normed, masked, gain, factor):
     owners = lax.axis_size("dp")
     width = normed.shape[1]
     depth = masked.shape[1]
     owned = (width + width * depth) // owners
-    if depth != lanes or owned % lanes or owners % (2 * pair):
+    quad = 2 * pair
+    if depth != lanes or owned % lanes or owners % quad:
         weight_term = lax.dot_general(normed, masked, contract_rows, preferred_element_type=f32)
         flat = jnp.concatenate([gain.reshape(-1), weight_term.reshape(-1)]) * factor
         return lax.psum_scatter(flat, "dp", scatter_dimension=0, tiled=True)[None, :]
-    keep, give = pair_terms(normed, masked, gain, owned // lanes, owners)
-    taken = lax.ppermute(give, "dp", [(i, i ^ 1) for i in range(owners)])
-    return plane_sum(owners, owned // lanes, factor, keep, taken)
+    owned_rows = owned // lanes
+    cut = -(-owned_rows * 2 // 3 // pack_rows) * pack_rows
+    swap = [(i, i ^ 1) for i in range(owners)]
+    near_by = [(i, i ^ pair) for i in range(owners)]
+    farther = [[(i, (i + shift) % owners) for i in range(owners)] for shift in range(quad, owners, quad)]
+    keep, give, keep_low, give_low = pair_terms(normed, masked, gain, cut, owned_rows, owners)
+    taken = lax.ppermute(give, "dp", swap)
+    taken_low = lax.ppermute(give_low, "dp", swap)
+    hold, give = merge_terms(keep, taken)
+    across = lax.ppermute(give, "dp", near_by)
+    hold_low, *parts_low = spread_terms(keep_low, taken_low)
+    landed_low = [lax.ppermute(part, "dp", hops) for part, hops in zip(parts_low, farther)]
+    own, *parts = split_terms(hold, across)
+    landed = [lax.ppermute(part, "dp", hops) for part, hops in zip(parts, farther)]
+    own_low, cross_low = cross_terms(hold_low, landed_low)
+    return total_terms(owned_rows, factor, own_low, lax.ppermute(cross_low, "dp", near_by), own, landed)
 
 
 def shards(layer_inputs, top_grad, value_grads, weights, norm_gains, counts):
@@ -387,7 +422,8 @@
     room = -(-rows * 3 // 4 // pack_rows) * pack_rows
     spare = rows - room
     inputs = (counts, layer_inputs, top_grad, value_grads, weights, norm_gains)
-    packed, addend, scatter, more, normed, masked, gain = branch_rows(0, room, *inputs)
+    *made, packed = branch_rows(0, room, True, inputs)
+    addend, scatter, more, normed, masked, gain = branch_rows(0, room, False, inputs, made)
     owned = weight_owned(normed, masked, gain, factor)
     result = None
     for hop in range(sections - 1):
@@ -400,7 +436,7 @@
         updated, more = receive(target, scatter, landed, addend, more, (owned,), before)
 
         def rest(updated):
-            packed, addend, scatter, more, *_ = branch_rows(room, spare, *inputs)
+            addend, scatter, more, *_, packed = branch_rows(room, spare, None, inputs)
             if hop:
                 packed = pack(scatter, before)
             landed = lax.ppermute(packed, "section", hops)

time: 28.9 us -> 27.7 us (0.958)
  waiting for transfers between devices: 4.21 us -> 3.55 us
  starting transfers between devices: 17.3 us -> 17 us
    ppermute x1, waiting for transfers between devices: 0.84 us -> 0.01 us  [shards(): landed = lax.ppermute(packed, 'section', hops)]
    ppermute x9 -> x10, starting transfers between devices: 16 us -> 15.7 us  [the longest x6 10.6 us: weight_owned(): lax.ppermute(part, 'dp', hops)]
    pallas_call x2 -> x4, Pallas kernels: 3.91 us -> 3.69 us  [the longest x2 3.58 us: branch_rows(): pl.pallas_call(functools.partial(branch_kernel, low, sending), in_specs=[...]
    ppermute x9 -> x10, waiting for transfers between devices: 3.38 us -> 3.55 us  [the longest x1 2.3 us: weight_owned(): lax.ppermute(cross_low, 'dp', near_by)]
  transfers between devices with their start and end apart: 10 -> 11, of which waited for: 3 -> 2; matrix products, arithmetic and copies ran while one was open for 0% -> 0% of each run, Pallas kernels for 3% -> 18%
where the time goes in v5:
time: 27.7 us; the launch traced here: 27.5 us
  starting transfers between devices  17 us (61%)
  Pallas kernels  6.27 us (23%)
  waiting for transfers between devices  3.55 us (13%)
  between operations  0.7 us (3%)
    ppermute x6, starting transfers between devices, weight_owned(): lax.ppermute(part, 'dp', hops)  10.6 us
    pallas_call x2, Pallas kernels, branch_rows(): pl.pallas_call(functools.partial(branch_kernel, low, sending), in_specs=[...  3.58 us
    ppermute x1, starting transfers between devices, weight_owned(): across = lax.ppermute(give, 'dp', near_by)  2.96 us
    ppermute x1, waiting for transfers between devices, weight_owned(): lax.ppermute(cross_low, 'dp', near_by)  2.3 us
    ppermute x1, starting transfers between devices, weight_owned(): lax.ppermute(cross_low, 'dp', near_by)  1.59 us
    ppermute x1, starting transfers between devices, shards(): landed = lax.ppermute(packed, 'section', hops)  1.29 us
    ppermute x1, waiting for transfers between devices, weight_owned(): taken = lax.ppermute(give, 'dp', swap)  1.22 us
    pallas_call x1, Pallas kernels, receive(): pl.pallas_call(functools.partial(receive_kernel, target, previous is None...  1.2 us
  transfers between devices with their start and end apart: 11, of which 2 were waited for; matrix products, arithmetic and copies ran while one was open for 0% of the time, Pallas kernels for 18%

profile of v5, /device:TPU:0, one launch (start us, length us, event | category | flops | bytes accessed | tf_op | source)
XLA Modules:
  0.0 27.5 jit_solution(986129103025014104)
XLA Ops:
  0.6 0.1 shard_map.77
  0.7 1.3 %collective-permute-start.1 = (bf16[96,4096]{1,0:T(8,128)(2,1)S(1)}, bf16[96,4096]{1,0:T(8,128)(2,1)S(1)}, u32[]{:S(2)}, u32[]{:S(2)}) collective-permute-start(bf16[96,4096]{1,0:T(8,128)(2,1)S(1)} %get-tuple-element.70), channel_id=1, source_target_pairs={{1,0},{3,2},{5,4},{7,6},{9,8},{11,10},{13,12},{15,14},{17,16},{19,... | collective-permute-start | bytes 2359304 | tf_op jit(solution)/shard_map/ppermute | solution.py:435
  2.0 3.5 %shard_map.78 = (f32[128,4096]{1,0:T(8,128)S(1)}, bf16[128,96]{1,0:T(8,128)(2,1)S(1)}, s32[1]{0:T(128)S(4)}, bf16[128,4096]{1,0:T(8,128)(2,1)S(1)}, bf16[128,128]{1,0:T(8,128)(2,1)S(1)}, /*index=5*/f32[1,4096]{1,0:T(1,128)S(1)}) custom-call(s32[8]{0:T(128)} %counts_far.3, ...), custom_call_target="tpu_custom_call", output_to_operand_aliasing={{0}: (6, {}), {1}: (7, {}), {2}: (8, {}), {3}: (9, {}), {4}... | custom-call | flops 1048576 | bytes 65536 | tf_op jit(solution)/shard_map/pallas_call | solution.py:155
  5.5 0.6 %shard_map.79 = (f32[8,176,128]{2,1,0:T(8,128)S(1)}, bf16[8,176,128]{2,1,0:T(8,128)(2,1)S(1)}, f32[8,96,128]{2,1,0:T(8,128)S(1)}, bf16[8,96,128]{2,1,0:T(8,128)(2,1)S(1)}) custom-call(bf16[128,4096]{1,0:T(8,128)(2,1)S(1)} %get-tuple-element.73.normed, bf16[128,128]{1,0:T(8,128)(2,1)S(1)} %get-tuple-element.74.masked, f32[1,4096]{1,0:T(1,128)S(1)} %get-tuple-element.75.gain), custom_call_target="tpu_custom_call" | custom-call | flops 1048576 | bytes 65536 | tf_op jit(solution)/shard_map/pallas_call | solution.py:260
  6.1 0.5 %collective-permute-start.7 = (bf16[8,176,128]{2,1,0:T(8,128)(2,1)S(1)}, bf16[8,176,128]{2,1,0:T(8,128)(2,1)S(1)}, u32[]{:S(2)}, u32[]{:S(2)}) collective-permute-start(bf16[8,176,128]{2,1,0:T(8,128)(2,1)S(1)} %get-tuple-element.85), channel_id=1, source_target_pairs={{0,2},{2,0},{4,6},{6,4},{8,10},{10,8},{12,14},{14,12},{16,18},{18,... | collective-permute-start | bytes 1081352 | tf_op jit(solution)/shard_map/ppermute | solution.py:406
  6.6 0.1 collective-permute-start.2
  6.7 1.2 %collective-permute-done.7.taken = bf16[8,176,128]{2,1,0:T(8,128)(2,1)S(1)} collective-permute-done((bf16[8,176,128]{2,1,0:T(8,128)(2,1)S(1)}, bf16[8,176,128]{2,1,0:T(8,128)(2,1)S(1)}, u32[]{:S(2)}, u32[]{:S(2)}) %collective-permute-start.7) | collective-permute-done | bytes 360480 | tf_op jit(solution)/shard_map/ppermute | solution.py:406
  7.9 0.1 shard_map.82
  8.0 3.0 %collective-permute-start.8 = (bf16[4,176,128]{2,1,0:T(8,128)(2,1)S(1)}, bf16[4,176,128]{2,1,0:T(8,128)(2,1)S(1)}, u32[]{:S(2)}, u32[]{:S(2)}) collective-permute-start(bf16[4,176,128]{2,1,0:T(8,128)(2,1)S(1)} %get-tuple-element.87), channel_id=1, source_target_pairs={{0,4},{2,6},{4,0},{6,2},{8,12},{10,14},{12,8},{14,10},{16,20},{18,... | collective-permute-start | bytes 540680 | tf_op jit(solution)/shard_map/ppermute | solution.py:409
  10.9 0.0 collective-permute-done.2.taken
  11.0 1.6 %collective-permute-start.3 = (bf16[2,96,128]{2,1,0:T(8,128)(2,1)S(1)}, bf16[2,96,128]{2,1,0:T(8,128)(2,1)S(1)}, u32[]{:S(2)}, u32[]{:S(2)}) collective-permute-start(bf16[2,96,128]{2,1,0:T(8,128)(2,1)S(1)} %get-tuple-element.79), channel_id=1, source_target_pairs={{0,8},{2,10},{4,12},{6,14},{8,16},{10,18},{12,20},{14,22},{16,24},... | collective-permute-start | bytes 147464 | tf_op jit(solution)/shard_map/ppermute | solution.py:411
  12.6 2.6 %collective-permute-start.4 = (bf16[2,96,128]{2,1,0:T(8,128)(2,1)S(1)}, bf16[2,96,128]{2,1,0:T(8,128)(2,1)S(1)}, u32[]{:S(2)}, u32[]{:S(2)}) collective-permute-start(bf16[2,96,128]{2,1,0:T(8,128)(2,1)S(1)} %get-tuple-element.80), channel_id=1, source_target_pairs={{0,16},{2,18},{4,20},{6,22},{8,24},{10,26},{12,28},{14,30},{16,0},... | collective-permute-start | bytes 147464 | tf_op jit(solution)/shard_map/ppermute | solution.py:411
  15.2 1.4 %collective-permute-start.5 = (bf16[2,96,128]{2,1,0:T(8,128)(2,1)S(1)}, bf16[2,96,128]{2,1,0:T(8,128)(2,1)S(1)}, u32[]{:S(2)}, u32[]{:S(2)}) collective-permute-start(bf16[2,96,128]{2,1,0:T(8,128)(2,1)S(1)} %get-tuple-element.81), channel_id=1, source_target_pairs={{0,24},{2,26},{4,28},{6,30},{8,0},{10,2},{12,4},{14,6},{16,8},{18,... | collective-permute-start | bytes 147464 | tf_op jit(solution)/shard_map/ppermute | solution.py:411
  16.5 0.0 collective-permute-done.8.taken
  16.6 1.1 %collective-permute-start.9 = (bf16[176,128]{1,0:T(8,128)(2,1)S(1)}, bf16[176,128]{1,0:T(8,128)(2,1)S(1)}, u32[]{:S(2)}, u32[]{:S(2)}) collective-permute-start(bf16[176,128]{1,0:T(8,128)(2,1)S(1)} %get-tuple-element.89), channel_id=1, source_target_pairs={{0,8},{2,10},{4,12},{6,14},{8,16},{10,18},{12,20},{14,22},{16,24},... | collective-permute-start | bytes 135176 | tf_op jit(solution)/shard_map/ppermute | solution.py:413
  17.7 0.0 collective-permute-done.3.refs_0_
  17.7 2.6 %collective-permute-start.10 = (bf16[176,128]{1,0:T(8,128)(2,1)S(1)}, bf16[176,128]{1,0:T(8,128)(2,1)S(1)}, u32[]{:S(2)}, u32[]{:S(2)}) collective-permute-start(bf16[176,128]{1,0:T(8,128)(2,1)S(1)} %get-tuple-element.90), channel_id=1, source_target_pairs={{0,16},{2,18},{4,20},{6,22},{8,24},{10,26},{12,28},{14,30},{16,0},... | collective-permute-start | bytes 135176 | tf_op jit(solution)/shard_map/ppermute | solution.py:413
  20.3 0.0 collective-permute-done.4.refs_1_
  20.3 1.3 %collective-permute-start.11 = (bf16[176,128]{1,0:T(8,128)(2,1)S(1)}, bf16[176,128]{1,0:T(8,128)(2,1)S(1)}, u32[]{:S(2)}, u32[]{:S(2)}) collective-permute-start(bf16[176,128]{1,0:T(8,128)(2,1)S(1)} %get-tuple-element.91), channel_id=1, source_target_pairs={{0,24},{2,26},{4,28},{6,30},{8,0},{10,2},{12,4},{14,6},{16,8},{18,... | collective-permute-start | bytes 135176 | tf_op jit(solution)/shard_map/ppermute | solution.py:413
  21.6 0.0 collective-permute-done.5.refs_2_
  21.7 1.6 %collective-permute-start.6 = (bf16[96,128]{1,0:T(8,128)(2,1)S(1)}, bf16[96,128]{1,0:T(8,128)(2,1)S(1)}, u32[]{:S(2)}, u32[]{:S(2)}) collective-permute-start(bf16[96,128]{1,0:T(8,128)(2,1)S(1)} %get-tuple-element.83), channel_id=1, source_target_pairs={{0,4},{2,6},{4,0},{6,2},{8,12},{10,14},{12,8},{14,10},{16,20},{18,... | collective-permute-start | bytes 73736 | tf_op jit(solution)/shard_map/ppermute | solution.py:415
  23.2 2.3 %collective-permute-done.6.landed_low = bf16[96,128]{1,0:T(8,128)(2,1)S(1)} collective-permute-done((bf16[96,128]{1,0:T(8,128)(2,1)S(1)}, bf16[96,128]{1,0:T(8,128)(2,1)S(1)}, u32[]{:S(2)}, u32[]{:S(2)}) %collective-permute-start.6) | collective-permute-done | bytes 24608 | tf_op jit(solution)/shard_map/ppermute | solution.py:415
  25.6 0.0 collective-permute-done.9.rest_0_
  25.6 0.0 collective-permute-done.10.rest_1_
  25.6 0.0 collective-permute-done.11.rest_2_
  25.6 0.8 %shard_map.84.rest_0_ = f32[1,33024]{1,0:T(1,128)} custom-call(f32[96,128]{1,0:T(8,128)S(1)} %get-tuple-element.82.own_low, bf16[96,128]{1,0:T(8,128)(2,1)S(1)} %collective-permute-done.6.landed_low, f32[176,128]{1,0:T(8,128)S(1)} %get-tuple-element.88.own, bf16[176,128]{1,0:T(8,128)(2,1)S(1)} %collective-permute-done.9.rest_0_, ...), custom_call_target="tpu_custom_call" | custom-call | flops 1048576 | bytes 65536 | tf_op jit(solution)/shard_map/pallas_call | solution.py:380
  26.3 0.0 collective-permute-done.1.received
  26.3 1.2 %shard_map.85 = (bf16[1,128,4096]{2,1,0:T(8,128)(2,1)}, s32[1]{0:T(128)S(4)}) custom-call(bf16[128,96]{1,0:T(8,128)(2,1)S(1)} %get-tuple-element.69.scatter, bf16[96,4096]{1,0:T(8,128)(2,1)S(1)} %collective-permute-done.1.received, f32[128,4096]{1,0:T(8,128)S(1)} %get-tuple-element.71.addend, s32[1]{0:T(128)S(4)} %get-tuple-element.72.more, ...), custom_call_target="tpu_custom_call" | custom-call | flops 1048576 | bytes 65536 | tf_op jit(solution)/shard_map/pallas_call | solution.py:221
  (4 shorter events, 0.1 us)
Async XLA Ops:
  0.7 25.6 %collective-permute-start.1 = (bf16[96,4096]{1,0:T(8,128)(2,1)S(1)}, bf16[96,4096]{1,0:T(8,128)(2,1)S(1)}, u32[]{:S(2)}, u32[]{:S(2)}) collective-permute-start(bf16[96,4096]{1,0:T(8,128)(2,1)S(1)} %get-tuple-element.70), channel_id=1, source_target_pairs={{1,0},{3,2},{5,4},{7,6},{9,8},{11,10},{13,12},{15,14},{17,16},{19,... | collective-permute-start | bytes 2359304 | tf_op jit(solution)/shard_map/ppermute | solution.py:435
  6.1 1.8 %collective-permute-start.7 = (bf16[8,176,128]{2,1,0:T(8,128)(2,1)S(1)}, bf16[8,176,128]{2,1,0:T(8,128)(2,1)S(1)}, u32[]{:S(2)}, u32[]{:S(2)}) collective-permute-start(bf16[8,176,128]{2,1,0:T(8,128)(2,1)S(1)} %get-tuple-element.85), channel_id=1, source_target_pairs={{0,2},{2,0},{4,6},{6,4},{8,10},{10,8},{12,14},{14,12},{16,18},{18,... | collective-permute-start | bytes 1081352 | tf_op jit(solution)/shard_map/ppermute | solution.py:406
  6.6 4.3 %collective-permute-start.2 = (bf16[8,96,128]{2,1,0:T(8,128)(2,1)S(1)}, bf16[8,96,128]{2,1,0:T(8,128)(2,1)S(1)}, u32[]{:S(2)}, u32[]{:S(2)}) collective-permute-start(bf16[8,96,128]{2,1,0:T(8,128)(2,1)S(1)} %get-tuple-element.77), channel_id=1, source_target_pairs={{0,2},{2,0},{4,6},{6,4},{8,10},{10,8},{12,14},{14,12},{16,18},{18,... | collective-permute-start | bytes 589832 | tf_op jit(solution)/shard_map/ppermute | solution.py:407
  8.0 8.6 %collective-permute-start.8 = (bf16[4,176,128]{2,1,0:T(8,128)(2,1)S(1)}, bf16[4,176,128]{2,1,0:T(8,128)(2,1)S(1)}, u32[]{:S(2)}, u32[]{:S(2)}) collective-permute-start(bf16[4,176,128]{2,1,0:T(8,128)(2,1)S(1)} %get-tuple-element.87), channel_id=1, source_target_pairs={{0,4},{2,6},{4,0},{6,2},{8,12},{10,14},{12,8},{14,10},{16,20},{18,... | collective-permute-start | bytes 540680 | tf_op jit(solution)/shard_map/ppermute | solution.py:409
  11.0 6.7 %collective-permute-start.3 = (bf16[2,96,128]{2,1,0:T(8,128)(2,1)S(1)}, bf16[2,96,128]{2,1,0:T(8,128)(2,1)S(1)}, u32[]{:S(2)}, u32[]{:S(2)}) collective-permute-start(bf16[2,96,128]{2,1,0:T(8,128)(2,1)S(1)} %get-tuple-element.79), channel_id=1, source_target_pairs={{0,8},{2,10},{4,12},{6,14},{8,16},{10,18},{12,20},{14,22},{16,24},... | collective-permute-start | bytes 147464 | tf_op jit(solution)/shard_map/ppermute | solution.py:411
  12.6 7.7 %collective-permute-start.4 = (bf16[2,96,128]{2,1,0:T(8,128)(2,1)S(1)}, bf16[2,96,128]{2,1,0:T(8,128)(2,1)S(1)}, u32[]{:S(2)}, u32[]{:S(2)}) collective-permute-start(bf16[2,96,128]{2,1,0:T(8,128)(2,1)S(1)} %get-tuple-element.80), channel_id=1, source_target_pairs={{0,16},{2,18},{4,20},{6,22},{8,24},{10,26},{12,28},{14,30},{16,0},... | collective-permute-start | bytes 147464 | tf_op jit(solution)/shard_map/ppermute | solution.py:411
  15.2 6.4 %collective-permute-start.5 = (bf16[2,96,128]{2,1,0:T(8,128)(2,1)S(1)}, bf16[2,96,128]{2,1,0:T(8,128)(2,1)S(1)}, u32[]{:S(2)}, u32[]{:S(2)}) collective-permute-start(bf16[2,96,128]{2,1,0:T(8,128)(2,1)S(1)} %get-tuple-element.81), channel_id=1, source_target_pairs={{0,24},{2,26},{4,28},{6,30},{8,0},{10,2},{12,4},{14,6},{16,8},{18,... | collective-permute-start | bytes 147464 | tf_op jit(solution)/shard_map/ppermute | solution.py:411
  16.6 9.0 %collective-permute-start.9 = (bf16[176,128]{1,0:T(8,128)(2,1)S(1)}, bf16[176,128]{1,0:T(8,128)(2,1)S(1)}, u32[]{:S(2)}, u32[]{:S(2)}) collective-permute-start(bf16[176,128]{1,0:T(8,128)(2,1)S(1)} %get-tuple-element.89), channel_id=1, source_target_pairs={{0,8},{2,10},{4,12},{6,14},{8,16},{10,18},{12,20},{14,22},{16,24},... | collective-permute-start | bytes 135176 | tf_op jit(solution)/shard_map/ppermute | solution.py:413
  17.7 7.9 %collective-permute-start.10 = (bf16[176,128]{1,0:T(8,128)(2,1)S(1)}, bf16[176,128]{1,0:T(8,128)(2,1)S(1)}, u32[]{:S(2)}, u32[]{:S(2)}) collective-permute-start(bf16[176,128]{1,0:T(8,128)(2,1)S(1)} %get-tuple-element.90), channel_id=1, source_target_pairs={{0,16},{2,18},{4,20},{6,22},{8,24},{10,26},{12,28},{14,30},{16,0},... | collective-permute-start | bytes 135176 | tf_op jit(solution)/shard_map/ppermute | solution.py:413
  20.3 5.3 %collective-permute-start.11 = (bf16[176,128]{1,0:T(8,128)(2,1)S(1)}, bf16[176,128]{1,0:T(8,128)(2,1)S(1)}, u32[]{:S(2)}, u32[]{:S(2)}) collective-permute-start(bf16[176,128]{1,0:T(8,128)(2,1)S(1)} %get-tuple-element.91), channel_id=1, source_target_pairs={{0,24},{2,26},{4,28},{6,30},{8,0},{10,2},{12,4},{14,6},{16,8},{18,... | collective-permute-start | bytes 135176 | tf_op jit(solution)/shard_map/ppermute | solution.py:413
  21.7 3.9 %collective-permute-start.6 = (bf16[96,128]{1,0:T(8,128)(2,1)S(1)}, bf16[96,128]{1,0:T(8,128)(2,1)S(1)}, u32[]{:S(2)}, u32[]{:S(2)}) collective-permute-start(bf16[96,128]{1,0:T(8,128)(2,1)S(1)} %get-tuple-element.83), channel_id=1, source_target_pairs={{0,4},{2,6},{4,0},{6,2},{8,12},{10,14},{12,8},{14,10},{16,20},{18,... | collective-permute-start | bytes 73736 | tf_op jit(solution)/shard_map/ppermute | solution.py:415

commit v6 on v5

--- a/solution.py
+++ b/solution.py
@@ -294,80 +294,48 @@
     )(keep, taken)
 
 
-def spread_kernel(keep, taken, hold, *give):
-    place = lax.axis_index("dp") // (2 * pair)
-    count = keep.shape[0] // 2
-    for side in range(2):
-        at = 2 * place + side
-        hold[side] = keep[at] + taken[at].astype(f32)
-        for k in range(1, count):
-            at = 2 * lax.rem(place + k, count) + side
-            give[k - 1][side] = (keep[at] + taken[at].astype(f32)).astype(bf16)
-
-
-def spread_terms(keep, taken):
-    count = keep.shape[0] // 2
-    two = (2,) + keep.shape[1:]
-    return pl.pallas_call(
-        spread_kernel,
+def add_kernel(keep, taken, out):
+    for k in range(keep.shape[0]):
+        out[k] = (keep[k] + taken[k].astype(f32)).astype(bf16)
+
+
+def add_terms(keep, taken):
+    return pl.pallas_call(
+        add_kernel,
         in_specs=[near, near],
-        out_specs=[near] * count,
-        out_shape=[jax.ShapeDtypeStruct(two, f32)] + [jax.ShapeDtypeStruct(two, bf16)] * (count - 1),
+        out_specs=near,
+        out_shape=jax.ShapeDtypeStruct(keep.shape, bf16),
         compiler_params=roomy,
         cost_estimate=small_cost,
     )(keep, taken)
 
 
-def split_kernel(hold, taken, own, *parts):
-    count = hold.shape[0]
-    place = lax.axis_index("dp") // (2 * pair)
-    own[...] = hold[place] + taken[place].astype(f32)
-    for k in range(1, count):
-        at = lax.rem(place + k, count)
-        parts[k - 1][...] = (hold[at] + taken[at].astype(f32)).astype(bf16)
-
-
-def split_terms(hold, taken):
-    count = hold.shape[0]
-    return pl.pallas_call(
-        split_kernel,
-        in_specs=[near, near],
-        out_specs=[near] * count,
-        out_shape=[jax.ShapeDtypeStruct(hold.shape[1:], f32)]
-        + [jax.ShapeDtypeStruct(hold.shape[1:], bf16)] * (count - 1),
-        compiler_params=roomy,
-        cost_estimate=small_cost,
-    )(hold, taken)
-
-
-def cross_kernel(hold, *refs):
-    *landed, own, give = refs
+def cross_kernel(landed, own, give):
     mine = lax.axis_index("dp") // pair % 2
-    total = hold[mine]
-    passed = hold[1 - mine]
-    for part in landed:
-        total += part[mine].astype(f32)
-        passed += part[1 - mine].astype(f32)
+    total = landed[mine].astype(f32)
+    passed = landed[1 - mine].astype(f32)
+    for k in range(2, landed.shape[0], 2):
+        total += landed[k + mine].astype(f32)
+        passed += landed[k + 1 - mine].astype(f32)
     own[...] = total
     give[...] = passed.astype(bf16)
 
 
-def cross_terms(hold, landed):
+def cross_terms(landed):
     return pl.pallas_call(
         cross_kernel,
-        in_specs=[near] * (1 + len(landed)),
+        in_specs=[near],
         out_specs=[near, near],
-        out_shape=[jax.ShapeDtypeStruct(hold.shape[1:], f32), jax.ShapeDtypeStruct(hold.shape[1:], bf16)],
-        compiler_params=roomy,
-        cost_estimate=small_cost,
-    )(hold, *landed)
-
-
-def total_kernel(owned_rows, factor, own_low, landed_low, own, *rest):
-    out = rest[-1]
-    total = own[...]
-    for part in rest[:-1]:
-        total += part[...].astype(f32)
+        out_shape=[jax.ShapeDtypeStruct(landed.shape[1:], f32), jax.ShapeDtypeStruct(landed.shape[1:], bf16)],
+        compiler_params=roomy,
+        cost_estimate=small_cost,
+    )(landed)
+
+
+def total_kernel(owned_rows, factor, own_low, landed_low, landed, out):
+    total = landed[0].astype(f32)
+    for k in range(1, landed.shape[0]):
+        total += landed[k].astype(f32)
     low = (own_low[...] + landed_low[...].astype(f32)) * factor
     total = total * factor
     cut = total.shape[0]
@@ -376,15 +344,15 @@
         out[:, k * lanes : (k + 1) * lanes] = row
 
 
-def total_terms(owned_rows, factor, own_low, landed_low, own, landed):
+def total_terms(owned_rows, factor, own_low, landed_low, landed):
     return pl.pallas_call(
         functools.partial(total_kernel, owned_rows, factor),
-        in_specs=[near] * (3 + len(landed)),
+        in_specs=[near] * 3,
         out_specs=near,
         out_shape=jax.ShapeDtypeStruct((1, owned_rows * lanes), f32),
         compiler_params=roomy,
         cost_estimate=small_cost,
-    )(own_low, landed_low, own, *landed)
+    )(own_low, landed_low, landed)
 
 
 def weight_owned(normed, masked, gain, factor):
@@ -401,18 +369,17 @@
     cut = -(-owned_rows * 2 // 3 // pack_rows) * pack_rows
     swap = [(i, i ^ 1) for i in range(owners)]
     near_by = [(i, i ^ pair) for i in range(owners)]
-    farther = [[(i, (i + shift) % owners) for i in range(owners)] for shift in range(quad, owners, quad)]
+    lines = [list(range(first, owners, quad)) for first in range(quad)]
+    exchange = functools.partial(lax.all_to_all, axis_name="dp", split_axis=0, concat_axis=0, axis_index_groups=lines, tiled=True)
     keep, give, keep_low, give_low = pair_terms(normed, masked, gain, cut, owned_rows, owners)
     taken = lax.ppermute(give, "dp", swap)
     taken_low = lax.ppermute(give_low, "dp", swap)
     hold, give = merge_terms(keep, taken)
     across = lax.ppermute(give, "dp", near_by)
-    hold_low, *parts_low = spread_terms(keep_low, taken_low)
-    landed_low = [lax.ppermute(part, "dp", hops) for part, hops in zip(parts_low, farther)]
-    own, *parts = split_terms(hold, across)
-    landed = [lax.ppermute(part, "dp", hops) for part, hops in zip(parts, farther)]
-    own_low, cross_low = cross_terms(hold_low, landed_low)
-    return total_terms(owned_rows, factor, own_low, lax.ppermute(cross_low, "dp", near_by), own, landed)
+    landed_low = exchange(add_terms(keep_low, taken_low))
+    landed = exchange(add_terms(hold, across))
+    own_low, cross_low = cross_terms(landed_low)
+    return total_terms(owned_rows, factor, own_low, lax.ppermute(cross_low, "dp", near_by), landed)
 
 
 def shards(layer_inputs, top_grad, value_grads, weights, norm_gains, counts):

time: 27.7 us -> 39.1 us (1.41)
  waiting for transfers between devices: 3.55 us -> 10.9 us
  Pallas kernels: 6.27 us -> 9.22 us
  local copies, waits for them, and re-layouts: 0 us -> 1.98 us
  starting transfers between devices: 17 us -> 15.9 us
    all_to_all x0 -> x2, starting transfers between devices: none -> 10.8 us  [the longest x1 6.02 us: weight_owned(): landed_low = exchange(add_terms(keep_low, taken_low))]
    ppermute x6 -> x0, starting transfers between devices: 10.6 us -> none  [weight_owned(): lax.ppermute(part, 'dp', hops)]
    ppermute x1, waiting for transfers between devices: 0.01 us -> 5.02 us  [weight_owned(): across = lax.ppermute(give, 'dp', near_by)]
    all_to_all x0 -> x2, waiting for transfers between devices: none -> 2.21 us  [the longest x1 2.21 us: weight_owned(): landed = exchange(add_terms(hold, across))]
    unnamed x0 -> x4, local copies, waits for them, and re-layouts: none -> 1.98 us
    ppermute x1, waiting for transfers between devices: 0.01 us -> 1.38 us  [weight_owned(): taken_low = lax.ppermute(give_low, 'dp', swap)]
    ppermute x1, starting transfers between devices: 2.96 us -> 1.58 us  [weight_owned(): across = lax.ppermute(give, 'dp', near_by)]
    pallas_call x3, Pallas kernels: 0.1 us -> 1.44 us  [the longest x2 1.41 us: add_terms(): pl.pallas_call(add_kernel, in_specs=[near, near], out_specs=near, out_sha...]
  transfers between devices with their start and end apart: 11 -> 7, of which waited for: 2 -> 4; matrix products, arithmetic and copies ran while one was open for 0% -> 0% of each run, Pallas kernels for 18% -> 6%
where the time goes in v6:
time: 39.1 us; the launch traced here: 38.7 us
  starting transfers between devices  15.9 us (41%)
  waiting for transfers between devices  10.9 us (28%)
  Pallas kernels  9.22 us (24%)
  local copies, waits for them, and re-layouts  1.98 us (5%)
  between operations  0.68 us (2%)
    all_to_all x1, starting transfers between devices, weight_owned(): landed_low = exchange(add_terms(keep_low, taken_low))  6.02 us
    ppermute x1, waiting for transfers between devices, weight_owned(): across = lax.ppermute(give, 'dp', near_by)  5.02 us
    all_to_all x1, starting transfers between devices, weight_owned(): landed = exchange(add_terms(hold, across))  4.81 us
    pallas_call x2, Pallas kernels, branch_rows(): pl.pallas_call(functools.partial(branch_kernel, low, sending), in_specs=[...  4.46 us
    ppermute x1, waiting for transfers between devices, weight_owned(): lax.ppermute(cross_low, 'dp', near_by)  2.31 us
    all_to_all x1, waiting for transfers between devices, weight_owned(): landed = exchange(add_terms(hold, across))  2.21 us
    unnamed x4, local copies, waits for them, and re-layouts  1.98 us
    ppermute x1, starting transfers between devices, weight_owned(): across = lax.ppermute(give, 'dp', near_by)  1.58 us
  transfers between devices with their start and end apart: 7, of which 4 were waited for; matrix products, arithmetic and copies ran while one was open for 0% of the time, Pallas kernels for 6%

profile of v6, /device:TPU:0, one launch (start us, length us, event | category | flops | bytes accessed | tf_op | source)
XLA Modules:
  0.0 38.7 jit_solution(2132882115470405794)
XLA Ops:
  0.6 0.9 %shard_map.77 = (f32[128,4096]{1,0:T(8,128)S(1)}, bf16[128,96]{1,0:T(8,128)(2,1)S(1)}, s32[1]{0:T(128)S(4)}, bf16[128,4096]{1,0:T(8,128)(2,1)S(1)}, bf16[128,128...) custom-call(s32[8]{0:T(128)} %counts_far.3, bf16[1,128,4096]{2,1,0:T(8,128)(2,1)} %x_far.3, ...), custom_call_target="tpu_custom_call" | custom-call | flops 1048576 | bytes 65536 | tf_op jit(solution)/shard_map/pallas_call | solution.py:155
  1.6 3.5 %shard_map.78 = (f32[128,4096]{1,0:T(8,128)S(1)}, bf16[128,96]{1,0:T(8,128)(2,1)S(1)}, s32[1]{0:T(128)S(4)}, bf16[128,4096]{1,0:T(8,128)(2,1)S(1)}, bf16[128,128]{1,0:T(8,128)(2,1)S(1)}, /*index=5*/f32[1,4096]{1,0:T(1,128)S(1)}) custom-call(s32[8]{0:T(128)} %counts_far.3, ...), custom_call_target="tpu_custom_call", output_to_operand_aliasing={{0}: (6, {}), {1}: (7, {}), {2}: (8, {}), {3}: (9, {}), {4}... | custom-call | flops 1048576 | bytes 65536 | tf_op jit(solution)/shard_map/pallas_call | solution.py:155
  5.1 1.3 %shard_map.79 = (f32[8,176,128]{2,1,0:T(8,128)S(1)}, bf16[8,176,128]{2,1,0:T(8,128)(2,1)}, f32[8,96,128]{2,1,0:T(8,128)S(1)}, bf16[8,96,128]{2,1,0:T(8,128)(2,1)S(1)}) custom-call(bf16[128,4096]{1,0:T(8,128)(2,1)S(1)} %get-tuple-element.65.normed, bf16[128,128]{1,0:T(8,128)(2,1)S(1)} %get-tuple-element.66.masked, f32[1,4096]{1,0:T(1,128)S(1)} %get-tuple-element.67.gain), custom_call_target="tpu_custom_call" | custom-call | flops 1048576 | bytes 65536 | tf_op jit(solution)/shard_map/pallas_call | solution.py:260
  6.4 0.0 copy-start
  6.4 0.9 %copy-done = f32[8,176,128]{2,1,0:T(8,128)} copy-done((f32[8,176,128]{2,1,0:T(8,128)}, f32[8,176,128]{2,1,0:T(8,128)S(1)}, u32[]{:S(2)}) %copy-start) | copy-done | bytes 720920
  7.3 0.5 %collective-permute-start.4 = (bf16[8,176,128]{2,1,0:T(8,128)(2,1)}, bf16[8,176,128]{2,1,0:T(8,128)(2,1)S(1)}, u32[]{:S(2)}, u32[]{:S(2)}) collective-permute-start(bf16[8,176,128]{2,1,0:T(8,128)(2,1)} %get-tuple-element.73), channel_id=1, source_target_pairs={{0,2},{2,0},{4,6},{6,4},{8,10},{10,8},{12,14},{14,12},{16,18},{18,... | collective-permute-start | bytes 1081352 | tf_op jit(solution)/shard_map/ppermute | solution.py:375
  7.7 1.3 %collective-permute-start.1 = (bf16[96,4096]{1,0:T(8,128)(2,1)}, bf16[96,4096]{1,0:T(8,128)(2,1)S(1)}, u32[]{:S(2)}, u32[]{:S(2)}) collective-permute-start(bf16[96,4096]{1,0:T(8,128)(2,1)} %get-tuple-element.62), channel_id=1, source_target_pairs={{1,0},{3,2},{5,4},{7,6},{9,8},{11,10},{13,12},{15,14},{17,16},{19,... | collective-permute-start | bytes 2359304 | tf_op jit(solution)/shard_map/ppermute | solution.py:402
  9.0 0.1 collective-permute-start.2
  9.1 1.4 %collective-permute-done.2.taken = bf16[8,96,128]{2,1,0:T(8,128)(2,1)S(1)} collective-permute-done((bf16[8,96,128]{2,1,0:T(8,128)(2,1)S(1)}, bf16[8,96,128]{2,1,0:T(8,128)(2,1)S(1)}, u32[]{:S(2)}, u32[]{:S(2)}) %collective-permute-start.2) | collective-permute-done | bytes 196640 | tf_op jit(solution)/shard_map/ppermute | solution.py:376
  10.5 0.7 %shard_map.80 = bf16[8,96,128]{2,1,0:T(8,128)(2,1)} custom-call(f32[8,96,128]{2,1,0:T(8,128)S(1)} %get-tuple-element.68.keep, bf16[8,96,128]{2,1,0:T(8,128)(2,1)S(1)} %collective-permute-done.2.taken), custom_call_target="tpu_custom_call" | custom-call | flops 1048576 | bytes 65536 | tf_op jit(solution)/shard_map/pallas_call | solution.py:303
  11.2 6.0 %all-to-all-start = ((bf16[8,96,128]{2,1,0:T(8,128)(2,1)}), bf16[8,96,128]{2,1,0:T(8,128)(2,1)S(1)}, u32[]{:S(2)}, u32[]{:S(2)}) async-start(bf16[8,96,128]{2,1,0:T(8,128)(2,1)} %shard_map.80), calls=%async_computation | async-start | bytes 393216 | tf_op jit(solution)/shard_map/all_to_all | solution.py:379
  17.3 0.0 collective-permute-done.4.taken
  17.3 0.0 copy-start.1
  17.3 1.1 %copy-done.1 = f32[8,176,128]{2,1,0:T(8,128)S(1)} copy-done((f32[8,176,128]{2,1,0:T(8,128)S(1)}, f32[8,176,128]{2,1,0:T(8,128)}, u32[]{:S(2)}) %copy-start.1) | copy-done | bytes 720920
  18.4 0.1 shard_map.82
  18.5 1.6 %collective-permute-start.5 = (bf16[4,176,128]{2,1,0:T(8,128)(2,1)S(1)}, bf16[4,176,128]{2,1,0:T(8,128)(2,1)S(1)}, u32[]{:S(2)}, u32[]{:S(2)}) collective-permute-start(bf16[4,176,128]{2,1,0:T(8,128)(2,1)S(1)} %get-tuple-element.75), channel_id=1, source_target_pairs={{0,4},{2,6},{4,0},{6,2},{8,12},{10,14},{12,8},{14,10},{16,20},{18,... | collective-permute-start | bytes 540680 | tf_op jit(solution)/shard_map/ppermute | solution.py:378
  20.0 5.0 %collective-permute-done.5.taken = bf16[4,176,128]{2,1,0:T(8,128)(2,1)S(1)} collective-permute-done((bf16[4,176,128]{2,1,0:T(8,128)(2,1)S(1)}, bf16[4,176,128]{2,1,0:T(8,128)(2,1)S(1)}, u32[]{:S(2)}, u32[]{:S(2)}) %collective-permute-start.5) | collective-permute-done | bytes 180256 | tf_op jit(solution)/shard_map/ppermute | solution.py:378
  25.1 0.7 %shard_map.83 = bf16[4,176,128]{2,1,0:T(8,128)(2,1)} custom-call(f32[4,176,128]{2,1,0:T(8,128)S(1)} %get-tuple-element.74.keep, bf16[4,176,128]{2,1,0:T(8,128)(2,1)S(1)} %collective-permute-done.5.taken), custom_call_target="tpu_custom_call" | custom-call | flops 1048576 | bytes 65536 | tf_op jit(solution)/shard_map/pallas_call | solution.py:303
  25.7 0.0 all-to-all-done.landed
  25.7 4.8 %all-to-all-start.1 = ((bf16[4,176,128]{2,1,0:T(8,128)(2,1)}), bf16[4,176,128]{2,1,0:T(8,128)(2,1)S(1)}, u32[]{:S(2)}, u32[]{:S(2)}) async-start(bf16[4,176,128]{2,1,0:T(8,128)(2,1)} %shard_map.83), calls=%async_computation.1 | async-start | bytes 360448 | tf_op jit(solution)/shard_map/all_to_all | solution.py:380
  30.6 1.6 %collective-permute-start.3 = (bf16[96,128]{1,0:T(8,128)(2,1)S(1)}, bf16[96,128]{1,0:T(8,128)(2,1)S(1)}, u32[]{:S(2)}, u32[]{:S(2)}) collective-permute-start(bf16[96,128]{1,0:T(8,128)(2,1)S(1)} %get-tuple-element.71), channel_id=1, source_target_pairs={{0,4},{2,6},{4,0},{6,2},{8,12},{10,14},{12,8},{14,10},{16,20},{18,... | collective-permute-start | bytes 73736 | tf_op jit(solution)/shard_map/ppermute | solution.py:382
  32.2 2.3 %collective-permute-done.3.landed_low = bf16[96,128]{1,0:T(8,128)(2,1)S(1)} collective-permute-done((bf16[96,128]{1,0:T(8,128)(2,1)S(1)}, bf16[96,128]{1,0:T(8,128)(2,1)S(1)}, u32[]{:S(2)}, u32[]{:S(2)}) %collective-permute-start.3) | collective-permute-done | bytes 24608 | tf_op jit(solution)/shard_map/ppermute | solution.py:382
  34.5 2.2 %all-to-all-done.1.landed = bf16[4,176,128]{2,1,0:T(8,128)(2,1)S(1)} async-done(((bf16[4,176,128]{2,1,0:T(8,128)(2,1)}), bf16[4,176,128]{2,1,0:T(8,128)(2,1)S(1)}, u32[]{:S(2)}, u32[]{:S(2)}) %all-to-all-start.1) | async-done | bytes 180256 | tf_op jit(solution)/shard_map/all_to_all | solution.py:380
  36.7 0.7 %shard_map.84.rest_0_ = f32[1,33024]{1,0:T(1,128)} custom-call(f32[96,128]{1,0:T(8,128)S(1)} %get-tuple-element.70.own_low, bf16[96,128]{1,0:T(8,128)(2,1)S(1)} %collective-permute-done.3.landed_low, bf16[4,176,128]{2,1,0:T(8,128)(2,1)S(1)} %all-to-all-done.1.landed), custom_call_target="tpu_custom_call" | custom-call | flops 1048576 | bytes 65536 | tf_op jit(solution)/shard_map/pallas_call | solution.py:348
  37.4 0.0 collective-permute-done.1.received
  37.4 1.2 %shard_map.85 = (bf16[1,128,4096]{2,1,0:T(8,128)(2,1)}, s32[1]{0:T(128)S(4)}) custom-call(bf16[128,96]{1,0:T(8,128)(2,1)S(1)} %get-tuple-element.61.scatter, bf16[96,4096]{1,0:T(8,128)(2,1)S(1)} %collective-permute-done.1.received, f32[128,4096]{1,0:T(8,128)S(1)} %get-tuple-element.63.addend, s32[1]{0:T(128)S(4)} %get-tuple-element.64.more, ...), custom_call_target="tpu_custom_call" | custom-call | flops 1048576 | bytes 65536 | tf_op jit(solution)/shard_map/pallas_call | solution.py:221
  (2 shorter events, 0.0 us)
Async XLA Ops:
  6.4 0.9 %copy-start = (f32[8,176,128]{2,1,0:T(8,128)}, f32[8,176,128]{2,1,0:T(8,128)S(1)}, u32[]{:S(2)}) copy-start(f32[8,176,128]{2,1,0:T(8,128)S(1)} %get-tuple-element.72.keep) | copy-start | bytes 2162692
  7.3 10.0 %collective-permute-start.4 = (bf16[8,176,128]{2,1,0:T(8,128)(2,1)}, bf16[8,176,128]{2,1,0:T(8,128)(2,1)S(1)}, u32[]{:S(2)}, u32[]{:S(2)}) collective-permute-start(bf16[8,176,128]{2,1,0:T(8,128)(2,1)} %get-tuple-element.73), channel_id=1, source_target_pairs={{0,2},{2,0},{4,6},{6,4},{8,10},{10,8},{12,14},{14,12},{16,18},{18,... | collective-permute-start | bytes 1081352 | tf_op jit(solution)/shard_map/ppermute | solution.py:375
  7.7 29.7 %collective-permute-start.1 = (bf16[96,4096]{1,0:T(8,128)(2,1)}, bf16[96,4096]{1,0:T(8,128)(2,1)S(1)}, u32[]{:S(2)}, u32[]{:S(2)}) collective-permute-start(bf16[96,4096]{1,0:T(8,128)(2,1)} %get-tuple-element.62), channel_id=1, source_target_pairs={{1,0},{3,2},{5,4},{7,6},{9,8},{11,10},{13,12},{15,14},{17,16},{19,... | collective-permute-start | bytes 2359304 | tf_op jit(solution)/shard_map/ppermute | solution.py:402
  9.0 1.5 %collective-permute-start.2 = (bf16[8,96,128]{2,1,0:T(8,128)(2,1)S(1)}, bf16[8,96,128]{2,1,0:T(8,128)(2,1)S(1)}, u32[]{:S(2)}, u32[]{:S(2)}) collective-permute-start(bf16[8,96,128]{2,1,0:T(8,128)(2,1)S(1)} %get-tuple-element.69), channel_id=1, source_target_pairs={{0,2},{2,0},{4,6},{6,4},{8,10},{10,8},{12,14},{14,12},{16,18},{18,... | collective-permute-start | bytes 589832 | tf_op jit(solution)/shard_map/ppermute | solution.py:376
  11.2 14.5 %all-to-all-start = ((bf16[8,96,128]{2,1,0:T(8,128)(2,1)}), bf16[8,96,128]{2,1,0:T(8,128)(2,1)S(1)}, u32[]{:S(2)}, u32[]{:S(2)}) async-start(bf16[8,96,128]{2,1,0:T(8,128)(2,1)} %shard_map.80), calls=%async_computation | async-start | bytes 393216 | tf_op jit(solution)/shard_map/all_to_all | solution.py:379
  17.3 1.1 %copy-start.1 = (f32[8,176,128]{2,1,0:T(8,128)S(1)}, f32[8,176,128]{2,1,0:T(8,128)}, u32[]{:S(2)}) copy-start(f32[8,176,128]{2,1,0:T(8,128)} %copy-done) | copy-start | bytes 2162692
  18.5 6.6 %collective-permute-start.5 = (bf16[4,176,128]{2,1,0:T(8,128)(2,1)S(1)}, bf16[4,176,128]{2,1,0:T(8,128)(2,1)S(1)}, u32[]{:S(2)}, u32[]{:S(2)}) collective-permute-start(bf16[4,176,128]{2,1,0:T(8,128)(2,1)S(1)} %get-tuple-element.75), channel_id=1, source_target_pairs={{0,4},{2,6},{4,0},{6,2},{8,12},{10,14},{12,8},{14,10},{16,20},{18,... | collective-permute-start | bytes 540680 | tf_op jit(solution)/shard_map/ppermute | solution.py:378
  25.7 10.9 %all-to-all-start.1 = ((bf16[4,176,128]{2,1,0:T(8,128)(2,1)}), bf16[4,176,128]{2,1,0:T(8,128)(2,1)S(1)}, u32[]{:S(2)}, u32[]{:S(2)}) async-start(bf16[4,176,128]{2,1,0:T(8,128)(2,1)} %shard_map.83), calls=%async_computation.1 | async-start | bytes 360448 | tf_op jit(solution)/shard_map/all_to_all | solution.py:380
  30.6 3.9 %collective-permute-start.3 = (bf16[96,128]{1,0:T(8,128)(2,1)S(1)}, bf16[96,128]{1,0:T(8,128)(2,1)S(1)}, u32[]{:S(2)}, u32[]{:S(2)}) collective-permute-start(bf16[96,128]{1,0:T(8,128)(2,1)S(1)} %get-tuple-element.71), channel_id=1, source_target_pairs={{0,4},{2,6},{4,0},{6,2},{8,12},{10,14},{12,8},{14,10},{16,20},{18,... | collective-permute-start | bytes 73736 | tf_op jit(solution)/shard_map/ppermute | solution.py:382

commit v7 on v4

--- a/solution.py
+++ b/solution.py
@@ -171,19 +171,26 @@
     )(gather, sent)
 
 
-def receive_kernel(target, first, scatter, received, addend, more, *rest):
-    out_far, more_out, out, done = rest[-4:]
+def receive_kernel(target, first, factor, scatter, received, addend, more, *refs):
+    rows, width = addend.shape
+    if first:
+        *parts, out_far, more_out, owned_far, out, owned, done = refs
+    else:
+        previous, out_far, more_out, out, done = refs
     more_out[0] = more[0]
-    rows, width = addend.shape
     place = scatter[...]
+    writes = []
+    if first and parts:
+        total_rows(factor, owned, *parts)
+        writes.append(pltpu.make_async_copy(owned, owned_far, done.at[width // tile_width]))
+        writes[0].start()
     if not first:
         here = (lax.axis_index("section") == target).astype(f32)
         covered = jnp.sum(place.astype(f32), axis=1, keepdims=True) * here > 0.5
-    writes = []
     for k, cut in enumerate(cuts(width, tile_width)):
         total = jnp.dot(place, received[:, cut], preferred_element_type=f32) + addend[:, cut]
         if not first:
-            total = jnp.where(covered, total, rest[0][:, cut].astype(f32))
+            total = jnp.where(covered, total, previous[:, cut].astype(f32))
         out[:, cut] = total.astype(bf16)
         write = pltpu.make_async_copy(out.at[:, cut], out_far.at[0, :, cut], done.at[k])
         write.start()
@@ -192,16 +199,22 @@
         write.wait()
 
 
-def receive(target, scatter, received, addend, more, after, previous=None):
+def receive(target, scatter, received, addend, more, previous=None, parts=(), owned=lanes, factor=1.0):
     rows, width = addend.shape
     away = pl.BlockSpec(memory_space=pltpu.HBM)
-    others = [far(a) for a in after] if previous is None else [previous]
-    return pl.pallas_call(
-        functools.partial(receive_kernel, target, previous is None),
-        in_specs=[near, near, near, scalar] + [away if previous is None else near] * len(others),
-        out_specs=[away, scalar],
-        out_shape=[pltpu.HBM((1, rows, width), bf16), pltpu.SMEM(more.shape, more.dtype)],
-        scratch_shapes=[pltpu.VMEM((rows, width), bf16), pltpu.SemaphoreType.DMA((width // tile_width,))],
+    first = previous is None
+    others = parts if first else [previous]
+    outs = [pltpu.HBM((1, rows, width), bf16), pltpu.SMEM(more.shape, more.dtype)]
+    scratch = [pltpu.VMEM((rows, width), bf16)]
+    if first:
+        outs.append(pltpu.HBM((1, owned), f32))
+        scratch.append(pltpu.VMEM((1, owned), f32))
+    return pl.pallas_call(
+        functools.partial(receive_kernel, target, first, factor),
+        in_specs=[near, near, near, scalar] + [near] * len(others),
+        out_specs=[away, scalar] + [away] * first,
+        out_shape=outs,
+        scratch_shapes=scratch + [pltpu.SemaphoreType.DMA((width // tile_width + 1,))],
         compiler_params=roomy,
         cost_estimate=small_cost,
     )(scatter, received, addend, more, *others)
@@ -222,12 +235,12 @@
     for j in range(keep.shape[0]):
         even = total[2 * j * owned_rows : (2 * j + 1) * owned_rows, :]
         odd = total[(2 * j + 1) * owned_rows : (2 * j + 2) * owned_rows, :]
-        keep[j, :owned_rows, :] = jnp.where(even_core, even, odd)
-        give[j, :owned_rows, :] = jnp.where(even_core, odd, even)
         if padded > owned_rows:
             blank = jnp.zeros((padded - owned_rows, lanes), f32)
-            keep[j, owned_rows:, :] = blank
-            give[j, owned_rows:, :] = blank
+            even = jnp.concatenate([even, blank], axis=0)
+            odd = jnp.concatenate([odd, blank], axis=0)
+        keep[j] = jnp.where(even_core, even, odd)
+        give[j] = jnp.where(even_core, odd, even)
 
 
 def pair_terms(normed, masked, gain, owned_rows, owners):
@@ -252,14 +265,14 @@
     for k in range(count):
         here = 2 * k + mine
         there = 2 * k + 1 - mine
-        hold[k] = keep[here, :cut, :] + taken[here, :cut, :]
-        give[k] = (keep[there, :cut, :] + taken[there, :cut, :]).astype(bf16)
+        hold[k] = keep[here, :cut, :] + taken[here, :cut, :].astype(f32)
+        give[k] = (keep[there, :cut, :] + taken[there, :cut, :].astype(f32)).astype(bf16)
     for side in range(2):
         at = 2 * place + side
-        hold_low[side] = keep[at, cut:, :] + taken[at, cut:, :]
+        hold_low[side] = keep[at, cut:, :] + taken[at, cut:, :].astype(f32)
         for k in range(1, count):
             at = 2 * lax.rem(place + k, count) + side
-            give_low[k - 1][side] = (keep[at, cut:, :] + taken[at, cut:, :]).astype(bf16)
+            give_low[k - 1][side] = (keep[at, cut:, :] + taken[at, cut:, :].astype(f32)).astype(bf16)
 
 
 def merge_terms(cut, keep, taken):
@@ -327,43 +340,31 @@
     )(hold, *landed)
 
 
-def total_kernel(owned_rows, factor, own_low, landed_low, own, *rest):
-    out = rest[-1]
+def total_rows(factor, out, own_low, landed_low, own, *landed):
     total = own[...]
-    for part in rest[:-1]:
+    for part in landed:
         total += part[...].astype(f32)
     low = (own_low[...] + landed_low[...].astype(f32)) * factor
     total = total * factor
     cut = total.shape[0]
-    for k in range(owned_rows):
+    for k in range(out.shape[1] // lanes):
         row = total[k : k + 1, :] if k < cut else low[k - cut : k - cut + 1, :]
         out[:, k * lanes : (k + 1) * lanes] = row
 
 
-def total_terms(owned_rows, factor, own_low, landed_low, own, landed):
-    return pl.pallas_call(
-        functools.partial(total_kernel, owned_rows, factor),
-        in_specs=[near] * (3 + len(landed)),
-        out_specs=near,
-        out_shape=jax.ShapeDtypeStruct((1, owned_rows * lanes), f32),
-        compiler_params=roomy,
-        cost_estimate=small_cost,
-    )(own_low, landed_low, own, *landed)
-
-
-def plane_sum(owners, owned_rows, factor, keep, taken):
+def plane_parts(owners, owned_rows, keep, taken):
     quad = 2 * pair
     shifts = range(quad, owners, quad)
     near_by = [(i, i ^ pair) for i in range(owners)]
     farther = [[(i, (i + shift) % owners) for i in range(owners)] for shift in shifts]
-    cut = -(-keep.shape[1] * 2 // 3 // pack_rows) * pack_rows
+    cut = -(-owned_rows * 2 // 3 // pack_rows) * pack_rows
     hold, give, hold_low, *give_low = merge_terms(cut, keep, taken)
     across = lax.ppermute(give, "dp", near_by)
     landed_low = [lax.ppermute(part, "dp", hops) for part, hops in zip(give_low, farther)]
     own, *parts = split_terms(hold, across)
     landed = [lax.ppermute(part, "dp", hops) for part, hops in zip(parts, farther)]
     own_low, cross_low = cross_terms(hold_low, landed_low)
-    return total_terms(owned_rows, factor, own_low, lax.ppermute(cross_low, "dp", near_by), own, landed)
+    return own_low, lax.ppermute(cross_low, "dp", near_by), own, *landed
 
 
 def weight_owned(normed, masked, gain, factor):
@@ -374,10 +375,10 @@
     if depth != lanes or owned % lanes or owners % (2 * pair):
         weight_term = lax.dot_general(normed, masked, contract_rows, preferred_element_type=f32)
         flat = jnp.concatenate([gain.reshape(-1), weight_term.reshape(-1)]) * factor
-        return lax.psum_scatter(flat, "dp", scatter_dimension=0, tiled=True)[None, :]
+        return (), owned, lax.psum_scatter(flat, "dp", scatter_dimension=0, tiled=True)[None, :]
     keep, give = pair_terms(normed, masked, gain, owned // lanes, owners)
     taken = lax.ppermute(give, "dp", [(i, i ^ 1) for i in range(owners)])
-    return plane_sum(owners, owned // lanes, factor, keep, taken)
+    return plane_parts(owners, owned // lanes, keep, taken), owned, None
 
 
 def shards(layer_inputs, top_grad, value_grads, weights, norm_gains, counts):
@@ -388,27 +389,30 @@
     spare = rows - room
     inputs = (counts, layer_inputs, top_grad, value_grads, weights, norm_gains)
     packed, addend, scatter, more, normed, masked, gain = branch_rows(0, room, *inputs)
-    owned = weight_owned(normed, masked, gain, factor)
+    parts, owned_size, owned = weight_owned(normed, masked, gain, factor)
     result = None
     for hop in range(sections - 1):
         target = sections - 2 - hop
-        hops = [(target + 1, target)]
+        hops = [(target + 1, target), (target, target + 1)]
         before = result
         if hop:
             packed = pack(scatter, before)
         landed = lax.ppermute(packed, "section", hops)
-        updated, more = receive(target, scatter, landed, addend, more, (owned,), before)
+        if hop:
+            updated, more = receive(target, scatter, landed, addend, more, before)
+        else:
+            updated, more, summed = receive(target, scatter, landed, addend, more, None, parts, owned_size, factor)
 
         def rest(updated):
             packed, addend, scatter, more, *_ = branch_rows(room, spare, *inputs)
             if hop:
                 packed = pack(scatter, before)
             landed = lax.ppermute(packed, "section", hops)
-            return receive(target, scatter, landed, addend, more, (), updated[0])[0]
+            return receive(target, scatter, landed, addend, more, updated[0])[0]
 
         updated = lax.cond(more.reshape(()) > 0, rest, lambda updated: updated, updated)
         result = updated[0]
-    return (result[None], owned)
+    return (result[None], summed if owned is None else owned)
 
 
 def solution(mesh):

time: 28.9 us -> 27.8 us (0.962)
  waiting for transfers between devices: 4.21 us -> 2.97 us
  starting transfers between devices: 17.3 us -> 18.1 us
  Pallas kernels: 6.52 us -> 5.9 us
    ppermute x8, waiting for transfers between devices: 2.28 us -> 0.02 us  [the longest x6 0.02 us: plane_parts(): lax.ppermute(part, 'dp', hops)]
    ppermute x1, waiting for transfers between devices: 0.84 us -> 2.95 us  [shards(): landed = lax.ppermute(packed, 'section', hops)]
    ppermute x1, starting transfers between devices: 1.28 us -> 2.56 us  [shards(): landed = lax.ppermute(packed, 'section', hops)]
    ppermute x1, waiting for transfers between devices: 1.09 us -> 0.01 us  [weight_owned(): taken = lax.ppermute(give, 'dp', [(i, i ^ 1) for i in range(owners)])]
    pallas_call x2 -> x1, Pallas kernels: 1.95 us -> 1.33 us  [receive(): pl.pallas_call(functools.partial(receive_kernel, target, first, factor),...]
    ppermute x8, starting transfers between devices: 15.5 us -> 15 us  [the longest x6 10.6 us: plane_parts(): lax.ppermute(part, 'dp', hops)]
  transfers between devices with their start and end apart: 10 -> 10, of which waited for: 3 -> 1; matrix products, arithmetic and copies ran while one was open for 0% -> 0% of each run, Pallas kernels for 3% -> 1%
where the time goes in v7:
time: 27.8 us; the launch traced here: 27.6 us
  starting transfers between devices  18.1 us (65%)
  Pallas kernels  5.9 us (21%)
  waiting for transfers between devices  2.97 us (11%)
  between operations  0.69 us (2%)
    ppermute x6, starting transfers between devices, plane_parts(): lax.ppermute(part, 'dp', hops)  10.6 us
    pallas_call x1, Pallas kernels, branch_rows(): pl.pallas_call(functools.partial(branch_kernel, low), in_specs=[pl.BlockS...  3.8 us
    ppermute x1, waiting for transfers between devices, shards(): landed = lax.ppermute(packed, 'section', hops)  2.95 us
    ppermute x1, starting transfers between devices, plane_parts(): across = lax.ppermute(give, 'dp', near_by)  2.77 us
    ppermute x1, starting transfers between devices, shards(): landed = lax.ppermute(packed, 'section', hops)  2.56 us
    ppermute x1, starting transfers between devices, plane_parts(): return (own_low, lax.ppermute(cross_low, 'dp', near_by), own, *landed)  1.58 us
    pallas_call x1, Pallas kernels, receive(): pl.pallas_call(functools.partial(receive_kernel, target, first, factor),...  1.33 us
    pallas_call x1, Pallas kernels, pair_terms(): pl.pallas_call(functools.partial(terms_kernel, owned_rows), in_specs=[nea...  0.6 us
  transfers between devices with their start and end apart: 10, of which 1 were waited for; matrix products, arithmetic and copies ran while one was open for 0% of the time, Pallas kernels for 1%

profile of v7, /device:TPU:0, one launch (start us, length us, event | category | flops | bytes accessed | tf_op | source)
XLA Modules:
  0.0 27.6 jit_solution(6875694639143379829)
XLA Ops:
  0.6 3.8 %shard_map.77 = (bf16[96,4096]{1,0:T(8,128)(2,1)S(1)}, f32[128,4096]{1,0:T(8,128)S(1)}, bf16[128,96]{1,0:T(8,128)(2,1)S(1)}, s32[1]{0:T(128)S(4)}, bf16[128,4096...) custom-call(s32[8]{0:T(128)} %counts_far.1, bf16[1,128,4096]{2,1,0:T(8,128)(2,1)} %x_far.1, ...), custom_call_target="tpu_custom_call" | custom-call | flops 1048576 | bytes 65536 | tf_op jit(solution)/shard_map/pallas_call | solution.py:126
  4.4 0.6 %shard_map.78 = (f32[8,272,128]{2,1,0:T(8,128)S(1)}, f32[8,272,128]{2,1,0:T(8,128)S(1)}) custom-call(bf16[128,4096]{1,0:T(8,128)(2,1)S(1)} %get-tuple-element.60.normed, bf16[128,128]{1,0:T(8,128)(2,1)S(1)} %get-tuple-element.61.masked, f32[1,4096]{1,0:T(1,128)S(1)} %get-tuple-element.62.gain), custom_call_target="tpu_custom_call" | custom-call | flops 1048576 | bytes 65536 | tf_op jit(solution)/shard_map/pallas_call | solution.py:249
  5.0 0.5 %collective-permute-start.2 = (f32[8,272,128]{2,1,0:T(8,128)S(1)}, f32[8,272,128]{2,1,0:T(8,128)S(1)}, u32[]{:S(2)}, u32[]{:S(2)}) collective-permute-start(f32[8,272,128]{2,1,0:T(8,128)S(1)} %get-tuple-element.64), channel_id=1, source_target_pairs={{0,2},{2,0},{4,6},{6,4},{8,10},{10,8},{12,14},{14,12},{16,18},{18,... | collective-permute-start | bytes 3342344 | tf_op jit(solution)/shard_map/ppermute | solution.py:380
  5.6 2.6 %collective-permute-start.1 = (bf16[96,4096]{1,0:T(8,128)(2,1)S(1)}, bf16[96,4096]{1,0:T(8,128)(2,1)S(1)}, u32[]{:S(2)}, u32[]{:S(2)}) collective-permute-start(bf16[96,4096]{1,0:T(8,128)(2,1)S(1)} %get-tuple-element.57), channel_id=1, source_target_pairs={{1,0},{0,1},{3,2},{2,3},{5,4},{4,5},{7,6},{6,7},{9,8},{8,9},{11,10... | collective-permute-start | bytes 2359304 | tf_op jit(solution)/shard_map/ppermute | solution.py:400
  8.1 0.0 collective-permute-done.2.taken
  8.1 0.1 shard_map.79
  8.2 2.8 %collective-permute-start.7 = (bf16[4,176,128]{2,1,0:T(8,128)(2,1)S(1)}, bf16[4,176,128]{2,1,0:T(8,128)(2,1)S(1)}, u32[]{:S(2)}, u32[]{:S(2)}) collective-permute-start(bf16[4,176,128]{2,1,0:T(8,128)(2,1)S(1)} %get-tuple-element.72), channel_id=1, source_target_pairs={{0,4},{2,6},{4,0},{6,2},{8,12},{10,14},{12,8},{14,10},{16,20},{18,... | collective-permute-start | bytes 540680 | tf_op jit(solution)/shard_map/ppermute | solution.py:362
  11.0 1.6 %collective-permute-start.3 = (bf16[2,96,128]{2,1,0:T(8,128)(2,1)S(1)}, bf16[2,96,128]{2,1,0:T(8,128)(2,1)S(1)}, u32[]{:S(2)}, u32[]{:S(2)}) collective-permute-start(bf16[2,96,128]{2,1,0:T(8,128)(2,1)S(1)} %get-tuple-element.66), channel_id=1, source_target_pairs={{0,8},{2,10},{4,12},{6,14},{8,16},{10,18},{12,20},{14,22},{16,24},... | collective-permute-start | bytes 147464 | tf_op jit(solution)/shard_map/ppermute | solution.py:363
  12.6 2.6 %collective-permute-start.4 = (bf16[2,96,128]{2,1,0:T(8,128)(2,1)S(1)}, bf16[2,96,128]{2,1,0:T(8,128)(2,1)S(1)}, u32[]{:S(2)}, u32[]{:S(2)}) collective-permute-start(bf16[2,96,128]{2,1,0:T(8,128)(2,1)S(1)} %get-tuple-element.67), channel_id=1, source_target_pairs={{0,16},{2,18},{4,20},{6,22},{8,24},{10,26},{12,28},{14,30},{16,0},... | collective-permute-start | bytes 147464 | tf_op jit(solution)/shard_map/ppermute | solution.py:363
  15.2 1.3 %collective-permute-start.5 = (bf16[2,96,128]{2,1,0:T(8,128)(2,1)S(1)}, bf16[2,96,128]{2,1,0:T(8,128)(2,1)S(1)}, u32[]{:S(2)}, u32[]{:S(2)}) collective-permute-start(bf16[2,96,128]{2,1,0:T(8,128)(2,1)S(1)} %get-tuple-element.68), channel_id=1, source_target_pairs={{0,24},{2,26},{4,28},{6,30},{8,0},{10,2},{12,4},{14,6},{16,8},{18,... | collective-permute-start | bytes 147464 | tf_op jit(solution)/shard_map/ppermute | solution.py:363
  16.5 0.0 collective-permute-done.7.taken
  16.6 1.2 %collective-permute-start.8 = (bf16[176,128]{1,0:T(8,128)(2,1)S(1)}, bf16[176,128]{1,0:T(8,128)(2,1)S(1)}, u32[]{:S(2)}, u32[]{:S(2)}) collective-permute-start(bf16[176,128]{1,0:T(8,128)(2,1)S(1)} %get-tuple-element.74), channel_id=1, source_target_pairs={{0,8},{2,10},{4,12},{6,14},{8,16},{10,18},{12,20},{14,22},{16,24},... | collective-permute-start | bytes 135176 | tf_op jit(solution)/shard_map/ppermute | solution.py:365
  17.7 0.0 collective-permute-done.3.refs_0_
  17.7 2.6 %collective-permute-start.9 = (bf16[176,128]{1,0:T(8,128)(2,1)S(1)}, bf16[176,128]{1,0:T(8,128)(2,1)S(1)}, u32[]{:S(2)}, u32[]{:S(2)}) collective-permute-start(bf16[176,128]{1,0:T(8,128)(2,1)S(1)} %get-tuple-element.75), channel_id=1, source_target_pairs={{0,16},{2,18},{4,20},{6,22},{8,24},{10,26},{12,28},{14,30},{16,0},... | collective-permute-start | bytes 135176 | tf_op jit(solution)/shard_map/ppermute | solution.py:365
  20.3 0.0 collective-permute-done.4.refs_1_
  20.3 1.3 %collective-permute-start.10 = (bf16[176,128]{1,0:T(8,128)(2,1)S(1)}, bf16[176,128]{1,0:T(8,128)(2,1)S(1)}, u32[]{:S(2)}, u32[]{:S(2)}) collective-permute-start(bf16[176,128]{1,0:T(8,128)(2,1)S(1)} %get-tuple-element.76), channel_id=1, source_target_pairs={{0,24},{2,26},{4,28},{6,30},{8,0},{10,2},{12,4},{14,6},{16,8},{18,... | collective-permute-start | bytes 135176 | tf_op jit(solution)/shard_map/ppermute | solution.py:365
  21.7 0.0 collective-permute-done.5.refs_2_
  21.7 1.6 %collective-permute-start.6 = (bf16[96,128]{1,0:T(8,128)(2,1)S(1)}, bf16[96,128]{1,0:T(8,128)(2,1)S(1)}, u32[]{:S(2)}, u32[]{:S(2)}) collective-permute-start(bf16[96,128]{1,0:T(8,128)(2,1)S(1)} %get-tuple-element.70), channel_id=1, source_target_pairs={{0,4},{2,6},{4,0},{6,2},{8,12},{10,14},{12,8},{14,10},{16,20},{18,... | collective-permute-start | bytes 73736 | tf_op jit(solution)/shard_map/ppermute | solution.py:367
  23.3 2.9 %collective-permute-done.1.received = bf16[96,4096]{1,0:T(8,128)(2,1)S(1)} collective-permute-done((bf16[96,4096]{1,0:T(8,128)(2,1)S(1)}, bf16[96,4096]{1,0:T(8,128)(2,1)S(1)}, u32[]{:S(2)}, u32[]{:S(2)}) %collective-permute-start.1) | collective-permute-done | bytes 786464 | tf_op jit(solution)/shard_map/ppermute | solution.py:400
  26.3 0.0 collective-permute-done.6.refs_1_
  26.3 0.0 collective-permute-done.8.refs_3_
  26.3 0.0 collective-permute-done.9.refs_4_
  26.3 0.0 collective-permute-done.10.refs_5_
  26.3 1.3 %shard_map.82 = (bf16[1,128,4096]{2,1,0:T(8,128)(2,1)}, s32[1]{0:T(128)S(4)}, f32[1,33024]{1,0:T(1,128)}) custom-call(bf16[128,96]{1,0:T(8,128)(2,1)S(1)} %get-tuple-element.56.scatter, bf16[96,4096]{1,0:T(8,128)(2,1)S(1)} %collective-permute-done.1.received, f32[128,4096]{1,0:T(8,128)S(1)} %get-tuple-element.58.addend, s32[1]{0:T(128)S(4)} %get-tuple-element.59.more, ...), custom_call_target="tpu_custom_call" | custom-call | flops 1048576 | bytes 65536 | tf_op jit(solution)/shard_map/pallas_call | solution.py:212
  (3 shorter events, 0.1 us)
Async XLA Ops:
  5.0 3.1 %collective-permute-start.2 = (f32[8,272,128]{2,1,0:T(8,128)S(1)}, f32[8,272,128]{2,1,0:T(8,128)S(1)}, u32[]{:S(2)}, u32[]{:S(2)}) collective-permute-start(f32[8,272,128]{2,1,0:T(8,128)S(1)} %get-tuple-element.64), channel_id=1, source_target_pairs={{0,2},{2,0},{4,6},{6,4},{8,10},{10,8},{12,14},{14,12},{16,18},{18,... | collective-permute-start | bytes 3342344 | tf_op jit(solution)/shard_map/ppermute | solution.py:380
  5.6 20.7 %collective-permute-start.1 = (bf16[96,4096]{1,0:T(8,128)(2,1)S(1)}, bf16[96,4096]{1,0:T(8,128)(2,1)S(1)}, u32[]{:S(2)}, u32[]{:S(2)}) collective-permute-start(bf16[96,4096]{1,0:T(8,128)(2,1)S(1)} %get-tuple-element.57), channel_id=1, source_target_pairs={{1,0},{0,1},{3,2},{2,3},{5,4},{4,5},{7,6},{6,7},{9,8},{8,9},{11,10... | collective-permute-start | bytes 2359304 | tf_op jit(solution)/shard_map/ppermute | solution.py:400
  8.2 8.3 %collective-permute-start.7 = (bf16[4,176,128]{2,1,0:T(8,128)(2,1)S(1)}, bf16[4,176,128]{2,1,0:T(8,128)(2,1)S(1)}, u32[]{:S(2)}, u32[]{:S(2)}) collective-permute-start(bf16[4,176,128]{2,1,0:T(8,128)(2,1)S(1)} %get-tuple-element.72), channel_id=1, source_target_pairs={{0,4},{2,6},{4,0},{6,2},{8,12},{10,14},{12,8},{14,10},{16,20},{18,... | collective-permute-start | bytes 540680 | tf_op jit(solution)/shard_map/ppermute | solution.py:362
  11.0 6.7 %collective-permute-start.3 = (bf16[2,96,128]{2,1,0:T(8,128)(2,1)S(1)}, bf16[2,96,128]{2,1,0:T(8,128)(2,1)S(1)}, u32[]{:S(2)}, u32[]{:S(2)}) collective-permute-start(bf16[2,96,128]{2,1,0:T(8,128)(2,1)S(1)} %get-tuple-element.66), channel_id=1, source_target_pairs={{0,8},{2,10},{4,12},{6,14},{8,16},{10,18},{12,20},{14,22},{16,24},... | collective-permute-start | bytes 147464 | tf_op jit(solution)/shard_map/ppermute | solution.py:363
  12.6 7.8 %collective-permute-start.4 = (bf16[2,96,128]{2,1,0:T(8,128)(2,1)S(1)}, bf16[2,96,128]{2,1,0:T(8,128)(2,1)S(1)}, u32[]{:S(2)}, u32[]{:S(2)}) collective-permute-start(bf16[2,96,128]{2,1,0:T(8,128)(2,1)S(1)} %get-tuple-element.67), channel_id=1, source_target_pairs={{0,16},{2,18},{4,20},{6,22},{8,24},{10,26},{12,28},{14,30},{16,0},... | collective-permute-start | bytes 147464 | tf_op jit(solution)/shard_map/ppermute | solution.py:363
  15.2 6.5 %collective-permute-start.5 = (bf16[2,96,128]{2,1,0:T(8,128)(2,1)S(1)}, bf16[2,96,128]{2,1,0:T(8,128)(2,1)S(1)}, u32[]{:S(2)}, u32[]{:S(2)}) collective-permute-start(bf16[2,96,128]{2,1,0:T(8,128)(2,1)S(1)} %get-tuple-element.68), channel_id=1, source_target_pairs={{0,24},{2,26},{4,28},{6,30},{8,0},{10,2},{12,4},{14,6},{16,8},{18,... | collective-permute-start | bytes 147464 | tf_op jit(solution)/shard_map/ppermute | solution.py:363
  16.6 9.7 %collective-permute-start.8 = (bf16[176,128]{1,0:T(8,128)(2,1)S(1)}, bf16[176,128]{1,0:T(8,128)(2,1)S(1)}, u32[]{:S(2)}, u32[]{:S(2)}) collective-permute-start(bf16[176,128]{1,0:T(8,128)(2,1)S(1)} %get-tuple-element.74), channel_id=1, source_target_pairs={{0,8},{2,10},{4,12},{6,14},{8,16},{10,18},{12,20},{14,22},{16,24},... | collective-permute-start | bytes 135176 | tf_op jit(solution)/shard_map/ppermute | solution.py:365
  17.7 8.5 %collective-permute-start.9 = (bf16[176,128]{1,0:T(8,128)(2,1)S(1)}, bf16[176,128]{1,0:T(8,128)(2,1)S(1)}, u32[]{:S(2)}, u32[]{:S(2)}) collective-permute-start(bf16[176,128]{1,0:T(8,128)(2,1)S(1)} %get-tuple-element.75), channel_id=1, source_target_pairs={{0,16},{2,18},{4,20},{6,22},{8,24},{10,26},{12,28},{14,30},{16,0},... | collective-permute-start | bytes 135176 | tf_op jit(solution)/shard_map/ppermute | solution.py:365
  20.3 5.9 %collective-permute-start.10 = (bf16[176,128]{1,0:T(8,128)(2,1)S(1)}, bf16[176,128]{1,0:T(8,128)(2,1)S(1)}, u32[]{:S(2)}, u32[]{:S(2)}) collective-permute-start(bf16[176,128]{1,0:T(8,128)(2,1)S(1)} %get-tuple-element.76), channel_id=1, source_target_pairs={{0,24},{2,26},{4,28},{6,30},{8,0},{10,2},{12,4},{14,6},{16,8},{18,... | collective-permute-start | bytes 135176 | tf_op jit(solution)/shard_map/ppermute | solution.py:365
  21.7 4.5 %collective-permute-start.6 = (bf16[96,128]{1,0:T(8,128)(2,1)S(1)}, bf16[96,128]{1,0:T(8,128)(2,1)S(1)}, u32[]{:S(2)}, u32[]{:S(2)}) collective-permute-start(bf16[96,128]{1,0:T(8,128)(2,1)S(1)} %get-tuple-element.70), channel_id=1, source_target_pairs={{0,4},{2,6},{4,0},{6,2},{8,12},{10,14},{12,8},{14,10},{16,20},{18,... | collective-permute-start | bytes 73736 | tf_op jit(solution)/shard_map/ppermute | solution.py:367

commit v8 on v7

--- a/solution.py
+++ b/solution.py
@@ -240,7 +240,7 @@
             even = jnp.concatenate([even, blank], axis=0)
             odd = jnp.concatenate([odd, blank], axis=0)
         keep[j] = jnp.where(even_core, even, odd)
-        give[j] = jnp.where(even_core, odd, even)
+        give[j] = jnp.where(even_core, odd, even).astype(bf16)
 
 
 def pair_terms(normed, masked, gain, owned_rows, owners):
@@ -250,121 +250,116 @@
         functools.partial(terms_kernel, owned_rows),
         in_specs=[near, near, near],
         out_specs=[near, near],
-        out_shape=[half, half],
+        out_shape=[half, jax.ShapeDtypeStruct(half.shape, bf16)],
         scratch_shapes=[pltpu.VMEM((owners * owned_rows, lanes), f32)],
         compiler_params=roomy,
         cost_estimate=small_cost,
     )(normed, masked, gain)
 
 
-def merge_kernel(keep, taken, hold, give, hold_low, *give_low):
-    cut = hold.shape[1]
-    chip = lax.axis_index("dp") // pair
+def merge_kernel(keep, taken, hold, *give):
+    spot = lax.axis_index("dp")
+    even = spot % pair == 0
+    chip = spot // pair
     mine, place = chip % 2, chip // 2
     count = hold.shape[0]
+
+    def block(across, along):
+        at = jnp.where(even, across, along)
+        return keep[at] + taken[at].astype(f32)
+
     for k in range(count):
-        here = 2 * k + mine
-        there = 2 * k + 1 - mine
-        hold[k] = keep[here, :cut, :] + taken[here, :cut, :].astype(f32)
-        give[k] = (keep[there, :cut, :] + taken[there, :cut, :].astype(f32)).astype(bf16)
-    for side in range(2):
-        at = 2 * place + side
-        hold_low[side] = keep[at, cut:, :] + taken[at, cut:, :].astype(f32)
-        for k in range(1, count):
+        hold[k] = block(2 * k + mine, 2 * place + k % 2)
+    for k in range(1, count):
+        for side in range(2):
+            across = min(2 * (k - 1) + side, count - 1)
             at = 2 * lax.rem(place + k, count) + side
-            give_low[k - 1][side] = (keep[at, cut:, :] + taken[at, cut:, :].astype(f32)).astype(bf16)
-
-
-def merge_terms(cut, keep, taken):
-    blocks, padded, _ = keep.shape
-    count = blocks // 2
-    high = (count, cut, lanes)
-    low = (2, padded - cut, lanes)
+            give[k - 1][side] = block(2 * across + 1 - mine, at).astype(bf16)
+
+
+def merge_terms(keep, taken):
+    count = keep.shape[0] // 2
     return pl.pallas_call(
         merge_kernel,
         in_specs=[near, near],
-        out_specs=[near] * (2 + count),
-        out_shape=[
-            jax.ShapeDtypeStruct(high, f32),
-            jax.ShapeDtypeStruct(high, bf16),
-            jax.ShapeDtypeStruct(low, f32),
-        ]
-        + [jax.ShapeDtypeStruct(low, bf16)] * (count - 1),
+        out_specs=[near] * count,
+        out_shape=[jax.ShapeDtypeStruct((count,) + keep.shape[1:], f32)]
+        + [jax.ShapeDtypeStruct((2,) + keep.shape[1:], bf16)] * (count - 1),
         compiler_params=roomy,
         cost_estimate=small_cost,
     )(keep, taken)
 
 
-def split_kernel(hold, taken, own, *parts):
+def split_kernel(hold, *refs):
     count = hold.shape[0]
-    place = lax.axis_index("dp") // (2 * pair)
-    own[...] = hold[place] + taken[place].astype(f32)
-    for k in range(1, count):
-        at = lax.rem(place + k, count)
-        parts[k - 1][...] = (hold[at] + taken[at].astype(f32)).astype(bf16)
-
-
-def split_terms(hold, taken):
+    landed, own, parts = refs[: count - 1], refs[count - 1], refs[count:]
+    spot = lax.axis_index("dp")
+    chip = spot // pair
+    mine, place = chip % 2, chip // 2
+
+    @pl.when(spot % pair == 0)
+    def _():
+        sums = [hold[k] + landed[k // 2][k % 2].astype(f32) for k in range(count)]
+
+        def pick(at):
+            total = sums[0]
+            for k in range(1, count):
+                total = jnp.where(at == k, sums[k], total)
+            return total
+
+        own[...] = pick(place)
+        for k in range(1, count):
+            parts[k - 1][...] = pick(lax.rem(place + k, count)).astype(bf16)
+
+    @pl.when(spot % pair != 0)
+    def _():
+        total = hold[mine]
+        passed = hold[1 - mine]
+        for part in landed:
+            total += part[mine].astype(f32)
+            passed += part[1 - mine].astype(f32)
+        own[...] = total
+        parts[0][...] = passed.astype(bf16)
+        for part in parts[1:]:
+            part[...] = jnp.zeros_like(part)
+
+
+def split_terms(hold, landed):
     count = hold.shape[0]
     return pl.pallas_call(
         split_kernel,
-        in_specs=[near, near],
+        in_specs=[near] * count,
         out_specs=[near] * count,
         out_shape=[jax.ShapeDtypeStruct(hold.shape[1:], f32)]
         + [jax.ShapeDtypeStruct(hold.shape[1:], bf16)] * (count - 1),
         compiler_params=roomy,
         cost_estimate=small_cost,
-    )(hold, taken)
-
-
-def cross_kernel(hold, *refs):
-    *landed, own, give = refs
-    mine = lax.axis_index("dp") // pair % 2
-    total = hold[mine]
-    passed = hold[1 - mine]
-    for part in landed:
-        total += part[mine].astype(f32)
-        passed += part[1 - mine].astype(f32)
-    own[...] = total
-    give[...] = passed.astype(bf16)
-
-
-def cross_terms(hold, landed):
-    return pl.pallas_call(
-        cross_kernel,
-        in_specs=[near] * (1 + len(landed)),
-        out_specs=[near, near],
-        out_shape=[jax.ShapeDtypeStruct(hold.shape[1:], f32), jax.ShapeDtypeStruct(hold.shape[1:], bf16)],
-        compiler_params=roomy,
-        cost_estimate=small_cost,
     )(hold, *landed)
 
 
-def total_rows(factor, out, own_low, landed_low, own, *landed):
+def total_rows(factor, out, own, *landed):
     total = own[...]
     for part in landed:
         total += part[...].astype(f32)
-    low = (own_low[...] + landed_low[...].astype(f32)) * factor
     total = total * factor
-    cut = total.shape[0]
     for k in range(out.shape[1] // lanes):
-        row = total[k : k + 1, :] if k < cut else low[k - cut : k - cut + 1, :]
-        out[:, k * lanes : (k + 1) * lanes] = row
-
-
-def plane_parts(owners, owned_rows, keep, taken):
+        out[:, k * lanes : (k + 1) * lanes] = total[k : k + 1, :]
+
+
+def plane_parts(owners, keep, taken):
     quad = 2 * pair
     shifts = range(quad, owners, quad)
-    near_by = [(i, i ^ pair) for i in range(owners)]
-    farther = [[(i, (i + shift) % owners) for i in range(owners)] for shift in shifts]
-    cut = -(-owned_rows * 2 // 3 // pack_rows) * pack_rows
-    hold, give, hold_low, *give_low = merge_terms(cut, keep, taken)
-    across = lax.ppermute(give, "dp", near_by)
-    landed_low = [lax.ppermute(part, "dp", hops) for part, hops in zip(give_low, farther)]
-    own, *parts = split_terms(hold, across)
-    landed = [lax.ppermute(part, "dp", hops) for part, hops in zip(parts, farther)]
-    own_low, cross_low = cross_terms(hold_low, landed_low)
-    return own_low, lax.ppermute(cross_low, "dp", near_by), own, *landed
+    even, odd = range(0, owners, pair), range(1, owners, pair)
+    across = [[(i, i ^ pair) for i in one] for one in (even, odd)]
+    along = [[[(i, (i + shift) % owners) for i in one] for shift in shifts] for one in (even, odd)]
+    hold, *give = merge_terms(keep, taken)
+    landed = []
+    for k, part in enumerate(give):
+        hops = along[1][k] + (across[0] if 2 * k < owners // quad else [])
+        landed.append(lax.ppermute(part, "dp", hops))
+    own, *parts = split_terms(hold, landed)
+    arrived = [lax.ppermute(part, "dp", along[0][k] + (across[1] if k == 0 else [])) for k, part in enumerate(parts)]
+    return own, *arrived
 
 
 def weight_owned(normed, masked, gain, factor):
@@ -378,7 +373,7 @@
         return (), owned, lax.psum_scatter(flat, "dp", scatter_dimension=0, tiled=True)[None, :]
     keep, give = pair_terms(normed, masked, gain, owned // lanes, owners)
     taken = lax.ppermute(give, "dp", [(i, i ^ 1) for i in range(owners)])
-    return plane_parts(owners, owned // lanes, keep, taken), owned, None
+    return plane_parts(owners, keep, taken), owned, None
 
 
 def shards(layer_inputs, top_grad, value_grads, weights, norm_gains, counts):

time: 27.8 us -> 30.8 us (1.11)
  waiting for transfers between devices: 2.97 us -> 8.75 us
  starting transfers between devices: 18.1 us -> 15.2 us
    ppermute x8 -> x6, waiting for transfers between devices: 0.02 us -> 6.8 us  [the longest x3 3.89 us: plane_parts(): landed.append(lax.ppermute(part, 'dp', hops))]
    ppermute x1, waiting for transfers between devices: 2.95 us -> 0.01 us  [shards(): landed = lax.ppermute(packed, 'section', hops)]
    ppermute x8 -> x6, starting transfers between devices: 15 us -> 12.1 us  [the longest x3 9.37 us: plane_parts(): lax.ppermute(part, 'dp', along[0][k] + (across[1] if k == 0 else []))]
    ppermute x1, waiting for transfers between devices: 0.01 us -> 1.94 us  [weight_owned(): taken = lax.ppermute(give, 'dp', [(i, i ^ 1) for i in range(owners)])]
    ppermute x1, starting transfers between devices: 0.52 us -> 0.07 us  [weight_owned(): taken = lax.ppermute(give, 'dp', [(i, i ^ 1) for i in range(owners)])]
    ppermute x1, starting transfers between devices: 2.56 us -> 3.01 us  [shards(): landed = lax.ppermute(packed, 'section', hops)]
  transfers between devices with their start and end apart: 10 -> 8, of which waited for: 1 -> 4; matrix products, arithmetic and copies ran while one was open for 0% -> 0% of each run, Pallas kernels for 1% -> 3%
where the time goes in v8:
time: 30.8 us; the launch traced here: 30.6 us
  starting transfers between devices  15.2 us (49%)
  waiting for transfers between devices  8.75 us (28%)
  Pallas kernels  5.96 us (19%)
  between operations  0.72 us (2%)
    ppermute x3, starting transfers between devices, plane_parts(): lax.ppermute(part, 'dp', along[0][k] + (across[1] if k == 0 else []))  9.37 us
    ppermute x3, waiting for transfers between devices, plane_parts(): landed.append(lax.ppermute(part, 'dp', hops))  3.89 us
    pallas_call x1, Pallas kernels, branch_rows(): pl.pallas_call(functools.partial(branch_kernel, low), in_specs=[pl.BlockS...  3.8 us
    ppermute x1, starting transfers between devices, shards(): landed = lax.ppermute(packed, 'section', hops)  3.01 us
    ppermute x3, waiting for transfers between devices, plane_parts(): lax.ppermute(part, 'dp', along[0][k] + (across[1] if k == 0 else []))  2.92 us
    ppermute x3, starting transfers between devices, plane_parts(): landed.append(lax.ppermute(part, 'dp', hops))  2.73 us
    ppermute x1, waiting for transfers between devices, weight_owned(): taken = lax.ppermute(give, 'dp', [(i, i ^ 1) for i in range(owners)])  1.94 us
    pallas_call x1, Pallas kernels, receive(): pl.pallas_call(functools.partial(receive_kernel, target, first, factor),...  1.34 us
  transfers between devices with their start and end apart: 8, of which 4 were waited for; matrix products, arithmetic and copies ran while one was open for 0% of the time, Pallas kernels for 3%

profile of v8, /device:TPU:0, one launch (start us, length us, event | category | flops | bytes accessed | tf_op | source)
XLA Modules:
  0.0 30.6 jit_solution(8990951561977478441)
XLA Ops:
  0.6 3.8 %shard_map.77 = (bf16[96,4096]{1,0:T(8,128)(2,1)S(1)}, f32[128,4096]{1,0:T(8,128)S(1)}, bf16[128,96]{1,0:T(8,128)(2,1)S(1)}, s32[1]{0:T(128)S(4)}, bf16[128,4096...) custom-call(s32[8]{0:T(128)} %counts_far.1, bf16[1,128,4096]{2,1,0:T(8,128)(2,1)} %x_far.1, ...), custom_call_target="tpu_custom_call" | custom-call | flops 1048576 | bytes 65536 | tf_op jit(solution)/shard_map/pallas_call | solution.py:126
  4.4 3.0 %collective-permute-start.1 = (bf16[96,4096]{1,0:T(8,128)(2,1)S(1)}, bf16[96,4096]{1,0:T(8,128)(2,1)S(1)}, u32[]{:S(2)}, u32[]{:S(2)}) collective-permute-start(bf16[96,4096]{1,0:T(8,128)(2,1)S(1)} %get-tuple-element.53), channel_id=1, source_target_pairs={{1,0},{0,1},{3,2},{2,3},{5,4},{4,5},{7,6},{6,7},{9,8},{8,9},{11,10... | collective-permute-start | bytes 2359304 | tf_op jit(solution)/shard_map/ppermute | solution.py:395
  7.4 0.6 %shard_map.78 = (f32[8,272,128]{2,1,0:T(8,128)S(1)}, bf16[8,272,128]{2,1,0:T(8,128)(2,1)S(1)}) custom-call(bf16[128,4096]{1,0:T(8,128)(2,1)S(1)} %get-tuple-element.56.normed, bf16[128,128]{1,0:T(8,128)(2,1)S(1)} %get-tuple-element.57.masked, f32[1,4096]{1,0:T(1,128)S(1)} %get-tuple-element.58.gain), custom_call_target="tpu_custom_call" | custom-call | flops 1048576 | bytes 65536 | tf_op jit(solution)/shard_map/pallas_call | solution.py:249
  8.0 0.1 collective-permute-start.2
  8.1 1.9 %collective-permute-done.2.taken = bf16[8,272,128]{2,1,0:T(8,128)(2,1)S(1)} collective-permute-done((bf16[8,272,128]{2,1,0:T(8,128)(2,1)S(1)}, bf16[8,272,128]{2,1,0:T(8,128)(2,1)S(1)}, u32[]{:S(2)}, u32[]{:S(2)}) %collective-permute-start.2) | collective-permute-done | bytes 557088 | tf_op jit(solution)/shard_map/ppermute | solution.py:375
  10.0 0.1 shard_map.79
  10.2 1.6 %collective-permute-start.3 = (bf16[2,272,128]{2,1,0:T(8,128)(2,1)S(1)}, bf16[2,272,128]{2,1,0:T(8,128)(2,1)S(1)}, u32[]{:S(2)}, u32[]{:S(2)}) collective-permute-start(bf16[2,272,128]{2,1,0:T(8,128)(2,1)S(1)} %get-tuple-element.62), channel_id=1, source_target_pairs={{2,10},{6,14},{10,18},{14,22},{18,26},{22,30},{26,2},{30,6},{0,4},... | collective-permute-start | bytes 417800 | tf_op jit(solution)/shard_map/ppermute | solution.py:359
  11.7 0.5 %collective-permute-start.4 = (bf16[2,272,128]{2,1,0:T(8,128)(2,1)S(1)}, bf16[2,272,128]{2,1,0:T(8,128)(2,1)S(1)}, u32[]{:S(2)}, u32[]{:S(2)}) collective-permute-start(bf16[2,272,128]{2,1,0:T(8,128)(2,1)S(1)} %get-tuple-element.63), channel_id=1, source_target_pairs={{2,18},{6,22},{10,26},{14,30},{18,2},{22,6},{26,10},{30,14},{0,4},... | collective-permute-start | bytes 417800 | tf_op jit(solution)/shard_map/ppermute | solution.py:359
  12.3 0.7 %collective-permute-start.5 = (bf16[2,272,128]{2,1,0:T(8,128)(2,1)S(1)}, bf16[2,272,128]{2,1,0:T(8,128)(2,1)S(1)}, u32[]{:S(2)}, u32[]{:S(2)}) collective-permute-start(bf16[2,272,128]{2,1,0:T(8,128)(2,1)S(1)} %get-tuple-element.64), channel_id=1, source_target_pairs={{2,26},{6,30},{10,2},{14,6},{18,10},{22,14},{26,18},{30,22},{3,27}... | collective-permute-start | bytes 417800 | tf_op jit(solution)/shard_map/ppermute | solution.py:359
  12.9 2.4 %collective-permute-done.3.refs_0_ = bf16[2,272,128]{2,1,0:T(8,128)(2,1)S(1)} collective-permute-done((bf16[2,272,128]{2,1,0:T(8,128)(2,1)S(1)}, bf16[2,272,128]{2,1,0:T(8,128)(2,1)S(1)}, u32[]{:S(2)}, u32[]{:S(2)}) %collective-permute-start.3) | collective-permute-done | bytes 139296 | tf_op jit(solution)/shard_map/ppermute | solution.py:359
  15.3 1.5 %collective-permute-done.4.refs_1_ = bf16[2,272,128]{2,1,0:T(8,128)(2,1)S(1)} collective-permute-done((bf16[2,272,128]{2,1,0:T(8,128)(2,1)S(1)}, bf16[2,272,128]{2,1,0:T(8,128)(2,1)S(1)}, u32[]{:S(2)}, u32[]{:S(2)}) %collective-permute-start.4) | collective-permute-done | bytes 139296 | tf_op jit(solution)/shard_map/ppermute | solution.py:359
  16.8 0.0 collective-permute-done.5.refs_2_
  16.8 0.1 shard_map.80
  16.9 1.6 %collective-permute-start.6 = (bf16[272,128]{1,0:T(8,128)(2,1)S(1)}, bf16[272,128]{1,0:T(8,128)(2,1)S(1)}, u32[]{:S(2)}, u32[]{:S(2)}) collective-permute-start(bf16[272,128]{1,0:T(8,128)(2,1)S(1)} %get-tuple-element.66), channel_id=1, source_target_pairs={{0,8},{4,12},{8,16},{12,20},{16,24},{20,28},{24,0},{28,4},{2,6},{6... | collective-permute-start | bytes 208904 | tf_op jit(solution)/shard_map/ppermute | solution.py:361
  18.6 4.5 %collective-permute-start.7 = (bf16[272,128]{1,0:T(8,128)(2,1)S(1)}, bf16[272,128]{1,0:T(8,128)(2,1)S(1)}, u32[]{:S(2)}, u32[]{:S(2)}) collective-permute-start(bf16[272,128]{1,0:T(8,128)(2,1)S(1)} %get-tuple-element.67), channel_id=1, source_target_pairs={{0,16},{4,20},{8,24},{12,28},{16,0},{20,4},{24,8},{28,12},{1,17},{... | collective-permute-start | bytes 208904 | tf_op jit(solution)/shard_map/ppermute | solution.py:361
  23.1 3.3 %collective-permute-start.8 = (bf16[272,128]{1,0:T(8,128)(2,1)S(1)}, bf16[272,128]{1,0:T(8,128)(2,1)S(1)}, u32[]{:S(2)}, u32[]{:S(2)}) collective-permute-start(bf16[272,128]{1,0:T(8,128)(2,1)S(1)} %get-tuple-element.68), channel_id=1, source_target_pairs={{0,24},{4,28},{8,0},{12,4},{16,8},{20,12},{24,16},{28,20},{1,25},{... | collective-permute-start | bytes 208904 | tf_op jit(solution)/shard_map/ppermute | solution.py:361
  26.3 0.0 collective-permute-done.6.refs_1_
  26.3 0.0 collective-permute-done.7.refs_2_
  26.4 2.9 %collective-permute-done.8.refs_3_ = bf16[272,128]{1,0:T(8,128)(2,1)S(1)} collective-permute-done((bf16[272,128]{1,0:T(8,128)(2,1)S(1)}, bf16[272,128]{1,0:T(8,128)(2,1)S(1)}, u32[]{:S(2)}, u32[]{:S(2)}) %collective-permute-start.8) | collective-permute-done | bytes 69664 | tf_op jit(solution)/shard_map/ppermute | solution.py:361
  29.3 0.0 collective-permute-done.1.received
  29.3 1.3 %shard_map.81 = (bf16[1,128,4096]{2,1,0:T(8,128)(2,1)}, s32[1]{0:T(128)S(4)}, f32[1,33024]{1,0:T(1,128)}) custom-call(bf16[128,96]{1,0:T(8,128)(2,1)S(1)} %get-tuple-element.52.scatter, bf16[96,4096]{1,0:T(8,128)(2,1)S(1)} %collective-permute-done.1.received, f32[128,4096]{1,0:T(8,128)S(1)} %get-tuple-element.54.addend, s32[1]{0:T(128)S(4)} %get-tuple-element.55.more, ...), custom_call_target="tpu_custom_call" | custom-call | flops 1048576 | bytes 65536 | tf_op jit(solution)/shard_map/pallas_call | solution.py:212
  (1 shorter events, 0.0 us)
Async XLA Ops:
  4.4 24.8 %collective-permute-start.1 = (bf16[96,4096]{1,0:T(8,128)(2,1)S(1)}, bf16[96,4096]{1,0:T(8,128)(2,1)S(1)}, u32[]{:S(2)}, u32[]{:S(2)}) collective-permute-start(bf16[96,4096]{1,0:T(8,128)(2,1)S(1)} %get-tuple-element.53), channel_id=1, source_target_pairs={{1,0},{0,1},{3,2},{2,3},{5,4},{4,5},{7,6},{6,7},{9,8},{8,9},{11,10... | collective-permute-start | bytes 2359304 | tf_op jit(solution)/shard_map/ppermute | solution.py:395
  8.0 2.0 %collective-permute-start.2 = (bf16[8,272,128]{2,1,0:T(8,128)(2,1)S(1)}, bf16[8,272,128]{2,1,0:T(8,128)(2,1)S(1)}, u32[]{:S(2)}, u32[]{:S(2)}) collective-permute-start(bf16[8,272,128]{2,1,0:T(8,128)(2,1)S(1)} %get-tuple-element.60), channel_id=1, source_target_pairs={{0,2},{2,0},{4,6},{6,4},{8,10},{10,8},{12,14},{14,12},{16,18},{18,... | collective-permute-start | bytes 1671176 | tf_op jit(solution)/shard_map/ppermute | solution.py:375
  10.2 5.1 %collective-permute-start.3 = (bf16[2,272,128]{2,1,0:T(8,128)(2,1)S(1)}, bf16[2,272,128]{2,1,0:T(8,128)(2,1)S(1)}, u32[]{:S(2)}, u32[]{:S(2)}) collective-permute-start(bf16[2,272,128]{2,1,0:T(8,128)(2,1)S(1)} %get-tuple-element.62), channel_id=1, source_target_pairs={{2,10},{6,14},{10,18},{14,22},{18,26},{22,30},{26,2},{30,6},{0,4},... | collective-permute-start | bytes 417800 | tf_op jit(solution)/shard_map/ppermute | solution.py:359
  11.7 5.1 %collective-permute-start.4 = (bf16[2,272,128]{2,1,0:T(8,128)(2,1)S(1)}, bf16[2,272,128]{2,1,0:T(8,128)(2,1)S(1)}, u32[]{:S(2)}, u32[]{:S(2)}) collective-permute-start(bf16[2,272,128]{2,1,0:T(8,128)(2,1)S(1)} %get-tuple-element.63), channel_id=1, source_target_pairs={{2,18},{6,22},{10,26},{14,30},{18,2},{22,6},{26,10},{30,14},{0,4},... | collective-permute-start | bytes 417800 | tf_op jit(solution)/shard_map/ppermute | solution.py:359
  12.3 4.6 %collective-permute-start.5 = (bf16[2,272,128]{2,1,0:T(8,128)(2,1)S(1)}, bf16[2,272,128]{2,1,0:T(8,128)(2,1)S(1)}, u32[]{:S(2)}, u32[]{:S(2)}) collective-permute-start(bf16[2,272,128]{2,1,0:T(8,128)(2,1)S(1)} %get-tuple-element.64), channel_id=1, source_target_pairs={{2,26},{6,30},{10,2},{14,6},{18,10},{22,14},{26,18},{30,22},{3,27}... | collective-permute-start | bytes 417800 | tf_op jit(solution)/shard_map/ppermute | solution.py:359
  16.9 9.4 %collective-permute-start.6 = (bf16[272,128]{1,0:T(8,128)(2,1)S(1)}, bf16[272,128]{1,0:T(8,128)(2,1)S(1)}, u32[]{:S(2)}, u32[]{:S(2)}) collective-permute-start(bf16[272,128]{1,0:T(8,128)(2,1)S(1)} %get-tuple-element.66), channel_id=1, source_target_pairs={{0,8},{4,12},{8,16},{12,20},{16,24},{20,28},{24,0},{28,4},{2,6},{6... | collective-permute-start | bytes 208904 | tf_op jit(solution)/shard_map/ppermute | solution.py:361
  18.6 7.8 %collective-permute-start.7 = (bf16[272,128]{1,0:T(8,128)(2,1)S(1)}, bf16[272,128]{1,0:T(8,128)(2,1)S(1)}, u32[]{:S(2)}, u32[]{:S(2)}) collective-permute-start(bf16[272,128]{1,0:T(8,128)(2,1)S(1)} %get-tuple-element.67), channel_id=1, source_target_pairs={{0,16},{4,20},{8,24},{12,28},{16,0},{20,4},{24,8},{28,12},{1,17},{... | collective-permute-start | bytes 208904 | tf_op jit(solution)/shard_map/ppermute | solution.py:361
  23.1 6.2 %collective-permute-start.8 = (bf16[272,128]{1,0:T(8,128)(2,1)S(1)}, bf16[272,128]{1,0:T(8,128)(2,1)S(1)}, u32[]{:S(2)}, u32[]{:S(2)}) collective-permute-start(bf16[272,128]{1,0:T(8,128)(2,1)S(1)} %get-tuple-element.68), channel_id=1, source_target_pairs={{0,24},{4,28},{8,0},{12,4},{16,8},{20,12},{24,16},{28,20},{1,25},{... | collective-permute-start | bytes 208904 | tf_op jit(solution)/shard_map/ppermute | solution.py:361

commit v9 on v8

--- a/solution.py
+++ b/solution.py
@@ -257,84 +257,30 @@
     )(normed, masked, gain)
 
 
-def merge_kernel(keep, taken, hold, *give):
-    spot = lax.axis_index("dp")
-    even = spot % pair == 0
-    chip = spot // pair
-    mine, place = chip % 2, chip // 2
-    count = hold.shape[0]
-
-    def block(across, along):
-        at = jnp.where(even, across, along)
-        return keep[at] + taken[at].astype(f32)
-
-    for k in range(count):
-        hold[k] = block(2 * k + mine, 2 * place + k % 2)
-    for k in range(1, count):
-        for side in range(2):
-            across = min(2 * (k - 1) + side, count - 1)
-            at = 2 * lax.rem(place + k, count) + side
-            give[k - 1][side] = block(2 * across + 1 - mine, at).astype(bf16)
+def partner(chips, chip, step):
+    return chip ^ step if chips & (chips - 1) == 0 else (chip + step) % chips
+
+
+def merge_kernel(keep, taken, own, *parts):
+    chip = lax.axis_index("dp") // pair
+    chips = keep.shape[0]
+    own[...] = keep[chip] + taken[chip].astype(f32)
+    for k, part in enumerate(parts):
+        at = partner(chips, chip, k + 1)
+        part[...] = (keep[at] + taken[at].astype(f32)).astype(bf16)
 
 
 def merge_terms(keep, taken):
-    count = keep.shape[0] // 2
+    chips = keep.shape[0]
     return pl.pallas_call(
         merge_kernel,
         in_specs=[near, near],
-        out_specs=[near] * count,
-        out_shape=[jax.ShapeDtypeStruct((count,) + keep.shape[1:], f32)]
-        + [jax.ShapeDtypeStruct((2,) + keep.shape[1:], bf16)] * (count - 1),
+        out_specs=[near] * chips,
+        out_shape=[jax.ShapeDtypeStruct(keep.shape[1:], f32)]
+        + [jax.ShapeDtypeStruct(keep.shape[1:], bf16)] * (chips - 1),
         compiler_params=roomy,
         cost_estimate=small_cost,
     )(keep, taken)
-
-
-def split_kernel(hold, *refs):
-    count = hold.shape[0]
-    landed, own, parts = refs[: count - 1], refs[count - 1], refs[count:]
-    spot = lax.axis_index("dp")
-    chip = spot // pair
-    mine, place = chip % 2, chip // 2
-
-    @pl.when(spot % pair == 0)
-    def _():
-        sums = [hold[k] + landed[k // 2][k % 2].astype(f32) for k in range(count)]
-
-        def pick(at):
-            total = sums[0]
-            for k in range(1, count):
-                total = jnp.where(at == k, sums[k], total)
-            return total
-
-        own[...] = pick(place)
-        for k in range(1, count):
-            parts[k - 1][...] = pick(lax.rem(place + k, count)).astype(bf16)
-
-    @pl.when(spot % pair != 0)
-    def _():
-        total = hold[mine]
-        passed = hold[1 - mine]
-        for part in landed:
-            total += part[mine].astype(f32)
-            passed += part[1 - mine].astype(f32)
-        own[...] = total
-        parts[0][...] = passed.astype(bf16)
-        for part in parts[1:]:
-            part[...] = jnp.zeros_like(part)
-
-
-def split_terms(hold, landed):
-    count = hold.shape[0]
-    return pl.pallas_call(
-        split_kernel,
-        in_specs=[near] * count,
-        out_specs=[near] * count,
-        out_shape=[jax.ShapeDtypeStruct(hold.shape[1:], f32)]
-        + [jax.ShapeDtypeStruct(hold.shape[1:], bf16)] * (count - 1),
-        compiler_params=roomy,
-        cost_estimate=small_cost,
-    )(hold, *landed)
 
 
 def total_rows(factor, out, own, *landed):
@@ -347,18 +293,11 @@
 
 
 def plane_parts(owners, keep, taken):
-    quad = 2 * pair
-    shifts = range(quad, owners, quad)
-    even, odd = range(0, owners, pair), range(1, owners, pair)
-    across = [[(i, i ^ pair) for i in one] for one in (even, odd)]
-    along = [[[(i, (i + shift) % owners) for i in one] for shift in shifts] for one in (even, odd)]
-    hold, *give = merge_terms(keep, taken)
-    landed = []
-    for k, part in enumerate(give):
-        hops = along[1][k] + (across[0] if 2 * k < owners // quad else [])
-        landed.append(lax.ppermute(part, "dp", hops))
-    own, *parts = split_terms(hold, landed)
-    arrived = [lax.ppermute(part, "dp", along[0][k] + (across[1] if k == 0 else [])) for k, part in enumerate(parts)]
+    own, *parts = merge_terms(keep, taken)
+    arrived = []
+    for k, part in enumerate(parts):
+        hops = [(i, partner(owners // pair, i // pair, k + 1) * pair + i % pair) for i in range(owners)]
+        arrived.append(lax.ppermute(part, "dp", hops))
     return own, *arrived
 
 

time: 30.8 us -> 29.9 us (0.971)
  waiting for transfers between devices: 8.75 us -> 7.99 us
    ppermute x6 -> x7, waiting for transfers between devices: 6.8 us -> 6.04 us  [plane_parts(): arrived.append(lax.ppermute(part, 'dp', hops))]
    ppermute x6 -> x7, starting transfers between devices: 12.1 us -> 12.1 us  [plane_parts(): arrived.append(lax.ppermute(part, 'dp', hops))]
  transfers between devices with their start and end apart: 8 -> 9, of which waited for: 4 -> 3; matrix products, arithmetic and copies ran while one was open for 0% -> 0% of each run, Pallas kernels for 3% -> 2%
where the time goes in v9:
time: 29.9 us; the launch traced here: 29.7 us
  starting transfers between devices  15.2 us (51%)
  waiting for transfers between devices  7.99 us (27%)
  Pallas kernels  5.87 us (20%)
  between operations  0.68 us (2%)
    ppermute x7, starting transfers between devices, plane_parts(): arrived.append(lax.ppermute(part, 'dp', hops))  12.1 us
    ppermute x7, waiting for transfers between devices, plane_parts(): arrived.append(lax.ppermute(part, 'dp', hops))  6.04 us
    pallas_call x1, Pallas kernels, branch_rows(): pl.pallas_call(functools.partial(branch_kernel, low), in_specs=[pl.BlockS...  3.8 us
    ppermute x1, starting transfers between devices, shards(): landed = lax.ppermute(packed, 'section', hops)  3.01 us
    ppermute x1, waiting for transfers between devices, weight_owned(): taken = lax.ppermute(give, 'dp', [(i, i ^ 1) for i in range(owners)])  1.94 us
    pallas_call x1, Pallas kernels, receive(): pl.pallas_call(functools.partial(receive_kernel, target, first, factor),...  1.41 us
  transfers between devices with their start and end apart: 9, of which 3 were waited for; matrix products, arithmetic and copies ran while one was open for 0% of the time, Pallas kernels for 2%

profile of v9, /device:TPU:0, one launch (start us, length us, event | category | flops | bytes accessed | tf_op | source)
XLA Modules:
  0.0 29.7 jit_solution(9123727396308350506)
XLA Ops:
  0.6 3.8 %shard_map.77 = (bf16[96,4096]{1,0:T(8,128)(2,1)S(1)}, f32[128,4096]{1,0:T(8,128)S(1)}, bf16[128,96]{1,0:T(8,128)(2,1)S(1)}, s32[1]{0:T(128)S(4)}, bf16[128,4096...) custom-call(s32[8]{0:T(128)} %counts_far.1, bf16[1,128,4096]{2,1,0:T(8,128)(2,1)} %x_far.1, ...), custom_call_target="tpu_custom_call" | custom-call | flops 1048576 | bytes 65536 | tf_op jit(solution)/shard_map/pallas_call | solution.py:126
  4.4 3.0 %collective-permute-start.1 = (bf16[96,4096]{1,0:T(8,128)(2,1)S(1)}, bf16[96,4096]{1,0:T(8,128)(2,1)S(1)}, u32[]{:S(2)}, u32[]{:S(2)}) collective-permute-start(bf16[96,4096]{1,0:T(8,128)(2,1)S(1)} %get-tuple-element.53), channel_id=1, source_target_pairs={{1,0},{0,1},{3,2},{2,3},{5,4},{4,5},{7,6},{6,7},{9,8},{8,9},{11,10... | collective-permute-start | bytes 2359304 | tf_op jit(solution)/shard_map/ppermute | solution.py:334
  7.4 0.6 %shard_map.78 = (f32[8,272,128]{2,1,0:T(8,128)S(1)}, bf16[8,272,128]{2,1,0:T(8,128)(2,1)S(1)}) custom-call(bf16[128,4096]{1,0:T(8,128)(2,1)S(1)} %get-tuple-element.56.normed, bf16[128,128]{1,0:T(8,128)(2,1)S(1)} %get-tuple-element.57.masked, f32[1,4096]{1,0:T(1,128)S(1)} %get-tuple-element.58.gain), custom_call_target="tpu_custom_call" | custom-call | flops 1048576 | bytes 65536 | tf_op jit(solution)/shard_map/pallas_call | solution.py:249
  8.0 0.1 collective-permute-start.2
  8.1 1.9 %collective-permute-done.2.taken = bf16[8,272,128]{2,1,0:T(8,128)(2,1)S(1)} collective-permute-done((bf16[8,272,128]{2,1,0:T(8,128)(2,1)S(1)}, bf16[8,272,128]{2,1,0:T(8,128)(2,1)S(1)}, u32[]{:S(2)}, u32[]{:S(2)}) %collective-permute-start.2) | collective-permute-done | bytes 557088 | tf_op jit(solution)/shard_map/ppermute | solution.py:314
  10.0 0.1 shard_map.79
  10.1 1.6 %collective-permute-start.3 = (bf16[272,128]{1,0:T(8,128)(2,1)S(1)}, bf16[272,128]{1,0:T(8,128)(2,1)S(1)}, u32[]{:S(2)}, u32[]{:S(2)}) collective-permute-start(bf16[272,128]{1,0:T(8,128)(2,1)S(1)} %get-tuple-element.62), channel_id=1, source_target_pairs={{0,4},{2,6},{4,0},{6,2},{8,12},{10,14},{12,8},{14,10},{16,20},{18,... | collective-permute-start | bytes 208904 | tf_op jit(solution)/shard_map/ppermute | solution.py:300
  11.7 1.6 %collective-permute-start.4 = (bf16[272,128]{1,0:T(8,128)(2,1)S(1)}, bf16[272,128]{1,0:T(8,128)(2,1)S(1)}, u32[]{:S(2)}, u32[]{:S(2)}) collective-permute-start(bf16[272,128]{1,0:T(8,128)(2,1)S(1)} %get-tuple-element.63), channel_id=1, source_target_pairs={{0,8},{2,10},{4,12},{6,14},{8,0},{10,2},{12,4},{14,6},{16,24},{18,... | collective-permute-start | bytes 208904 | tf_op jit(solution)/shard_map/ppermute | solution.py:300
  13.3 0.4 %collective-permute-start.5 = (bf16[272,128]{1,0:T(8,128)(2,1)S(1)}, bf16[272,128]{1,0:T(8,128)(2,1)S(1)}, u32[]{:S(2)}, u32[]{:S(2)}) collective-permute-start(bf16[272,128]{1,0:T(8,128)(2,1)S(1)} %get-tuple-element.64), channel_id=1, source_target_pairs={{0,12},{2,14},{4,8},{6,10},{8,4},{10,6},{12,0},{14,2},{16,28},{18,... | collective-permute-start | bytes 208904 | tf_op jit(solution)/shard_map/ppermute | solution.py:300
  13.7 2.6 %collective-permute-start.6 = (bf16[272,128]{1,0:T(8,128)(2,1)S(1)}, bf16[272,128]{1,0:T(8,128)(2,1)S(1)}, u32[]{:S(2)}, u32[]{:S(2)}) collective-permute-start(bf16[272,128]{1,0:T(8,128)(2,1)S(1)} %get-tuple-element.65), channel_id=1, source_target_pairs={{0,16},{2,18},{4,20},{6,22},{8,24},{10,26},{12,28},{14,30},{16,0},... | collective-permute-start | bytes 208904 | tf_op jit(solution)/shard_map/ppermute | solution.py:300
  16.3 0.0 collective-permute-done.3.refs_1_
  16.3 1.8 %collective-permute-start.7 = (bf16[272,128]{1,0:T(8,128)(2,1)S(1)}, bf16[272,128]{1,0:T(8,128)(2,1)S(1)}, u32[]{:S(2)}, u32[]{:S(2)}) collective-permute-start(bf16[272,128]{1,0:T(8,128)(2,1)S(1)} %get-tuple-element.66), channel_id=1, source_target_pairs={{0,20},{2,22},{4,16},{6,18},{8,28},{10,30},{12,24},{14,26},{16,4},... | collective-permute-start | bytes 208904 | tf_op jit(solution)/shard_map/ppermute | solution.py:300
  18.1 0.0 collective-permute-done.4.refs_2_
  18.1 3.1 %collective-permute-start.8 = (bf16[272,128]{1,0:T(8,128)(2,1)S(1)}, bf16[272,128]{1,0:T(8,128)(2,1)S(1)}, u32[]{:S(2)}, u32[]{:S(2)}) collective-permute-start(bf16[272,128]{1,0:T(8,128)(2,1)S(1)} %get-tuple-element.67), channel_id=1, source_target_pairs={{0,24},{2,26},{4,28},{6,30},{8,16},{10,18},{12,20},{14,22},{16,8},... | collective-permute-start | bytes 208904 | tf_op jit(solution)/shard_map/ppermute | solution.py:300
  21.2 0.0 collective-permute-done.5.refs_3_
  21.2 1.1 %collective-permute-start.9 = (bf16[272,128]{1,0:T(8,128)(2,1)S(1)}, bf16[272,128]{1,0:T(8,128)(2,1)S(1)}, u32[]{:S(2)}, u32[]{:S(2)}) collective-permute-start(bf16[272,128]{1,0:T(8,128)(2,1)S(1)} %get-tuple-element.68), channel_id=1, source_target_pairs={{0,28},{2,30},{4,24},{6,26},{8,20},{10,22},{12,16},{14,18},{16,12}... | collective-permute-start | bytes 208904 | tf_op jit(solution)/shard_map/ppermute | solution.py:300
  22.3 0.0 collective-permute-done.6.refs_4_
  22.3 4.9 %collective-permute-done.7.refs_5_ = bf16[272,128]{1,0:T(8,128)(2,1)S(1)} collective-permute-done((bf16[272,128]{1,0:T(8,128)(2,1)S(1)}, bf16[272,128]{1,0:T(8,128)(2,1)S(1)}, u32[]{:S(2)}, u32[]{:S(2)}) %collective-permute-start.7) | collective-permute-done | bytes 69664 | tf_op jit(solution)/shard_map/ppermute | solution.py:300
  27.2 0.0 collective-permute-done.8.refs_6_
  27.2 1.1 %collective-permute-done.9.refs_7_ = bf16[272,128]{1,0:T(8,128)(2,1)S(1)} collective-permute-done((bf16[272,128]{1,0:T(8,128)(2,1)S(1)}, bf16[272,128]{1,0:T(8,128)(2,1)S(1)}, u32[]{:S(2)}, u32[]{:S(2)}) %collective-permute-start.9) | collective-permute-done | bytes 69664 | tf_op jit(solution)/shard_map/ppermute | solution.py:300
  28.3 0.0 collective-permute-done.1.received
  28.3 1.4 %shard_map.80 = (bf16[1,128,4096]{2,1,0:T(8,128)(2,1)}, s32[1]{0:T(128)S(4)}, f32[1,33024]{1,0:T(1,128)}) custom-call(bf16[128,96]{1,0:T(8,128)(2,1)S(1)} %get-tuple-element.52.scatter, bf16[96,4096]{1,0:T(8,128)(2,1)S(1)} %collective-permute-done.1.received, f32[128,4096]{1,0:T(8,128)S(1)} %get-tuple-element.54.addend, s32[1]{0:T(128)S(4)} %get-tuple-element.55.more, ...), custom_call_target="tpu_custom_call" | custom-call | flops 1048576 | bytes 65536 | tf_op jit(solution)/shard_map/pallas_call | solution.py:212
  (1 shorter events, 0.0 us)
Async XLA Ops:
  4.4 23.9 %collective-permute-start.1 = (bf16[96,4096]{1,0:T(8,128)(2,1)S(1)}, bf16[96,4096]{1,0:T(8,128)(2,1)S(1)}, u32[]{:S(2)}, u32[]{:S(2)}) collective-permute-start(bf16[96,4096]{1,0:T(8,128)(2,1)S(1)} %get-tuple-element.53), channel_id=1, source_target_pairs={{1,0},{0,1},{3,2},{2,3},{5,4},{4,5},{7,6},{6,7},{9,8},{8,9},{11,10... | collective-permute-start | bytes 2359304 | tf_op jit(solution)/shard_map/ppermute | solution.py:334
  8.0 2.0 %collective-permute-start.2 = (bf16[8,272,128]{2,1,0:T(8,128)(2,1)S(1)}, bf16[8,272,128]{2,1,0:T(8,128)(2,1)S(1)}, u32[]{:S(2)}, u32[]{:S(2)}) collective-permute-start(bf16[8,272,128]{2,1,0:T(8,128)(2,1)S(1)} %get-tuple-element.60), channel_id=1, source_target_pairs={{0,2},{2,0},{4,6},{6,4},{8,10},{10,8},{12,14},{14,12},{16,18},{18,... | collective-permute-start | bytes 1671176 | tf_op jit(solution)/shard_map/ppermute | solution.py:314
  10.1 6.1 %collective-permute-start.3 = (bf16[272,128]{1,0:T(8,128)(2,1)S(1)}, bf16[272,128]{1,0:T(8,128)(2,1)S(1)}, u32[]{:S(2)}, u32[]{:S(2)}) collective-permute-start(bf16[272,128]{1,0:T(8,128)(2,1)S(1)} %get-tuple-element.62), channel_id=1, source_target_pairs={{0,4},{2,6},{4,0},{6,2},{8,12},{10,14},{12,8},{14,10},{16,20},{18,... | collective-permute-start | bytes 208904 | tf_op jit(solution)/shard_map/ppermute | solution.py:300
  11.7 6.3 %collective-permute-start.4 = (bf16[272,128]{1,0:T(8,128)(2,1)S(1)}, bf16[272,128]{1,0:T(8,128)(2,1)S(1)}, u32[]{:S(2)}, u32[]{:S(2)}) collective-permute-start(bf16[272,128]{1,0:T(8,128)(2,1)S(1)} %get-tuple-element.63), channel_id=1, source_target_pairs={{0,8},{2,10},{4,12},{6,14},{8,0},{10,2},{12,4},{14,6},{16,24},{18,... | collective-permute-start | bytes 208904 | tf_op jit(solution)/shard_map/ppermute | solution.py:300
  13.3 7.9 %collective-permute-start.5 = (bf16[272,128]{1,0:T(8,128)(2,1)S(1)}, bf16[272,128]{1,0:T(8,128)(2,1)S(1)}, u32[]{:S(2)}, u32[]{:S(2)}) collective-permute-start(bf16[272,128]{1,0:T(8,128)(2,1)S(1)} %get-tuple-element.64), channel_id=1, source_target_pairs={{0,12},{2,14},{4,8},{6,10},{8,4},{10,6},{12,0},{14,2},{16,28},{18,... | collective-permute-start | bytes 208904 | tf_op jit(solution)/shard_map/ppermute | solution.py:300
  13.7 8.6 %collective-permute-start.6 = (bf16[272,128]{1,0:T(8,128)(2,1)S(1)}, bf16[272,128]{1,0:T(8,128)(2,1)S(1)}, u32[]{:S(2)}, u32[]{:S(2)}) collective-permute-start(bf16[272,128]{1,0:T(8,128)(2,1)S(1)} %get-tuple-element.65), channel_id=1, source_target_pairs={{0,16},{2,18},{4,20},{6,22},{8,24},{10,26},{12,28},{14,30},{16,0},... | collective-permute-start | bytes 208904 | tf_op jit(solution)/shard_map/ppermute | solution.py:300
  16.3 10.9 %collective-permute-start.7 = (bf16[272,128]{1,0:T(8,128)(2,1)S(1)}, bf16[272,128]{1,0:T(8,128)(2,1)S(1)}, u32[]{:S(2)}, u32[]{:S(2)}) collective-permute-start(bf16[272,128]{1,0:T(8,128)(2,1)S(1)} %get-tuple-element.66), channel_id=1, source_target_pairs={{0,20},{2,22},{4,16},{6,18},{8,28},{10,30},{12,24},{14,26},{16,4},... | collective-permute-start | bytes 208904 | tf_op jit(solution)/shard_map/ppermute | solution.py:300
  18.1 9.1 %collective-permute-start.8 = (bf16[272,128]{1,0:T(8,128)(2,1)S(1)}, bf16[272,128]{1,0:T(8,128)(2,1)S(1)}, u32[]{:S(2)}, u32[]{:S(2)}) collective-permute-start(bf16[272,128]{1,0:T(8,128)(2,1)S(1)} %get-tuple-element.67), channel_id=1, source_target_pairs={{0,24},{2,26},{4,28},{6,30},{8,16},{10,18},{12,20},{14,22},{16,8},... | collective-permute-start | bytes 208904 | tf_op jit(solution)/shard_map/ppermute | solution.py:300
  21.2 7.1 %collective-permute-start.9 = (bf16[272,128]{1,0:T(8,128)(2,1)S(1)}, bf16[272,128]{1,0:T(8,128)(2,1)S(1)}, u32[]{:S(2)}, u32[]{:S(2)}) collective-permute-start(bf16[272,128]{1,0:T(8,128)(2,1)S(1)} %get-tuple-element.68), channel_id=1, source_target_pairs={{0,28},{2,30},{4,24},{6,26},{8,20},{10,22},{12,16},{14,18},{16,12}... | collective-permute-start | bytes 208904 | tf_op jit(solution)/shard_map/ppermute | solution.py:300

commit v10 on v9

--- a/solution.py
+++ b/solution.py
@@ -257,30 +257,46 @@
     )(normed, masked, gain)
 
 
-def partner(chips, chip, step):
-    return chip ^ step if chips & (chips - 1) == 0 else (chip + step) % chips
-
-
-def merge_kernel(keep, taken, own, *parts):
+def merge_kernel(offsets, keep, taken, *halves):
     chip = lax.axis_index("dp") // pair
-    chips = keep.shape[0]
-    own[...] = keep[chip] + taken[chip].astype(f32)
+    mine, place = chip % 2, chip // 2
+    count = keep.shape[0] // 2
+    for part, (hold, give) in zip(offsets, (halves[:2], halves[2:])):
+        for k, offset in enumerate(part):
+            at = 2 * lax.rem(place + offset, count)
+            hold[k] = keep[at + mine] + taken[at + mine].astype(f32)
+            give[k] = (keep[at + 1 - mine] + taken[at + 1 - mine].astype(f32)).astype(bf16)
+
+
+def merge_terms(offsets, keep, taken):
+    outs = []
+    for part in offsets:
+        block = (len(part),) + keep.shape[1:]
+        outs += [jax.ShapeDtypeStruct(block, f32), jax.ShapeDtypeStruct(block, bf16)]
+    return pl.pallas_call(
+        functools.partial(merge_kernel, offsets),
+        in_specs=[near, near],
+        out_specs=[near] * len(outs),
+        out_shape=outs,
+        compiler_params=roomy,
+        cost_estimate=small_cost,
+    )(keep, taken)
+
+
+def split_kernel(hold, taken, *parts):
     for k, part in enumerate(parts):
-        at = partner(chips, chip, k + 1)
-        part[...] = (keep[at] + taken[at].astype(f32)).astype(bf16)
-
-
-def merge_terms(keep, taken):
-    chips = keep.shape[0]
-    return pl.pallas_call(
-        merge_kernel,
+        part[...] = (hold[k] + taken[k].astype(f32)).astype(part.dtype)
+
+
+def split_terms(part, hold, taken):
+    return pl.pallas_call(
+        split_kernel,
         in_specs=[near, near],
-        out_specs=[near] * chips,
-        out_shape=[jax.ShapeDtypeStruct(keep.shape[1:], f32)]
-        + [jax.ShapeDtypeStruct(keep.shape[1:], bf16)] * (chips - 1),
-        compiler_params=roomy,
-        cost_estimate=small_cost,
-    )(keep, taken)
+        out_specs=[near] * len(part),
+        out_shape=[jax.ShapeDtypeStruct(hold.shape[1:], bf16 if offset else f32) for offset in part],
+        compiler_params=roomy,
+        cost_estimate=small_cost,
+    )(hold, taken)
 
 
 def total_rows(factor, out, own, *landed):
@@ -293,11 +309,18 @@
 
 
 def plane_parts(owners, keep, taken):
-    own, *parts = merge_terms(keep, taken)
+    quad = 2 * pair
+    count = owners // quad
+    order = [0, count // 2, *(k for k in range(1, count) if k != count // 2)]
+    offsets = (order[:2], order[2:])
+    hold, give, hold_next, give_next = merge_terms(offsets, keep, taken)
+    near_by = [(i, i ^ pair) for i in range(owners)]
+    across = [lax.ppermute(part, "dp", near_by) for part in (give, give_next)]
+    own, *parts = split_terms(offsets[0], hold, across[0])
+    parts += split_terms(offsets[1], hold_next, across[1])
     arrived = []
-    for k, part in enumerate(parts):
-        hops = [(i, partner(owners // pair, i // pair, k + 1) * pair + i % pair) for i in range(owners)]
-        arrived.append(lax.ppermute(part, "dp", hops))
+    for offset, part in zip(order[1:], parts):
+        arrived.append(lax.ppermute(part, "dp", [(i, (i + quad * offset) % owners) for i in range(owners)]))
     return own, *arrived
 
 

time: 29.9 us -> 27.6 us (0.923)
  starting transfers between devices: 15.2 us -> 11.7 us
  waiting for transfers between devices: 7.99 us -> 9.24 us
    ppermute x7 -> x5, starting transfers between devices: 12.1 us -> 8.61 us  [the longest x3 6.52 us: plane_parts(): lax.ppermute(part, 'dp', [(i, (i + quad * offset) % owners) for i in rang...]
    ppermute x7 -> x5, waiting for transfers between devices: 6.04 us -> 7.3 us  [the longest x2 4.49 us: plane_parts(): across = [lax.ppermute(part, 'dp', near_by) for part in (give, give_next)]]
  transfers between devices with their start and end apart: 9 -> 7, of which waited for: 3 -> 4; matrix products, arithmetic and copies ran while one was open for 0% -> 0% of each run, Pallas kernels for 2% -> 3%
where the time goes in v10:
time: 27.6 us; the launch traced here: 27.5 us
  starting transfers between devices  11.7 us (42%)
  waiting for transfers between devices  9.24 us (33%)
  Pallas kernels  5.87 us (21%)
  between operations  0.68 us (2%)
    ppermute x3, starting transfers between devices, plane_parts(): lax.ppermute(part, 'dp', [(i, (i + quad * offset) % owners) for i in rang...  6.52 us
    ppermute x2, waiting for transfers between devices, plane_parts(): across = [lax.ppermute(part, 'dp', near_by) for part in (give, give_next)]  4.49 us
    pallas_call x1, Pallas kernels, branch_rows(): pl.pallas_call(functools.partial(branch_kernel, low), in_specs=[pl.BlockS...  3.8 us
    ppermute x1, starting transfers between devices, shards(): landed = lax.ppermute(packed, 'section', hops)  3.01 us
    ppermute x3, waiting for transfers between devices, plane_parts(): lax.ppermute(part, 'dp', [(i, (i + quad * offset) % owners) for i in rang...  2.81 us
    ppermute x2, starting transfers between devices, plane_parts(): across = [lax.ppermute(part, 'dp', near_by) for part in (give, give_next)]  2.09 us
    ppermute x1, waiting for transfers between devices, weight_owned(): taken = lax.ppermute(give, 'dp', [(i, i ^ 1) for i in range(owners)])  1.94 us
    pallas_call x1, Pallas kernels, receive(): pl.pallas_call(functools.partial(receive_kernel, target, first, factor),...  1.35 us
  transfers between devices with their start and end apart: 7, of which 4 were waited for; matrix products, arithmetic and copies ran while one was open for 0% of the time, Pallas kernels for 3%

profile of v10, /device:TPU:0, one launch (start us, length us, event | category | flops | bytes accessed | tf_op | source)
XLA Modules:
  0.0 27.5 jit_solution(8383541888730927405)
XLA Ops:
  0.6 3.8 %shard_map.77 = (bf16[96,4096]{1,0:T(8,128)(2,1)S(1)}, f32[128,4096]{1,0:T(8,128)S(1)}, bf16[128,96]{1,0:T(8,128)(2,1)S(1)}, s32[1]{0:T(128)S(4)}, bf16[128,4096...) custom-call(s32[8]{0:T(128)} %counts_far.1, bf16[1,128,4096]{2,1,0:T(8,128)(2,1)} %x_far.1, ...), custom_call_target="tpu_custom_call" | custom-call | flops 1048576 | bytes 65536 | tf_op jit(solution)/shard_map/pallas_call | solution.py:126
  4.4 3.0 %collective-permute-start.1 = (bf16[96,4096]{1,0:T(8,128)(2,1)S(1)}, bf16[96,4096]{1,0:T(8,128)(2,1)S(1)}, u32[]{:S(2)}, u32[]{:S(2)}) collective-permute-start(bf16[96,4096]{1,0:T(8,128)(2,1)S(1)} %get-tuple-element.53), channel_id=1, source_target_pairs={{1,0},{0,1},{3,2},{2,3},{5,4},{4,5},{7,6},{6,7},{9,8},{8,9},{11,10... | collective-permute-start | bytes 2359304 | tf_op jit(solution)/shard_map/ppermute | solution.py:357
  7.4 0.6 %shard_map.78 = (f32[8,272,128]{2,1,0:T(8,128)S(1)}, bf16[8,272,128]{2,1,0:T(8,128)(2,1)S(1)}) custom-call(bf16[128,4096]{1,0:T(8,128)(2,1)S(1)} %get-tuple-element.56.normed, bf16[128,128]{1,0:T(8,128)(2,1)S(1)} %get-tuple-element.57.masked, f32[1,4096]{1,0:T(1,128)S(1)} %get-tuple-element.58.gain), custom_call_target="tpu_custom_call" | custom-call | flops 1048576 | bytes 65536 | tf_op jit(solution)/shard_map/pallas_call | solution.py:249
  8.0 0.1 collective-permute-start.2
  8.1 1.9 %collective-permute-done.2.taken = bf16[8,272,128]{2,1,0:T(8,128)(2,1)S(1)} collective-permute-done((bf16[8,272,128]{2,1,0:T(8,128)(2,1)S(1)}, bf16[8,272,128]{2,1,0:T(8,128)(2,1)S(1)}, u32[]{:S(2)}, u32[]{:S(2)}) %collective-permute-start.2) | collective-permute-done | bytes 557088 | tf_op jit(solution)/shard_map/ppermute | solution.py:337
  10.0 0.1 shard_map.79
  10.1 1.6 %collective-permute-start.3 = (bf16[2,272,128]{2,1,0:T(8,128)(2,1)S(1)}, bf16[2,272,128]{2,1,0:T(8,128)(2,1)S(1)}, u32[]{:S(2)}, u32[]{:S(2)}) collective-permute-start(bf16[2,272,128]{2,1,0:T(8,128)(2,1)S(1)} %get-tuple-element.62), channel_id=1, source_target_pairs={{0,4},{2,6},{4,0},{6,2},{8,12},{10,14},{12,8},{14,10},{16,20},{18,... | collective-permute-start | bytes 417800 | tf_op jit(solution)/shard_map/ppermute | solution.py:318
  11.7 0.5 %collective-permute-start.5 = (bf16[2,272,128]{2,1,0:T(8,128)(2,1)S(1)}, bf16[2,272,128]{2,1,0:T(8,128)(2,1)S(1)}, u32[]{:S(2)}, u32[]{:S(2)}) collective-permute-start(bf16[2,272,128]{2,1,0:T(8,128)(2,1)S(1)} %get-tuple-element.66), channel_id=1, source_target_pairs={{0,4},{2,6},{4,0},{6,2},{8,12},{10,14},{12,8},{14,10},{16,20},{18,... | collective-permute-start | bytes 417800 | tf_op jit(solution)/shard_map/ppermute | solution.py:318
  12.2 4.5 %collective-permute-done.3.taken = bf16[2,272,128]{2,1,0:T(8,128)(2,1)S(1)} collective-permute-done((bf16[2,272,128]{2,1,0:T(8,128)(2,1)S(1)}, bf16[2,272,128]{2,1,0:T(8,128)(2,1)S(1)}, u32[]{:S(2)}, u32[]{:S(2)}) %collective-permute-start.3) | collective-permute-done | bytes 139296 | tf_op jit(solution)/shard_map/ppermute | solution.py:318
  16.8 2.6 %collective-permute-start.4 = (bf16[272,128]{1,0:T(8,128)(2,1)S(1)}, bf16[272,128]{1,0:T(8,128)(2,1)S(1)}, u32[]{:S(2)}, u32[]{:S(2)}) collective-permute-start(bf16[272,128]{1,0:T(8,128)(2,1)S(1)} %get-tuple-element.64), channel_id=1, source_target_pairs={{0,16},{2,18},{4,20},{6,22},{8,24},{10,26},{12,28},{14,30},{16,0},... | collective-permute-start | bytes 208904 | tf_op jit(solution)/shard_map/ppermute | solution.py:323
  19.4 0.0 collective-permute-done.5.taken
  19.4 1.6 %collective-permute-start.6 = (bf16[272,128]{1,0:T(8,128)(2,1)S(1)}, bf16[272,128]{1,0:T(8,128)(2,1)S(1)}, u32[]{:S(2)}, u32[]{:S(2)}) collective-permute-start(bf16[272,128]{1,0:T(8,128)(2,1)S(1)} %get-tuple-element.67), channel_id=1, source_target_pairs={{0,8},{2,10},{4,12},{6,14},{8,16},{10,18},{12,20},{14,22},{16,24},... | collective-permute-start | bytes 208904 | tf_op jit(solution)/shard_map/ppermute | solution.py:323
  21.1 2.2 %collective-permute-start.7 = (bf16[272,128]{1,0:T(8,128)(2,1)S(1)}, bf16[272,128]{1,0:T(8,128)(2,1)S(1)}, u32[]{:S(2)}, u32[]{:S(2)}) collective-permute-start(bf16[272,128]{1,0:T(8,128)(2,1)S(1)} %get-tuple-element.68), channel_id=1, source_target_pairs={{0,24},{2,26},{4,28},{6,30},{8,0},{10,2},{12,4},{14,6},{16,8},{18,... | collective-permute-start | bytes 208904 | tf_op jit(solution)/shard_map/ppermute | solution.py:323
  23.3 0.0 collective-permute-done.4.refs_1_
  23.3 2.5 %collective-permute-done.6.refs_2_ = bf16[272,128]{1,0:T(8,128)(2,1)S(1)} collective-permute-done((bf16[272,128]{1,0:T(8,128)(2,1)S(1)}, bf16[272,128]{1,0:T(8,128)(2,1)S(1)}, u32[]{:S(2)}, u32[]{:S(2)}) %collective-permute-start.6) | collective-permute-done | bytes 69664 | tf_op jit(solution)/shard_map/ppermute | solution.py:323
  25.8 0.3 %collective-permute-done.7.refs_3_ = bf16[272,128]{1,0:T(8,128)(2,1)S(1)} collective-permute-done((bf16[272,128]{1,0:T(8,128)(2,1)S(1)}, bf16[272,128]{1,0:T(8,128)(2,1)S(1)}, u32[]{:S(2)}, u32[]{:S(2)}) %collective-permute-start.7) | collective-permute-done | bytes 69664 | tf_op jit(solution)/shard_map/ppermute | solution.py:323
  26.1 0.0 collective-permute-done.1.received
  26.1 1.3 %shard_map.82 = (bf16[1,128,4096]{2,1,0:T(8,128)(2,1)}, s32[1]{0:T(128)S(4)}, f32[1,33024]{1,0:T(1,128)}) custom-call(bf16[128,96]{1,0:T(8,128)(2,1)S(1)} %get-tuple-element.52.scatter, bf16[96,4096]{1,0:T(8,128)(2,1)S(1)} %collective-permute-done.1.received, f32[128,4096]{1,0:T(8,128)S(1)} %get-tuple-element.54.addend, s32[1]{0:T(128)S(4)} %get-tuple-element.55.more, ...), custom_call_target="tpu_custom_call" | custom-call | flops 1048576 | bytes 65536 | tf_op jit(solution)/shard_map/pallas_call | solution.py:212
  (3 shorter events, 0.1 us)
Async XLA Ops:
  4.4 21.7 %collective-permute-start.1 = (bf16[96,4096]{1,0:T(8,128)(2,1)S(1)}, bf16[96,4096]{1,0:T(8,128)(2,1)S(1)}, u32[]{:S(2)}, u32[]{:S(2)}) collective-permute-start(bf16[96,4096]{1,0:T(8,128)(2,1)S(1)} %get-tuple-element.53), channel_id=1, source_target_pairs={{1,0},{0,1},{3,2},{2,3},{5,4},{4,5},{7,6},{6,7},{9,8},{8,9},{11,10... | collective-permute-start | bytes 2359304 | tf_op jit(solution)/shard_map/ppermute | solution.py:357
  8.0 2.0 %collective-permute-start.2 = (bf16[8,272,128]{2,1,0:T(8,128)(2,1)S(1)}, bf16[8,272,128]{2,1,0:T(8,128)(2,1)S(1)}, u32[]{:S(2)}, u32[]{:S(2)}) collective-permute-start(bf16[8,272,128]{2,1,0:T(8,128)(2,1)S(1)} %get-tuple-element.60), channel_id=1, source_target_pairs={{0,2},{2,0},{4,6},{6,4},{8,10},{10,8},{12,14},{14,12},{16,18},{18,... | collective-permute-start | bytes 1671176 | tf_op jit(solution)/shard_map/ppermute | solution.py:337
  10.1 6.6 %collective-permute-start.3 = (bf16[2,272,128]{2,1,0:T(8,128)(2,1)S(1)}, bf16[2,272,128]{2,1,0:T(8,128)(2,1)S(1)}, u32[]{:S(2)}, u32[]{:S(2)}) collective-permute-start(bf16[2,272,128]{2,1,0:T(8,128)(2,1)S(1)} %get-tuple-element.62), channel_id=1, source_target_pairs={{0,4},{2,6},{4,0},{6,2},{8,12},{10,14},{12,8},{14,10},{16,20},{18,... | collective-permute-start | bytes 417800 | tf_op jit(solution)/shard_map/ppermute | solution.py:318
  11.7 7.7 %collective-permute-start.5 = (bf16[2,272,128]{2,1,0:T(8,128)(2,1)S(1)}, bf16[2,272,128]{2,1,0:T(8,128)(2,1)S(1)}, u32[]{:S(2)}, u32[]{:S(2)}) collective-permute-start(bf16[2,272,128]{2,1,0:T(8,128)(2,1)S(1)} %get-tuple-element.66), channel_id=1, source_target_pairs={{0,4},{2,6},{4,0},{6,2},{8,12},{10,14},{12,8},{14,10},{16,20},{18,... | collective-permute-start | bytes 417800 | tf_op jit(solution)/shard_map/ppermute | solution.py:318
  16.8 6.6 %collective-permute-start.4 = (bf16[272,128]{1,0:T(8,128)(2,1)S(1)}, bf16[272,128]{1,0:T(8,128)(2,1)S(1)}, u32[]{:S(2)}, u32[]{:S(2)}) collective-permute-start(bf16[272,128]{1,0:T(8,128)(2,1)S(1)} %get-tuple-element.64), channel_id=1, source_target_pairs={{0,16},{2,18},{4,20},{6,22},{8,24},{10,26},{12,28},{14,30},{16,0},... | collective-permute-start | bytes 208904 | tf_op jit(solution)/shard_map/ppermute | solution.py:323
  19.4 6.3 %collective-permute-start.6 = (bf16[272,128]{1,0:T(8,128)(2,1)S(1)}, bf16[272,128]{1,0:T(8,128)(2,1)S(1)}, u32[]{:S(2)}, u32[]{:S(2)}) collective-permute-start(bf16[272,128]{1,0:T(8,128)(2,1)S(1)} %get-tuple-element.67), channel_id=1, source_target_pairs={{0,8},{2,10},{4,12},{6,14},{8,16},{10,18},{12,20},{14,22},{16,24},... | collective-permute-start | bytes 208904 | tf_op jit(solution)/shard_map/ppermute | solution.py:323
  21.1 5.1 %collective-permute-start.7 = (bf16[272,128]{1,0:T(8,128)(2,1)S(1)}, bf16[272,128]{1,0:T(8,128)(2,1)S(1)}, u32[]{:S(2)}, u32[]{:S(2)}) collective-permute-start(bf16[272,128]{1,0:T(8,128)(2,1)S(1)} %get-tuple-element.68), channel_id=1, source_target_pairs={{0,24},{2,26},{4,28},{6,30},{8,0},{10,2},{12,4},{14,6},{16,8},{18,... | collective-permute-start | bytes 208904 | tf_op jit(solution)/shard_map/ppermute | solution.py:323

commit v11 on v10

--- a/solution.py
+++ b/solution.py
@@ -220,7 +220,7 @@
     )(scatter, received, addend, more, *others)
 
 
-def terms_kernel(owned_rows, normed, masked, gain, keep, give, total):
+def terms_kernel(owned_rows, normed, masked, gain, keep, give, give_low, total):
     width = normed.shape[1]
     values = masked[...]
     gain_rows = width // lanes
@@ -240,47 +240,66 @@
             even = jnp.concatenate([even, blank], axis=0)
             odd = jnp.concatenate([odd, blank], axis=0)
         keep[j] = jnp.where(even_core, even, odd)
-        give[j] = jnp.where(even_core, odd, even).astype(bf16)
+        other = jnp.where(even_core, odd, even).astype(bf16)
+        give[j] = other[: give.shape[1], :]
+        give_low[j] = other[give.shape[1] :, :]
 
 
 def pair_terms(normed, masked, gain, owned_rows, owners):
     padded = -(-owned_rows // pack_rows) * pack_rows
-    half = jax.ShapeDtypeStruct((owners // pair, padded, lanes), f32)
+    cut = padded // 2 // pack_rows * pack_rows
+    blocks = owners // pair
     return pl.pallas_call(
         functools.partial(terms_kernel, owned_rows),
         in_specs=[near, near, near],
-        out_specs=[near, near],
-        out_shape=[half, jax.ShapeDtypeStruct(half.shape, bf16)],
+        out_specs=[near, near, near],
+        out_shape=[
+            jax.ShapeDtypeStruct((blocks, padded, lanes), f32),
+            jax.ShapeDtypeStruct((blocks, cut, lanes), bf16),
+            jax.ShapeDtypeStruct((blocks, padded - cut, lanes), bf16),
+        ],
         scratch_shapes=[pltpu.VMEM((owners * owned_rows, lanes), f32)],
         compiler_params=roomy,
         cost_estimate=small_cost,
     )(normed, masked, gain)
 
 
-def merge_kernel(offsets, keep, taken, *halves):
+def merge_kernel(offsets, direct, keep, taken, taken_low, hold, give, *straight):
     chip = lax.axis_index("dp") // pair
     mine, place = chip % 2, chip // 2
     count = keep.shape[0] // 2
-    for part, (hold, give) in zip(offsets, (halves[:2], halves[2:])):
-        for k, offset in enumerate(part):
-            at = 2 * lax.rem(place + offset, count)
-            hold[k] = keep[at + mine] + taken[at + mine].astype(f32)
-            give[k] = (keep[at + 1 - mine] + taken[at + 1 - mine].astype(f32)).astype(bf16)
-
-
-def merge_terms(offsets, keep, taken):
-    outs = []
-    for part in offsets:
-        block = (len(part),) + keep.shape[1:]
-        outs += [jax.ShapeDtypeStruct(block, f32), jax.ShapeDtypeStruct(block, bf16)]
-    return pl.pallas_call(
-        functools.partial(merge_kernel, offsets),
-        in_specs=[near, near],
+    cut = taken.shape[1]
+
+    def total(at, out):
+        high = keep[at, :cut, :] + taken[at].astype(f32)
+        low = keep[at, cut:, :] + taken_low[at].astype(f32)
+        out[:cut, :] = high.astype(out.dtype)
+        out[cut:, :] = low.astype(out.dtype)
+
+    for k, offset in enumerate(offsets):
+        at = 2 * lax.rem(place + offset, count)
+        total(at + mine, hold.at[k])
+        total(at + 1 - mine, give.at[k])
+    for k, offset in enumerate(direct):
+        at = 2 * lax.rem(place + offset, count)
+        total(at + mine, straight[2 * k])
+        total(at + 1 - mine, straight[2 * k + 1])
+
+
+def merge_terms(offsets, direct, keep, taken, taken_low):
+    block = keep.shape[1:]
+    outs = [
+        jax.ShapeDtypeStruct((len(offsets),) + block, f32),
+        jax.ShapeDtypeStruct((len(offsets),) + block, bf16),
+    ] + [jax.ShapeDtypeStruct(block, bf16)] * (2 * len(direct))
+    return pl.pallas_call(
+        functools.partial(merge_kernel, offsets, direct),
+        in_specs=[near, near, near],
         out_specs=[near] * len(outs),
         out_shape=outs,
         compiler_params=roomy,
         cost_estimate=small_cost,
-    )(keep, taken)
+    )(keep, taken, taken_low)
 
 
 def split_kernel(hold, taken, *parts):
@@ -308,19 +327,25 @@
         out[:, k * lanes : (k + 1) * lanes] = total[k : k + 1, :]
 
 
-def plane_parts(owners, keep, taken):
+def plane_parts(owners, keep, *taken):
     quad = 2 * pair
     count = owners // quad
-    order = [0, count // 2, *(k for k in range(1, count) if k != count // 2)]
-    offsets = (order[:2], order[2:])
-    hold, give, hold_next, give_next = merge_terms(offsets, keep, taken)
-    near_by = [(i, i ^ pair) for i in range(owners)]
-    across = [lax.ppermute(part, "dp", near_by) for part in (give, give_next)]
-    own, *parts = split_terms(offsets[0], hold, across[0])
-    parts += split_terms(offsets[1], hold_next, across[1])
-    arrived = []
-    for offset, part in zip(order[1:], parts):
-        arrived.append(lax.ppermute(part, "dp", [(i, (i + quad * offset) % owners) for i in range(owners)]))
+    direct = [count // 2] if count > 2 else []
+    offsets = [k for k in range(count) if k not in direct]
+
+    def along(offset, side):
+        return [(i, (i + quad * offset) % owners ^ pair * side) for i in range(owners)]
+
+    hold, give, *straight = merge_terms(offsets, direct, keep, *taken)
+    across = lax.ppermute(give, "dp", along(0, 1))
+    arrived = [
+        lax.ppermute(straight[2 * k + side], "dp", along(offset, side))
+        for k, offset in enumerate(direct)
+        for side in range(2)
+    ]
+    own, *parts = split_terms(offsets, hold, across)
+    for offset, part in zip(offsets[1:], parts):
+        arrived.append(lax.ppermute(part, "dp", along(offset, 0)))
     return own, *arrived
 
 
@@ -333,9 +358,9 @@
         weight_term = lax.dot_general(normed, masked, contract_rows, preferred_element_type=f32)
         flat = jnp.concatenate([gain.reshape(-1), weight_term.reshape(-1)]) * factor
         return (), owned, lax.psum_scatter(flat, "dp", scatter_dimension=0, tiled=True)[None, :]
-    keep, give = pair_terms(normed, masked, gain, owned // lanes, owners)
-    taken = lax.ppermute(give, "dp", [(i, i ^ 1) for i in range(owners)])
-    return plane_parts(owners, keep, taken), owned, None
+    keep, *give = pair_terms(normed, masked, gain, owned // lanes, owners)
+    taken = [lax.ppermute(part, "dp", [(i, i ^ 1) for i in range(owners)]) for part in give]
+    return plane_parts(owners, keep, *taken), owned, None
 
 
 def shards(layer_inputs, top_grad, value_grads, weights, norm_gains, counts):

time: 27.6 us -> 26.5 us (0.960)
  waiting for transfers between devices: 9.24 us -> 7.9 us
    ppermute x6 -> x7, waiting for transfers between devices: 9.24 us -> 7.7 us  [the longest x2 3.43 us: plane_parts(): arrived.append(lax.ppermute(part, 'dp', along(offset, 0)))]
    ppermute x6 -> x7, starting transfers between devices: 8.68 us -> 8.9 us  [the longest x2 3.88 us: plane_parts(): arrived.append(lax.ppermute(part, 'dp', along(offset, 0)))]
  transfers between devices with their start and end apart: 7 -> 8, of which waited for: 4 -> 5; matrix products, arithmetic and copies ran while one was open for 0% -> 0% of each run, Pallas kernels for 3% -> 3%
where the time goes in v11:
time: 26.5 us; the launch traced here: 26.3 us
  starting transfers between devices  11.9 us (45%)
  waiting for transfers between devices  7.9 us (30%)
  Pallas kernels  5.86 us (22%)
  between operations  0.68 us (3%)
    ppermute x2, starting transfers between devices, plane_parts(): arrived.append(lax.ppermute(part, 'dp', along(offset, 0)))  3.88 us
    pallas_call x1, Pallas kernels, branch_rows(): pl.pallas_call(functools.partial(branch_kernel, low), in_specs=[pl.BlockS...  3.8 us
    ppermute x2, waiting for transfers between devices, plane_parts(): arrived.append(lax.ppermute(part, 'dp', along(offset, 0)))  3.43 us
    ppermute x1, starting transfers between devices, shards(): landed = lax.ppermute(packed, 'section', hops)  3.01 us
    ppermute x2, starting transfers between devices, plane_parts(): lax.ppermute(straight[2 * k + side], 'dp', along(offset, side))  2.87 us
    ppermute x1, waiting for transfers between devices, plane_parts(): across = lax.ppermute(give, 'dp', along(0, 1))  2.82 us
    ppermute x1, starting transfers between devices, plane_parts(): across = lax.ppermute(give, 'dp', along(0, 1))  1.58 us
    ppermute x2, waiting for transfers between devices, weight_owned(): lax.ppermute(part, 'dp', [(i, i ^ 1) for i in range(owners)])  1.45 us
  transfers between devices with their start and end apart: 8, of which 5 were waited for; matrix products, arithmetic and copies ran while one was open for 0% of the time, Pallas kernels for 3%

profile of v11, /device:TPU:0, one launch (start us, length us, event | category | flops | bytes accessed | tf_op | source)
XLA Modules:
  0.0 26.3 jit_solution(2654381448858255142)
XLA Ops:
  0.6 3.8 %shard_map.77 = (bf16[96,4096]{1,0:T(8,128)(2,1)S(1)}, f32[128,4096]{1,0:T(8,128)S(1)}, bf16[128,96]{1,0:T(8,128)(2,1)S(1)}, s32[1]{0:T(128)S(4)}, bf16[128,4096...) custom-call(s32[8]{0:T(128)} %counts_far.1, bf16[1,128,4096]{2,1,0:T(8,128)(2,1)} %x_far.1, ...), custom_call_target="tpu_custom_call" | custom-call | flops 1048576 | bytes 65536 | tf_op jit(solution)/shard_map/pallas_call | solution.py:126
  4.4 3.0 %collective-permute-start.1 = (bf16[96,4096]{1,0:T(8,128)(2,1)S(1)}, bf16[96,4096]{1,0:T(8,128)(2,1)S(1)}, u32[]{:S(2)}, u32[]{:S(2)}) collective-permute-start(bf16[96,4096]{1,0:T(8,128)(2,1)S(1)} %get-tuple-element.53), channel_id=1, source_target_pairs={{1,0},{0,1},{3,2},{2,3},{5,4},{4,5},{7,6},{6,7},{9,8},{8,9},{11,10... | collective-permute-start | bytes 2359304 | tf_op jit(solution)/shard_map/ppermute | solution.py:382
  7.4 0.6 %shard_map.78 = (f32[8,272,128]{2,1,0:T(8,128)S(1)}, bf16[8,128,128]{2,1,0:T(8,128)(2,1)S(1)}, bf16[8,144,128]{2,1,0:T(8,128)(2,1)S(1)}) custom-call(bf16[128,4096]{1,0:T(8,128)(2,1)S(1)} %get-tuple-element.56.normed, bf16[128,128]{1,0:T(8,128)(2,1)S(1)} %get-tuple-element.57.masked, f32[1,4096]{1,0:T(1,128)S(1)} %get-tuple-element.58.gain), custom_call_target="tpu_custom_call" | custom-call | flops 1048576 | bytes 65536 | tf_op jit(solution)/shard_map/pallas_call | solution.py:252
  8.0 0.1 collective-permute-start.3
  8.1 0.5 %collective-permute-start.2 = (bf16[8,128,128]{2,1,0:T(8,128)(2,1)S(1)}, bf16[8,128,128]{2,1,0:T(8,128)(2,1)S(1)}, u32[]{:S(2)}, u32[]{:S(2)}) collective-permute-start(bf16[8,128,128]{2,1,0:T(8,128)(2,1)S(1)} %get-tuple-element.60), channel_id=1, source_target_pairs={{0,2},{2,0},{4,6},{6,4},{8,10},{10,8},{12,14},{14,12},{16,18},{18,... | collective-permute-start | bytes 786440 | tf_op jit(solution)/shard_map/ppermute | solution.py:362
  8.6 1.4 %collective-permute-done.2.taken = bf16[8,128,128]{2,1,0:T(8,128)(2,1)S(1)} collective-permute-done((bf16[8,128,128]{2,1,0:T(8,128)(2,1)S(1)}, bf16[8,128,128]{2,1,0:T(8,128)(2,1)S(1)}, u32[]{:S(2)}, u32[]{:S(2)}) %collective-permute-start.2) | collective-permute-done | bytes 262176 | tf_op jit(solution)/shard_map/ppermute | solution.py:362
  10.0 0.0 collective-permute-done.3.taken_low
  10.0 0.1 shard_map.79
  10.1 1.6 %collective-permute-start.4 = (bf16[3,272,128]{2,1,0:T(8,128)(2,1)S(1)}, bf16[3,272,128]{2,1,0:T(8,128)(2,1)S(1)}, u32[]{:S(2)}, u32[]{:S(2)}) collective-permute-start(bf16[3,272,128]{2,1,0:T(8,128)(2,1)S(1)} %get-tuple-element.63), channel_id=1, source_target_pairs={{0,4},{2,6},{4,0},{6,2},{8,12},{10,14},{12,8},{14,10},{16,20},{18,... | collective-permute-start | bytes 626696 | tf_op jit(solution)/shard_map/ppermute | solution.py:340
  11.7 2.6 %collective-permute-start.5 = (bf16[272,128]{1,0:T(8,128)(2,1)S(1)}, bf16[272,128]{1,0:T(8,128)(2,1)S(1)}, u32[]{:S(2)}, u32[]{:S(2)}) collective-permute-start(bf16[272,128]{1,0:T(8,128)(2,1)S(1)} %get-tuple-element.65), channel_id=1, source_target_pairs={{0,16},{2,18},{4,20},{6,22},{8,24},{10,26},{12,28},{14,30},{16,0},... | collective-permute-start | bytes 208904 | tf_op jit(solution)/shard_map/ppermute | solution.py:342
  14.3 0.3 %collective-permute-start.6 = (bf16[272,128]{1,0:T(8,128)(2,1)S(1)}, bf16[272,128]{1,0:T(8,128)(2,1)S(1)}, u32[]{:S(2)}, u32[]{:S(2)}) collective-permute-start(bf16[272,128]{1,0:T(8,128)(2,1)S(1)} %get-tuple-element.66), channel_id=1, source_target_pairs={{0,20},{2,22},{4,16},{6,18},{8,28},{10,30},{12,24},{14,26},{16,4},... | collective-permute-start | bytes 208904 | tf_op jit(solution)/shard_map/ppermute | solution.py:342
  14.6 2.8 %collective-permute-done.4.taken = bf16[3,272,128]{2,1,0:T(8,128)(2,1)S(1)} collective-permute-done((bf16[3,272,128]{2,1,0:T(8,128)(2,1)S(1)}, bf16[3,272,128]{2,1,0:T(8,128)(2,1)S(1)}, u32[]{:S(2)}, u32[]{:S(2)}) %collective-permute-start.4) | collective-permute-done | bytes 208928 | tf_op jit(solution)/shard_map/ppermute | solution.py:340
  17.4 0.1 shard_map.80
  17.5 1.6 %collective-permute-start.7 = (bf16[272,128]{1,0:T(8,128)(2,1)S(1)}, bf16[272,128]{1,0:T(8,128)(2,1)S(1)}, u32[]{:S(2)}, u32[]{:S(2)}) collective-permute-start(bf16[272,128]{1,0:T(8,128)(2,1)S(1)} %get-tuple-element.67), channel_id=1, source_target_pairs={{0,8},{2,10},{4,12},{6,14},{8,16},{10,18},{12,20},{14,22},{16,24},... | collective-permute-start | bytes 208904 | tf_op jit(solution)/shard_map/ppermute | solution.py:348
  19.1 2.2 %collective-permute-start.8 = (bf16[272,128]{1,0:T(8,128)(2,1)S(1)}, bf16[272,128]{1,0:T(8,128)(2,1)S(1)}, u32[]{:S(2)}, u32[]{:S(2)}) collective-permute-start(bf16[272,128]{1,0:T(8,128)(2,1)S(1)} %get-tuple-element.68), channel_id=1, source_target_pairs={{0,24},{2,26},{4,28},{6,30},{8,0},{10,2},{12,4},{14,6},{16,8},{18,... | collective-permute-start | bytes 208904 | tf_op jit(solution)/shard_map/ppermute | solution.py:348
  21.3 0.0 collective-permute-done.5.refs_1_
  21.4 0.0 collective-permute-done.6.refs_2_
  21.4 3.0 %collective-permute-done.7.refs_3_ = bf16[272,128]{1,0:T(8,128)(2,1)S(1)} collective-permute-done((bf16[272,128]{1,0:T(8,128)(2,1)S(1)}, bf16[272,128]{1,0:T(8,128)(2,1)S(1)}, u32[]{:S(2)}, u32[]{:S(2)}) %collective-permute-start.7) | collective-permute-done | bytes 69664 | tf_op jit(solution)/shard_map/ppermute | solution.py:348
  24.3 0.4 %collective-permute-done.8.refs_4_ = bf16[272,128]{1,0:T(8,128)(2,1)S(1)} collective-permute-done((bf16[272,128]{1,0:T(8,128)(2,1)S(1)}, bf16[272,128]{1,0:T(8,128)(2,1)S(1)}, u32[]{:S(2)}, u32[]{:S(2)}) %collective-permute-start.8) | collective-permute-done | bytes 69664 | tf_op jit(solution)/shard_map/ppermute | solution.py:348
  24.8 0.2 collective-permute-done.1.received
  25.0 1.3 %shard_map.81 = (bf16[1,128,4096]{2,1,0:T(8,128)(2,1)}, s32[1]{0:T(128)S(4)}, f32[1,33024]{1,0:T(1,128)}) custom-call(bf16[128,96]{1,0:T(8,128)(2,1)S(1)} %get-tuple-element.52.scatter, bf16[96,4096]{1,0:T(8,128)(2,1)S(1)} %collective-permute-done.1.received, f32[128,4096]{1,0:T(8,128)S(1)} %get-tuple-element.54.addend, s32[1]{0:T(128)S(4)} %get-tuple-element.55.more, ...), custom_call_target="tpu_custom_call" | custom-call | flops 1048576 | bytes 65536 | tf_op jit(solution)/shard_map/pallas_call | solution.py:212
  (1 shorter events, 0.0 us)
Async XLA Ops:
  4.4 20.5 %collective-permute-start.1 = (bf16[96,4096]{1,0:T(8,128)(2,1)S(1)}, bf16[96,4096]{1,0:T(8,128)(2,1)S(1)}, u32[]{:S(2)}, u32[]{:S(2)}) collective-permute-start(bf16[96,4096]{1,0:T(8,128)(2,1)S(1)} %get-tuple-element.53), channel_id=1, source_target_pairs={{1,0},{0,1},{3,2},{2,3},{5,4},{4,5},{7,6},{6,7},{9,8},{8,9},{11,10... | collective-permute-start | bytes 2359304 | tf_op jit(solution)/shard_map/ppermute | solution.py:382
  8.0 2.0 %collective-permute-start.3 = (bf16[8,144,128]{2,1,0:T(8,128)(2,1)S(1)}, bf16[8,144,128]{2,1,0:T(8,128)(2,1)S(1)}, u32[]{:S(2)}, u32[]{:S(2)}) collective-permute-start(bf16[8,144,128]{2,1,0:T(8,128)(2,1)S(1)} %get-tuple-element.61), channel_id=1, source_target_pairs={{0,2},{2,0},{4,6},{6,4},{8,10},{10,8},{12,14},{14,12},{16,18},{18,... | collective-permute-start | bytes 884744 | tf_op jit(solution)/shard_map/ppermute | solution.py:362
  8.1 1.9 %collective-permute-start.2 = (bf16[8,128,128]{2,1,0:T(8,128)(2,1)S(1)}, bf16[8,128,128]{2,1,0:T(8,128)(2,1)S(1)}, u32[]{:S(2)}, u32[]{:S(2)}) collective-permute-start(bf16[8,128,128]{2,1,0:T(8,128)(2,1)S(1)} %get-tuple-element.60), channel_id=1, source_target_pairs={{0,2},{2,0},{4,6},{6,4},{8,10},{10,8},{12,14},{14,12},{16,18},{18,... | collective-permute-start | bytes 786440 | tf_op jit(solution)/shard_map/ppermute | solution.py:362
  10.1 7.3 %collective-permute-start.4 = (bf16[3,272,128]{2,1,0:T(8,128)(2,1)S(1)}, bf16[3,272,128]{2,1,0:T(8,128)(2,1)S(1)}, u32[]{:S(2)}, u32[]{:S(2)}) collective-permute-start(bf16[3,272,128]{2,1,0:T(8,128)(2,1)S(1)} %get-tuple-element.63), channel_id=1, source_target_pairs={{0,4},{2,6},{4,0},{6,2},{8,12},{10,14},{12,8},{14,10},{16,20},{18,... | collective-permute-start | bytes 626696 | tf_op jit(solution)/shard_map/ppermute | solution.py:340
  11.7 9.6 %collective-permute-start.5 = (bf16[272,128]{1,0:T(8,128)(2,1)S(1)}, bf16[272,128]{1,0:T(8,128)(2,1)S(1)}, u32[]{:S(2)}, u32[]{:S(2)}) collective-permute-start(bf16[272,128]{1,0:T(8,128)(2,1)S(1)} %get-tuple-element.65), channel_id=1, source_target_pairs={{0,16},{2,18},{4,20},{6,22},{8,24},{10,26},{12,28},{14,30},{16,0},... | collective-permute-start | bytes 208904 | tf_op jit(solution)/shard_map/ppermute | solution.py:342
  14.3 7.0 %collective-permute-start.6 = (bf16[272,128]{1,0:T(8,128)(2,1)S(1)}, bf16[272,128]{1,0:T(8,128)(2,1)S(1)}, u32[]{:S(2)}, u32[]{:S(2)}) collective-permute-start(bf16[272,128]{1,0:T(8,128)(2,1)S(1)} %get-tuple-element.66), channel_id=1, source_target_pairs={{0,20},{2,22},{4,16},{6,18},{8,28},{10,30},{12,24},{14,26},{16,4},... | collective-permute-start | bytes 208904 | tf_op jit(solution)/shard_map/ppermute | solution.py:342
  17.5 6.9 %collective-permute-start.7 = (bf16[272,128]{1,0:T(8,128)(2,1)S(1)}, bf16[272,128]{1,0:T(8,128)(2,1)S(1)}, u32[]{:S(2)}, u32[]{:S(2)}) collective-permute-start(bf16[272,128]{1,0:T(8,128)(2,1)S(1)} %get-tuple-element.67), channel_id=1, source_target_pairs={{0,8},{2,10},{4,12},{6,14},{8,16},{10,18},{12,20},{14,22},{16,24},... | collective-permute-start | bytes 208904 | tf_op jit(solution)/shard_map/ppermute | solution.py:348
  19.1 5.7 %collective-permute-start.8 = (bf16[272,128]{1,0:T(8,128)(2,1)S(1)}, bf16[272,128]{1,0:T(8,128)(2,1)S(1)}, u32[]{:S(2)}, u32[]{:S(2)}) collective-permute-start(bf16[272,128]{1,0:T(8,128)(2,1)S(1)} %get-tuple-element.68), channel_id=1, source_target_pairs={{0,24},{2,26},{4,28},{6,30},{8,0},{10,2},{12,4},{14,6},{16,8},{18,... | collective-permute-start | bytes 208904 | tf_op jit(solution)/shard_map/ppermute | solution.py:348

commit v12 on v11

--- a/solution.py
+++ b/solution.py
@@ -14,6 +14,8 @@
 pack_rows = 16
 tile_width = 512
 pair = 2
+block_rows = 32
+pieces = 4
 f32 = jnp.float32
 bf16 = jnp.bfloat16
 contract_last = (((1,), (1,)), ((), ()))
@@ -52,16 +54,18 @@
     rows, width = addend.shape
     micro_count = counts.shape[0]
     slots = rows // micro_count
-    fetches = [
-        pltpu.make_async_copy(v_far.at[0], v, ready.at[0]),
-        pltpu.make_async_copy(counts_far, counts, ready.at[1]),
-        pltpu.make_async_copy(w_far.at[0], w, ready.at[2]),
-        pltpu.make_async_copy(x_far.at[0], x, ready.at[3]),
-        pltpu.make_async_copy(gain_far, gain, ready.at[4]),
-        pltpu.make_async_copy(top_far, top, ready.at[5]),
-    ]
+    bands = cuts(width, width // pieces)
+    blocks = [pl.ds(at, block_rows) for at in range(0, rows, block_rows)]
+    pairs = [(v_far.at[0], v), (counts_far, counts), (gain_far, gain)]
+    pairs += [(w_far.at[0, band, :], w.at[band, :]) for band in bands]
+    pairs += [(x_far.at[0, part, :], x.at[part, :]) for part in blocks]
+    pairs += [(top_far.at[part, :], top.at[part, :]) for part in blocks]
+    fetches = [pltpu.make_async_copy(*ends, ready.at[k]) for k, ends in enumerate(pairs)]
     for fetch in fetches:
         fetch.start()
+    w_fetch = fetches[3 : 3 + pieces]
+    x_fetch = fetches[3 + pieces : 3 + pieces + len(blocks)]
+    top_fetch = fetches[3 + pieces + len(blocks) :]
     fetches[0].wait()
     fetches[1].wait()
     slot = lax.broadcasted_iota(jnp.int32, (slots, v.shape[1]), 0)
@@ -76,16 +80,17 @@
     receives = lax.axis_index("section") < lax.axis_size("section") - 1
     scatter[...] = jnp.where(receives, gather.astype(f32), 0.0).astype(bf16)
     values = masked[...]
+    for band in range(pieces):
+        w_fetch[band].wait()
+        for at in range(band * width // pieces, (band + 1) * width // pieces, tile_width):
+            cut = pl.ds(at, tile_width)
+            back[:, cut] = lax.dot_general(values, w[cut, :], contract_last, preferred_element_type=f32)
     fetches[2].wait()
-    for cut in cuts(width, tile_width):
-        back[:, cut] = lax.dot_general(values, w[cut, :], contract_last, preferred_element_type=f32)
-    fetches[3].wait()
-    fetches[4].wait()
-    fetches[5].wait()
-    for at in range(0, rows, 32):
-        part = slice(at, at + 32)
-        squares = jnp.zeros((32, lanes), f32)
-        products = jnp.zeros((32, lanes), f32)
+    for block, at in enumerate(range(0, rows, block_rows)):
+        part = slice(at, at + block_rows)
+        x_fetch[block].wait()
+        squares = jnp.zeros((block_rows, lanes), f32)
+        products = jnp.zeros((block_rows, lanes), f32)
         for cut in cuts(width, lanes):
             wide = x[part, cut].astype(f32)
             squares += wide * wide
@@ -95,23 +100,24 @@
         waits = jnp.concatenate(
             [
                 lax.broadcasted_iota(jnp.int32, (slots, 1), 0) < jnp.where(receives, counts[m], 0)
-                for m in range(at // slots, (at + 32) // slots)
+                for m in range(at // slots, (at + block_rows) // slots)
             ],
             axis=0,
         )
+        top_fetch[block].wait()
         for cut in cuts(width, 2 * lanes):
             unit = x[part, cut].astype(f32) * scale
             here = back[part, cut]
             scaled = gain[:, cut]
-            product = (unit * here).reshape(32 // sublanes, sublanes, 2 * lanes).sum(axis=0)
+            product = (unit * here).reshape(block_rows // sublanes, sublanes, 2 * lanes).sum(axis=0)
             if at:
                 product += gain_part[:, cut]
             gain_part[:, cut] = product
             normed[part, cut] = (unit * scaled).astype(bf16)
             own = scale * (scaled * here - unit * pull)
-            whole = (top[part, cut].astype(f32) + own).astype(bf16)
-            sent[part, cut] = whole
-            addend[part, cut] = jnp.where(waits, own, whole.astype(f32))
+            whole = top[part, cut].astype(f32) + own
+            sent[part, cut] = whole.astype(bf16)
+            addend[part, cut] = jnp.where(waits, own, whole)
     for cut in cuts(width, tile_width):
         packed[:, cut] = lax.dot_general(
             gather, sent[:, cut], contract_rows, preferred_element_type=f32
@@ -146,7 +152,7 @@
             pltpu.VMEM((rows, width), f32),
             pltpu.VMEM((sublanes, width), f32),
             pltpu.VMEM((rows, width), bf16),
-            pltpu.SemaphoreType.DMA((6,)),
+            pltpu.SemaphoreType.DMA((3 + pieces + 2 * (rows // block_rows),)),
         ],
         compiler_params=roomy,
         cost_estimate=small_cost,

time: 26.5 us -> 26.8 us (1.011)
  Pallas kernels: 5.86 us -> 6.14 us
    pallas_call x1, Pallas kernels: 3.8 us -> 4.08 us  [branch_rows(): pl.pallas_call(functools.partial(branch_kernel, low), in_specs=[pl.BlockS...]
where the time goes in v12:
time: 26.8 us; the launch traced here: 26.6 us
  starting transfers between devices  11.9 us (44%)
  waiting for transfers between devices  7.89 us (29%)
  Pallas kernels  6.14 us (23%)
  between operations  0.68 us (3%)
    pallas_call x1, Pallas kernels, branch_rows(): pl.pallas_call(functools.partial(branch_kernel, low), in_specs=[pl.BlockS...  4.08 us
    ppermute x2, starting transfers between devices, plane_parts(): arrived.append(lax.ppermute(part, 'dp', along(offset, 0)))  3.88 us
    ppermute x2, waiting for transfers between devices, plane_parts(): arrived.append(lax.ppermute(part, 'dp', along(offset, 0)))  3.43 us
    ppermute x1, starting transfers between devices, shards(): landed = lax.ppermute(packed, 'section', hops)  3.01 us
    ppermute x2, starting transfers between devices, plane_parts(): lax.ppermute(straight[2 * k + side], 'dp', along(offset, side))  2.87 us
    ppermute x1, waiting for transfers between devices, plane_parts(): across = lax.ppermute(give, 'dp', along(0, 1))  2.82 us
    ppermute x1, starting transfers between devices, plane_parts(): across = lax.ppermute(give, 'dp', along(0, 1))  1.58 us
    ppermute x2, waiting for transfers between devices, weight_owned(): lax.ppermute(part, 'dp', [(i, i ^ 1) for i in range(owners)])  1.45 us
  transfers between devices with their start and end apart: 8, of which 5 were waited for; matrix products, arithmetic and copies ran while one was open for 0% of the time, Pallas kernels for 3%

profile of v12, /device:TPU:0, one launch (start us, length us, event | category | flops | bytes accessed | tf_op | source)
XLA Modules:
  0.0 26.6 jit_solution(5114125226897731264)
XLA Ops:
  0.6 4.1 %shard_map.77 = (bf16[96,4096]{1,0:T(8,128)(2,1)S(1)}, f32[128,4096]{1,0:T(8,128)S(1)}, bf16[128,96]{1,0:T(8,128)(2,1)S(1)}, s32[1]{0:T(128)S(4)}, bf16[128,4096...) custom-call(s32[8]{0:T(128)} %counts_far.1, bf16[1,128,4096]{2,1,0:T(8,128)(2,1)} %x_far.1, ...), custom_call_target="tpu_custom_call" | custom-call | flops 1048576 | bytes 65536 | tf_op jit(solution)/shard_map/pallas_call | solution.py:132
  4.7 3.0 %collective-permute-start.1 = (bf16[96,4096]{1,0:T(8,128)(2,1)S(1)}, bf16[96,4096]{1,0:T(8,128)(2,1)S(1)}, u32[]{:S(2)}, u32[]{:S(2)}) collective-permute-start(bf16[96,4096]{1,0:T(8,128)(2,1)S(1)} %get-tuple-element.53), channel_id=1, source_target_pairs={{1,0},{0,1},{3,2},{2,3},{5,4},{4,5},{7,6},{6,7},{9,8},{8,9},{11,10... | collective-permute-start | bytes 2359304 | tf_op jit(solution)/shard_map/ppermute | solution.py:388
  7.7 0.6 %shard_map.78 = (f32[8,272,128]{2,1,0:T(8,128)S(1)}, bf16[8,128,128]{2,1,0:T(8,128)(2,1)S(1)}, bf16[8,144,128]{2,1,0:T(8,128)(2,1)S(1)}) custom-call(bf16[128,4096]{1,0:T(8,128)(2,1)S(1)} %get-tuple-element.56.normed, bf16[128,128]{1,0:T(8,128)(2,1)S(1)} %get-tuple-element.57.masked, f32[1,4096]{1,0:T(1,128)S(1)} %get-tuple-element.58.gain), custom_call_target="tpu_custom_call" | custom-call | flops 1048576 | bytes 65536 | tf_op jit(solution)/shard_map/pallas_call | solution.py:258
  8.3 0.1 collective-permute-start.3
  8.4 0.5 %collective-permute-start.2 = (bf16[8,128,128]{2,1,0:T(8,128)(2,1)S(1)}, bf16[8,128,128]{2,1,0:T(8,128)(2,1)S(1)}, u32[]{:S(2)}, u32[]{:S(2)}) collective-permute-start(bf16[8,128,128]{2,1,0:T(8,128)(2,1)S(1)} %get-tuple-element.60), channel_id=1, source_target_pairs={{0,2},{2,0},{4,6},{6,4},{8,10},{10,8},{12,14},{14,12},{16,18},{18,... | collective-permute-start | bytes 786440 | tf_op jit(solution)/shard_map/ppermute | solution.py:368
  8.9 1.4 %collective-permute-done.2.taken = bf16[8,128,128]{2,1,0:T(8,128)(2,1)S(1)} collective-permute-done((bf16[8,128,128]{2,1,0:T(8,128)(2,1)S(1)}, bf16[8,128,128]{2,1,0:T(8,128)(2,1)S(1)}, u32[]{:S(2)}, u32[]{:S(2)}) %collective-permute-start.2) | collective-permute-done | bytes 262176 | tf_op jit(solution)/shard_map/ppermute | solution.py:368
  10.3 0.0 collective-permute-done.3.taken_low
  10.3 0.1 shard_map.79
  10.4 1.6 %collective-permute-start.4 = (bf16[3,272,128]{2,1,0:T(8,128)(2,1)S(1)}, bf16[3,272,128]{2,1,0:T(8,128)(2,1)S(1)}, u32[]{:S(2)}, u32[]{:S(2)}) collective-permute-start(bf16[3,272,128]{2,1,0:T(8,128)(2,1)S(1)} %get-tuple-element.63), channel_id=1, source_target_pairs={{0,4},{2,6},{4,0},{6,2},{8,12},{10,14},{12,8},{14,10},{16,20},{18,... | collective-permute-start | bytes 626696 | tf_op jit(solution)/shard_map/ppermute | solution.py:346
  12.0 2.6 %collective-permute-start.5 = (bf16[272,128]{1,0:T(8,128)(2,1)S(1)}, bf16[272,128]{1,0:T(8,128)(2,1)S(1)}, u32[]{:S(2)}, u32[]{:S(2)}) collective-permute-start(bf16[272,128]{1,0:T(8,128)(2,1)S(1)} %get-tuple-element.65), channel_id=1, source_target_pairs={{0,16},{2,18},{4,20},{6,22},{8,24},{10,26},{12,28},{14,30},{16,0},... | collective-permute-start | bytes 208904 | tf_op jit(solution)/shard_map/ppermute | solution.py:348
  14.6 0.3 %collective-permute-start.6 = (bf16[272,128]{1,0:T(8,128)(2,1)S(1)}, bf16[272,128]{1,0:T(8,128)(2,1)S(1)}, u32[]{:S(2)}, u32[]{:S(2)}) collective-permute-start(bf16[272,128]{1,0:T(8,128)(2,1)S(1)} %get-tuple-element.66), channel_id=1, source_target_pairs={{0,20},{2,22},{4,16},{6,18},{8,28},{10,30},{12,24},{14,26},{16,4},... | collective-permute-start | bytes 208904 | tf_op jit(solution)/shard_map/ppermute | solution.py:348
  14.9 2.8 %collective-permute-done.4.taken = bf16[3,272,128]{2,1,0:T(8,128)(2,1)S(1)} collective-permute-done((bf16[3,272,128]{2,1,0:T(8,128)(2,1)S(1)}, bf16[3,272,128]{2,1,0:T(8,128)(2,1)S(1)}, u32[]{:S(2)}, u32[]{:S(2)}) %collective-permute-start.4) | collective-permute-done | bytes 208928 | tf_op jit(solution)/shard_map/ppermute | solution.py:346
  17.7 0.1 shard_map.80
  17.8 1.6 %collective-permute-start.7 = (bf16[272,128]{1,0:T(8,128)(2,1)S(1)}, bf16[272,128]{1,0:T(8,128)(2,1)S(1)}, u32[]{:S(2)}, u32[]{:S(2)}) collective-permute-start(bf16[272,128]{1,0:T(8,128)(2,1)S(1)} %get-tuple-element.67), channel_id=1, source_target_pairs={{0,8},{2,10},{4,12},{6,14},{8,16},{10,18},{12,20},{14,22},{16,24},... | collective-permute-start | bytes 208904 | tf_op jit(solution)/shard_map/ppermute | solution.py:354
  19.4 2.3 %collective-permute-start.8 = (bf16[272,128]{1,0:T(8,128)(2,1)S(1)}, bf16[272,128]{1,0:T(8,128)(2,1)S(1)}, u32[]{:S(2)}, u32[]{:S(2)}) collective-permute-start(bf16[272,128]{1,0:T(8,128)(2,1)S(1)} %get-tuple-element.68), channel_id=1, source_target_pairs={{0,24},{2,26},{4,28},{6,30},{8,0},{10,2},{12,4},{14,6},{16,8},{18,... | collective-permute-start | bytes 208904 | tf_op jit(solution)/shard_map/ppermute | solution.py:354
  21.6 0.0 collective-permute-done.5.refs_1_
  21.6 0.0 collective-permute-done.6.refs_2_
  21.6 3.0 %collective-permute-done.7.refs_3_ = bf16[272,128]{1,0:T(8,128)(2,1)S(1)} collective-permute-done((bf16[272,128]{1,0:T(8,128)(2,1)S(1)}, bf16[272,128]{1,0:T(8,128)(2,1)S(1)}, u32[]{:S(2)}, u32[]{:S(2)}) %collective-permute-start.7) | collective-permute-done | bytes 69664 | tf_op jit(solution)/shard_map/ppermute | solution.py:354
  24.6 0.4 %collective-permute-done.8.refs_4_ = bf16[272,128]{1,0:T(8,128)(2,1)S(1)} collective-permute-done((bf16[272,128]{1,0:T(8,128)(2,1)S(1)}, bf16[272,128]{1,0:T(8,128)(2,1)S(1)}, u32[]{:S(2)}, u32[]{:S(2)}) %collective-permute-start.8) | collective-permute-done | bytes 69664 | tf_op jit(solution)/shard_map/ppermute | solution.py:354
  25.1 0.2 collective-permute-done.1.received
  25.3 1.3 %shard_map.81 = (bf16[1,128,4096]{2,1,0:T(8,128)(2,1)}, s32[1]{0:T(128)S(4)}, f32[1,33024]{1,0:T(1,128)}) custom-call(bf16[128,96]{1,0:T(8,128)(2,1)S(1)} %get-tuple-element.52.scatter, bf16[96,4096]{1,0:T(8,128)(2,1)S(1)} %collective-permute-done.1.received, f32[128,4096]{1,0:T(8,128)S(1)} %get-tuple-element.54.addend, s32[1]{0:T(128)S(4)} %get-tuple-element.55.more, ...), custom_call_target="tpu_custom_call" | custom-call | flops 1048576 | bytes 65536 | tf_op jit(solution)/shard_map/pallas_call | solution.py:218
  (1 shorter events, 0.0 us)
Async XLA Ops:
  4.7 20.5 %collective-permute-start.1 = (bf16[96,4096]{1,0:T(8,128)(2,1)S(1)}, bf16[96,4096]{1,0:T(8,128)(2,1)S(1)}, u32[]{:S(2)}, u32[]{:S(2)}) collective-permute-start(bf16[96,4096]{1,0:T(8,128)(2,1)S(1)} %get-tuple-element.53), channel_id=1, source_target_pairs={{1,0},{0,1},{3,2},{2,3},{5,4},{4,5},{7,6},{6,7},{9,8},{8,9},{11,10... | collective-permute-start | bytes 2359304 | tf_op jit(solution)/shard_map/ppermute | solution.py:388
  8.3 2.0 %collective-permute-start.3 = (bf16[8,144,128]{2,1,0:T(8,128)(2,1)S(1)}, bf16[8,144,128]{2,1,0:T(8,128)(2,1)S(1)}, u32[]{:S(2)}, u32[]{:S(2)}) collective-permute-start(bf16[8,144,128]{2,1,0:T(8,128)(2,1)S(1)} %get-tuple-element.61), channel_id=1, source_target_pairs={{0,2},{2,0},{4,6},{6,4},{8,10},{10,8},{12,14},{14,12},{16,18},{18,... | collective-permute-start | bytes 884744 | tf_op jit(solution)/shard_map/ppermute | solution.py:368
  8.4 1.9 %collective-permute-start.2 = (bf16[8,128,128]{2,1,0:T(8,128)(2,1)S(1)}, bf16[8,128,128]{2,1,0:T(8,128)(2,1)S(1)}, u32[]{:S(2)}, u32[]{:S(2)}) collective-permute-start(bf16[8,128,128]{2,1,0:T(8,128)(2,1)S(1)} %get-tuple-element.60), channel_id=1, source_target_pairs={{0,2},{2,0},{4,6},{6,4},{8,10},{10,8},{12,14},{14,12},{16,18},{18,... | collective-permute-start | bytes 786440 | tf_op jit(solution)/shard_map/ppermute | solution.py:368
  10.4 7.3 %collective-permute-start.4 = (bf16[3,272,128]{2,1,0:T(8,128)(2,1)S(1)}, bf16[3,272,128]{2,1,0:T(8,128)(2,1)S(1)}, u32[]{:S(2)}, u32[]{:S(2)}) collective-permute-start(bf16[3,272,128]{2,1,0:T(8,128)(2,1)S(1)} %get-tuple-element.63), channel_id=1, source_target_pairs={{0,4},{2,6},{4,0},{6,2},{8,12},{10,14},{12,8},{14,10},{16,20},{18,... | collective-permute-start | bytes 626696 | tf_op jit(solution)/shard_map/ppermute | solution.py:346
  12.0 9.6 %collective-permute-start.5 = (bf16[272,128]{1,0:T(8,128)(2,1)S(1)}, bf16[272,128]{1,0:T(8,128)(2,1)S(1)}, u32[]{:S(2)}, u32[]{:S(2)}) collective-permute-start(bf16[272,128]{1,0:T(8,128)(2,1)S(1)} %get-tuple-element.65), channel_id=1, source_target_pairs={{0,16},{2,18},{4,20},{6,22},{8,24},{10,26},{12,28},{14,30},{16,0},... | collective-permute-start | bytes 208904 | tf_op jit(solution)/shard_map/ppermute | solution.py:348
  14.6 7.0 %collective-permute-start.6 = (bf16[272,128]{1,0:T(8,128)(2,1)S(1)}, bf16[272,128]{1,0:T(8,128)(2,1)S(1)}, u32[]{:S(2)}, u32[]{:S(2)}) collective-permute-start(bf16[272,128]{1,0:T(8,128)(2,1)S(1)} %get-tuple-element.66), channel_id=1, source_target_pairs={{0,20},{2,22},{4,16},{6,18},{8,28},{10,30},{12,24},{14,26},{16,4},... | collective-permute-start | bytes 208904 | tf_op jit(solution)/shard_map/ppermute | solution.py:348
  17.8 6.9 %collective-permute-start.7 = (bf16[272,128]{1,0:T(8,128)(2,1)S(1)}, bf16[272,128]{1,0:T(8,128)(2,1)S(1)}, u32[]{:S(2)}, u32[]{:S(2)}) collective-permute-start(bf16[272,128]{1,0:T(8,128)(2,1)S(1)} %get-tuple-element.67), channel_id=1, source_target_pairs={{0,8},{2,10},{4,12},{6,14},{8,16},{10,18},{12,20},{14,22},{16,24},... | collective-permute-start | bytes 208904 | tf_op jit(solution)/shard_map/ppermute | solution.py:354
  19.4 5.7 %collective-permute-start.8 = (bf16[272,128]{1,0:T(8,128)(2,1)S(1)}, bf16[272,128]{1,0:T(8,128)(2,1)S(1)}, u32[]{:S(2)}, u32[]{:S(2)}) collective-permute-start(bf16[272,128]{1,0:T(8,128)(2,1)S(1)} %get-tuple-element.68), channel_id=1, source_target_pairs={{0,24},{2,26},{4,28},{6,30},{8,0},{10,2},{12,4},{14,6},{16,8},{18,... | collective-permute-start | bytes 208904 | tf_op jit(solution)/shard_map/ppermute | solution.py:354

commit v13 on v11

--- a/solution.py
+++ b/solution.py
@@ -14,6 +14,7 @@
 pack_rows = 16
 tile_width = 512
 pair = 2
+block_rows = 32
 f32 = jnp.float32
 bf16 = jnp.bfloat16
 contract_last = (((1,), (1,)), ((), ()))
@@ -75,47 +76,51 @@
     gather = one_hot(counts, micro_count, slots, low, packed.shape[0])
     receives = lax.axis_index("section") < lax.axis_size("section") - 1
     scatter[...] = jnp.where(receives, gather.astype(f32), 0.0).astype(bf16)
+    gather = jnp.transpose(gather.astype(f32)).astype(bf16)
     values = masked[...]
     fetches[2].wait()
     for cut in cuts(width, tile_width):
         back[:, cut] = lax.dot_general(values, w[cut, :], contract_last, preferred_element_type=f32)
     fetches[3].wait()
     fetches[4].wait()
-    fetches[5].wait()
-    for at in range(0, rows, 32):
-        part = slice(at, at + 32)
-        squares = jnp.zeros((32, lanes), f32)
-        products = jnp.zeros((32, lanes), f32)
+    blocks = [slice(at, at + block_rows) for at in range(0, rows, block_rows)]
+    squares, products = [], []
+    for part in blocks:
+        square = jnp.zeros((block_rows, lanes), f32)
+        product = jnp.zeros((block_rows, lanes), f32)
         for cut in cuts(width, lanes):
             wide = x[part, cut].astype(f32)
-            squares += wide * wide
-            products += wide * back[part, cut] * gain[:, cut]
-        scale = lax.rsqrt(jnp.sum(squares, axis=1, keepdims=True) / width + eps_norm)
-        pull = scale * jnp.sum(products, axis=1, keepdims=True) / width
-        waits = jnp.concatenate(
-            [
-                lax.broadcasted_iota(jnp.int32, (slots, 1), 0) < jnp.where(receives, counts[m], 0)
-                for m in range(at // slots, (at + 32) // slots)
-            ],
-            axis=0,
-        )
+            square += wide * wide
+            product += wide * back[part, cut] * gain[:, cut]
+        squares.append(square)
+        products.append(product)
+    scales = lax.rsqrt(jnp.sum(jnp.concatenate(squares, axis=0), axis=1, keepdims=True) / width + eps_norm)
+    pulls = scales * jnp.sum(jnp.concatenate(products, axis=0), axis=1, keepdims=True) / width
+    waits = jnp.concatenate(
+        [
+            lax.broadcasted_iota(jnp.int32, (slots, 1), 0) < jnp.where(receives, counts[m], 0)
+            for m in range(micro_count)
+        ],
+        axis=0,
+    )
+    fetches[5].wait()
+    for part in blocks:
+        scale, pull, wait = scales[part], pulls[part], waits[part]
         for cut in cuts(width, 2 * lanes):
             unit = x[part, cut].astype(f32) * scale
             here = back[part, cut]
             scaled = gain[:, cut]
-            product = (unit * here).reshape(32 // sublanes, sublanes, 2 * lanes).sum(axis=0)
-            if at:
+            product = (unit * here).reshape(block_rows // sublanes, sublanes, 2 * lanes).sum(axis=0)
+            if part.start:
                 product += gain_part[:, cut]
             gain_part[:, cut] = product
             normed[part, cut] = (unit * scaled).astype(bf16)
             own = scale * (scaled * here - unit * pull)
-            whole = (top[part, cut].astype(f32) + own).astype(bf16)
-            sent[part, cut] = whole
-            addend[part, cut] = jnp.where(waits, own, whole.astype(f32))
+            whole = top[part, cut].astype(f32) + own
+            sent[part, cut] = whole.astype(bf16)
+            addend[part, cut] = jnp.where(wait, own, whole)
     for cut in cuts(width, tile_width):
-        packed[:, cut] = lax.dot_general(
-            gather, sent[:, cut], contract_rows, preferred_element_type=f32
-        ).astype(bf16)
+        packed[:, cut] = jnp.dot(gather, sent[:, cut], preferred_element_type=f32).astype(bf16)
     for cut in cuts(width, tile_width):
         gain_out[:, cut] = jnp.sum(gain_part[:, cut], axis=0, keepdims=True)
 

time: 26.5 us -> 26.3 us (level)
  no operation moved by 1% of the time
where the time goes in v13:
time: 26.3 us; the launch traced here: 26.2 us
  starting transfers between devices  11.9 us (45%)
  waiting for transfers between devices  7.9 us (30%)
  Pallas kernels  5.68 us (22%)
  between operations  0.68 us (3%)
    ppermute x2, starting transfers between devices, plane_parts(): arrived.append(lax.ppermute(part, 'dp', along(offset, 0)))  3.88 us
    pallas_call x1, Pallas kernels, branch_rows(): pl.pallas_call(functools.partial(branch_kernel, low), in_specs=[pl.BlockS...  3.62 us
    ppermute x2, waiting for transfers between devices, plane_parts(): arrived.append(lax.ppermute(part, 'dp', along(offset, 0)))  3.44 us
    ppermute x1, starting transfers between devices, shards(): landed = lax.ppermute(packed, 'section', hops)  3 us
    ppermute x2, starting transfers between devices, plane_parts(): lax.ppermute(straight[2 * k + side], 'dp', along(offset, side))  2.87 us
    ppermute x1, waiting for transfers between devices, plane_parts(): across = lax.ppermute(give, 'dp', along(0, 1))  2.82 us
    ppermute x1, starting transfers between devices, plane_parts(): across = lax.ppermute(give, 'dp', along(0, 1))  1.59 us
    ppermute x2, waiting for transfers between devices, weight_owned(): lax.ppermute(part, 'dp', [(i, i ^ 1) for i in range(owners)])  1.45 us
  transfers between devices with their start and end apart: 8, of which 5 were waited for; matrix products, arithmetic and copies ran while one was open for 0% of the time, Pallas kernels for 3%

profile of v13, /device:TPU:0, one launch (start us, length us, event | category | flops | bytes accessed | tf_op | source)
XLA Modules:
  0.0 26.2 jit_solution(3648980482735650930)
XLA Ops:
  0.6 3.6 %shard_map.77 = (bf16[96,4096]{1,0:T(8,128)(2,1)S(1)}, f32[128,4096]{1,0:T(8,128)S(1)}, bf16[128,96]{1,0:T(8,128)(2,1)S(1)}, s32[1]{0:T(128)S(4)}, bf16[128,4096...) custom-call(s32[8]{0:T(128)} %counts_far.1, bf16[1,128,4096]{2,1,0:T(8,128)(2,1)} %x_far.1, ...), custom_call_target="tpu_custom_call" | custom-call | flops 1048576 | bytes 65536 | tf_op jit(solution)/shard_map/pallas_call | solution.py:131
  4.3 3.0 %collective-permute-start.1 = (bf16[96,4096]{1,0:T(8,128)(2,1)S(1)}, bf16[96,4096]{1,0:T(8,128)(2,1)S(1)}, u32[]{:S(2)}, u32[]{:S(2)}) collective-permute-start(bf16[96,4096]{1,0:T(8,128)(2,1)S(1)} %get-tuple-element.53), channel_id=1, source_target_pairs={{1,0},{0,1},{3,2},{2,3},{5,4},{4,5},{7,6},{6,7},{9,8},{8,9},{11,10... | collective-permute-start | bytes 2359304 | tf_op jit(solution)/shard_map/ppermute | solution.py:387
  7.3 0.6 %shard_map.78 = (f32[8,272,128]{2,1,0:T(8,128)S(1)}, bf16[8,128,128]{2,1,0:T(8,128)(2,1)S(1)}, bf16[8,144,128]{2,1,0:T(8,128)(2,1)S(1)}) custom-call(bf16[128,4096]{1,0:T(8,128)(2,1)S(1)} %get-tuple-element.56.normed, bf16[128,128]{1,0:T(8,128)(2,1)S(1)} %get-tuple-element.57.masked, f32[1,4096]{1,0:T(1,128)S(1)} %get-tuple-element.58.gain), custom_call_target="tpu_custom_call" | custom-call | flops 1048576 | bytes 65536 | tf_op jit(solution)/shard_map/pallas_call | solution.py:257
  7.8 0.1 collective-permute-start.3
  7.9 0.5 %collective-permute-start.2 = (bf16[8,128,128]{2,1,0:T(8,128)(2,1)S(1)}, bf16[8,128,128]{2,1,0:T(8,128)(2,1)S(1)}, u32[]{:S(2)}, u32[]{:S(2)}) collective-permute-start(bf16[8,128,128]{2,1,0:T(8,128)(2,1)S(1)} %get-tuple-element.60), channel_id=1, source_target_pairs={{0,2},{2,0},{4,6},{6,4},{8,10},{10,8},{12,14},{14,12},{16,18},{18,... | collective-permute-start | bytes 786440 | tf_op jit(solution)/shard_map/ppermute | solution.py:367
  8.4 1.4 %collective-permute-done.2.taken = bf16[8,128,128]{2,1,0:T(8,128)(2,1)S(1)} collective-permute-done((bf16[8,128,128]{2,1,0:T(8,128)(2,1)S(1)}, bf16[8,128,128]{2,1,0:T(8,128)(2,1)S(1)}, u32[]{:S(2)}, u32[]{:S(2)}) %collective-permute-start.2) | collective-permute-done | bytes 262176 | tf_op jit(solution)/shard_map/ppermute | solution.py:367
  9.8 0.0 collective-permute-done.3.taken_low
  9.8 0.1 shard_map.79
  10.0 1.6 %collective-permute-start.4 = (bf16[3,272,128]{2,1,0:T(8,128)(2,1)S(1)}, bf16[3,272,128]{2,1,0:T(8,128)(2,1)S(1)}, u32[]{:S(2)}, u32[]{:S(2)}) collective-permute-start(bf16[3,272,128]{2,1,0:T(8,128)(2,1)S(1)} %get-tuple-element.63), channel_id=1, source_target_pairs={{0,4},{2,6},{4,0},{6,2},{8,12},{10,14},{12,8},{14,10},{16,20},{18,... | collective-permute-start | bytes 626696 | tf_op jit(solution)/shard_map/ppermute | solution.py:345
  11.6 2.6 %collective-permute-start.5 = (bf16[272,128]{1,0:T(8,128)(2,1)S(1)}, bf16[272,128]{1,0:T(8,128)(2,1)S(1)}, u32[]{:S(2)}, u32[]{:S(2)}) collective-permute-start(bf16[272,128]{1,0:T(8,128)(2,1)S(1)} %get-tuple-element.65), channel_id=1, source_target_pairs={{0,16},{2,18},{4,20},{6,22},{8,24},{10,26},{12,28},{14,30},{16,0},... | collective-permute-start | bytes 208904 | tf_op jit(solution)/shard_map/ppermute | solution.py:347
  14.1 0.3 %collective-permute-start.6 = (bf16[272,128]{1,0:T(8,128)(2,1)S(1)}, bf16[272,128]{1,0:T(8,128)(2,1)S(1)}, u32[]{:S(2)}, u32[]{:S(2)}) collective-permute-start(bf16[272,128]{1,0:T(8,128)(2,1)S(1)} %get-tuple-element.66), channel_id=1, source_target_pairs={{0,20},{2,22},{4,16},{6,18},{8,28},{10,30},{12,24},{14,26},{16,4},... | collective-permute-start | bytes 208904 | tf_op jit(solution)/shard_map/ppermute | solution.py:347
  14.4 2.8 %collective-permute-done.4.taken = bf16[3,272,128]{2,1,0:T(8,128)(2,1)S(1)} collective-permute-done((bf16[3,272,128]{2,1,0:T(8,128)(2,1)S(1)}, bf16[3,272,128]{2,1,0:T(8,128)(2,1)S(1)}, u32[]{:S(2)}, u32[]{:S(2)}) %collective-permute-start.4) | collective-permute-done | bytes 208928 | tf_op jit(solution)/shard_map/ppermute | solution.py:345
  17.2 0.1 shard_map.80
  17.3 1.6 %collective-permute-start.7 = (bf16[272,128]{1,0:T(8,128)(2,1)S(1)}, bf16[272,128]{1,0:T(8,128)(2,1)S(1)}, u32[]{:S(2)}, u32[]{:S(2)}) collective-permute-start(bf16[272,128]{1,0:T(8,128)(2,1)S(1)} %get-tuple-element.67), channel_id=1, source_target_pairs={{0,8},{2,10},{4,12},{6,14},{8,16},{10,18},{12,20},{14,22},{16,24},... | collective-permute-start | bytes 208904 | tf_op jit(solution)/shard_map/ppermute | solution.py:353
  18.9 2.2 %collective-permute-start.8 = (bf16[272,128]{1,0:T(8,128)(2,1)S(1)}, bf16[272,128]{1,0:T(8,128)(2,1)S(1)}, u32[]{:S(2)}, u32[]{:S(2)}) collective-permute-start(bf16[272,128]{1,0:T(8,128)(2,1)S(1)} %get-tuple-element.68), channel_id=1, source_target_pairs={{0,24},{2,26},{4,28},{6,30},{8,0},{10,2},{12,4},{14,6},{16,8},{18,... | collective-permute-start | bytes 208904 | tf_op jit(solution)/shard_map/ppermute | solution.py:353
  21.2 0.0 collective-permute-done.5.refs_1_
  21.2 0.0 collective-permute-done.6.refs_2_
  21.2 3.0 %collective-permute-done.7.refs_3_ = bf16[272,128]{1,0:T(8,128)(2,1)S(1)} collective-permute-done((bf16[272,128]{1,0:T(8,128)(2,1)S(1)}, bf16[272,128]{1,0:T(8,128)(2,1)S(1)}, u32[]{:S(2)}, u32[]{:S(2)}) %collective-permute-start.7) | collective-permute-done | bytes 69664 | tf_op jit(solution)/shard_map/ppermute | solution.py:353
  24.2 0.4 %collective-permute-done.8.refs_4_ = bf16[272,128]{1,0:T(8,128)(2,1)S(1)} collective-permute-done((bf16[272,128]{1,0:T(8,128)(2,1)S(1)}, bf16[272,128]{1,0:T(8,128)(2,1)S(1)}, u32[]{:S(2)}, u32[]{:S(2)}) %collective-permute-start.8) | collective-permute-done | bytes 69664 | tf_op jit(solution)/shard_map/ppermute | solution.py:353
  24.6 0.2 collective-permute-done.1.received
  24.8 1.3 %shard_map.81 = (bf16[1,128,4096]{2,1,0:T(8,128)(2,1)}, s32[1]{0:T(128)S(4)}, f32[1,33024]{1,0:T(1,128)}) custom-call(bf16[128,96]{1,0:T(8,128)(2,1)S(1)} %get-tuple-element.52.scatter, bf16[96,4096]{1,0:T(8,128)(2,1)S(1)} %collective-permute-done.1.received, f32[128,4096]{1,0:T(8,128)S(1)} %get-tuple-element.54.addend, s32[1]{0:T(128)S(4)} %get-tuple-element.55.more, ...), custom_call_target="tpu_custom_call" | custom-call | flops 1048576 | bytes 65536 | tf_op jit(solution)/shard_map/pallas_call | solution.py:217
  (1 shorter events, 0.0 us)
Async XLA Ops:
  4.3 20.5 %collective-permute-start.1 = (bf16[96,4096]{1,0:T(8,128)(2,1)S(1)}, bf16[96,4096]{1,0:T(8,128)(2,1)S(1)}, u32[]{:S(2)}, u32[]{:S(2)}) collective-permute-start(bf16[96,4096]{1,0:T(8,128)(2,1)S(1)} %get-tuple-element.53), channel_id=1, source_target_pairs={{1,0},{0,1},{3,2},{2,3},{5,4},{4,5},{7,6},{6,7},{9,8},{8,9},{11,10... | collective-permute-start | bytes 2359304 | tf_op jit(solution)/shard_map/ppermute | solution.py:387
  7.8 2.0 %collective-permute-start.3 = (bf16[8,144,128]{2,1,0:T(8,128)(2,1)S(1)}, bf16[8,144,128]{2,1,0:T(8,128)(2,1)S(1)}, u32[]{:S(2)}, u32[]{:S(2)}) collective-permute-start(bf16[8,144,128]{2,1,0:T(8,128)(2,1)S(1)} %get-tuple-element.61), channel_id=1, source_target_pairs={{0,2},{2,0},{4,6},{6,4},{8,10},{10,8},{12,14},{14,12},{16,18},{18,... | collective-permute-start | bytes 884744 | tf_op jit(solution)/shard_map/ppermute | solution.py:367
  7.9 1.9 %collective-permute-start.2 = (bf16[8,128,128]{2,1,0:T(8,128)(2,1)S(1)}, bf16[8,128,128]{2,1,0:T(8,128)(2,1)S(1)}, u32[]{:S(2)}, u32[]{:S(2)}) collective-permute-start(bf16[8,128,128]{2,1,0:T(8,128)(2,1)S(1)} %get-tuple-element.60), channel_id=1, source_target_pairs={{0,2},{2,0},{4,6},{6,4},{8,10},{10,8},{12,14},{14,12},{16,18},{18,... | collective-permute-start | bytes 786440 | tf_op jit(solution)/shard_map/ppermute | solution.py:367
  10.0 7.3 %collective-permute-start.4 = (bf16[3,272,128]{2,1,0:T(8,128)(2,1)S(1)}, bf16[3,272,128]{2,1,0:T(8,128)(2,1)S(1)}, u32[]{:S(2)}, u32[]{:S(2)}) collective-permute-start(bf16[3,272,128]{2,1,0:T(8,128)(2,1)S(1)} %get-tuple-element.63), channel_id=1, source_target_pairs={{0,4},{2,6},{4,0},{6,2},{8,12},{10,14},{12,8},{14,10},{16,20},{18,... | collective-permute-start | bytes 626696 | tf_op jit(solution)/shard_map/ppermute | solution.py:345
  11.6 9.6 %collective-permute-start.5 = (bf16[272,128]{1,0:T(8,128)(2,1)S(1)}, bf16[272,128]{1,0:T(8,128)(2,1)S(1)}, u32[]{:S(2)}, u32[]{:S(2)}) collective-permute-start(bf16[272,128]{1,0:T(8,128)(2,1)S(1)} %get-tuple-element.65), channel_id=1, source_target_pairs={{0,16},{2,18},{4,20},{6,22},{8,24},{10,26},{12,28},{14,30},{16,0},... | collective-permute-start | bytes 208904 | tf_op jit(solution)/shard_map/ppermute | solution.py:347
  14.1 7.0 %collective-permute-start.6 = (bf16[272,128]{1,0:T(8,128)(2,1)S(1)}, bf16[272,128]{1,0:T(8,128)(2,1)S(1)}, u32[]{:S(2)}, u32[]{:S(2)}) collective-permute-start(bf16[272,128]{1,0:T(8,128)(2,1)S(1)} %get-tuple-element.66), channel_id=1, source_target_pairs={{0,20},{2,22},{4,16},{6,18},{8,28},{10,30},{12,24},{14,26},{16,4},... | collective-permute-start | bytes 208904 | tf_op jit(solution)/shard_map/ppermute | solution.py:347
  17.3 6.9 %collective-permute-start.7 = (bf16[272,128]{1,0:T(8,128)(2,1)S(1)}, bf16[272,128]{1,0:T(8,128)(2,1)S(1)}, u32[]{:S(2)}, u32[]{:S(2)}) collective-permute-start(bf16[272,128]{1,0:T(8,128)(2,1)S(1)} %get-tuple-element.67), channel_id=1, source_target_pairs={{0,8},{2,10},{4,12},{6,14},{8,16},{10,18},{12,20},{14,22},{16,24},... | collective-permute-start | bytes 208904 | tf_op jit(solution)/shard_map/ppermute | solution.py:353
  18.9 5.7 %collective-permute-start.8 = (bf16[272,128]{1,0:T(8,128)(2,1)S(1)}, bf16[272,128]{1,0:T(8,128)(2,1)S(1)}, u32[]{:S(2)}, u32[]{:S(2)}) collective-permute-start(bf16[272,128]{1,0:T(8,128)(2,1)S(1)} %get-tuple-element.68), channel_id=1, source_target_pairs={{0,24},{2,26},{4,28},{6,30},{8,0},{10,2},{12,4},{14,6},{16,8},{18,... | collective-permute-start | bytes 208904 | tf_op jit(solution)/shard_map/ppermute | solution.py:353

commit v14 on v13

--- a/solution.py
+++ b/solution.py
@@ -15,6 +15,7 @@
 tile_width = 512
 pair = 2
 block_rows = 32
+band_width = 256
 f32 = jnp.float32
 bf16 = jnp.bfloat16
 contract_last = (((1,), (1,)), ((), ()))
@@ -48,7 +49,7 @@
 def branch_kernel(
     low, counts_far, x_far, top_far, v_far, w_far, gain_far,
     packed, addend, scatter, more, normed, masked, gain_out,
-    counts, x, top, v, w, gain, back, gain_part, sent, ready,
+    counts, x, top, v, w, gain, back, sent, ready,
 ):
     rows, width = addend.shape
     micro_count = counts.shape[0]
@@ -78,22 +79,22 @@
     scatter[...] = jnp.where(receives, gather.astype(f32), 0.0).astype(bf16)
     gather = jnp.transpose(gather.astype(f32)).astype(bf16)
     values = masked[...]
-    fetches[2].wait()
-    for cut in cuts(width, tile_width):
-        back[:, cut] = lax.dot_general(values, w[cut, :], contract_last, preferred_element_type=f32)
-    fetches[3].wait()
-    fetches[4].wait()
+    for fetch in fetches[2:5]:
+        fetch.wait()
     blocks = [slice(at, at + block_rows) for at in range(0, rows, block_rows)]
-    squares, products = [], []
-    for part in blocks:
-        square = jnp.zeros((block_rows, lanes), f32)
-        product = jnp.zeros((block_rows, lanes), f32)
-        for cut in cuts(width, lanes):
-            wide = x[part, cut].astype(f32)
-            square += wide * wide
-            product += wide * back[part, cut] * gain[:, cut]
-        squares.append(square)
-        products.append(product)
+    squares = [jnp.zeros((block_rows, lanes), f32) for _ in blocks]
+    products = [jnp.zeros((block_rows, lanes), f32) for _ in blocks]
+    for tile in range(0, width, tile_width):
+        here = lax.dot_general(
+            values, w[tile : tile + tile_width, :], contract_last, preferred_element_type=f32
+        )
+        back[:, tile : tile + tile_width] = here
+        for k, part in enumerate(blocks):
+            for at in range(0, tile_width, lanes):
+                cut = pl.ds(tile + at, lanes)
+                wide = x[part, cut].astype(f32)
+                squares[k] += wide * wide
+                products[k] += wide * here[part, at : at + lanes] * gain[:, cut]
     scales = lax.rsqrt(jnp.sum(jnp.concatenate(squares, axis=0), axis=1, keepdims=True) / width + eps_norm)
     pulls = scales * jnp.sum(jnp.concatenate(products, axis=0), axis=1, keepdims=True) / width
     waits = jnp.concatenate(
@@ -103,26 +104,25 @@
         ],
         axis=0,
     )
+    spread = (rows, band_width)
+    scales = jnp.broadcast_to(scales, spread)
+    pulls = jnp.broadcast_to(pulls, spread)
+    waits = jnp.broadcast_to(waits, spread)
     fetches[5].wait()
-    for part in blocks:
-        scale, pull, wait = scales[part], pulls[part], waits[part]
-        for cut in cuts(width, 2 * lanes):
-            unit = x[part, cut].astype(f32) * scale
+    for cut in cuts(width, band_width):
+        scaled = gain[:, cut]
+        partial = jnp.zeros((sublanes, band_width), f32)
+        for part in blocks:
+            unit = x[part, cut].astype(f32) * scales[part]
             here = back[part, cut]
-            scaled = gain[:, cut]
-            product = (unit * here).reshape(block_rows // sublanes, sublanes, 2 * lanes).sum(axis=0)
-            if part.start:
-                product += gain_part[:, cut]
-            gain_part[:, cut] = product
+            partial += (unit * here).reshape(block_rows // sublanes, sublanes, band_width).sum(axis=0)
             normed[part, cut] = (unit * scaled).astype(bf16)
-            own = scale * (scaled * here - unit * pull)
+            own = scales[part] * (scaled * here - unit * pulls[part])
             whole = top[part, cut].astype(f32) + own
             sent[part, cut] = whole.astype(bf16)
-            addend[part, cut] = jnp.where(wait, own, whole)
-    for cut in cuts(width, tile_width):
+            addend[part, cut] = jnp.where(waits[part], own, whole)
+        gain_out[:, cut] = jnp.sum(partial, axis=0, keepdims=True)
         packed[:, cut] = jnp.dot(gather, sent[:, cut], preferred_element_type=f32).astype(bf16)
-    for cut in cuts(width, tile_width):
-        gain_out[:, cut] = jnp.sum(gain_part[:, cut], axis=0, keepdims=True)
 
 
 def branch_rows(low, room, counts, x, top, v, w, gain):
@@ -149,7 +149,6 @@
             pltpu.VMEM((width, depth), bf16),
             pltpu.VMEM((1, width), f32),
             pltpu.VMEM((rows, width), f32),
-            pltpu.VMEM((sublanes, width), f32),
             pltpu.VMEM((rows, width), bf16),
             pltpu.SemaphoreType.DMA((6,)),
         ],

time: 26.3 us -> 26.3 us (level)
  no operation moved by 1% of the time
where the time goes in v14:
time: 26.3 us; the launch traced here: 26.1 us
  starting transfers between devices  11.9 us (45%)
  waiting for transfers between devices  7.9 us (30%)
  Pallas kernels  5.62 us (21%)
  between operations  0.68 us (3%)
    ppermute x2, starting transfers between devices, plane_parts(): arrived.append(lax.ppermute(part, 'dp', along(offset, 0)))  3.88 us
    pallas_call x1, Pallas kernels, branch_rows(): pl.pallas_call(functools.partial(branch_kernel, low), in_specs=[pl.BlockS...  3.56 us
    ppermute x2, waiting for transfers between devices, plane_parts(): arrived.append(lax.ppermute(part, 'dp', along(offset, 0)))  3.44 us
    ppermute x1, starting transfers between devices, shards(): landed = lax.ppermute(packed, 'section', hops)  3 us
    ppermute x2, starting transfers between devices, plane_parts(): lax.ppermute(straight[2 * k + side], 'dp', along(offset, side))  2.86 us
    ppermute x1, waiting for transfers between devices, plane_parts(): across = lax.ppermute(give, 'dp', along(0, 1))  2.82 us
    ppermute x1, starting transfers between devices, plane_parts(): across = lax.ppermute(give, 'dp', along(0, 1))  1.59 us
    ppermute x2, waiting for transfers between devices, weight_owned(): lax.ppermute(part, 'dp', [(i, i ^ 1) for i in range(owners)])  1.45 us
  transfers between devices with their start and end apart: 8, of which 5 were waited for; matrix products, arithmetic and copies ran while one was open for 0% of the time, Pallas kernels for 3%

profile of v14, /device:TPU:0, one launch (start us, length us, event | category | flops | bytes accessed | tf_op | source)
XLA Modules:
  0.0 26.1 jit_solution(6896189025693858130)
XLA Ops:
  0.6 3.6 %shard_map.77 = (bf16[96,4096]{1,0:T(8,128)(2,1)S(1)}, f32[128,4096]{1,0:T(8,128)S(1)}, bf16[128,96]{1,0:T(8,128)(2,1)S(1)}, s32[1]{0:T(128)S(4)}, bf16[128,4096...) custom-call(s32[8]{0:T(128)} %counts_far.1, bf16[1,128,4096]{2,1,0:T(8,128)(2,1)} %x_far.1, ...), custom_call_target="tpu_custom_call" | custom-call | flops 1048576 | bytes 65536 | tf_op jit(solution)/shard_map/pallas_call | solution.py:131
  4.2 3.0 %collective-permute-start.1 = (bf16[96,4096]{1,0:T(8,128)(2,1)S(1)}, bf16[96,4096]{1,0:T(8,128)(2,1)S(1)}, u32[]{:S(2)}, u32[]{:S(2)}) collective-permute-start(bf16[96,4096]{1,0:T(8,128)(2,1)S(1)} %get-tuple-element.53), channel_id=1, source_target_pairs={{1,0},{0,1},{3,2},{2,3},{5,4},{4,5},{7,6},{6,7},{9,8},{8,9},{11,10... | collective-permute-start | bytes 2359304 | tf_op jit(solution)/shard_map/ppermute | solution.py:386
  7.2 0.6 %shard_map.78 = (f32[8,272,128]{2,1,0:T(8,128)S(1)}, bf16[8,128,128]{2,1,0:T(8,128)(2,1)S(1)}, bf16[8,144,128]{2,1,0:T(8,128)(2,1)S(1)}) custom-call(bf16[128,4096]{1,0:T(8,128)(2,1)S(1)} %get-tuple-element.56.normed, bf16[128,128]{1,0:T(8,128)(2,1)S(1)} %get-tuple-element.57.masked, f32[1,4096]{1,0:T(1,128)S(1)} %get-tuple-element.58.gain), custom_call_target="tpu_custom_call" | custom-call | flops 1048576 | bytes 65536 | tf_op jit(solution)/shard_map/pallas_call | solution.py:256
  7.8 0.1 collective-permute-start.3
  7.8 0.5 %collective-permute-start.2 = (bf16[8,128,128]{2,1,0:T(8,128)(2,1)S(1)}, bf16[8,128,128]{2,1,0:T(8,128)(2,1)S(1)}, u32[]{:S(2)}, u32[]{:S(2)}) collective-permute-start(bf16[8,128,128]{2,1,0:T(8,128)(2,1)S(1)} %get-tuple-element.60), channel_id=1, source_target_pairs={{0,2},{2,0},{4,6},{6,4},{8,10},{10,8},{12,14},{14,12},{16,18},{18,... | collective-permute-start | bytes 786440 | tf_op jit(solution)/shard_map/ppermute | solution.py:366
  8.3 1.4 %collective-permute-done.2.taken = bf16[8,128,128]{2,1,0:T(8,128)(2,1)S(1)} collective-permute-done((bf16[8,128,128]{2,1,0:T(8,128)(2,1)S(1)}, bf16[8,128,128]{2,1,0:T(8,128)(2,1)S(1)}, u32[]{:S(2)}, u32[]{:S(2)}) %collective-permute-start.2) | collective-permute-done | bytes 262176 | tf_op jit(solution)/shard_map/ppermute | solution.py:366
  9.8 0.0 collective-permute-done.3.taken_low
  9.8 0.1 shard_map.79
  9.9 1.6 %collective-permute-start.4 = (bf16[3,272,128]{2,1,0:T(8,128)(2,1)S(1)}, bf16[3,272,128]{2,1,0:T(8,128)(2,1)S(1)}, u32[]{:S(2)}, u32[]{:S(2)}) collective-permute-start(bf16[3,272,128]{2,1,0:T(8,128)(2,1)S(1)} %get-tuple-element.63), channel_id=1, source_target_pairs={{0,4},{2,6},{4,0},{6,2},{8,12},{10,14},{12,8},{14,10},{16,20},{18,... | collective-permute-start | bytes 626696 | tf_op jit(solution)/shard_map/ppermute | solution.py:344
  11.5 2.6 %collective-permute-start.5 = (bf16[272,128]{1,0:T(8,128)(2,1)S(1)}, bf16[272,128]{1,0:T(8,128)(2,1)S(1)}, u32[]{:S(2)}, u32[]{:S(2)}) collective-permute-start(bf16[272,128]{1,0:T(8,128)(2,1)S(1)} %get-tuple-element.65), channel_id=1, source_target_pairs={{0,16},{2,18},{4,20},{6,22},{8,24},{10,26},{12,28},{14,30},{16,0},... | collective-permute-start | bytes 208904 | tf_op jit(solution)/shard_map/ppermute | solution.py:346
  14.1 0.3 %collective-permute-start.6 = (bf16[272,128]{1,0:T(8,128)(2,1)S(1)}, bf16[272,128]{1,0:T(8,128)(2,1)S(1)}, u32[]{:S(2)}, u32[]{:S(2)}) collective-permute-start(bf16[272,128]{1,0:T(8,128)(2,1)S(1)} %get-tuple-element.66), channel_id=1, source_target_pairs={{0,20},{2,22},{4,16},{6,18},{8,28},{10,30},{12,24},{14,26},{16,4},... | collective-permute-start | bytes 208904 | tf_op jit(solution)/shard_map/ppermute | solution.py:346
  14.4 2.8 %collective-permute-done.4.taken = bf16[3,272,128]{2,1,0:T(8,128)(2,1)S(1)} collective-permute-done((bf16[3,272,128]{2,1,0:T(8,128)(2,1)S(1)}, bf16[3,272,128]{2,1,0:T(8,128)(2,1)S(1)}, u32[]{:S(2)}, u32[]{:S(2)}) %collective-permute-start.4) | collective-permute-done | bytes 208928 | tf_op jit(solution)/shard_map/ppermute | solution.py:344
  17.2 0.1 shard_map.80
  17.2 1.6 %collective-permute-start.7 = (bf16[272,128]{1,0:T(8,128)(2,1)S(1)}, bf16[272,128]{1,0:T(8,128)(2,1)S(1)}, u32[]{:S(2)}, u32[]{:S(2)}) collective-permute-start(bf16[272,128]{1,0:T(8,128)(2,1)S(1)} %get-tuple-element.67), channel_id=1, source_target_pairs={{0,8},{2,10},{4,12},{6,14},{8,16},{10,18},{12,20},{14,22},{16,24},... | collective-permute-start | bytes 208904 | tf_op jit(solution)/shard_map/ppermute | solution.py:352
  18.9 2.2 %collective-permute-start.8 = (bf16[272,128]{1,0:T(8,128)(2,1)S(1)}, bf16[272,128]{1,0:T(8,128)(2,1)S(1)}, u32[]{:S(2)}, u32[]{:S(2)}) collective-permute-start(bf16[272,128]{1,0:T(8,128)(2,1)S(1)} %get-tuple-element.68), channel_id=1, source_target_pairs={{0,24},{2,26},{4,28},{6,30},{8,0},{10,2},{12,4},{14,6},{16,8},{18,... | collective-permute-start | bytes 208904 | tf_op jit(solution)/shard_map/ppermute | solution.py:352
  21.1 0.0 collective-permute-done.5.refs_1_
  21.1 0.0 collective-permute-done.6.refs_2_
  21.1 3.0 %collective-permute-done.7.refs_3_ = bf16[272,128]{1,0:T(8,128)(2,1)S(1)} collective-permute-done((bf16[272,128]{1,0:T(8,128)(2,1)S(1)}, bf16[272,128]{1,0:T(8,128)(2,1)S(1)}, u32[]{:S(2)}, u32[]{:S(2)}) %collective-permute-start.7) | collective-permute-done | bytes 69664 | tf_op jit(solution)/shard_map/ppermute | solution.py:352
  24.1 0.4 %collective-permute-done.8.refs_4_ = bf16[272,128]{1,0:T(8,128)(2,1)S(1)} collective-permute-done((bf16[272,128]{1,0:T(8,128)(2,1)S(1)}, bf16[272,128]{1,0:T(8,128)(2,1)S(1)}, u32[]{:S(2)}, u32[]{:S(2)}) %collective-permute-start.8) | collective-permute-done | bytes 69664 | tf_op jit(solution)/shard_map/ppermute | solution.py:352
  24.5 0.2 collective-permute-done.1.received
  24.7 1.3 %shard_map.81 = (bf16[1,128,4096]{2,1,0:T(8,128)(2,1)}, s32[1]{0:T(128)S(4)}, f32[1,33024]{1,0:T(1,128)}) custom-call(bf16[128,96]{1,0:T(8,128)(2,1)S(1)} %get-tuple-element.52.scatter, bf16[96,4096]{1,0:T(8,128)(2,1)S(1)} %collective-permute-done.1.received, f32[128,4096]{1,0:T(8,128)S(1)} %get-tuple-element.54.addend, s32[1]{0:T(128)S(4)} %get-tuple-element.55.more, ...), custom_call_target="tpu_custom_call" | custom-call | flops 1048576 | bytes 65536 | tf_op jit(solution)/shard_map/pallas_call | solution.py:216
  (1 shorter events, 0.0 us)
Async XLA Ops:
  4.2 20.5 %collective-permute-start.1 = (bf16[96,4096]{1,0:T(8,128)(2,1)S(1)}, bf16[96,4096]{1,0:T(8,128)(2,1)S(1)}, u32[]{:S(2)}, u32[]{:S(2)}) collective-permute-start(bf16[96,4096]{1,0:T(8,128)(2,1)S(1)} %get-tuple-element.53), channel_id=1, source_target_pairs={{1,0},{0,1},{3,2},{2,3},{5,4},{4,5},{7,6},{6,7},{9,8},{8,9},{11,10... | collective-permute-start | bytes 2359304 | tf_op jit(solution)/shard_map/ppermute | solution.py:386
  7.8 2.0 %collective-permute-start.3 = (bf16[8,144,128]{2,1,0:T(8,128)(2,1)S(1)}, bf16[8,144,128]{2,1,0:T(8,128)(2,1)S(1)}, u32[]{:S(2)}, u32[]{:S(2)}) collective-permute-start(bf16[8,144,128]{2,1,0:T(8,128)(2,1)S(1)} %get-tuple-element.61), channel_id=1, source_target_pairs={{0,2},{2,0},{4,6},{6,4},{8,10},{10,8},{12,14},{14,12},{16,18},{18,... | collective-permute-start | bytes 884744 | tf_op jit(solution)/shard_map/ppermute | solution.py:366
  7.8 1.9 %collective-permute-start.2 = (bf16[8,128,128]{2,1,0:T(8,128)(2,1)S(1)}, bf16[8,128,128]{2,1,0:T(8,128)(2,1)S(1)}, u32[]{:S(2)}, u32[]{:S(2)}) collective-permute-start(bf16[8,128,128]{2,1,0:T(8,128)(2,1)S(1)} %get-tuple-element.60), channel_id=1, source_target_pairs={{0,2},{2,0},{4,6},{6,4},{8,10},{10,8},{12,14},{14,12},{16,18},{18,... | collective-permute-start | bytes 786440 | tf_op jit(solution)/shard_map/ppermute | solution.py:366
  9.9 7.3 %collective-permute-start.4 = (bf16[3,272,128]{2,1,0:T(8,128)(2,1)S(1)}, bf16[3,272,128]{2,1,0:T(8,128)(2,1)S(1)}, u32[]{:S(2)}, u32[]{:S(2)}) collective-permute-start(bf16[3,272,128]{2,1,0:T(8,128)(2,1)S(1)} %get-tuple-element.63), channel_id=1, source_target_pairs={{0,4},{2,6},{4,0},{6,2},{8,12},{10,14},{12,8},{14,10},{16,20},{18,... | collective-permute-start | bytes 626696 | tf_op jit(solution)/shard_map/ppermute | solution.py:344
  11.5 9.6 %collective-permute-start.5 = (bf16[272,128]{1,0:T(8,128)(2,1)S(1)}, bf16[272,128]{1,0:T(8,128)(2,1)S(1)}, u32[]{:S(2)}, u32[]{:S(2)}) collective-permute-start(bf16[272,128]{1,0:T(8,128)(2,1)S(1)} %get-tuple-element.65), channel_id=1, source_target_pairs={{0,16},{2,18},{4,20},{6,22},{8,24},{10,26},{12,28},{14,30},{16,0},... | collective-permute-start | bytes 208904 | tf_op jit(solution)/shard_map/ppermute | solution.py:346
  14.1 7.0 %collective-permute-start.6 = (bf16[272,128]{1,0:T(8,128)(2,1)S(1)}, bf16[272,128]{1,0:T(8,128)(2,1)S(1)}, u32[]{:S(2)}, u32[]{:S(2)}) collective-permute-start(bf16[272,128]{1,0:T(8,128)(2,1)S(1)} %get-tuple-element.66), channel_id=1, source_target_pairs={{0,20},{2,22},{4,16},{6,18},{8,28},{10,30},{12,24},{14,26},{16,4},... | collective-permute-start | bytes 208904 | tf_op jit(solution)/shard_map/ppermute | solution.py:346
  17.2 6.9 %collective-permute-start.7 = (bf16[272,128]{1,0:T(8,128)(2,1)S(1)}, bf16[272,128]{1,0:T(8,128)(2,1)S(1)}, u32[]{:S(2)}, u32[]{:S(2)}) collective-permute-start(bf16[272,128]{1,0:T(8,128)(2,1)S(1)} %get-tuple-element.67), channel_id=1, source_target_pairs={{0,8},{2,10},{4,12},{6,14},{8,16},{10,18},{12,20},{14,22},{16,24},... | collective-permute-start | bytes 208904 | tf_op jit(solution)/shard_map/ppermute | solution.py:352
  18.9 5.7 %collective-permute-start.8 = (bf16[272,128]{1,0:T(8,128)(2,1)S(1)}, bf16[272,128]{1,0:T(8,128)(2,1)S(1)}, u32[]{:S(2)}, u32[]{:S(2)}) collective-permute-start(bf16[272,128]{1,0:T(8,128)(2,1)S(1)} %get-tuple-element.68), channel_id=1, source_target_pairs={{0,24},{2,26},{4,28},{6,30},{8,0},{10,2},{12,4},{14,6},{16,8},{18,... | collective-permute-start | bytes 208904 | tf_op jit(solution)/shard_map/ppermute | solution.py:352

commit v15 on v14

--- a/solution.py
+++ b/solution.py
@@ -62,7 +62,7 @@
         pltpu.make_async_copy(gain_far, gain, ready.at[4]),
         pltpu.make_async_copy(top_far, top, ready.at[5]),
     ]
-    for fetch in fetches:
+    for fetch in fetches[:5]:
         fetch.start()
     fetches[0].wait()
     fetches[1].wait()
@@ -79,6 +79,7 @@
     scatter[...] = jnp.where(receives, gather.astype(f32), 0.0).astype(bf16)
     gather = jnp.transpose(gather.astype(f32)).astype(bf16)
     values = masked[...]
+    fetches[5].start()
     for fetch in fetches[2:5]:
         fetch.wait()
     blocks = [slice(at, at + block_rows) for at in range(0, rows, block_rows)]

time: 26.3 us -> 26.3 us (level)
  no operation moved by 1% of the time
where the time goes in v15:
time: 26.3 us; the launch traced here: 26.1 us
  starting transfers between devices  11.9 us (45%)
  waiting for transfers between devices  7.9 us (30%)
  Pallas kernels  5.63 us (21%)
  between operations  0.68 us (3%)
    ppermute x2, starting transfers between devices, plane_parts(): arrived.append(lax.ppermute(part, 'dp', along(offset, 0)))  3.88 us
    pallas_call x1, Pallas kernels, branch_rows(): pl.pallas_call(functools.partial(branch_kernel, low), in_specs=[pl.BlockS...  3.57 us
    ppermute x2, waiting for transfers between devices, plane_parts(): arrived.append(lax.ppermute(part, 'dp', along(offset, 0)))  3.43 us
    ppermute x1, starting transfers between devices, shards(): landed = lax.ppermute(packed, 'section', hops)  3 us
    ppermute x2, starting transfers between devices, plane_parts(): lax.ppermute(straight[2 * k + side], 'dp', along(offset, side))  2.87 us
    ppermute x1, waiting for transfers between devices, plane_parts(): across = lax.ppermute(give, 'dp', along(0, 1))  2.82 us
    ppermute x1, starting transfers between devices, plane_parts(): across = lax.ppermute(give, 'dp', along(0, 1))  1.59 us
    ppermute x2, waiting for transfers between devices, weight_owned(): lax.ppermute(part, 'dp', [(i, i ^ 1) for i in range(owners)])  1.45 us
  transfers between devices with their start and end apart: 8, of which 5 were waited for; matrix products, arithmetic and copies ran while one was open for 0% of the time, Pallas kernels for 3%

profile of v15, /device:TPU:0, one launch (start us, length us, event | category | flops | bytes accessed | tf_op | source)
XLA Modules:
  0.0 26.1 jit_solution(11303761671328867721)
XLA Ops:
  0.6 3.6 %shard_map.77 = (bf16[96,4096]{1,0:T(8,128)(2,1)S(1)}, f32[128,4096]{1,0:T(8,128)S(1)}, bf16[128,96]{1,0:T(8,128)(2,1)S(1)}, s32[1]{0:T(128)S(4)}, bf16[128,4096...) custom-call(s32[8]{0:T(128)} %counts_far.1, bf16[1,128,4096]{2,1,0:T(8,128)(2,1)} %x_far.1, ...), custom_call_target="tpu_custom_call" | custom-call | flops 1048576 | bytes 65536 | tf_op jit(solution)/shard_map/pallas_call | solution.py:132
  4.2 3.0 %collective-permute-start.1 = (bf16[96,4096]{1,0:T(8,128)(2,1)S(1)}, bf16[96,4096]{1,0:T(8,128)(2,1)S(1)}, u32[]{:S(2)}, u32[]{:S(2)}) collective-permute-start(bf16[96,4096]{1,0:T(8,128)(2,1)S(1)} %get-tuple-element.53), channel_id=1, source_target_pairs={{1,0},{0,1},{3,2},{2,3},{5,4},{4,5},{7,6},{6,7},{9,8},{8,9},{11,10... | collective-permute-start | bytes 2359304 | tf_op jit(solution)/shard_map/ppermute | solution.py:387
  7.2 0.6 %shard_map.78 = (f32[8,272,128]{2,1,0:T(8,128)S(1)}, bf16[8,128,128]{2,1,0:T(8,128)(2,1)S(1)}, bf16[8,144,128]{2,1,0:T(8,128)(2,1)S(1)}) custom-call(bf16[128,4096]{1,0:T(8,128)(2,1)S(1)} %get-tuple-element.56.normed, bf16[128,128]{1,0:T(8,128)(2,1)S(1)} %get-tuple-element.57.masked, f32[1,4096]{1,0:T(1,128)S(1)} %get-tuple-element.58.gain), custom_call_target="tpu_custom_call" | custom-call | flops 1048576 | bytes 65536 | tf_op jit(solution)/shard_map/pallas_call | solution.py:257
  7.8 0.1 collective-permute-start.3
  7.9 0.5 %collective-permute-start.2 = (bf16[8,128,128]{2,1,0:T(8,128)(2,1)S(1)}, bf16[8,128,128]{2,1,0:T(8,128)(2,1)S(1)}, u32[]{:S(2)}, u32[]{:S(2)}) collective-permute-start(bf16[8,128,128]{2,1,0:T(8,128)(2,1)S(1)} %get-tuple-element.60), channel_id=1, source_target_pairs={{0,2},{2,0},{4,6},{6,4},{8,10},{10,8},{12,14},{14,12},{16,18},{18,... | collective-permute-start | bytes 786440 | tf_op jit(solution)/shard_map/ppermute | solution.py:367
  8.4 1.4 %collective-permute-done.2.taken = bf16[8,128,128]{2,1,0:T(8,128)(2,1)S(1)} collective-permute-done((bf16[8,128,128]{2,1,0:T(8,128)(2,1)S(1)}, bf16[8,128,128]{2,1,0:T(8,128)(2,1)S(1)}, u32[]{:S(2)}, u32[]{:S(2)}) %collective-permute-start.2) | collective-permute-done | bytes 262176 | tf_op jit(solution)/shard_map/ppermute | solution.py:367
  9.8 0.0 collective-permute-done.3.taken_low
  9.8 0.1 shard_map.79
  9.9 1.6 %collective-permute-start.4 = (bf16[3,272,128]{2,1,0:T(8,128)(2,1)S(1)}, bf16[3,272,128]{2,1,0:T(8,128)(2,1)S(1)}, u32[]{:S(2)}, u32[]{:S(2)}) collective-permute-start(bf16[3,272,128]{2,1,0:T(8,128)(2,1)S(1)} %get-tuple-element.63), channel_id=1, source_target_pairs={{0,4},{2,6},{4,0},{6,2},{8,12},{10,14},{12,8},{14,10},{16,20},{18,... | collective-permute-start | bytes 626696 | tf_op jit(solution)/shard_map/ppermute | solution.py:345
  11.5 2.6 %collective-permute-start.5 = (bf16[272,128]{1,0:T(8,128)(2,1)S(1)}, bf16[272,128]{1,0:T(8,128)(2,1)S(1)}, u32[]{:S(2)}, u32[]{:S(2)}) collective-permute-start(bf16[272,128]{1,0:T(8,128)(2,1)S(1)} %get-tuple-element.65), channel_id=1, source_target_pairs={{0,16},{2,18},{4,20},{6,22},{8,24},{10,26},{12,28},{14,30},{16,0},... | collective-permute-start | bytes 208904 | tf_op jit(solution)/shard_map/ppermute | solution.py:347
  14.1 0.3 %collective-permute-start.6 = (bf16[272,128]{1,0:T(8,128)(2,1)S(1)}, bf16[272,128]{1,0:T(8,128)(2,1)S(1)}, u32[]{:S(2)}, u32[]{:S(2)}) collective-permute-start(bf16[272,128]{1,0:T(8,128)(2,1)S(1)} %get-tuple-element.66), channel_id=1, source_target_pairs={{0,20},{2,22},{4,16},{6,18},{8,28},{10,30},{12,24},{14,26},{16,4},... | collective-permute-start | bytes 208904 | tf_op jit(solution)/shard_map/ppermute | solution.py:347
  14.4 2.8 %collective-permute-done.4.taken = bf16[3,272,128]{2,1,0:T(8,128)(2,1)S(1)} collective-permute-done((bf16[3,272,128]{2,1,0:T(8,128)(2,1)S(1)}, bf16[3,272,128]{2,1,0:T(8,128)(2,1)S(1)}, u32[]{:S(2)}, u32[]{:S(2)}) %collective-permute-start.4) | collective-permute-done | bytes 208928 | tf_op jit(solution)/shard_map/ppermute | solution.py:345
  17.2 0.1 shard_map.80
  17.2 1.6 %collective-permute-start.7 = (bf16[272,128]{1,0:T(8,128)(2,1)S(1)}, bf16[272,128]{1,0:T(8,128)(2,1)S(1)}, u32[]{:S(2)}, u32[]{:S(2)}) collective-permute-start(bf16[272,128]{1,0:T(8,128)(2,1)S(1)} %get-tuple-element.67), channel_id=1, source_target_pairs={{0,8},{2,10},{4,12},{6,14},{8,16},{10,18},{12,20},{14,22},{16,24},... | collective-permute-start | bytes 208904 | tf_op jit(solution)/shard_map/ppermute | solution.py:353
  18.9 2.2 %collective-permute-start.8 = (bf16[272,128]{1,0:T(8,128)(2,1)S(1)}, bf16[272,128]{1,0:T(8,128)(2,1)S(1)}, u32[]{:S(2)}, u32[]{:S(2)}) collective-permute-start(bf16[272,128]{1,0:T(8,128)(2,1)S(1)} %get-tuple-element.68), channel_id=1, source_target_pairs={{0,24},{2,26},{4,28},{6,30},{8,0},{10,2},{12,4},{14,6},{16,8},{18,... | collective-permute-start | bytes 208904 | tf_op jit(solution)/shard_map/ppermute | solution.py:353
  21.1 0.0 collective-permute-done.5.refs_1_
  21.1 0.0 collective-permute-done.6.refs_2_
  21.1 3.0 %collective-permute-done.7.refs_3_ = bf16[272,128]{1,0:T(8,128)(2,1)S(1)} collective-permute-done((bf16[272,128]{1,0:T(8,128)(2,1)S(1)}, bf16[272,128]{1,0:T(8,128)(2,1)S(1)}, u32[]{:S(2)}, u32[]{:S(2)}) %collective-permute-start.7) | collective-permute-done | bytes 69664 | tf_op jit(solution)/shard_map/ppermute | solution.py:353
  24.1 0.4 %collective-permute-done.8.refs_4_ = bf16[272,128]{1,0:T(8,128)(2,1)S(1)} collective-permute-done((bf16[272,128]{1,0:T(8,128)(2,1)S(1)}, bf16[272,128]{1,0:T(8,128)(2,1)S(1)}, u32[]{:S(2)}, u32[]{:S(2)}) %collective-permute-start.8) | collective-permute-done | bytes 69664 | tf_op jit(solution)/shard_map/ppermute | solution.py:353
  24.6 0.2 collective-permute-done.1.received
  24.8 1.3 %shard_map.81 = (bf16[1,128,4096]{2,1,0:T(8,128)(2,1)}, s32[1]{0:T(128)S(4)}, f32[1,33024]{1,0:T(1,128)}) custom-call(bf16[128,96]{1,0:T(8,128)(2,1)S(1)} %get-tuple-element.52.scatter, bf16[96,4096]{1,0:T(8,128)(2,1)S(1)} %collective-permute-done.1.received, f32[128,4096]{1,0:T(8,128)S(1)} %get-tuple-element.54.addend, s32[1]{0:T(128)S(4)} %get-tuple-element.55.more, ...), custom_call_target="tpu_custom_call" | custom-call | flops 1048576 | bytes 65536 | tf_op jit(solution)/shard_map/pallas_call | solution.py:217
  (1 shorter events, 0.0 us)
Async XLA Ops:
  4.2 20.5 %collective-permute-start.1 = (bf16[96,4096]{1,0:T(8,128)(2,1)S(1)}, bf16[96,4096]{1,0:T(8,128)(2,1)S(1)}, u32[]{:S(2)}, u32[]{:S(2)}) collective-permute-start(bf16[96,4096]{1,0:T(8,128)(2,1)S(1)} %get-tuple-element.53), channel_id=1, source_target_pairs={{1,0},{0,1},{3,2},{2,3},{5,4},{4,5},{7,6},{6,7},{9,8},{8,9},{11,10... | collective-permute-start | bytes 2359304 | tf_op jit(solution)/shard_map/ppermute | solution.py:387
  7.8 2.0 %collective-permute-start.3 = (bf16[8,144,128]{2,1,0:T(8,128)(2,1)S(1)}, bf16[8,144,128]{2,1,0:T(8,128)(2,1)S(1)}, u32[]{:S(2)}, u32[]{:S(2)}) collective-permute-start(bf16[8,144,128]{2,1,0:T(8,128)(2,1)S(1)} %get-tuple-element.61), channel_id=1, source_target_pairs={{0,2},{2,0},{4,6},{6,4},{8,10},{10,8},{12,14},{14,12},{16,18},{18,... | collective-permute-start | bytes 884744 | tf_op jit(solution)/shard_map/ppermute | solution.py:367
  7.9 1.9 %collective-permute-start.2 = (bf16[8,128,128]{2,1,0:T(8,128)(2,1)S(1)}, bf16[8,128,128]{2,1,0:T(8,128)(2,1)S(1)}, u32[]{:S(2)}, u32[]{:S(2)}) collective-permute-start(bf16[8,128,128]{2,1,0:T(8,128)(2,1)S(1)} %get-tuple-element.60), channel_id=1, source_target_pairs={{0,2},{2,0},{4,6},{6,4},{8,10},{10,8},{12,14},{14,12},{16,18},{18,... | collective-permute-start | bytes 786440 | tf_op jit(solution)/shard_map/ppermute | solution.py:367
  9.9 7.3 %collective-permute-start.4 = (bf16[3,272,128]{2,1,0:T(8,128)(2,1)S(1)}, bf16[3,272,128]{2,1,0:T(8,128)(2,1)S(1)}, u32[]{:S(2)}, u32[]{:S(2)}) collective-permute-start(bf16[3,272,128]{2,1,0:T(8,128)(2,1)S(1)} %get-tuple-element.63), channel_id=1, source_target_pairs={{0,4},{2,6},{4,0},{6,2},{8,12},{10,14},{12,8},{14,10},{16,20},{18,... | collective-permute-start | bytes 626696 | tf_op jit(solution)/shard_map/ppermute | solution.py:345
  11.5 9.6 %collective-permute-start.5 = (bf16[272,128]{1,0:T(8,128)(2,1)S(1)}, bf16[272,128]{1,0:T(8,128)(2,1)S(1)}, u32[]{:S(2)}, u32[]{:S(2)}) collective-permute-start(bf16[272,128]{1,0:T(8,128)(2,1)S(1)} %get-tuple-element.65), channel_id=1, source_target_pairs={{0,16},{2,18},{4,20},{6,22},{8,24},{10,26},{12,28},{14,30},{16,0},... | collective-permute-start | bytes 208904 | tf_op jit(solution)/shard_map/ppermute | solution.py:347
  14.1 7.0 %collective-permute-start.6 = (bf16[272,128]{1,0:T(8,128)(2,1)S(1)}, bf16[272,128]{1,0:T(8,128)(2,1)S(1)}, u32[]{:S(2)}, u32[]{:S(2)}) collective-permute-start(bf16[272,128]{1,0:T(8,128)(2,1)S(1)} %get-tuple-element.66), channel_id=1, source_target_pairs={{0,20},{2,22},{4,16},{6,18},{8,28},{10,30},{12,24},{14,26},{16,4},... | collective-permute-start | bytes 208904 | tf_op jit(solution)/shard_map/ppermute | solution.py:347
  17.2 6.9 %collective-permute-start.7 = (bf16[272,128]{1,0:T(8,128)(2,1)S(1)}, bf16[272,128]{1,0:T(8,128)(2,1)S(1)}, u32[]{:S(2)}, u32[]{:S(2)}) collective-permute-start(bf16[272,128]{1,0:T(8,128)(2,1)S(1)} %get-tuple-element.67), channel_id=1, source_target_pairs={{0,8},{2,10},{4,12},{6,14},{8,16},{10,18},{12,20},{14,22},{16,24},... | collective-permute-start | bytes 208904 | tf_op jit(solution)/shard_map/ppermute | solution.py:353
  18.9 5.7 %collective-permute-start.8 = (bf16[272,128]{1,0:T(8,128)(2,1)S(1)}, bf16[272,128]{1,0:T(8,128)(2,1)S(1)}, u32[]{:S(2)}, u32[]{:S(2)}) collective-permute-start(bf16[272,128]{1,0:T(8,128)(2,1)S(1)} %get-tuple-element.68), channel_id=1, source_target_pairs={{0,24},{2,26},{4,28},{6,30},{8,0},{10,2},{12,4},{14,6},{16,8},{18,... | collective-permute-start | bytes 208904 | tf_op jit(solution)/shard_map/ppermute | solution.py:353

commit v16 on v14

--- a/solution.py
+++ b/solution.py
@@ -48,8 +48,8 @@
 
 def branch_kernel(
     low, counts_far, x_far, top_far, v_far, w_far, gain_far,
-    packed, addend, scatter, more, normed, masked, gain_out,
-    counts, x, top, v, w, gain, back, sent, ready,
+    packed, addend, scatter, more, masked, x, back, scale_out, gain,
+    counts, top, v, w, sent, ready,
 ):
     rows, width = addend.shape
     micro_count = counts.shape[0]
@@ -106,22 +106,19 @@
     )
     spread = (rows, band_width)
     scales = jnp.broadcast_to(scales, spread)
+    scale_out[...] = scales[:, :lanes]
     pulls = jnp.broadcast_to(pulls, spread)
     waits = jnp.broadcast_to(waits, spread)
     fetches[5].wait()
     for cut in cuts(width, band_width):
         scaled = gain[:, cut]
-        partial = jnp.zeros((sublanes, band_width), f32)
         for part in blocks:
             unit = x[part, cut].astype(f32) * scales[part]
             here = back[part, cut]
-            partial += (unit * here).reshape(block_rows // sublanes, sublanes, band_width).sum(axis=0)
-            normed[part, cut] = (unit * scaled).astype(bf16)
             own = scales[part] * (scaled * here - unit * pulls[part])
             whole = top[part, cut].astype(f32) + own
             sent[part, cut] = whole.astype(bf16)
             addend[part, cut] = jnp.where(waits[part], own, whole)
-        gain_out[:, cut] = jnp.sum(partial, axis=0, keepdims=True)
         packed[:, cut] = jnp.dot(gather, sent[:, cut], preferred_element_type=f32).astype(bf16)
 
 
@@ -131,24 +128,23 @@
     return pl.pallas_call(
         functools.partial(branch_kernel, low),
         in_specs=[pl.BlockSpec(memory_space=pltpu.HBM)] * 6,
-        out_specs=[near] * 3 + [scalar] + [near] * 3,
+        out_specs=[near] * 3 + [scalar] + [near] * 5,
         out_shape=[
             jax.ShapeDtypeStruct((room, width), bf16),
             jax.ShapeDtypeStruct((rows, width), f32),
             jax.ShapeDtypeStruct((rows, room), bf16),
             pltpu.SMEM((1,), jnp.int32),
+            jax.ShapeDtypeStruct((rows, depth), bf16),
             jax.ShapeDtypeStruct((rows, width), bf16),
-            jax.ShapeDtypeStruct((rows, depth), bf16),
+            jax.ShapeDtypeStruct((rows, width), f32),
+            jax.ShapeDtypeStruct((rows, lanes), f32),
             jax.ShapeDtypeStruct((1, width), f32),
         ],
         scratch_shapes=[
             pltpu.SMEM(counts.shape, jnp.int32),
             pltpu.VMEM((rows, width), bf16),
-            pltpu.VMEM((rows, width), bf16),
             pltpu.VMEM((rows, depth), bf16),
             pltpu.VMEM((width, depth), bf16),
-            pltpu.VMEM((1, width), f32),
-            pltpu.VMEM((rows, width), f32),
             pltpu.VMEM((rows, width), bf16),
             pltpu.SemaphoreType.DMA((6,)),
         ],
@@ -224,15 +220,22 @@
     )(scatter, received, addend, more, *others)
 
 
-def terms_kernel(owned_rows, normed, masked, gain, keep, give, give_low, total):
-    width = normed.shape[1]
+def terms_kernel(owned_rows, masked, x, back, scale, gain, keep, give, give_low, total):
+    rows, width = x.shape
     values = masked[...]
     gain_rows = width // lanes
-    for k in range(gain_rows):
-        total[k : k + 1, :] = gain[:, k * lanes : (k + 1) * lanes]
-    for at in range(0, width, tile_width):
-        total[gain_rows + at : gain_rows + at + tile_width, :] = lax.dot_general(
-            normed[:, at : at + tile_width], values, contract_rows, preferred_element_type=f32
+    spread = jnp.concatenate([scale[...]] * (band_width // lanes), axis=1)
+    for at in range(0, width, band_width):
+        cut = pl.ds(at, band_width)
+        unit = x[:, cut].astype(f32) * spread
+        summed = (unit * back[:, cut]).reshape(rows // sublanes, sublanes, band_width).sum(axis=0)
+        summed = jnp.sum(summed, axis=0, keepdims=True)
+        for k in range(0, band_width, lanes):
+            spot = (at + k) // lanes
+            total[spot : spot + 1, :] = summed[:, k : k + lanes]
+        normed = (unit * gain[:, cut]).astype(bf16)
+        total[gain_rows + at : gain_rows + at + band_width, :] = lax.dot_general(
+            normed, values, contract_rows, preferred_element_type=f32
         )
     even_core = lax.axis_index("dp") % pair == 0
     padded = keep.shape[1]
@@ -249,13 +252,13 @@
         give_low[j] = other[give.shape[1] :, :]
 
 
-def pair_terms(normed, masked, gain, owned_rows, owners):
+def pair_terms(made, owned_rows, owners):
     padded = -(-owned_rows // pack_rows) * pack_rows
     cut = padded // 2 // pack_rows * pack_rows
     blocks = owners // pair
     return pl.pallas_call(
         functools.partial(terms_kernel, owned_rows),
-        in_specs=[near, near, near],
+        in_specs=[near] * len(made),
         out_specs=[near, near, near],
         out_shape=[
             jax.ShapeDtypeStruct((blocks, padded, lanes), f32),
@@ -265,7 +268,7 @@
         scratch_shapes=[pltpu.VMEM((owners * owned_rows, lanes), f32)],
         compiler_params=roomy,
         cost_estimate=small_cost,
-    )(normed, masked, gain)
+    )(*made)
 
 
 def merge_kernel(offsets, direct, keep, taken, taken_low, hold, give, *straight):
@@ -353,16 +356,19 @@
     return own, *arrived
 
 
-def weight_owned(normed, masked, gain, factor):
+def weight_owned(made, factor):
     owners = lax.axis_size("dp")
-    width = normed.shape[1]
+    masked, x, back, scale, gain = made
+    width = x.shape[1]
     depth = masked.shape[1]
     owned = (width + width * depth) // owners
     if depth != lanes or owned % lanes or owners % (2 * pair):
+        unit = x.astype(f32) * scale[:, :1]
+        normed = (unit * gain).astype(bf16)
         weight_term = lax.dot_general(normed, masked, contract_rows, preferred_element_type=f32)
-        flat = jnp.concatenate([gain.reshape(-1), weight_term.reshape(-1)]) * factor
+        flat = jnp.concatenate([jnp.sum(unit * back, axis=0), weight_term.reshape(-1)]) * factor
         return (), owned, lax.psum_scatter(flat, "dp", scatter_dimension=0, tiled=True)[None, :]
-    keep, *give = pair_terms(normed, masked, gain, owned // lanes, owners)
+    keep, *give = pair_terms(made, owned // lanes, owners)
     taken = [lax.ppermute(part, "dp", [(i, i ^ 1) for i in range(owners)]) for part in give]
     return plane_parts(owners, keep, *taken), owned, None
 
@@ -374,8 +380,8 @@
     room = -(-rows * 3 // 4 // pack_rows) * pack_rows
     spare = rows - room
     inputs = (counts, layer_inputs, top_grad, value_grads, weights, norm_gains)
-    packed, addend, scatter, more, normed, masked, gain = branch_rows(0, room, *inputs)
-    parts, owned_size, owned = weight_owned(normed, masked, gain, factor)
+    packed, addend, scatter, more, *made = branch_rows(0, room, *inputs)
+    parts, owned_size, owned = weight_owned(made, factor)
     result = None
     for hop in range(sections - 1):
         target = sections - 2 - hop

time: 26.3 us -> 26 us (0.989)
    pallas_call x1, Pallas kernels: 3.56 us -> 3.29 us  [branch_rows(): pl.pallas_call(functools.partial(branch_kernel, low), in_specs=[pl.BlockS...]
  transfers between devices with their start and end apart: 8 -> 8, of which waited for: 5 -> 4; matrix products, arithmetic and copies ran while one was open for 0% -> 0% of each run, Pallas kernels for 3% -> 4%
where the time goes in v16:
time: 26 us; the launch traced here: 25.9 us
  starting transfers between devices  11.9 us (46%)
  waiting for transfers between devices  7.71 us (30%)
  Pallas kernels  5.58 us (21%)
  between operations  0.68 us (3%)
    ppermute x2, starting transfers between devices, plane_parts(): arrived.append(lax.ppermute(part, 'dp', along(offset, 0)))  3.88 us
    ppermute x2, waiting for transfers between devices, plane_parts(): arrived.append(lax.ppermute(part, 'dp', along(offset, 0)))  3.43 us
    pallas_call x1, Pallas kernels, branch_rows(): pl.pallas_call(functools.partial(branch_kernel, low), in_specs=[pl.BlockS...  3.29 us
    ppermute x1, starting transfers between devices, shards(): landed = lax.ppermute(packed, 'section', hops)  3.01 us
    ppermute x2, starting transfers between devices, plane_parts(): lax.ppermute(straight[2 * k + side], 'dp', along(offset, side))  2.87 us
    ppermute x1, waiting for transfers between devices, plane_parts(): across = lax.ppermute(give, 'dp', along(0, 1))  2.82 us
    ppermute x1, starting transfers between devices, plane_parts(): across = lax.ppermute(give, 'dp', along(0, 1))  1.58 us
    ppermute x2, waiting for transfers between devices, weight_owned(): lax.ppermute(part, 'dp', [(i, i ^ 1) for i in range(owners)])  1.45 us
  transfers between devices with their start and end apart: 8, of which 4 were waited for; matrix products, arithmetic and copies ran while one was open for 0% of the time, Pallas kernels for 4%

profile of v16, /device:TPU:0, one launch (start us, length us, event | category | flops | bytes accessed | tf_op | source)
XLA Modules:
  0.0 25.9 jit_solution(17614414995526813893)
XLA Ops:
  0.6 3.3 %shard_map.77 = (bf16[96,4096]{1,0:T(8,128)(2,1)S(1)}, f32[128,4096]{1,0:T(8,128)S(1)}, bf16[128,96]{1,0:T(8,128)(2,1)S(1)}, s32[1]{0:T(128)S(4)}, bf16[128,128]...) custom-call(s32[8]{0:T(128)} %counts_far.1, ...), custom_call_target="tpu_custom_call" | custom-call | flops 1048576 | bytes 65536 | tf_op jit(solution)/shard_map/pallas_call | solution.py:128
  3.9 3.0 %collective-permute-start.1 = (bf16[96,4096]{1,0:T(8,128)(2,1)S(1)}, bf16[96,4096]{1,0:T(8,128)(2,1)S(1)}, u32[]{:S(2)}, u32[]{:S(2)}) collective-permute-start(bf16[96,4096]{1,0:T(8,128)(2,1)S(1)} %get-tuple-element.55), channel_id=1, source_target_pairs={{1,0},{0,1},{3,2},{2,3},{5,4},{4,5},{7,6},{6,7},{9,8},{8,9},{11,10... | collective-permute-start | bytes 2359304 | tf_op jit(solution)/shard_map/ppermute | solution.py:392
  6.9 0.8 %shard_map.78 = (f32[8,272,128]{2,1,0:T(8,128)S(1)}, bf16[8,128,128]{2,1,0:T(8,128)(2,1)S(1)}, bf16[8,144,128]{2,1,0:T(8,128)(2,1)S(1)}) custom-call(bf16[128,128]{1,0:T(8,128)(2,1)S(1)} %get-tuple-element.58.masked, bf16[128,4096]{1,0:T(8,128)(2,1)S(1)} %get-tuple-element.59.x, f32[128,4096]{1,0:T(8,128)S(1)} %get-tuple-element.60.back, ...), custom_call_target="tpu_custom_call" | custom-call | flops 1048576 | bytes 65536 | tf_op jit(solution)/shard_map/pallas_call | solution.py:259
  7.7 0.1 collective-permute-start.3
  7.8 0.5 %collective-permute-start.2 = (bf16[8,128,128]{2,1,0:T(8,128)(2,1)S(1)}, bf16[8,128,128]{2,1,0:T(8,128)(2,1)S(1)}, u32[]{:S(2)}, u32[]{:S(2)}) collective-permute-start(bf16[8,128,128]{2,1,0:T(8,128)(2,1)S(1)} %get-tuple-element.64), channel_id=1, source_target_pairs={{0,2},{2,0},{4,6},{6,4},{8,10},{10,8},{12,14},{14,12},{16,18},{18,... | collective-permute-start | bytes 786440 | tf_op jit(solution)/shard_map/ppermute | solution.py:372
  8.3 1.4 %collective-permute-done.2.taken = bf16[8,128,128]{2,1,0:T(8,128)(2,1)S(1)} collective-permute-done((bf16[8,128,128]{2,1,0:T(8,128)(2,1)S(1)}, bf16[8,128,128]{2,1,0:T(8,128)(2,1)S(1)}, u32[]{:S(2)}, u32[]{:S(2)}) %collective-permute-start.2) | collective-permute-done | bytes 262176 | tf_op jit(solution)/shard_map/ppermute | solution.py:372
  9.8 0.0 collective-permute-done.3.taken_low
  9.8 0.1 shard_map.79
  9.9 1.6 %collective-permute-start.4 = (bf16[3,272,128]{2,1,0:T(8,128)(2,1)S(1)}, bf16[3,272,128]{2,1,0:T(8,128)(2,1)S(1)}, u32[]{:S(2)}, u32[]{:S(2)}) collective-permute-start(bf16[3,272,128]{2,1,0:T(8,128)(2,1)S(1)} %get-tuple-element.67), channel_id=1, source_target_pairs={{0,4},{2,6},{4,0},{6,2},{8,12},{10,14},{12,8},{14,10},{16,20},{18,... | collective-permute-start | bytes 626696 | tf_op jit(solution)/shard_map/ppermute | solution.py:347
  11.5 2.6 %collective-permute-start.5 = (bf16[272,128]{1,0:T(8,128)(2,1)S(1)}, bf16[272,128]{1,0:T(8,128)(2,1)S(1)}, u32[]{:S(2)}, u32[]{:S(2)}) collective-permute-start(bf16[272,128]{1,0:T(8,128)(2,1)S(1)} %get-tuple-element.69), channel_id=1, source_target_pairs={{0,16},{2,18},{4,20},{6,22},{8,24},{10,26},{12,28},{14,30},{16,0},... | collective-permute-start | bytes 208904 | tf_op jit(solution)/shard_map/ppermute | solution.py:349
  14.0 0.3 %collective-permute-start.6 = (bf16[272,128]{1,0:T(8,128)(2,1)S(1)}, bf16[272,128]{1,0:T(8,128)(2,1)S(1)}, u32[]{:S(2)}, u32[]{:S(2)}) collective-permute-start(bf16[272,128]{1,0:T(8,128)(2,1)S(1)} %get-tuple-element.70), channel_id=1, source_target_pairs={{0,20},{2,22},{4,16},{6,18},{8,28},{10,30},{12,24},{14,26},{16,4},... | collective-permute-start | bytes 208904 | tf_op jit(solution)/shard_map/ppermute | solution.py:349
  14.3 2.8 %collective-permute-done.4.taken = bf16[3,272,128]{2,1,0:T(8,128)(2,1)S(1)} collective-permute-done((bf16[3,272,128]{2,1,0:T(8,128)(2,1)S(1)}, bf16[3,272,128]{2,1,0:T(8,128)(2,1)S(1)}, u32[]{:S(2)}, u32[]{:S(2)}) %collective-permute-start.4) | collective-permute-done | bytes 208928 | tf_op jit(solution)/shard_map/ppermute | solution.py:347
  17.2 1.6 %collective-permute-start.7 = (bf16[272,128]{1,0:T(8,128)(2,1)S(1)}, bf16[272,128]{1,0:T(8,128)(2,1)S(1)}, u32[]{:S(2)}, u32[]{:S(2)}) collective-permute-start(bf16[272,128]{1,0:T(8,128)(2,1)S(1)} %get-tuple-element.71), channel_id=1, source_target_pairs={{0,8},{2,10},{4,12},{6,14},{8,16},{10,18},{12,20},{14,22},{16,24},... | collective-permute-start | bytes 208904 | tf_op jit(solution)/shard_map/ppermute | solution.py:355
  18.8 2.3 %collective-permute-start.8 = (bf16[272,128]{1,0:T(8,128)(2,1)S(1)}, bf16[272,128]{1,0:T(8,128)(2,1)S(1)}, u32[]{:S(2)}, u32[]{:S(2)}) collective-permute-start(bf16[272,128]{1,0:T(8,128)(2,1)S(1)} %get-tuple-element.72), channel_id=1, source_target_pairs={{0,24},{2,26},{4,28},{6,30},{8,0},{10,2},{12,4},{14,6},{16,8},{18,... | collective-permute-start | bytes 208904 | tf_op jit(solution)/shard_map/ppermute | solution.py:355
  21.1 0.0 collective-permute-done.5.refs_1_
  21.1 0.0 collective-permute-done.6.refs_2_
  21.1 3.0 %collective-permute-done.7.refs_3_ = bf16[272,128]{1,0:T(8,128)(2,1)S(1)} collective-permute-done((bf16[272,128]{1,0:T(8,128)(2,1)S(1)}, bf16[272,128]{1,0:T(8,128)(2,1)S(1)}, u32[]{:S(2)}, u32[]{:S(2)}) %collective-permute-start.7) | collective-permute-done | bytes 69664 | tf_op jit(solution)/shard_map/ppermute | solution.py:355
  24.1 0.4 %collective-permute-done.8.refs_4_ = bf16[272,128]{1,0:T(8,128)(2,1)S(1)} collective-permute-done((bf16[272,128]{1,0:T(8,128)(2,1)S(1)}, bf16[272,128]{1,0:T(8,128)(2,1)S(1)}, u32[]{:S(2)}, u32[]{:S(2)}) %collective-permute-start.8) | collective-permute-done | bytes 69664 | tf_op jit(solution)/shard_map/ppermute | solution.py:355
  24.5 0.0 collective-permute-done.1.received
  24.5 1.3 %shard_map.81 = (bf16[1,128,4096]{2,1,0:T(8,128)(2,1)}, s32[1]{0:T(128)S(4)}, f32[1,33024]{1,0:T(1,128)}) custom-call(bf16[128,96]{1,0:T(8,128)(2,1)S(1)} %get-tuple-element.54.scatter, bf16[96,4096]{1,0:T(8,128)(2,1)S(1)} %collective-permute-done.1.received, f32[128,4096]{1,0:T(8,128)S(1)} %get-tuple-element.56.addend, s32[1]{0:T(128)S(4)} %get-tuple-element.57.more, ...), custom_call_target="tpu_custom_call" | custom-call | flops 1048576 | bytes 65536 | tf_op jit(solution)/shard_map/pallas_call | solution.py:212
  (2 shorter events, 0.0 us)
Async XLA Ops:
  3.9 20.6 %collective-permute-start.1 = (bf16[96,4096]{1,0:T(8,128)(2,1)S(1)}, bf16[96,4096]{1,0:T(8,128)(2,1)S(1)}, u32[]{:S(2)}, u32[]{:S(2)}) collective-permute-start(bf16[96,4096]{1,0:T(8,128)(2,1)S(1)} %get-tuple-element.55), channel_id=1, source_target_pairs={{1,0},{0,1},{3,2},{2,3},{5,4},{4,5},{7,6},{6,7},{9,8},{8,9},{11,10... | collective-permute-start | bytes 2359304 | tf_op jit(solution)/shard_map/ppermute | solution.py:392
  7.7 2.0 %collective-permute-start.3 = (bf16[8,144,128]{2,1,0:T(8,128)(2,1)S(1)}, bf16[8,144,128]{2,1,0:T(8,128)(2,1)S(1)}, u32[]{:S(2)}, u32[]{:S(2)}) collective-permute-start(bf16[8,144,128]{2,1,0:T(8,128)(2,1)S(1)} %get-tuple-element.65), channel_id=1, source_target_pairs={{0,2},{2,0},{4,6},{6,4},{8,10},{10,8},{12,14},{14,12},{16,18},{18,... | collective-permute-start | bytes 884744 | tf_op jit(solution)/shard_map/ppermute | solution.py:372
  7.8 1.9 %collective-permute-start.2 = (bf16[8,128,128]{2,1,0:T(8,128)(2,1)S(1)}, bf16[8,128,128]{2,1,0:T(8,128)(2,1)S(1)}, u32[]{:S(2)}, u32[]{:S(2)}) collective-permute-start(bf16[8,128,128]{2,1,0:T(8,128)(2,1)S(1)} %get-tuple-element.64), channel_id=1, source_target_pairs={{0,2},{2,0},{4,6},{6,4},{8,10},{10,8},{12,14},{14,12},{16,18},{18,... | collective-permute-start | bytes 786440 | tf_op jit(solution)/shard_map/ppermute | solution.py:372
  9.9 7.3 %collective-permute-start.4 = (bf16[3,272,128]{2,1,0:T(8,128)(2,1)S(1)}, bf16[3,272,128]{2,1,0:T(8,128)(2,1)S(1)}, u32[]{:S(2)}, u32[]{:S(2)}) collective-permute-start(bf16[3,272,128]{2,1,0:T(8,128)(2,1)S(1)} %get-tuple-element.67), channel_id=1, source_target_pairs={{0,4},{2,6},{4,0},{6,2},{8,12},{10,14},{12,8},{14,10},{16,20},{18,... | collective-permute-start | bytes 626696 | tf_op jit(solution)/shard_map/ppermute | solution.py:347
  11.5 9.6 %collective-permute-start.5 = (bf16[272,128]{1,0:T(8,128)(2,1)S(1)}, bf16[272,128]{1,0:T(8,128)(2,1)S(1)}, u32[]{:S(2)}, u32[]{:S(2)}) collective-permute-start(bf16[272,128]{1,0:T(8,128)(2,1)S(1)} %get-tuple-element.69), channel_id=1, source_target_pairs={{0,16},{2,18},{4,20},{6,22},{8,24},{10,26},{12,28},{14,30},{16,0},... | collective-permute-start | bytes 208904 | tf_op jit(solution)/shard_map/ppermute | solution.py:349
  14.0 7.0 %collective-permute-start.6 = (bf16[272,128]{1,0:T(8,128)(2,1)S(1)}, bf16[272,128]{1,0:T(8,128)(2,1)S(1)}, u32[]{:S(2)}, u32[]{:S(2)}) collective-permute-start(bf16[272,128]{1,0:T(8,128)(2,1)S(1)} %get-tuple-element.70), channel_id=1, source_target_pairs={{0,20},{2,22},{4,16},{6,18},{8,28},{10,30},{12,24},{14,26},{16,4},... | collective-permute-start | bytes 208904 | tf_op jit(solution)/shard_map/ppermute | solution.py:349
  17.2 6.9 %collective-permute-start.7 = (bf16[272,128]{1,0:T(8,128)(2,1)S(1)}, bf16[272,128]{1,0:T(8,128)(2,1)S(1)}, u32[]{:S(2)}, u32[]{:S(2)}) collective-permute-start(bf16[272,128]{1,0:T(8,128)(2,1)S(1)} %get-tuple-element.71), channel_id=1, source_target_pairs={{0,8},{2,10},{4,12},{6,14},{8,16},{10,18},{12,20},{14,22},{16,24},... | collective-permute-start | bytes 208904 | tf_op jit(solution)/shard_map/ppermute | solution.py:355
  18.8 5.7 %collective-permute-start.8 = (bf16[272,128]{1,0:T(8,128)(2,1)S(1)}, bf16[272,128]{1,0:T(8,128)(2,1)S(1)}, u32[]{:S(2)}, u32[]{:S(2)}) collective-permute-start(bf16[272,128]{1,0:T(8,128)(2,1)S(1)} %get-tuple-element.72), channel_id=1, source_target_pairs={{0,24},{2,26},{4,28},{6,30},{8,0},{10,2},{12,4},{14,6},{16,8},{18,... | collective-permute-start | bytes 208904 | tf_op jit(solution)/shard_map/ppermute | solution.py:355

commit v17 on v16

--- a/solution.py
+++ b/solution.py
@@ -84,13 +84,13 @@
     blocks = [slice(at, at + block_rows) for at in range(0, rows, block_rows)]
     squares = [jnp.zeros((block_rows, lanes), f32) for _ in blocks]
     products = [jnp.zeros((block_rows, lanes), f32) for _ in blocks]
-    for tile in range(0, width, tile_width):
+    for tile in range(0, width, band_width):
         here = lax.dot_general(
-            values, w[tile : tile + tile_width, :], contract_last, preferred_element_type=f32
+            values, w[tile : tile + band_width, :], contract_last, preferred_element_type=f32
         )
-        back[:, tile : tile + tile_width] = here
+        back[:, tile : tile + band_width] = here
         for k, part in enumerate(blocks):
-            for at in range(0, tile_width, lanes):
+            for at in range(0, band_width, lanes):
                 cut = pl.ds(tile + at, lanes)
                 wide = x[part, cut].astype(f32)
                 squares[k] += wide * wide
@@ -237,19 +237,25 @@
         total[gain_rows + at : gain_rows + at + band_width, :] = lax.dot_general(
             normed, values, contract_rows, preferred_element_type=f32
         )
-    even_core = lax.axis_index("dp") % pair == 0
-    padded = keep.shape[1]
-    for j in range(keep.shape[0]):
-        even = total[2 * j * owned_rows : (2 * j + 1) * owned_rows, :]
-        odd = total[(2 * j + 1) * owned_rows : (2 * j + 2) * owned_rows, :]
-        if padded > owned_rows:
-            blank = jnp.zeros((padded - owned_rows, lanes), f32)
-            even = jnp.concatenate([even, blank], axis=0)
-            odd = jnp.concatenate([odd, blank], axis=0)
-        keep[j] = jnp.where(even_core, even, odd)
-        other = jnp.where(even_core, odd, even).astype(bf16)
-        give[j] = other[: give.shape[1], :]
-        give_low[j] = other[give.shape[1] :, :]
+    blocks, padded, _ = keep.shape
+    cut = give.shape[1]
+
+    def hand_out(side):
+        for j in range(blocks):
+            mine = (2 * j + side) * owned_rows
+            other = (2 * j + 1 - side) * owned_rows
+            keep[j, :owned_rows, :] = total[mine : mine + owned_rows, :]
+            give[j] = total[other : other + cut, :].astype(bf16)
+            low = total[other + cut : other + owned_rows, :]
+            if padded > owned_rows:
+                blank = jnp.zeros((padded - owned_rows, lanes), f32)
+                keep[j, owned_rows:, :] = blank
+                low = jnp.concatenate([low, blank], axis=0)
+            give_low[j] = low.astype(bf16)
+
+    side = lax.axis_index("dp") % pair
+    for core in range(pair):
+        pl.when(side == core)(functools.partial(hand_out, core))
 
 
 def pair_terms(made, owned_rows, owners):

time: 26 us -> 26.1 us (level)
  no operation moved by 1% of the time
where the time goes in v17:
time: 26.1 us; the launch traced here: 25.9 us
  starting transfers between devices  11.9 us (46%)
  waiting for transfers between devices  7.71 us (30%)
  Pallas kernels  5.61 us (21%)
  between operations  0.68 us (3%)
    ppermute x2, starting transfers between devices, plane_parts(): arrived.append(lax.ppermute(part, 'dp', along(offset, 0)))  3.88 us
    ppermute x2, waiting for transfers between devices, plane_parts(): arrived.append(lax.ppermute(part, 'dp', along(offset, 0)))  3.43 us
    pallas_call x1, Pallas kernels, branch_rows(): pl.pallas_call(functools.partial(branch_kernel, low), in_specs=[pl.BlockS...  3.28 us
    ppermute x1, starting transfers between devices, shards(): landed = lax.ppermute(packed, 'section', hops)  3 us
    ppermute x2, starting transfers between devices, plane_parts(): lax.ppermute(straight[2 * k + side], 'dp', along(offset, side))  2.87 us
    ppermute x1, waiting for transfers between devices, plane_parts(): across = lax.ppermute(give, 'dp', along(0, 1))  2.82 us
    ppermute x1, starting transfers between devices, plane_parts(): across = lax.ppermute(give, 'dp', along(0, 1))  1.58 us
    ppermute x2, waiting for transfers between devices, weight_owned(): lax.ppermute(part, 'dp', [(i, i ^ 1) for i in range(owners)])  1.45 us
  transfers between devices with their start and end apart: 8, of which 4 were waited for; matrix products, arithmetic and copies ran while one was open for 0% of the time, Pallas kernels for 4%

profile of v17, /device:TPU:0, one launch (start us, length us, event | category | flops | bytes accessed | tf_op | source)
XLA Modules:
  0.0 25.9 jit_solution(6526944692194139773)
XLA Ops:
  0.6 3.3 %shard_map.77 = (bf16[96,4096]{1,0:T(8,128)(2,1)S(1)}, f32[128,4096]{1,0:T(8,128)S(1)}, bf16[128,96]{1,0:T(8,128)(2,1)S(1)}, s32[1]{0:T(128)S(4)}, bf16[128,128]...) custom-call(s32[8]{0:T(128)} %counts_far.1, ...), custom_call_target="tpu_custom_call" | custom-call | flops 1048576 | bytes 65536 | tf_op jit(solution)/shard_map/pallas_call | solution.py:128
  3.9 3.0 %collective-permute-start.1 = (bf16[96,4096]{1,0:T(8,128)(2,1)S(1)}, bf16[96,4096]{1,0:T(8,128)(2,1)S(1)}, u32[]{:S(2)}, u32[]{:S(2)}) collective-permute-start(bf16[96,4096]{1,0:T(8,128)(2,1)S(1)} %get-tuple-element.55), channel_id=1, source_target_pairs={{1,0},{0,1},{3,2},{2,3},{5,4},{4,5},{7,6},{6,7},{9,8},{8,9},{11,10... | collective-permute-start | bytes 2359304 | tf_op jit(solution)/shard_map/ppermute | solution.py:398
  6.9 0.8 %shard_map.78 = (f32[8,272,128]{2,1,0:T(8,128)S(1)}, bf16[8,128,128]{2,1,0:T(8,128)(2,1)S(1)}, bf16[8,144,128]{2,1,0:T(8,128)(2,1)S(1)}) custom-call(bf16[128,128]{1,0:T(8,128)(2,1)S(1)} %get-tuple-element.58.masked, bf16[128,4096]{1,0:T(8,128)(2,1)S(1)} %get-tuple-element.59.x, f32[128,4096]{1,0:T(8,128)S(1)} %get-tuple-element.60.back, ...), custom_call_target="tpu_custom_call" | custom-call | flops 1048576 | bytes 65536 | tf_op jit(solution)/shard_map/pallas_call | solution.py:265
  7.8 0.1 collective-permute-start.3
  7.8 0.5 %collective-permute-start.2 = (bf16[8,128,128]{2,1,0:T(8,128)(2,1)S(1)}, bf16[8,128,128]{2,1,0:T(8,128)(2,1)S(1)}, u32[]{:S(2)}, u32[]{:S(2)}) collective-permute-start(bf16[8,128,128]{2,1,0:T(8,128)(2,1)S(1)} %get-tuple-element.64), channel_id=1, source_target_pairs={{0,2},{2,0},{4,6},{6,4},{8,10},{10,8},{12,14},{14,12},{16,18},{18,... | collective-permute-start | bytes 786440 | tf_op jit(solution)/shard_map/ppermute | solution.py:378
  8.3 1.4 %collective-permute-done.2.taken = bf16[8,128,128]{2,1,0:T(8,128)(2,1)S(1)} collective-permute-done((bf16[8,128,128]{2,1,0:T(8,128)(2,1)S(1)}, bf16[8,128,128]{2,1,0:T(8,128)(2,1)S(1)}, u32[]{:S(2)}, u32[]{:S(2)}) %collective-permute-start.2) | collective-permute-done | bytes 262176 | tf_op jit(solution)/shard_map/ppermute | solution.py:378
  9.8 0.0 collective-permute-done.3.taken_low
  9.8 0.1 shard_map.79
  9.9 1.6 %collective-permute-start.4 = (bf16[3,272,128]{2,1,0:T(8,128)(2,1)S(1)}, bf16[3,272,128]{2,1,0:T(8,128)(2,1)S(1)}, u32[]{:S(2)}, u32[]{:S(2)}) collective-permute-start(bf16[3,272,128]{2,1,0:T(8,128)(2,1)S(1)} %get-tuple-element.67), channel_id=1, source_target_pairs={{0,4},{2,6},{4,0},{6,2},{8,12},{10,14},{12,8},{14,10},{16,20},{18,... | collective-permute-start | bytes 626696 | tf_op jit(solution)/shard_map/ppermute | solution.py:353
  11.5 2.6 %collective-permute-start.5 = (bf16[272,128]{1,0:T(8,128)(2,1)S(1)}, bf16[272,128]{1,0:T(8,128)(2,1)S(1)}, u32[]{:S(2)}, u32[]{:S(2)}) collective-permute-start(bf16[272,128]{1,0:T(8,128)(2,1)S(1)} %get-tuple-element.69), channel_id=1, source_target_pairs={{0,16},{2,18},{4,20},{6,22},{8,24},{10,26},{12,28},{14,30},{16,0},... | collective-permute-start | bytes 208904 | tf_op jit(solution)/shard_map/ppermute | solution.py:355
  14.1 0.3 %collective-permute-start.6 = (bf16[272,128]{1,0:T(8,128)(2,1)S(1)}, bf16[272,128]{1,0:T(8,128)(2,1)S(1)}, u32[]{:S(2)}, u32[]{:S(2)}) collective-permute-start(bf16[272,128]{1,0:T(8,128)(2,1)S(1)} %get-tuple-element.70), channel_id=1, source_target_pairs={{0,20},{2,22},{4,16},{6,18},{8,28},{10,30},{12,24},{14,26},{16,4},... | collective-permute-start | bytes 208904 | tf_op jit(solution)/shard_map/ppermute | solution.py:355
  14.4 2.8 %collective-permute-done.4.taken = bf16[3,272,128]{2,1,0:T(8,128)(2,1)S(1)} collective-permute-done((bf16[3,272,128]{2,1,0:T(8,128)(2,1)S(1)}, bf16[3,272,128]{2,1,0:T(8,128)(2,1)S(1)}, u32[]{:S(2)}, u32[]{:S(2)}) %collective-permute-start.4) | collective-permute-done | bytes 208928 | tf_op jit(solution)/shard_map/ppermute | solution.py:353
  17.2 1.6 %collective-permute-start.7 = (bf16[272,128]{1,0:T(8,128)(2,1)S(1)}, bf16[272,128]{1,0:T(8,128)(2,1)S(1)}, u32[]{:S(2)}, u32[]{:S(2)}) collective-permute-start(bf16[272,128]{1,0:T(8,128)(2,1)S(1)} %get-tuple-element.71), channel_id=1, source_target_pairs={{0,8},{2,10},{4,12},{6,14},{8,16},{10,18},{12,20},{14,22},{16,24},... | collective-permute-start | bytes 208904 | tf_op jit(solution)/shard_map/ppermute | solution.py:361
  18.8 2.3 %collective-permute-start.8 = (bf16[272,128]{1,0:T(8,128)(2,1)S(1)}, bf16[272,128]{1,0:T(8,128)(2,1)S(1)}, u32[]{:S(2)}, u32[]{:S(2)}) collective-permute-start(bf16[272,128]{1,0:T(8,128)(2,1)S(1)} %get-tuple-element.72), channel_id=1, source_target_pairs={{0,24},{2,26},{4,28},{6,30},{8,0},{10,2},{12,4},{14,6},{16,8},{18,... | collective-permute-start | bytes 208904 | tf_op jit(solution)/shard_map/ppermute | solution.py:361
  21.1 0.0 collective-permute-done.5.refs_1_
  21.1 0.0 collective-permute-done.6.refs_2_
  21.1 3.0 %collective-permute-done.7.refs_3_ = bf16[272,128]{1,0:T(8,128)(2,1)S(1)} collective-permute-done((bf16[272,128]{1,0:T(8,128)(2,1)S(1)}, bf16[272,128]{1,0:T(8,128)(2,1)S(1)}, u32[]{:S(2)}, u32[]{:S(2)}) %collective-permute-start.7) | collective-permute-done | bytes 69664 | tf_op jit(solution)/shard_map/ppermute | solution.py:361
  24.1 0.4 %collective-permute-done.8.refs_4_ = bf16[272,128]{1,0:T(8,128)(2,1)S(1)} collective-permute-done((bf16[272,128]{1,0:T(8,128)(2,1)S(1)}, bf16[272,128]{1,0:T(8,128)(2,1)S(1)}, u32[]{:S(2)}, u32[]{:S(2)}) %collective-permute-start.8) | collective-permute-done | bytes 69664 | tf_op jit(solution)/shard_map/ppermute | solution.py:361
  24.5 0.0 collective-permute-done.1.received
  24.5 1.3 %shard_map.81 = (bf16[1,128,4096]{2,1,0:T(8,128)(2,1)}, s32[1]{0:T(128)S(4)}, f32[1,33024]{1,0:T(1,128)}) custom-call(bf16[128,96]{1,0:T(8,128)(2,1)S(1)} %get-tuple-element.54.scatter, bf16[96,4096]{1,0:T(8,128)(2,1)S(1)} %collective-permute-done.1.received, f32[128,4096]{1,0:T(8,128)S(1)} %get-tuple-element.56.addend, s32[1]{0:T(128)S(4)} %get-tuple-element.57.more, ...), custom_call_target="tpu_custom_call" | custom-call | flops 1048576 | bytes 65536 | tf_op jit(solution)/shard_map/pallas_call | solution.py:212
  (2 shorter events, 0.0 us)
Async XLA Ops:
  3.9 20.6 %collective-permute-start.1 = (bf16[96,4096]{1,0:T(8,128)(2,1)S(1)}, bf16[96,4096]{1,0:T(8,128)(2,1)S(1)}, u32[]{:S(2)}, u32[]{:S(2)}) collective-permute-start(bf16[96,4096]{1,0:T(8,128)(2,1)S(1)} %get-tuple-element.55), channel_id=1, source_target_pairs={{1,0},{0,1},{3,2},{2,3},{5,4},{4,5},{7,6},{6,7},{9,8},{8,9},{11,10... | collective-permute-start | bytes 2359304 | tf_op jit(solution)/shard_map/ppermute | solution.py:398
  7.8 2.0 %collective-permute-start.3 = (bf16[8,144,128]{2,1,0:T(8,128)(2,1)S(1)}, bf16[8,144,128]{2,1,0:T(8,128)(2,1)S(1)}, u32[]{:S(2)}, u32[]{:S(2)}) collective-permute-start(bf16[8,144,128]{2,1,0:T(8,128)(2,1)S(1)} %get-tuple-element.65), channel_id=1, source_target_pairs={{0,2},{2,0},{4,6},{6,4},{8,10},{10,8},{12,14},{14,12},{16,18},{18,... | collective-permute-start | bytes 884744 | tf_op jit(solution)/shard_map/ppermute | solution.py:378
  7.8 1.9 %collective-permute-start.2 = (bf16[8,128,128]{2,1,0:T(8,128)(2,1)S(1)}, bf16[8,128,128]{2,1,0:T(8,128)(2,1)S(1)}, u32[]{:S(2)}, u32[]{:S(2)}) collective-permute-start(bf16[8,128,128]{2,1,0:T(8,128)(2,1)S(1)} %get-tuple-element.64), channel_id=1, source_target_pairs={{0,2},{2,0},{4,6},{6,4},{8,10},{10,8},{12,14},{14,12},{16,18},{18,... | collective-permute-start | bytes 786440 | tf_op jit(solution)/shard_map/ppermute | solution.py:378
  9.9 7.3 %collective-permute-start.4 = (bf16[3,272,128]{2,1,0:T(8,128)(2,1)S(1)}, bf16[3,272,128]{2,1,0:T(8,128)(2,1)S(1)}, u32[]{:S(2)}, u32[]{:S(2)}) collective-permute-start(bf16[3,272,128]{2,1,0:T(8,128)(2,1)S(1)} %get-tuple-element.67), channel_id=1, source_target_pairs={{0,4},{2,6},{4,0},{6,2},{8,12},{10,14},{12,8},{14,10},{16,20},{18,... | collective-permute-start | bytes 626696 | tf_op jit(solution)/shard_map/ppermute | solution.py:353
  11.5 9.6 %collective-permute-start.5 = (bf16[272,128]{1,0:T(8,128)(2,1)S(1)}, bf16[272,128]{1,0:T(8,128)(2,1)S(1)}, u32[]{:S(2)}, u32[]{:S(2)}) collective-permute-start(bf16[272,128]{1,0:T(8,128)(2,1)S(1)} %get-tuple-element.69), channel_id=1, source_target_pairs={{0,16},{2,18},{4,20},{6,22},{8,24},{10,26},{12,28},{14,30},{16,0},... | collective-permute-start | bytes 208904 | tf_op jit(solution)/shard_map/ppermute | solution.py:355
  14.1 7.0 %collective-permute-start.6 = (bf16[272,128]{1,0:T(8,128)(2,1)S(1)}, bf16[272,128]{1,0:T(8,128)(2,1)S(1)}, u32[]{:S(2)}, u32[]{:S(2)}) collective-permute-start(bf16[272,128]{1,0:T(8,128)(2,1)S(1)} %get-tuple-element.70), channel_id=1, source_target_pairs={{0,20},{2,22},{4,16},{6,18},{8,28},{10,30},{12,24},{14,26},{16,4},... | collective-permute-start | bytes 208904 | tf_op jit(solution)/shard_map/ppermute | solution.py:355
  17.2 6.9 %collective-permute-start.7 = (bf16[272,128]{1,0:T(8,128)(2,1)S(1)}, bf16[272,128]{1,0:T(8,128)(2,1)S(1)}, u32[]{:S(2)}, u32[]{:S(2)}) collective-permute-start(bf16[272,128]{1,0:T(8,128)(2,1)S(1)} %get-tuple-element.71), channel_id=1, source_target_pairs={{0,8},{2,10},{4,12},{6,14},{8,16},{10,18},{12,20},{14,22},{16,24},... | collective-permute-start | bytes 208904 | tf_op jit(solution)/shard_map/ppermute | solution.py:361
  18.8 5.7 %collective-permute-start.8 = (bf16[272,128]{1,0:T(8,128)(2,1)S(1)}, bf16[272,128]{1,0:T(8,128)(2,1)S(1)}, u32[]{:S(2)}, u32[]{:S(2)}) collective-permute-start(bf16[272,128]{1,0:T(8,128)(2,1)S(1)} %get-tuple-element.72), channel_id=1, source_target_pairs={{0,24},{2,26},{4,28},{6,30},{8,0},{10,2},{12,4},{14,6},{16,8},{18,... | collective-permute-start | bytes 208904 | tf_op jit(solution)/shard_map/ppermute | solution.py:361

commit v18 on v17

--- a/solution.py
+++ b/solution.py
@@ -343,7 +343,7 @@
 def plane_parts(owners, keep, *taken):
     quad = 2 * pair
     count = owners // quad
-    direct = [count // 2] if count > 2 else []
+    direct = [1] if count > 2 else []
     offsets = [k for k in range(count) if k not in direct]
 
     def along(offset, side):

time: 26.1 us -> 27.2 us (1.042)
  starting transfers between devices: 11.9 us -> 13.7 us
  waiting for transfers between devices: 7.71 us -> 7 us
    ppermute x2, starting transfers between devices: 3.88 us -> 5.49 us  [plane_parts(): arrived.append(lax.ppermute(part, 'dp', along(offset, 0)))]
    ppermute x2, waiting for transfers between devices: 3.43 us -> 2.96 us  [plane_parts(): arrived.append(lax.ppermute(part, 'dp', along(offset, 0)))]
where the time goes in v18:
time: 27.2 us; the launch traced here: 27 us
  starting transfers between devices  13.7 us (50%)
  waiting for transfers between devices  7 us (26%)
  Pallas kernels  5.6 us (21%)
  between operations  0.68 us (2%)
    ppermute x2, starting transfers between devices, plane_parts(): arrived.append(lax.ppermute(part, 'dp', along(offset, 0)))  5.49 us
    pallas_call x1, Pallas kernels, branch_rows(): pl.pallas_call(functools.partial(branch_kernel, low), in_specs=[pl.BlockS...  3.28 us
    ppermute x2, starting transfers between devices, plane_parts(): lax.ppermute(straight[2 * k + side], 'dp', along(offset, side))  3.09 us
    ppermute x1, starting transfers between devices, shards(): landed = lax.ppermute(packed, 'section', hops)  3 us
    ppermute x2, waiting for transfers between devices, plane_parts(): arrived.append(lax.ppermute(part, 'dp', along(offset, 0)))  2.96 us
    ppermute x1, waiting for transfers between devices, plane_parts(): across = lax.ppermute(give, 'dp', along(0, 1))  2.59 us
    ppermute x1, starting transfers between devices, plane_parts(): across = lax.ppermute(give, 'dp', along(0, 1))  1.59 us
    ppermute x2, waiting for transfers between devices, weight_owned(): lax.ppermute(part, 'dp', [(i, i ^ 1) for i in range(owners)])  1.45 us
  transfers between devices with their start and end apart: 8, of which 4 were waited for; matrix products, arithmetic and copies ran while one was open for 0% of the time, Pallas kernels for 4%

profile of v18, /device:TPU:0, one launch (start us, length us, event | category | flops | bytes accessed | tf_op | source)
XLA Modules:
  0.0 27.0 jit_solution(3311503381041623131)
XLA Ops:
  0.6 3.3 %shard_map.77 = (bf16[96,4096]{1,0:T(8,128)(2,1)S(1)}, f32[128,4096]{1,0:T(8,128)S(1)}, bf16[128,96]{1,0:T(8,128)(2,1)S(1)}, s32[1]{0:T(128)S(4)}, bf16[128,128]...) custom-call(s32[8]{0:T(128)} %counts_far.1, ...), custom_call_target="tpu_custom_call" | custom-call | flops 1048576 | bytes 65536 | tf_op jit(solution)/shard_map/pallas_call | solution.py:128
  3.9 3.0 %collective-permute-start.1 = (bf16[96,4096]{1,0:T(8,128)(2,1)S(1)}, bf16[96,4096]{1,0:T(8,128)(2,1)S(1)}, u32[]{:S(2)}, u32[]{:S(2)}) collective-permute-start(bf16[96,4096]{1,0:T(8,128)(2,1)S(1)} %get-tuple-element.55), channel_id=1, source_target_pairs={{1,0},{0,1},{3,2},{2,3},{5,4},{4,5},{7,6},{6,7},{9,8},{8,9},{11,10... | collective-permute-start | bytes 2359304 | tf_op jit(solution)/shard_map/ppermute | solution.py:398
  6.9 0.8 %shard_map.78 = (f32[8,272,128]{2,1,0:T(8,128)S(1)}, bf16[8,128,128]{2,1,0:T(8,128)(2,1)S(1)}, bf16[8,144,128]{2,1,0:T(8,128)(2,1)S(1)}) custom-call(bf16[128,128]{1,0:T(8,128)(2,1)S(1)} %get-tuple-element.58.masked, bf16[128,4096]{1,0:T(8,128)(2,1)S(1)} %get-tuple-element.59.x, f32[128,4096]{1,0:T(8,128)S(1)} %get-tuple-element.60.back, ...), custom_call_target="tpu_custom_call" | custom-call | flops 1048576 | bytes 65536 | tf_op jit(solution)/shard_map/pallas_call | solution.py:265
  7.8 0.1 collective-permute-start.3
  7.8 0.5 %collective-permute-start.2 = (bf16[8,128,128]{2,1,0:T(8,128)(2,1)S(1)}, bf16[8,128,128]{2,1,0:T(8,128)(2,1)S(1)}, u32[]{:S(2)}, u32[]{:S(2)}) collective-permute-start(bf16[8,128,128]{2,1,0:T(8,128)(2,1)S(1)} %get-tuple-element.64), channel_id=1, source_target_pairs={{0,2},{2,0},{4,6},{6,4},{8,10},{10,8},{12,14},{14,12},{16,18},{18,... | collective-permute-start | bytes 786440 | tf_op jit(solution)/shard_map/ppermute | solution.py:378
  8.3 1.4 %collective-permute-done.2.taken = bf16[8,128,128]{2,1,0:T(8,128)(2,1)S(1)} collective-permute-done((bf16[8,128,128]{2,1,0:T(8,128)(2,1)S(1)}, bf16[8,128,128]{2,1,0:T(8,128)(2,1)S(1)}, u32[]{:S(2)}, u32[]{:S(2)}) %collective-permute-start.2) | collective-permute-done | bytes 262176 | tf_op jit(solution)/shard_map/ppermute | solution.py:378
  9.8 0.0 collective-permute-done.3.taken_low
  9.8 0.1 shard_map.79
  9.9 1.6 %collective-permute-start.4 = (bf16[3,272,128]{2,1,0:T(8,128)(2,1)S(1)}, bf16[3,272,128]{2,1,0:T(8,128)(2,1)S(1)}, u32[]{:S(2)}, u32[]{:S(2)}) collective-permute-start(bf16[3,272,128]{2,1,0:T(8,128)(2,1)S(1)} %get-tuple-element.67), channel_id=1, source_target_pairs={{0,4},{2,6},{4,0},{6,2},{8,12},{10,14},{12,8},{14,10},{16,20},{18,... | collective-permute-start | bytes 626696 | tf_op jit(solution)/shard_map/ppermute | solution.py:353
  11.5 1.6 %collective-permute-start.5 = (bf16[272,128]{1,0:T(8,128)(2,1)S(1)}, bf16[272,128]{1,0:T(8,128)(2,1)S(1)}, u32[]{:S(2)}, u32[]{:S(2)}) collective-permute-start(bf16[272,128]{1,0:T(8,128)(2,1)S(1)} %get-tuple-element.69), channel_id=1, source_target_pairs={{0,8},{2,10},{4,12},{6,14},{8,16},{10,18},{12,20},{14,22},{16,24},... | collective-permute-start | bytes 208904 | tf_op jit(solution)/shard_map/ppermute | solution.py:355
  13.1 1.5 %collective-permute-start.6 = (bf16[272,128]{1,0:T(8,128)(2,1)S(1)}, bf16[272,128]{1,0:T(8,128)(2,1)S(1)}, u32[]{:S(2)}, u32[]{:S(2)}) collective-permute-start(bf16[272,128]{1,0:T(8,128)(2,1)S(1)} %get-tuple-element.70), channel_id=1, source_target_pairs={{0,12},{2,14},{4,8},{6,10},{8,20},{10,22},{12,16},{14,18},{16,28},... | collective-permute-start | bytes 208904 | tf_op jit(solution)/shard_map/ppermute | solution.py:355
  14.6 2.6 %collective-permute-done.4.taken = bf16[3,272,128]{2,1,0:T(8,128)(2,1)S(1)} collective-permute-done((bf16[3,272,128]{2,1,0:T(8,128)(2,1)S(1)}, bf16[3,272,128]{2,1,0:T(8,128)(2,1)S(1)}, u32[]{:S(2)}, u32[]{:S(2)}) %collective-permute-start.4) | collective-permute-done | bytes 208928 | tf_op jit(solution)/shard_map/ppermute | solution.py:353
  17.2 4.1 %collective-permute-start.7 = (bf16[272,128]{1,0:T(8,128)(2,1)S(1)}, bf16[272,128]{1,0:T(8,128)(2,1)S(1)}, u32[]{:S(2)}, u32[]{:S(2)}) collective-permute-start(bf16[272,128]{1,0:T(8,128)(2,1)S(1)} %get-tuple-element.71), channel_id=1, source_target_pairs={{0,16},{2,18},{4,20},{6,22},{8,24},{10,26},{12,28},{14,30},{16,0},... | collective-permute-start | bytes 208904 | tf_op jit(solution)/shard_map/ppermute | solution.py:361
  21.4 1.3 %collective-permute-start.8 = (bf16[272,128]{1,0:T(8,128)(2,1)S(1)}, bf16[272,128]{1,0:T(8,128)(2,1)S(1)}, u32[]{:S(2)}, u32[]{:S(2)}) collective-permute-start(bf16[272,128]{1,0:T(8,128)(2,1)S(1)} %get-tuple-element.72), channel_id=1, source_target_pairs={{0,24},{2,26},{4,28},{6,30},{8,0},{10,2},{12,4},{14,6},{16,8},{18,... | collective-permute-start | bytes 208904 | tf_op jit(solution)/shard_map/ppermute | solution.py:361
  22.7 0.0 collective-permute-done.5.refs_1_
  22.7 0.0 collective-permute-done.6.refs_2_
  22.7 1.4 %collective-permute-done.7.refs_3_ = bf16[272,128]{1,0:T(8,128)(2,1)S(1)} collective-permute-done((bf16[272,128]{1,0:T(8,128)(2,1)S(1)}, bf16[272,128]{1,0:T(8,128)(2,1)S(1)}, u32[]{:S(2)}, u32[]{:S(2)}) %collective-permute-start.7) | collective-permute-done | bytes 69664 | tf_op jit(solution)/shard_map/ppermute | solution.py:361
  24.1 1.5 %collective-permute-done.8.refs_4_ = bf16[272,128]{1,0:T(8,128)(2,1)S(1)} collective-permute-done((bf16[272,128]{1,0:T(8,128)(2,1)S(1)}, bf16[272,128]{1,0:T(8,128)(2,1)S(1)}, u32[]{:S(2)}, u32[]{:S(2)}) %collective-permute-start.8) | collective-permute-done | bytes 69664 | tf_op jit(solution)/shard_map/ppermute | solution.py:361
  25.7 0.0 collective-permute-done.1.received
  25.7 1.3 %shard_map.81 = (bf16[1,128,4096]{2,1,0:T(8,128)(2,1)}, s32[1]{0:T(128)S(4)}, f32[1,33024]{1,0:T(1,128)}) custom-call(bf16[128,96]{1,0:T(8,128)(2,1)S(1)} %get-tuple-element.54.scatter, bf16[96,4096]{1,0:T(8,128)(2,1)S(1)} %collective-permute-done.1.received, f32[128,4096]{1,0:T(8,128)S(1)} %get-tuple-element.56.addend, s32[1]{0:T(128)S(4)} %get-tuple-element.57.more, ...), custom_call_target="tpu_custom_call" | custom-call | flops 1048576 | bytes 65536 | tf_op jit(solution)/shard_map/pallas_call | solution.py:212
  (2 shorter events, 0.0 us)
Async XLA Ops:
  3.9 21.8 %collective-permute-start.1 = (bf16[96,4096]{1,0:T(8,128)(2,1)S(1)}, bf16[96,4096]{1,0:T(8,128)(2,1)S(1)}, u32[]{:S(2)}, u32[]{:S(2)}) collective-permute-start(bf16[96,4096]{1,0:T(8,128)(2,1)S(1)} %get-tuple-element.55), channel_id=1, source_target_pairs={{1,0},{0,1},{3,2},{2,3},{5,4},{4,5},{7,6},{6,7},{9,8},{8,9},{11,10... | collective-permute-start | bytes 2359304 | tf_op jit(solution)/shard_map/ppermute | solution.py:398
  7.8 2.0 %collective-permute-start.3 = (bf16[8,144,128]{2,1,0:T(8,128)(2,1)S(1)}, bf16[8,144,128]{2,1,0:T(8,128)(2,1)S(1)}, u32[]{:S(2)}, u32[]{:S(2)}) collective-permute-start(bf16[8,144,128]{2,1,0:T(8,128)(2,1)S(1)} %get-tuple-element.65), channel_id=1, source_target_pairs={{0,2},{2,0},{4,6},{6,4},{8,10},{10,8},{12,14},{14,12},{16,18},{18,... | collective-permute-start | bytes 884744 | tf_op jit(solution)/shard_map/ppermute | solution.py:378
  7.8 1.9 %collective-permute-start.2 = (bf16[8,128,128]{2,1,0:T(8,128)(2,1)S(1)}, bf16[8,128,128]{2,1,0:T(8,128)(2,1)S(1)}, u32[]{:S(2)}, u32[]{:S(2)}) collective-permute-start(bf16[8,128,128]{2,1,0:T(8,128)(2,1)S(1)} %get-tuple-element.64), channel_id=1, source_target_pairs={{0,2},{2,0},{4,6},{6,4},{8,10},{10,8},{12,14},{14,12},{16,18},{18,... | collective-permute-start | bytes 786440 | tf_op jit(solution)/shard_map/ppermute | solution.py:378
  9.9 7.3 %collective-permute-start.4 = (bf16[3,272,128]{2,1,0:T(8,128)(2,1)S(1)}, bf16[3,272,128]{2,1,0:T(8,128)(2,1)S(1)}, u32[]{:S(2)}, u32[]{:S(2)}) collective-permute-start(bf16[3,272,128]{2,1,0:T(8,128)(2,1)S(1)} %get-tuple-element.67), channel_id=1, source_target_pairs={{0,4},{2,6},{4,0},{6,2},{8,12},{10,14},{12,8},{14,10},{16,20},{18,... | collective-permute-start | bytes 626696 | tf_op jit(solution)/shard_map/ppermute | solution.py:353
  11.5 11.2 %collective-permute-start.5 = (bf16[272,128]{1,0:T(8,128)(2,1)S(1)}, bf16[272,128]{1,0:T(8,128)(2,1)S(1)}, u32[]{:S(2)}, u32[]{:S(2)}) collective-permute-start(bf16[272,128]{1,0:T(8,128)(2,1)S(1)} %get-tuple-element.69), channel_id=1, source_target_pairs={{0,8},{2,10},{4,12},{6,14},{8,16},{10,18},{12,20},{14,22},{16,24},... | collective-permute-start | bytes 208904 | tf_op jit(solution)/shard_map/ppermute | solution.py:355
  13.1 9.7 %collective-permute-start.6 = (bf16[272,128]{1,0:T(8,128)(2,1)S(1)}, bf16[272,128]{1,0:T(8,128)(2,1)S(1)}, u32[]{:S(2)}, u32[]{:S(2)}) collective-permute-start(bf16[272,128]{1,0:T(8,128)(2,1)S(1)} %get-tuple-element.70), channel_id=1, source_target_pairs={{0,12},{2,14},{4,8},{6,10},{8,20},{10,22},{12,16},{14,18},{16,28},... | collective-permute-start | bytes 208904 | tf_op jit(solution)/shard_map/ppermute | solution.py:355
  17.2 6.9 %collective-permute-start.7 = (bf16[272,128]{1,0:T(8,128)(2,1)S(1)}, bf16[272,128]{1,0:T(8,128)(2,1)S(1)}, u32[]{:S(2)}, u32[]{:S(2)}) collective-permute-start(bf16[272,128]{1,0:T(8,128)(2,1)S(1)} %get-tuple-element.71), channel_id=1, source_target_pairs={{0,16},{2,18},{4,20},{6,22},{8,24},{10,26},{12,28},{14,30},{16,0},... | collective-permute-start | bytes 208904 | tf_op jit(solution)/shard_map/ppermute | solution.py:361
  21.4 4.3 %collective-permute-start.8 = (bf16[272,128]{1,0:T(8,128)(2,1)S(1)}, bf16[272,128]{1,0:T(8,128)(2,1)S(1)}, u32[]{:S(2)}, u32[]{:S(2)}) collective-permute-start(bf16[272,128]{1,0:T(8,128)(2,1)S(1)} %get-tuple-element.72), channel_id=1, source_target_pairs={{0,24},{2,26},{4,28},{6,30},{8,0},{10,2},{12,4},{14,6},{16,8},{18,... | collective-permute-start | bytes 208904 | tf_op jit(solution)/shard_map/ppermute | solution.py:361

commit v19 on v17

--- a/solution.py
+++ b/solution.py
@@ -104,22 +104,23 @@
         ],
         axis=0,
     )
-    spread = (rows, band_width)
+    spread = (rows, lanes)
     scales = jnp.broadcast_to(scales, spread)
-    scale_out[...] = scales[:, :lanes]
-    pulls = jnp.broadcast_to(pulls, spread)
+    scale_out[...] = scales
+    pulls = jnp.broadcast_to(scales[:, :1] * pulls, spread)
     waits = jnp.broadcast_to(waits, spread)
     fetches[5].wait()
-    for cut in cuts(width, band_width):
-        scaled = gain[:, cut]
+    for band in cuts(width, band_width):
         for part in blocks:
-            unit = x[part, cut].astype(f32) * scales[part]
-            here = back[part, cut]
-            own = scales[part] * (scaled * here - unit * pulls[part])
-            whole = top[part, cut].astype(f32) + own
-            sent[part, cut] = whole.astype(bf16)
-            addend[part, cut] = jnp.where(waits[part], own, whole)
-        packed[:, cut] = jnp.dot(gather, sent[:, cut], preferred_element_type=f32).astype(bf16)
+            scale, pull, wait = scales[part], pulls[part], waits[part]
+            for at in range(0, band_width, lanes):
+                cut = pl.ds(band.start + at, lanes)
+                unit = x[part, cut].astype(f32) * scale
+                own = scale * (gain[:, cut] * back[part, cut]) - unit * pull
+                whole = top[part, cut].astype(f32) + own
+                sent[part, cut] = whole.astype(bf16)
+                addend[part, cut] = jnp.where(wait, own, whole)
+        packed[:, band] = jnp.dot(gather, sent[:, band], preferred_element_type=f32).astype(bf16)
 
 
 def branch_rows(low, room, counts, x, top, v, w, gain):

time: 26.1 us -> 26.2 us (level)
  no operation moved by 1% of the time
where the time goes in v19:
time: 26.2 us; the launch traced here: 26.1 us
  starting transfers between devices  11.9 us (45%)
  waiting for transfers between devices  7.71 us (29%)
  Pallas kernels  5.79 us (22%)
  between operations  0.68 us (3%)
    ppermute x2, starting transfers between devices, plane_parts(): arrived.append(lax.ppermute(part, 'dp', along(offset, 0)))  3.88 us
    pallas_call x1, Pallas kernels, branch_rows(): pl.pallas_call(functools.partial(branch_kernel, low), in_specs=[pl.BlockS...  3.45 us
    ppermute x2, waiting for transfers between devices, plane_parts(): arrived.append(lax.ppermute(part, 'dp', along(offset, 0)))  3.43 us
    ppermute x1, starting transfers between devices, shards(): landed = lax.ppermute(packed, 'section', hops)  3.01 us
    ppermute x2, starting transfers between devices, plane_parts(): lax.ppermute(straight[2 * k + side], 'dp', along(offset, side))  2.87 us
    ppermute x1, waiting for transfers between devices, plane_parts(): across = lax.ppermute(give, 'dp', along(0, 1))  2.82 us
    ppermute x1, starting transfers between devices, plane_parts(): across = lax.ppermute(give, 'dp', along(0, 1))  1.58 us
    ppermute x2, waiting for transfers between devices, weight_owned(): lax.ppermute(part, 'dp', [(i, i ^ 1) for i in range(owners)])  1.45 us
  transfers between devices with their start and end apart: 8, of which 4 were waited for; matrix products, arithmetic and copies ran while one was open for 0% of the time, Pallas kernels for 4%

profile of v19, /device:TPU:0, one launch (start us, length us, event | category | flops | bytes accessed | tf_op | source)
XLA Modules:
  0.0 26.1 jit_solution(7822234578980059176)
XLA Ops:
  0.6 3.5 %shard_map.77 = (bf16[96,4096]{1,0:T(8,128)(2,1)S(1)}, f32[128,4096]{1,0:T(8,128)S(1)}, bf16[128,96]{1,0:T(8,128)(2,1)S(1)}, s32[1]{0:T(128)S(4)}, bf16[128,128]...) custom-call(s32[8]{0:T(128)} %counts_far.1, ...), custom_call_target="tpu_custom_call" | custom-call | flops 1048576 | bytes 65536 | tf_op jit(solution)/shard_map/pallas_call | solution.py:129
  4.1 3.0 %collective-permute-start.1 = (bf16[96,4096]{1,0:T(8,128)(2,1)S(1)}, bf16[96,4096]{1,0:T(8,128)(2,1)S(1)}, u32[]{:S(2)}, u32[]{:S(2)}) collective-permute-start(bf16[96,4096]{1,0:T(8,128)(2,1)S(1)} %get-tuple-element.55), channel_id=1, source_target_pairs={{1,0},{0,1},{3,2},{2,3},{5,4},{4,5},{7,6},{6,7},{9,8},{8,9},{11,10... | collective-permute-start | bytes 2359304 | tf_op jit(solution)/shard_map/ppermute | solution.py:399
  7.1 0.8 %shard_map.78 = (f32[8,272,128]{2,1,0:T(8,128)S(1)}, bf16[8,128,128]{2,1,0:T(8,128)(2,1)S(1)}, bf16[8,144,128]{2,1,0:T(8,128)(2,1)S(1)}) custom-call(bf16[128,128]{1,0:T(8,128)(2,1)S(1)} %get-tuple-element.58.masked, bf16[128,4096]{1,0:T(8,128)(2,1)S(1)} %get-tuple-element.59.x, f32[128,4096]{1,0:T(8,128)S(1)} %get-tuple-element.60.back, ...), custom_call_target="tpu_custom_call" | custom-call | flops 1048576 | bytes 65536 | tf_op jit(solution)/shard_map/pallas_call | solution.py:266
  7.9 0.1 collective-permute-start.3
  8.0 0.5 %collective-permute-start.2 = (bf16[8,128,128]{2,1,0:T(8,128)(2,1)S(1)}, bf16[8,128,128]{2,1,0:T(8,128)(2,1)S(1)}, u32[]{:S(2)}, u32[]{:S(2)}) collective-permute-start(bf16[8,128,128]{2,1,0:T(8,128)(2,1)S(1)} %get-tuple-element.64), channel_id=1, source_target_pairs={{0,2},{2,0},{4,6},{6,4},{8,10},{10,8},{12,14},{14,12},{16,18},{18,... | collective-permute-start | bytes 786440 | tf_op jit(solution)/shard_map/ppermute | solution.py:379
  8.5 1.4 %collective-permute-done.2.taken = bf16[8,128,128]{2,1,0:T(8,128)(2,1)S(1)} collective-permute-done((bf16[8,128,128]{2,1,0:T(8,128)(2,1)S(1)}, bf16[8,128,128]{2,1,0:T(8,128)(2,1)S(1)}, u32[]{:S(2)}, u32[]{:S(2)}) %collective-permute-start.2) | collective-permute-done | bytes 262176 | tf_op jit(solution)/shard_map/ppermute | solution.py:379
  10.0 0.0 collective-permute-done.3.taken_low
  10.0 0.1 shard_map.79
  10.1 1.6 %collective-permute-start.4 = (bf16[3,272,128]{2,1,0:T(8,128)(2,1)S(1)}, bf16[3,272,128]{2,1,0:T(8,128)(2,1)S(1)}, u32[]{:S(2)}, u32[]{:S(2)}) collective-permute-start(bf16[3,272,128]{2,1,0:T(8,128)(2,1)S(1)} %get-tuple-element.67), channel_id=1, source_target_pairs={{0,4},{2,6},{4,0},{6,2},{8,12},{10,14},{12,8},{14,10},{16,20},{18,... | collective-permute-start | bytes 626696 | tf_op jit(solution)/shard_map/ppermute | solution.py:354
  11.7 2.6 %collective-permute-start.5 = (bf16[272,128]{1,0:T(8,128)(2,1)S(1)}, bf16[272,128]{1,0:T(8,128)(2,1)S(1)}, u32[]{:S(2)}, u32[]{:S(2)}) collective-permute-start(bf16[272,128]{1,0:T(8,128)(2,1)S(1)} %get-tuple-element.69), channel_id=1, source_target_pairs={{0,16},{2,18},{4,20},{6,22},{8,24},{10,26},{12,28},{14,30},{16,0},... | collective-permute-start | bytes 208904 | tf_op jit(solution)/shard_map/ppermute | solution.py:356
  14.2 0.3 %collective-permute-start.6 = (bf16[272,128]{1,0:T(8,128)(2,1)S(1)}, bf16[272,128]{1,0:T(8,128)(2,1)S(1)}, u32[]{:S(2)}, u32[]{:S(2)}) collective-permute-start(bf16[272,128]{1,0:T(8,128)(2,1)S(1)} %get-tuple-element.70), channel_id=1, source_target_pairs={{0,20},{2,22},{4,16},{6,18},{8,28},{10,30},{12,24},{14,26},{16,4},... | collective-permute-start | bytes 208904 | tf_op jit(solution)/shard_map/ppermute | solution.py:356
  14.5 2.8 %collective-permute-done.4.taken = bf16[3,272,128]{2,1,0:T(8,128)(2,1)S(1)} collective-permute-done((bf16[3,272,128]{2,1,0:T(8,128)(2,1)S(1)}, bf16[3,272,128]{2,1,0:T(8,128)(2,1)S(1)}, u32[]{:S(2)}, u32[]{:S(2)}) %collective-permute-start.4) | collective-permute-done | bytes 208928 | tf_op jit(solution)/shard_map/ppermute | solution.py:354
  17.4 1.6 %collective-permute-start.7 = (bf16[272,128]{1,0:T(8,128)(2,1)S(1)}, bf16[272,128]{1,0:T(8,128)(2,1)S(1)}, u32[]{:S(2)}, u32[]{:S(2)}) collective-permute-start(bf16[272,128]{1,0:T(8,128)(2,1)S(1)} %get-tuple-element.71), channel_id=1, source_target_pairs={{0,8},{2,10},{4,12},{6,14},{8,16},{10,18},{12,20},{14,22},{16,24},... | collective-permute-start | bytes 208904 | tf_op jit(solution)/shard_map/ppermute | solution.py:362
  19.0 2.3 %collective-permute-start.8 = (bf16[272,128]{1,0:T(8,128)(2,1)S(1)}, bf16[272,128]{1,0:T(8,128)(2,1)S(1)}, u32[]{:S(2)}, u32[]{:S(2)}) collective-permute-start(bf16[272,128]{1,0:T(8,128)(2,1)S(1)} %get-tuple-element.72), channel_id=1, source_target_pairs={{0,24},{2,26},{4,28},{6,30},{8,0},{10,2},{12,4},{14,6},{16,8},{18,... | collective-permute-start | bytes 208904 | tf_op jit(solution)/shard_map/ppermute | solution.py:362
  21.3 0.0 collective-permute-done.5.refs_1_
  21.3 0.0 collective-permute-done.6.refs_2_
  21.3 3.0 %collective-permute-done.7.refs_3_ = bf16[272,128]{1,0:T(8,128)(2,1)S(1)} collective-permute-done((bf16[272,128]{1,0:T(8,128)(2,1)S(1)}, bf16[272,128]{1,0:T(8,128)(2,1)S(1)}, u32[]{:S(2)}, u32[]{:S(2)}) %collective-permute-start.7) | collective-permute-done | bytes 69664 | tf_op jit(solution)/shard_map/ppermute | solution.py:362
  24.3 0.4 %collective-permute-done.8.refs_4_ = bf16[272,128]{1,0:T(8,128)(2,1)S(1)} collective-permute-done((bf16[272,128]{1,0:T(8,128)(2,1)S(1)}, bf16[272,128]{1,0:T(8,128)(2,1)S(1)}, u32[]{:S(2)}, u32[]{:S(2)}) %collective-permute-start.8) | collective-permute-done | bytes 69664 | tf_op jit(solution)/shard_map/ppermute | solution.py:362
  24.7 0.0 collective-permute-done.1.received
  24.7 1.4 %shard_map.81 = (bf16[1,128,4096]{2,1,0:T(8,128)(2,1)}, s32[1]{0:T(128)S(4)}, f32[1,33024]{1,0:T(1,128)}) custom-call(bf16[128,96]{1,0:T(8,128)(2,1)S(1)} %get-tuple-element.54.scatter, bf16[96,4096]{1,0:T(8,128)(2,1)S(1)} %collective-permute-done.1.received, f32[128,4096]{1,0:T(8,128)S(1)} %get-tuple-element.56.addend, s32[1]{0:T(128)S(4)} %get-tuple-element.57.more, ...), custom_call_target="tpu_custom_call" | custom-call | flops 1048576 | bytes 65536 | tf_op jit(solution)/shard_map/pallas_call | solution.py:213
  (2 shorter events, 0.0 us)
Async XLA Ops:
  4.1 20.6 %collective-permute-start.1 = (bf16[96,4096]{1,0:T(8,128)(2,1)S(1)}, bf16[96,4096]{1,0:T(8,128)(2,1)S(1)}, u32[]{:S(2)}, u32[]{:S(2)}) collective-permute-start(bf16[96,4096]{1,0:T(8,128)(2,1)S(1)} %get-tuple-element.55), channel_id=1, source_target_pairs={{1,0},{0,1},{3,2},{2,3},{5,4},{4,5},{7,6},{6,7},{9,8},{8,9},{11,10... | collective-permute-start | bytes 2359304 | tf_op jit(solution)/shard_map/ppermute | solution.py:399
  7.9 2.0 %collective-permute-start.3 = (bf16[8,144,128]{2,1,0:T(8,128)(2,1)S(1)}, bf16[8,144,128]{2,1,0:T(8,128)(2,1)S(1)}, u32[]{:S(2)}, u32[]{:S(2)}) collective-permute-start(bf16[8,144,128]{2,1,0:T(8,128)(2,1)S(1)} %get-tuple-element.65), channel_id=1, source_target_pairs={{0,2},{2,0},{4,6},{6,4},{8,10},{10,8},{12,14},{14,12},{16,18},{18,... | collective-permute-start | bytes 884744 | tf_op jit(solution)/shard_map/ppermute | solution.py:379
  8.0 1.9 %collective-permute-start.2 = (bf16[8,128,128]{2,1,0:T(8,128)(2,1)S(1)}, bf16[8,128,128]{2,1,0:T(8,128)(2,1)S(1)}, u32[]{:S(2)}, u32[]{:S(2)}) collective-permute-start(bf16[8,128,128]{2,1,0:T(8,128)(2,1)S(1)} %get-tuple-element.64), channel_id=1, source_target_pairs={{0,2},{2,0},{4,6},{6,4},{8,10},{10,8},{12,14},{14,12},{16,18},{18,... | collective-permute-start | bytes 786440 | tf_op jit(solution)/shard_map/ppermute | solution.py:379
  10.1 7.3 %collective-permute-start.4 = (bf16[3,272,128]{2,1,0:T(8,128)(2,1)S(1)}, bf16[3,272,128]{2,1,0:T(8,128)(2,1)S(1)}, u32[]{:S(2)}, u32[]{:S(2)}) collective-permute-start(bf16[3,272,128]{2,1,0:T(8,128)(2,1)S(1)} %get-tuple-element.67), channel_id=1, source_target_pairs={{0,4},{2,6},{4,0},{6,2},{8,12},{10,14},{12,8},{14,10},{16,20},{18,... | collective-permute-start | bytes 626696 | tf_op jit(solution)/shard_map/ppermute | solution.py:354
  11.7 9.6 %collective-permute-start.5 = (bf16[272,128]{1,0:T(8,128)(2,1)S(1)}, bf16[272,128]{1,0:T(8,128)(2,1)S(1)}, u32[]{:S(2)}, u32[]{:S(2)}) collective-permute-start(bf16[272,128]{1,0:T(8,128)(2,1)S(1)} %get-tuple-element.69), channel_id=1, source_target_pairs={{0,16},{2,18},{4,20},{6,22},{8,24},{10,26},{12,28},{14,30},{16,0},... | collective-permute-start | bytes 208904 | tf_op jit(solution)/shard_map/ppermute | solution.py:356
  14.2 7.0 %collective-permute-start.6 = (bf16[272,128]{1,0:T(8,128)(2,1)S(1)}, bf16[272,128]{1,0:T(8,128)(2,1)S(1)}, u32[]{:S(2)}, u32[]{:S(2)}) collective-permute-start(bf16[272,128]{1,0:T(8,128)(2,1)S(1)} %get-tuple-element.70), channel_id=1, source_target_pairs={{0,20},{2,22},{4,16},{6,18},{8,28},{10,30},{12,24},{14,26},{16,4},... | collective-permute-start | bytes 208904 | tf_op jit(solution)/shard_map/ppermute | solution.py:356
  17.4 6.9 %collective-permute-start.7 = (bf16[272,128]{1,0:T(8,128)(2,1)S(1)}, bf16[272,128]{1,0:T(8,128)(2,1)S(1)}, u32[]{:S(2)}, u32[]{:S(2)}) collective-permute-start(bf16[272,128]{1,0:T(8,128)(2,1)S(1)} %get-tuple-element.71), channel_id=1, source_target_pairs={{0,8},{2,10},{4,12},{6,14},{8,16},{10,18},{12,20},{14,22},{16,24},... | collective-permute-start | bytes 208904 | tf_op jit(solution)/shard_map/ppermute | solution.py:362
  19.0 5.7 %collective-permute-start.8 = (bf16[272,128]{1,0:T(8,128)(2,1)S(1)}, bf16[272,128]{1,0:T(8,128)(2,1)S(1)}, u32[]{:S(2)}, u32[]{:S(2)}) collective-permute-start(bf16[272,128]{1,0:T(8,128)(2,1)S(1)} %get-tuple-element.72), channel_id=1, source_target_pairs={{0,24},{2,26},{4,28},{6,30},{8,0},{10,2},{12,4},{14,6},{16,8},{18,... | collective-permute-start | bytes 208904 | tf_op jit(solution)/shard_map/ppermute | solution.py:362

commit v20 on v17

--- a/solution.py
+++ b/solution.py
@@ -104,13 +104,13 @@
         ],
         axis=0,
     )
-    spread = (rows, band_width)
+    spread = (rows, tile_width)
     scales = jnp.broadcast_to(scales, spread)
     scale_out[...] = scales[:, :lanes]
     pulls = jnp.broadcast_to(pulls, spread)
     waits = jnp.broadcast_to(waits, spread)
     fetches[5].wait()
-    for cut in cuts(width, band_width):
+    for cut in cuts(width, tile_width):
         scaled = gain[:, cut]
         for part in blocks:
             unit = x[part, cut].astype(f32) * scales[part]

time: 26.1 us -> 26.1 us (level)
  no operation moved by 1% of the time
where the time goes in v20:
time: 26.1 us; the launch traced here: 25.9 us
  starting transfers between devices  11.9 us (46%)
  waiting for transfers between devices  7.71 us (30%)
  Pallas kernels  5.61 us (21%)
  between operations  0.68 us (3%)
    ppermute x2, starting transfers between devices, plane_parts(): arrived.append(lax.ppermute(part, 'dp', along(offset, 0)))  3.88 us
    ppermute x2, waiting for transfers between devices, plane_parts(): arrived.append(lax.ppermute(part, 'dp', along(offset, 0)))  3.44 us
    pallas_call x1, Pallas kernels, branch_rows(): pl.pallas_call(functools.partial(branch_kernel, low), in_specs=[pl.BlockS...  3.29 us
    ppermute x1, starting transfers between devices, shards(): landed = lax.ppermute(packed, 'section', hops)  3 us
    ppermute x2, starting transfers between devices, plane_parts(): lax.ppermute(straight[2 * k + side], 'dp', along(offset, side))  2.87 us
    ppermute x1, waiting for transfers between devices, plane_parts(): across = lax.ppermute(give, 'dp', along(0, 1))  2.82 us
    ppermute x1, starting transfers between devices, plane_parts(): across = lax.ppermute(give, 'dp', along(0, 1))  1.59 us
    ppermute x2, waiting for transfers between devices, weight_owned(): lax.ppermute(part, 'dp', [(i, i ^ 1) for i in range(owners)])  1.45 us
  transfers between devices with their start and end apart: 8, of which 4 were waited for; matrix products, arithmetic and copies ran while one was open for 0% of the time, Pallas kernels for 4%

profile of v20, /device:TPU:0, one launch (start us, length us, event | category | flops | bytes accessed | tf_op | source)
XLA Modules:
  0.0 25.9 jit_solution(6971438584704897995)
XLA Ops:
  0.6 3.3 %shard_map.77 = (bf16[96,4096]{1,0:T(8,128)(2,1)S(1)}, f32[128,4096]{1,0:T(8,128)S(1)}, bf16[128,96]{1,0:T(8,128)(2,1)S(1)}, s32[1]{0:T(128)S(4)}, bf16[128,128]...) custom-call(s32[8]{0:T(128)} %counts_far.1, ...), custom_call_target="tpu_custom_call" | custom-call | flops 1048576 | bytes 65536 | tf_op jit(solution)/shard_map/pallas_call | solution.py:128
  3.9 3.0 %collective-permute-start.1 = (bf16[96,4096]{1,0:T(8,128)(2,1)S(1)}, bf16[96,4096]{1,0:T(8,128)(2,1)S(1)}, u32[]{:S(2)}, u32[]{:S(2)}) collective-permute-start(bf16[96,4096]{1,0:T(8,128)(2,1)S(1)} %get-tuple-element.55), channel_id=1, source_target_pairs={{1,0},{0,1},{3,2},{2,3},{5,4},{4,5},{7,6},{6,7},{9,8},{8,9},{11,10... | collective-permute-start | bytes 2359304 | tf_op jit(solution)/shard_map/ppermute | solution.py:398
  6.9 0.8 %shard_map.78 = (f32[8,272,128]{2,1,0:T(8,128)S(1)}, bf16[8,128,128]{2,1,0:T(8,128)(2,1)S(1)}, bf16[8,144,128]{2,1,0:T(8,128)(2,1)S(1)}) custom-call(bf16[128,128]{1,0:T(8,128)(2,1)S(1)} %get-tuple-element.58.masked, bf16[128,4096]{1,0:T(8,128)(2,1)S(1)} %get-tuple-element.59.x, f32[128,4096]{1,0:T(8,128)S(1)} %get-tuple-element.60.back, ...), custom_call_target="tpu_custom_call" | custom-call | flops 1048576 | bytes 65536 | tf_op jit(solution)/shard_map/pallas_call | solution.py:265
  7.8 0.1 collective-permute-start.3
  7.8 0.5 %collective-permute-start.2 = (bf16[8,128,128]{2,1,0:T(8,128)(2,1)S(1)}, bf16[8,128,128]{2,1,0:T(8,128)(2,1)S(1)}, u32[]{:S(2)}, u32[]{:S(2)}) collective-permute-start(bf16[8,128,128]{2,1,0:T(8,128)(2,1)S(1)} %get-tuple-element.64), channel_id=1, source_target_pairs={{0,2},{2,0},{4,6},{6,4},{8,10},{10,8},{12,14},{14,12},{16,18},{18,... | collective-permute-start | bytes 786440 | tf_op jit(solution)/shard_map/ppermute | solution.py:378
  8.3 1.4 %collective-permute-done.2.taken = bf16[8,128,128]{2,1,0:T(8,128)(2,1)S(1)} collective-permute-done((bf16[8,128,128]{2,1,0:T(8,128)(2,1)S(1)}, bf16[8,128,128]{2,1,0:T(8,128)(2,1)S(1)}, u32[]{:S(2)}, u32[]{:S(2)}) %collective-permute-start.2) | collective-permute-done | bytes 262176 | tf_op jit(solution)/shard_map/ppermute | solution.py:378
  9.8 0.0 collective-permute-done.3.taken_low
  9.8 0.1 shard_map.79
  9.9 1.6 %collective-permute-start.4 = (bf16[3,272,128]{2,1,0:T(8,128)(2,1)S(1)}, bf16[3,272,128]{2,1,0:T(8,128)(2,1)S(1)}, u32[]{:S(2)}, u32[]{:S(2)}) collective-permute-start(bf16[3,272,128]{2,1,0:T(8,128)(2,1)S(1)} %get-tuple-element.67), channel_id=1, source_target_pairs={{0,4},{2,6},{4,0},{6,2},{8,12},{10,14},{12,8},{14,10},{16,20},{18,... | collective-permute-start | bytes 626696 | tf_op jit(solution)/shard_map/ppermute | solution.py:353
  11.5 2.6 %collective-permute-start.5 = (bf16[272,128]{1,0:T(8,128)(2,1)S(1)}, bf16[272,128]{1,0:T(8,128)(2,1)S(1)}, u32[]{:S(2)}, u32[]{:S(2)}) collective-permute-start(bf16[272,128]{1,0:T(8,128)(2,1)S(1)} %get-tuple-element.69), channel_id=1, source_target_pairs={{0,16},{2,18},{4,20},{6,22},{8,24},{10,26},{12,28},{14,30},{16,0},... | collective-permute-start | bytes 208904 | tf_op jit(solution)/shard_map/ppermute | solution.py:355
  14.1 0.3 %collective-permute-start.6 = (bf16[272,128]{1,0:T(8,128)(2,1)S(1)}, bf16[272,128]{1,0:T(8,128)(2,1)S(1)}, u32[]{:S(2)}, u32[]{:S(2)}) collective-permute-start(bf16[272,128]{1,0:T(8,128)(2,1)S(1)} %get-tuple-element.70), channel_id=1, source_target_pairs={{0,20},{2,22},{4,16},{6,18},{8,28},{10,30},{12,24},{14,26},{16,4},... | collective-permute-start | bytes 208904 | tf_op jit(solution)/shard_map/ppermute | solution.py:355
  14.4 2.8 %collective-permute-done.4.taken = bf16[3,272,128]{2,1,0:T(8,128)(2,1)S(1)} collective-permute-done((bf16[3,272,128]{2,1,0:T(8,128)(2,1)S(1)}, bf16[3,272,128]{2,1,0:T(8,128)(2,1)S(1)}, u32[]{:S(2)}, u32[]{:S(2)}) %collective-permute-start.4) | collective-permute-done | bytes 208928 | tf_op jit(solution)/shard_map/ppermute | solution.py:353
  17.2 1.6 %collective-permute-start.7 = (bf16[272,128]{1,0:T(8,128)(2,1)S(1)}, bf16[272,128]{1,0:T(8,128)(2,1)S(1)}, u32[]{:S(2)}, u32[]{:S(2)}) collective-permute-start(bf16[272,128]{1,0:T(8,128)(2,1)S(1)} %get-tuple-element.71), channel_id=1, source_target_pairs={{0,8},{2,10},{4,12},{6,14},{8,16},{10,18},{12,20},{14,22},{16,24},... | collective-permute-start | bytes 208904 | tf_op jit(solution)/shard_map/ppermute | solution.py:361
  18.8 2.3 %collective-permute-start.8 = (bf16[272,128]{1,0:T(8,128)(2,1)S(1)}, bf16[272,128]{1,0:T(8,128)(2,1)S(1)}, u32[]{:S(2)}, u32[]{:S(2)}) collective-permute-start(bf16[272,128]{1,0:T(8,128)(2,1)S(1)} %get-tuple-element.72), channel_id=1, source_target_pairs={{0,24},{2,26},{4,28},{6,30},{8,0},{10,2},{12,4},{14,6},{16,8},{18,... | collective-permute-start | bytes 208904 | tf_op jit(solution)/shard_map/ppermute | solution.py:361
  21.1 0.0 collective-permute-done.5.refs_1_
  21.1 0.0 collective-permute-done.6.refs_2_
  21.1 3.0 %collective-permute-done.7.refs_3_ = bf16[272,128]{1,0:T(8,128)(2,1)S(1)} collective-permute-done((bf16[272,128]{1,0:T(8,128)(2,1)S(1)}, bf16[272,128]{1,0:T(8,128)(2,1)S(1)}, u32[]{:S(2)}, u32[]{:S(2)}) %collective-permute-start.7) | collective-permute-done | bytes 69664 | tf_op jit(solution)/shard_map/ppermute | solution.py:361
  24.1 0.4 %collective-permute-done.8.refs_4_ = bf16[272,128]{1,0:T(8,128)(2,1)S(1)} collective-permute-done((bf16[272,128]{1,0:T(8,128)(2,1)S(1)}, bf16[272,128]{1,0:T(8,128)(2,1)S(1)}, u32[]{:S(2)}, u32[]{:S(2)}) %collective-permute-start.8) | collective-permute-done | bytes 69664 | tf_op jit(solution)/shard_map/ppermute | solution.py:361
  24.5 0.0 collective-permute-done.1.received
  24.5 1.3 %shard_map.81 = (bf16[1,128,4096]{2,1,0:T(8,128)(2,1)}, s32[1]{0:T(128)S(4)}, f32[1,33024]{1,0:T(1,128)}) custom-call(bf16[128,96]{1,0:T(8,128)(2,1)S(1)} %get-tuple-element.54.scatter, bf16[96,4096]{1,0:T(8,128)(2,1)S(1)} %collective-permute-done.1.received, f32[128,4096]{1,0:T(8,128)S(1)} %get-tuple-element.56.addend, s32[1]{0:T(128)S(4)} %get-tuple-element.57.more, ...), custom_call_target="tpu_custom_call" | custom-call | flops 1048576 | bytes 65536 | tf_op jit(solution)/shard_map/pallas_call | solution.py:212
  (2 shorter events, 0.0 us)
Async XLA Ops:
  3.9 20.6 %collective-permute-start.1 = (bf16[96,4096]{1,0:T(8,128)(2,1)S(1)}, bf16[96,4096]{1,0:T(8,128)(2,1)S(1)}, u32[]{:S(2)}, u32[]{:S(2)}) collective-permute-start(bf16[96,4096]{1,0:T(8,128)(2,1)S(1)} %get-tuple-element.55), channel_id=1, source_target_pairs={{1,0},{0,1},{3,2},{2,3},{5,4},{4,5},{7,6},{6,7},{9,8},{8,9},{11,10... | collective-permute-start | bytes 2359304 | tf_op jit(solution)/shard_map/ppermute | solution.py:398
  7.8 2.0 %collective-permute-start.3 = (bf16[8,144,128]{2,1,0:T(8,128)(2,1)S(1)}, bf16[8,144,128]{2,1,0:T(8,128)(2,1)S(1)}, u32[]{:S(2)}, u32[]{:S(2)}) collective-permute-start(bf16[8,144,128]{2,1,0:T(8,128)(2,1)S(1)} %get-tuple-element.65), channel_id=1, source_target_pairs={{0,2},{2,0},{4,6},{6,4},{8,10},{10,8},{12,14},{14,12},{16,18},{18,... | collective-permute-start | bytes 884744 | tf_op jit(solution)/shard_map/ppermute | solution.py:378
  7.8 1.9 %collective-permute-start.2 = (bf16[8,128,128]{2,1,0:T(8,128)(2,1)S(1)}, bf16[8,128,128]{2,1,0:T(8,128)(2,1)S(1)}, u32[]{:S(2)}, u32[]{:S(2)}) collective-permute-start(bf16[8,128,128]{2,1,0:T(8,128)(2,1)S(1)} %get-tuple-element.64), channel_id=1, source_target_pairs={{0,2},{2,0},{4,6},{6,4},{8,10},{10,8},{12,14},{14,12},{16,18},{18,... | collective-permute-start | bytes 786440 | tf_op jit(solution)/shard_map/ppermute | solution.py:378
  9.9 7.3 %collective-permute-start.4 = (bf16[3,272,128]{2,1,0:T(8,128)(2,1)S(1)}, bf16[3,272,128]{2,1,0:T(8,128)(2,1)S(1)}, u32[]{:S(2)}, u32[]{:S(2)}) collective-permute-start(bf16[3,272,128]{2,1,0:T(8,128)(2,1)S(1)} %get-tuple-element.67), channel_id=1, source_target_pairs={{0,4},{2,6},{4,0},{6,2},{8,12},{10,14},{12,8},{14,10},{16,20},{18,... | collective-permute-start | bytes 626696 | tf_op jit(solution)/shard_map/ppermute | solution.py:353
  11.5 9.6 %collective-permute-start.5 = (bf16[272,128]{1,0:T(8,128)(2,1)S(1)}, bf16[272,128]{1,0:T(8,128)(2,1)S(1)}, u32[]{:S(2)}, u32[]{:S(2)}) collective-permute-start(bf16[272,128]{1,0:T(8,128)(2,1)S(1)} %get-tuple-element.69), channel_id=1, source_target_pairs={{0,16},{2,18},{4,20},{6,22},{8,24},{10,26},{12,28},{14,30},{16,0},... | collective-permute-start | bytes 208904 | tf_op jit(solution)/shard_map/ppermute | solution.py:355
  14.1 7.0 %collective-permute-start.6 = (bf16[272,128]{1,0:T(8,128)(2,1)S(1)}, bf16[272,128]{1,0:T(8,128)(2,1)S(1)}, u32[]{:S(2)}, u32[]{:S(2)}) collective-permute-start(bf16[272,128]{1,0:T(8,128)(2,1)S(1)} %get-tuple-element.70), channel_id=1, source_target_pairs={{0,20},{2,22},{4,16},{6,18},{8,28},{10,30},{12,24},{14,26},{16,4},... | collective-permute-start | bytes 208904 | tf_op jit(solution)/shard_map/ppermute | solution.py:355
  17.2 6.9 %collective-permute-start.7 = (bf16[272,128]{1,0:T(8,128)(2,1)S(1)}, bf16[272,128]{1,0:T(8,128)(2,1)S(1)}, u32[]{:S(2)}, u32[]{:S(2)}) collective-permute-start(bf16[272,128]{1,0:T(8,128)(2,1)S(1)} %get-tuple-element.71), channel_id=1, source_target_pairs={{0,8},{2,10},{4,12},{6,14},{8,16},{10,18},{12,20},{14,22},{16,24},... | collective-permute-start | bytes 208904 | tf_op jit(solution)/shard_map/ppermute | solution.py:361
  18.8 5.7 %collective-permute-start.8 = (bf16[272,128]{1,0:T(8,128)(2,1)S(1)}, bf16[272,128]{1,0:T(8,128)(2,1)S(1)}, u32[]{:S(2)}, u32[]{:S(2)}) collective-permute-start(bf16[272,128]{1,0:T(8,128)(2,1)S(1)} %get-tuple-element.72), channel_id=1, source_target_pairs={{0,24},{2,26},{4,28},{6,30},{8,0},{10,2},{12,4},{14,6},{16,8},{18,... | collective-permute-start | bytes 208904 | tf_op jit(solution)/shard_map/ppermute | solution.py:361

commit v21 on v17

--- a/solution.py
+++ b/solution.py
@@ -180,10 +180,6 @@
     more_out[0] = more[0]
     place = scatter[...]
     writes = []
-    if first and parts:
-        total_rows(factor, owned, *parts)
-        writes.append(pltpu.make_async_copy(owned, owned_far, done.at[width // tile_width]))
-        writes[0].start()
     if not first:
         here = (lax.axis_index("section") == target).astype(f32)
         covered = jnp.sum(place.astype(f32), axis=1, keepdims=True) * here > 0.5
@@ -195,6 +191,10 @@
         write = pltpu.make_async_copy(out.at[:, cut], out_far.at[0, :, cut], done.at[k])
         write.start()
         writes.append(write)
+    if first and parts:
+        total_rows(factor, owned, *parts)
+        writes.append(pltpu.make_async_copy(owned, owned_far, done.at[width // tile_width]))
+        writes[-1].start()
     for write in writes:
         write.wait()
 

time: 26.1 us -> 26 us (level)
  no operation moved by 1% of the time
where the time goes in v21:
time: 26 us; the launch traced here: 25.8 us
  starting transfers between devices  11.9 us (46%)
  waiting for transfers between devices  7.71 us (30%)
  Pallas kernels  5.52 us (21%)
  between operations  0.68 us (3%)
    ppermute x2, starting transfers between devices, plane_parts(): arrived.append(lax.ppermute(part, 'dp', along(offset, 0)))  3.88 us
    ppermute x2, waiting for transfers between devices, plane_parts(): arrived.append(lax.ppermute(part, 'dp', along(offset, 0)))  3.43 us
    pallas_call x1, Pallas kernels, branch_rows(): pl.pallas_call(functools.partial(branch_kernel, low), in_specs=[pl.BlockS...  3.28 us
    ppermute x1, starting transfers between devices, shards(): landed = lax.ppermute(packed, 'section', hops)  3 us
    ppermute x2, starting transfers between devices, plane_parts(): lax.ppermute(straight[2 * k + side], 'dp', along(offset, side))  2.87 us
    ppermute x1, waiting for transfers between devices, plane_parts(): across = lax.ppermute(give, 'dp', along(0, 1))  2.82 us
    ppermute x1, starting transfers between devices, plane_parts(): across = lax.ppermute(give, 'dp', along(0, 1))  1.58 us
    ppermute x2, waiting for transfers between devices, weight_owned(): lax.ppermute(part, 'dp', [(i, i ^ 1) for i in range(owners)])  1.45 us
  transfers between devices with their start and end apart: 8, of which 4 were waited for; matrix products, arithmetic and copies ran while one was open for 0% of the time, Pallas kernels for 4%

profile of v21, /device:TPU:0, one launch (start us, length us, event | category | flops | bytes accessed | tf_op | source)
XLA Modules:
  0.0 25.8 jit_solution(11648932867110514912)
XLA Ops:
  0.6 3.3 %shard_map.77 = (bf16[96,4096]{1,0:T(8,128)(2,1)S(1)}, f32[128,4096]{1,0:T(8,128)S(1)}, bf16[128,96]{1,0:T(8,128)(2,1)S(1)}, s32[1]{0:T(128)S(4)}, bf16[128,128]...) custom-call(s32[8]{0:T(128)} %counts_far.1, ...), custom_call_target="tpu_custom_call" | custom-call | flops 1048576 | bytes 65536 | tf_op jit(solution)/shard_map/pallas_call | solution.py:128
  3.9 3.0 %collective-permute-start.1 = (bf16[96,4096]{1,0:T(8,128)(2,1)S(1)}, bf16[96,4096]{1,0:T(8,128)(2,1)S(1)}, u32[]{:S(2)}, u32[]{:S(2)}) collective-permute-start(bf16[96,4096]{1,0:T(8,128)(2,1)S(1)} %get-tuple-element.55), channel_id=1, source_target_pairs={{1,0},{0,1},{3,2},{2,3},{5,4},{4,5},{7,6},{6,7},{9,8},{8,9},{11,10... | collective-permute-start | bytes 2359304 | tf_op jit(solution)/shard_map/ppermute | solution.py:398
  6.9 0.8 %shard_map.78 = (f32[8,272,128]{2,1,0:T(8,128)S(1)}, bf16[8,128,128]{2,1,0:T(8,128)(2,1)S(1)}, bf16[8,144,128]{2,1,0:T(8,128)(2,1)S(1)}) custom-call(bf16[128,128]{1,0:T(8,128)(2,1)S(1)} %get-tuple-element.58.masked, bf16[128,4096]{1,0:T(8,128)(2,1)S(1)} %get-tuple-element.59.x, f32[128,4096]{1,0:T(8,128)S(1)} %get-tuple-element.60.back, ...), custom_call_target="tpu_custom_call" | custom-call | flops 1048576 | bytes 65536 | tf_op jit(solution)/shard_map/pallas_call | solution.py:265
  7.8 0.1 collective-permute-start.3
  7.8 0.5 %collective-permute-start.2 = (bf16[8,128,128]{2,1,0:T(8,128)(2,1)S(1)}, bf16[8,128,128]{2,1,0:T(8,128)(2,1)S(1)}, u32[]{:S(2)}, u32[]{:S(2)}) collective-permute-start(bf16[8,128,128]{2,1,0:T(8,128)(2,1)S(1)} %get-tuple-element.64), channel_id=1, source_target_pairs={{0,2},{2,0},{4,6},{6,4},{8,10},{10,8},{12,14},{14,12},{16,18},{18,... | collective-permute-start | bytes 786440 | tf_op jit(solution)/shard_map/ppermute | solution.py:378
  8.3 1.4 %collective-permute-done.2.taken = bf16[8,128,128]{2,1,0:T(8,128)(2,1)S(1)} collective-permute-done((bf16[8,128,128]{2,1,0:T(8,128)(2,1)S(1)}, bf16[8,128,128]{2,1,0:T(8,128)(2,1)S(1)}, u32[]{:S(2)}, u32[]{:S(2)}) %collective-permute-start.2) | collective-permute-done | bytes 262176 | tf_op jit(solution)/shard_map/ppermute | solution.py:378
  9.8 0.0 collective-permute-done.3.taken_low
  9.8 0.1 shard_map.79
  9.9 1.6 %collective-permute-start.4 = (bf16[3,272,128]{2,1,0:T(8,128)(2,1)S(1)}, bf16[3,272,128]{2,1,0:T(8,128)(2,1)S(1)}, u32[]{:S(2)}, u32[]{:S(2)}) collective-permute-start(bf16[3,272,128]{2,1,0:T(8,128)(2,1)S(1)} %get-tuple-element.67), channel_id=1, source_target_pairs={{0,4},{2,6},{4,0},{6,2},{8,12},{10,14},{12,8},{14,10},{16,20},{18,... | collective-permute-start | bytes 626696 | tf_op jit(solution)/shard_map/ppermute | solution.py:353
  11.5 2.6 %collective-permute-start.5 = (bf16[272,128]{1,0:T(8,128)(2,1)S(1)}, bf16[272,128]{1,0:T(8,128)(2,1)S(1)}, u32[]{:S(2)}, u32[]{:S(2)}) collective-permute-start(bf16[272,128]{1,0:T(8,128)(2,1)S(1)} %get-tuple-element.69), channel_id=1, source_target_pairs={{0,16},{2,18},{4,20},{6,22},{8,24},{10,26},{12,28},{14,30},{16,0},... | collective-permute-start | bytes 208904 | tf_op jit(solution)/shard_map/ppermute | solution.py:355
  14.1 0.3 %collective-permute-start.6 = (bf16[272,128]{1,0:T(8,128)(2,1)S(1)}, bf16[272,128]{1,0:T(8,128)(2,1)S(1)}, u32[]{:S(2)}, u32[]{:S(2)}) collective-permute-start(bf16[272,128]{1,0:T(8,128)(2,1)S(1)} %get-tuple-element.70), channel_id=1, source_target_pairs={{0,20},{2,22},{4,16},{6,18},{8,28},{10,30},{12,24},{14,26},{16,4},... | collective-permute-start | bytes 208904 | tf_op jit(solution)/shard_map/ppermute | solution.py:355
  14.4 2.8 %collective-permute-done.4.taken = bf16[3,272,128]{2,1,0:T(8,128)(2,1)S(1)} collective-permute-done((bf16[3,272,128]{2,1,0:T(8,128)(2,1)S(1)}, bf16[3,272,128]{2,1,0:T(8,128)(2,1)S(1)}, u32[]{:S(2)}, u32[]{:S(2)}) %collective-permute-start.4) | collective-permute-done | bytes 208928 | tf_op jit(solution)/shard_map/ppermute | solution.py:353
  17.2 1.6 %collective-permute-start.7 = (bf16[272,128]{1,0:T(8,128)(2,1)S(1)}, bf16[272,128]{1,0:T(8,128)(2,1)S(1)}, u32[]{:S(2)}, u32[]{:S(2)}) collective-permute-start(bf16[272,128]{1,0:T(8,128)(2,1)S(1)} %get-tuple-element.71), channel_id=1, source_target_pairs={{0,8},{2,10},{4,12},{6,14},{8,16},{10,18},{12,20},{14,22},{16,24},... | collective-permute-start | bytes 208904 | tf_op jit(solution)/shard_map/ppermute | solution.py:361
  18.8 2.3 %collective-permute-start.8 = (bf16[272,128]{1,0:T(8,128)(2,1)S(1)}, bf16[272,128]{1,0:T(8,128)(2,1)S(1)}, u32[]{:S(2)}, u32[]{:S(2)}) collective-permute-start(bf16[272,128]{1,0:T(8,128)(2,1)S(1)} %get-tuple-element.72), channel_id=1, source_target_pairs={{0,24},{2,26},{4,28},{6,30},{8,0},{10,2},{12,4},{14,6},{16,8},{18,... | collective-permute-start | bytes 208904 | tf_op jit(solution)/shard_map/ppermute | solution.py:361
  21.1 0.0 collective-permute-done.5.refs_1_
  21.1 0.0 collective-permute-done.6.refs_2_
  21.1 3.0 %collective-permute-done.7.refs_3_ = bf16[272,128]{1,0:T(8,128)(2,1)S(1)} collective-permute-done((bf16[272,128]{1,0:T(8,128)(2,1)S(1)}, bf16[272,128]{1,0:T(8,128)(2,1)S(1)}, u32[]{:S(2)}, u32[]{:S(2)}) %collective-permute-start.7) | collective-permute-done | bytes 69664 | tf_op jit(solution)/shard_map/ppermute | solution.py:361
  24.1 0.4 %collective-permute-done.8.refs_4_ = bf16[272,128]{1,0:T(8,128)(2,1)S(1)} collective-permute-done((bf16[272,128]{1,0:T(8,128)(2,1)S(1)}, bf16[272,128]{1,0:T(8,128)(2,1)S(1)}, u32[]{:S(2)}, u32[]{:S(2)}) %collective-permute-start.8) | collective-permute-done | bytes 69664 | tf_op jit(solution)/shard_map/ppermute | solution.py:361
  24.5 0.0 collective-permute-done.1.received
  24.5 1.3 %shard_map.81 = (bf16[1,128,4096]{2,1,0:T(8,128)(2,1)}, s32[1]{0:T(128)S(4)}, f32[1,33024]{1,0:T(1,128)}) custom-call(bf16[128,96]{1,0:T(8,128)(2,1)S(1)} %get-tuple-element.54.scatter, bf16[96,4096]{1,0:T(8,128)(2,1)S(1)} %collective-permute-done.1.received, f32[128,4096]{1,0:T(8,128)S(1)} %get-tuple-element.56.addend, s32[1]{0:T(128)S(4)} %get-tuple-element.57.more, ...), custom_call_target="tpu_custom_call" | custom-call | flops 1048576 | bytes 65536 | tf_op jit(solution)/shard_map/pallas_call | solution.py:212
  (2 shorter events, 0.0 us)
Async XLA Ops:
  3.9 20.6 %collective-permute-start.1 = (bf16[96,4096]{1,0:T(8,128)(2,1)S(1)}, bf16[96,4096]{1,0:T(8,128)(2,1)S(1)}, u32[]{:S(2)}, u32[]{:S(2)}) collective-permute-start(bf16[96,4096]{1,0:T(8,128)(2,1)S(1)} %get-tuple-element.55), channel_id=1, source_target_pairs={{1,0},{0,1},{3,2},{2,3},{5,4},{4,5},{7,6},{6,7},{9,8},{8,9},{11,10... | collective-permute-start | bytes 2359304 | tf_op jit(solution)/shard_map/ppermute | solution.py:398
  7.8 2.0 %collective-permute-start.3 = (bf16[8,144,128]{2,1,0:T(8,128)(2,1)S(1)}, bf16[8,144,128]{2,1,0:T(8,128)(2,1)S(1)}, u32[]{:S(2)}, u32[]{:S(2)}) collective-permute-start(bf16[8,144,128]{2,1,0:T(8,128)(2,1)S(1)} %get-tuple-element.65), channel_id=1, source_target_pairs={{0,2},{2,0},{4,6},{6,4},{8,10},{10,8},{12,14},{14,12},{16,18},{18,... | collective-permute-start | bytes 884744 | tf_op jit(solution)/shard_map/ppermute | solution.py:378
  7.8 1.9 %collective-permute-start.2 = (bf16[8,128,128]{2,1,0:T(8,128)(2,1)S(1)}, bf16[8,128,128]{2,1,0:T(8,128)(2,1)S(1)}, u32[]{:S(2)}, u32[]{:S(2)}) collective-permute-start(bf16[8,128,128]{2,1,0:T(8,128)(2,1)S(1)} %get-tuple-element.64), channel_id=1, source_target_pairs={{0,2},{2,0},{4,6},{6,4},{8,10},{10,8},{12,14},{14,12},{16,18},{18,... | collective-permute-start | bytes 786440 | tf_op jit(solution)/shard_map/ppermute | solution.py:378
  9.9 7.3 %collective-permute-start.4 = (bf16[3,272,128]{2,1,0:T(8,128)(2,1)S(1)}, bf16[3,272,128]{2,1,0:T(8,128)(2,1)S(1)}, u32[]{:S(2)}, u32[]{:S(2)}) collective-permute-start(bf16[3,272,128]{2,1,0:T(8,128)(2,1)S(1)} %get-tuple-element.67), channel_id=1, source_target_pairs={{0,4},{2,6},{4,0},{6,2},{8,12},{10,14},{12,8},{14,10},{16,20},{18,... | collective-permute-start | bytes 626696 | tf_op jit(solution)/shard_map/ppermute | solution.py:353
  11.5 9.6 %collective-permute-start.5 = (bf16[272,128]{1,0:T(8,128)(2,1)S(1)}, bf16[272,128]{1,0:T(8,128)(2,1)S(1)}, u32[]{:S(2)}, u32[]{:S(2)}) collective-permute-start(bf16[272,128]{1,0:T(8,128)(2,1)S(1)} %get-tuple-element.69), channel_id=1, source_target_pairs={{0,16},{2,18},{4,20},{6,22},{8,24},{10,26},{12,28},{14,30},{16,0},... | collective-permute-start | bytes 208904 | tf_op jit(solution)/shard_map/ppermute | solution.py:355
  14.1 7.0 %collective-permute-start.6 = (bf16[272,128]{1,0:T(8,128)(2,1)S(1)}, bf16[272,128]{1,0:T(8,128)(2,1)S(1)}, u32[]{:S(2)}, u32[]{:S(2)}) collective-permute-start(bf16[272,128]{1,0:T(8,128)(2,1)S(1)} %get-tuple-element.70), channel_id=1, source_target_pairs={{0,20},{2,22},{4,16},{6,18},{8,28},{10,30},{12,24},{14,26},{16,4},... | collective-permute-start | bytes 208904 | tf_op jit(solution)/shard_map/ppermute | solution.py:355
  17.2 6.9 %collective-permute-start.7 = (bf16[272,128]{1,0:T(8,128)(2,1)S(1)}, bf16[272,128]{1,0:T(8,128)(2,1)S(1)}, u32[]{:S(2)}, u32[]{:S(2)}) collective-permute-start(bf16[272,128]{1,0:T(8,128)(2,1)S(1)} %get-tuple-element.71), channel_id=1, source_target_pairs={{0,8},{2,10},{4,12},{6,14},{8,16},{10,18},{12,20},{14,22},{16,24},... | collective-permute-start | bytes 208904 | tf_op jit(solution)/shard_map/ppermute | solution.py:361
  18.8 5.7 %collective-permute-start.8 = (bf16[272,128]{1,0:T(8,128)(2,1)S(1)}, bf16[272,128]{1,0:T(8,128)(2,1)S(1)}, u32[]{:S(2)}, u32[]{:S(2)}) collective-permute-start(bf16[272,128]{1,0:T(8,128)(2,1)S(1)} %get-tuple-element.72), channel_id=1, source_target_pairs={{0,24},{2,26},{4,28},{6,30},{8,0},{10,2},{12,4},{14,6},{16,8},{18,... | collective-permute-start | bytes 208904 | tf_op jit(solution)/shard_map/ppermute | solution.py:361
